TPU v7x, 32 devices: a whole 2x2x4 slice. The times are simulated.
32 devices in a mesh: row: 8 (over z, y), col: 4 (over x, core).
Axes of the slice: x: 2, y: 2, z: 4, core: 2. Of those that a mesh axis runs over, the one named last changes fastest.
Arguments:
- delta: bfloat16 [16384, 7168], P('row', 'col'), may hold values from -0.0625 to 0.0625
- omega: bfloat16 [7168, 256], P('col'), may hold values from -6 to 6
Outputs:
- sketch: float32 [16384, 256], P('row')
- corange: float32 [7168, 256], P('col', 'row')
All inputs are finite; a program needn't handle non-finite values.
Results may differ from a plain program's by a relative error of at most 0.0016.
Values sent between devices are 32-bit elements; how exact they have to be, the bound alone decides.
No kernel may reach another device: no remote copies, remote signals or barrier semaphores. Data moves between devices by JAX's collectives and lax.ppermute only.
A program may use at most 64 MiB of HBM per device.

v0:
```python
import jax
import jax.numpy as jnp
from jax import lax
from jax.sharding import PartitionSpec as P


def shards(delta, omega):
    partial_value = jnp.dot(delta, omega, preferred_element_type=jnp.float32)
    sketch = lax.psum(partial_value, "col")
    sketch_half = sketch.astype(jnp.bfloat16)
    local_terms = lax.dot_general(
        delta, sketch_half, (((0,), (0,)), ((), ())), preferred_element_type=jnp.float32
    )
    corange = lax.psum_scatter(local_terms, "row", scatter_dimension=1, tiled=True)
    return (sketch, corange)


def solution(mesh):
    in_specs = (P("row", "col"), P("col", None))
    out_specs = (P("row", None), P("col", "row"))
    return jax.shard_map(shards, mesh=mesh, in_specs=in_specs, out_specs=out_specs, check_vma=False)
```

profile of v0, /device:TPU:0, one launch (start us, length us, event | category | flops | bytes accessed | tf_op | source)
XLA Modules:
  0.0 151.0 jit_solution(17823707091142445850)
XLA Ops:
  7.2 0.0 copy-start
  7.2 0.0 all-reduce.2.cloned.1.call-start
  7.2 1.1 copy-done
  8.3 6.5 %fusion.1 = f32[2048,256]{1,0:T(8,128)} fusion(bf16[2048,1792]{1,0:T(8,128)(2,1)} %param.2, bf16[1792,256]{1,0:T(8,128)(2,1)S(1)} %copy-done), kind=kOutput, calls=%fused_computation.2 | convolution fusion | flops 1879048192 | bytes 10354688 | tf_op jit(solution)/shard_map/dot_general | solution.py:8
  14.8 0.0 all-reduce.2.cloned.1.call-update
  14.8 0.0 reduce-scatter.2.cloned.1.call-start
  14.9 54.2 %all-reduce.2.cloned.1.call-done = f32[2048,256]{1,0:T(8,128)} async-done(((f32[2048,256]{1,0:T(8,128)}), f32[2048,256]{1,0:T(8,128)}) %all-reduce.2.cloned.1.call-update) | async-done | bytes 2097168 | tf_op jit(solution)/shard_map/psum | solution.py:9
  69.1 0.0 copy-start.1
  69.1 7.2 %convolution_bitcast_fusion = f32[1792,256]{0,1:T(8,128)} fusion(bf16[2048,1792]{1,0:T(8,128)(2,1)} %param.2, f32[2048,256]{1,0:T(8,128)} %all-reduce.2.cloned.1.call-done), kind=kOutput, calls=%fused_computation | convolution fusion | flops 1879572480 | bytes 11272192 | tf_op jit(solution)/shard_map/dot_general | solution.py:11
  76.3 0.0 reduce-scatter.2.cloned.1.call-update
  76.3 66.6 %reduce-scatter.2.cloned.1.call-done = f32[1792,32]{0,1:T(8,128)} async-done(((f32[1792,256]{0,1:T(8,128)}), f32[1792,32]{0,1:T(8,128)}) %reduce-scatter.2.cloned.1.call-update) | async-done | bytes 229392 | tf_op jit(solution)/shard_map/reduce_scatter | solution.py:14
  142.9 0.0 copy-done.1
  142.9 1.3 copy.5
Async XLA Ops:
  7.2 1.2 copy-start
  7.2 61.9 %all-reduce.2.cloned.1.call-start = ((), (), s32[]{:S(2)}) async-start(), calls=%async_computation.1 | async-start | bytes 4194304 | tf_op jit(solution)/shard_map/psum | solution.py:9
  14.8 128.0 %reduce-scatter.2.cloned.1.call-start = ((), (), s32[]{:S(2)}) async-start(), calls=%async_computation.2 | async-start | bytes 2064384 | tf_op jit(solution)/shard_map/reduce_scatter | solution.py:14
  69.1 73.8 %copy-start.1 = (f32[2048,256]{1,0:T(8,128)S(1)}, f32[2048,256]{1,0:T(8,128)}, u32[]{:S(2)}) copy-start(f32[2048,256]{1,0:T(8,128)} %all-reduce.2.cloned.1.call-done) | copy-start | bytes 6291460
Sparse Core Ops, SparseCore 0:
  15.0 54.0 all-reduce.1
  76.4 66.4 reduce-scatter.1
where the time goes:
time: 151 us
  waiting for transfers between devices  121 us (80%)
  between operations  14 us (9%)
  matrix products  13.7 us (9%)
  local copies, waits for them, and re-layouts  2.45 us (2%)
    reduce_scatter x1, waiting for transfers between devices, shards(): lax.psum_scatter(local_terms, 'row', scatter_dimension=1, tiled=True)  66.6 us
    psum x1, waiting for transfers between devices, shards(): sketch = lax.psum(partial_value, 'col')  54.2 us
    dot_general x1, matrix products, shards(): lax.dot_general(delta, sketch_half, (((0,), (0,)), ((), ())), preferred_e...  7.19 us
    dot_general x1, matrix products, shards(): partial_value = jnp.dot(delta, omega, preferred_element_type=jnp.float32)  6.48 us
  transfers between devices with their start and end apart: 2, of which 2 were waited for; matrix products, arithmetic and copies ran while one was open for 0% of the time, Pallas kernels for 0%

commit v1 on v0

v1 whole, which is shorter than its diff:
```python
import functools

import jax
import jax.numpy as jnp
from jax import lax
from jax.experimental import pallas as pl
from jax.experimental.pallas import tpu as pltpu
from jax.sharding import PartitionSpec as P

CHUNKS = 4
BLOCK = 256
F32 = jnp.float32
BF16 = jnp.bfloat16
NT = (((1,), (1,)), ((), ()))
NN = (((1,), (0,)), ((), ()))


def vmem(shape, dtype=F32):
    return pltpu.VMEM(shape, dtype)


def call(body, ins, outs, scratch=(), flops=0, moved=0, limit=16):
    spec = {"v": pl.BlockSpec(memory_space=pltpu.VMEM), "a": pl.BlockSpec(memory_space=pl.ANY)}
    return pl.pallas_call(
        body,
        out_shape=[vmem(*shape) for shape in outs],
        in_specs=[spec[kind] for kind in ins],
        out_specs=[spec["v"]] * len(outs),
        scratch_shapes=list(scratch),
        cost_estimate=pl.CostEstimate(flops=flops, bytes_accessed=moved, transcendentals=0),
        compiler_params=pltpu.CompilerParams(vmem_limit_bytes=limit << 20),
    )


def column_of(position, k, chunks, n_row):
    width = k // chunks
    mine = k // n_row
    piece = mine // chunks
    chunk, rest = position // width, position % width
    low, rest = rest // (width // 2), rest % (width // 2)
    high, j = rest // piece, rest % piece
    return (2 * high + low) * mine + chunk * piece + j


def stream_half(delta, held, sem, first, rows):
    copies = []
    for b in range(rows // BLOCK):
        copies.append(
            pltpu.make_async_copy(
                delta.at[pl.ds(pl.multiple_of(first + b * BLOCK, BLOCK), BLOCK), :],
                held.at[pl.ds(b * BLOCK, BLOCK), :],
                sem.at[b],
            )
        )
        copies[-1].start()
    return copies


def send_half_body(n_row, delta, omega, held, omega_t, out, omega_v, sem, omega_sem):
    rows, k = held.shape[0], omega_t.shape[0]
    other = 1 - lax.rem(lax.axis_index("col"), 2)
    fetch = pltpu.make_async_copy(omega, omega_v, omega_sem)
    fetch.start()
    copies = stream_half(delta, held, sem, other * rows, rows)
    position = lax.broadcasted_iota(jnp.int32, (k, k), 0)
    column = lax.broadcasted_iota(jnp.int32, (k, k), 1)
    pick = jnp.where(column_of(position, k, CHUNKS, n_row) == column, 1.0, 0.0).astype(BF16)
    fetch.wait()
    omega_t[...] = lax.dot_general(pick, omega_v[...], NT, preferred_element_type=F32).astype(BF16)
    for b, copy in enumerate(copies):
        copy.wait()
        block = pl.ds(b * BLOCK, BLOCK)
        out[:, block] = lax.dot_general(omega_t[...], held[block, :], NT, preferred_element_type=F32)


def keep_half_body(delta, omega_t, held, out, sem):
    rows = held.shape[0]
    copies = stream_half(delta, held, sem, lax.rem(lax.axis_index("col"), 2) * rows, rows)
    for b, copy in enumerate(copies):
        copy.wait()
        block = pl.ds(b * BLOCK, BLOCK)
        out[:, block] = lax.dot_general(omega_t[...], held[block, :], NT, preferred_element_type=F32)


def add_chunks_body(kept, received, *outs):
    width = outs[0].shape[0]
    for c, out in enumerate(outs):
        part = pl.ds(c * width, width)
        out[...] = kept[part, :] + received[part, :]


def add_body(a, b, out):
    out[...] = a[...] + b[...]


def corange_body(own, other, held_own, held_other, send, keep):
    half = send.shape[0]
    low = lax.rem(lax.axis_index("row"), 2)
    theirs = pl.ds(pl.multiple_of((1 - low) * half, half), half)
    mine = pl.ds(pl.multiple_of(low * half, half), half)

    def ordered(ref):
        return jnp.concatenate([ref[theirs, :], ref[mine, :]], axis=0).astype(BF16)

    total = lax.dot_general(ordered(own), held_own[...], NN, preferred_element_type=F32)
    total += lax.dot_general(ordered(other), held_other[...], NN, preferred_element_type=F32)
    send[...] = total[:half]
    keep[...] = total[half:]


def split_high_body(n_high, kept, received, *outs):
    width = outs[0].shape[0]
    high = lax.axis_index("row") // 2
    for d, out in enumerate(outs):
        part = pl.ds(pl.multiple_of(lax.rem(high + d, n_high) * width, width), width)
        out[...] = kept[part, :] + received[part, :]


def final_corange_body(chunks, *refs):
    out = refs[-1]
    per = (len(refs) - 1) // chunks
    width = refs[0].shape[0]
    for c in range(chunks):
        parts = refs[c * per : (c + 1) * per]
        total = parts[0][...]
        for part in parts[1:]:
            total += part[...]
        out[pl.ds(c * width, width), :] = total


def final_sketch_body(chunks, n_row, *refs):
    out = refs[-1]
    rows = refs[0].shape[1]
    width = refs[0].shape[0]
    piece = width // n_row
    parity = lax.rem(lax.axis_index("col"), 2)
    for side in range(2):
        parts = refs[side * chunks : (side + 1) * chunks]
        first = (parity if side == 0 else 1 - parity) * rows
        for b in range(rows // 128):
            lanes = pl.ds(b * 128, 128)
            pieces = []
            for r in range(n_row):
                start = (r % 2) * (width // 2) + (r // 2) * piece
                for part in parts:
                    pieces.append(part[pl.ds(start, piece), lanes])
            block = jnp.concatenate(pieces, axis=0)
            out[pl.ds(pl.multiple_of(first + b * 128, 128), 128), :] = block.T


def swap(x, axis, size, bit):
    return lax.ppermute(x, axis, [(i, i ^ bit) for i in range(size)])


def shards(n_row, n_col, delta, omega):
    rows, d = delta.shape
    k = omega.shape[1]
    half = rows // 2
    width = k // CHUNKS
    n_high = n_row // 2
    piece = width // n_row
    blocks = half // BLOCK
    mm = 2 * half * d * k

    held_other, omega_t, to_send = call(
        functools.partial(send_half_body, n_row),
        "aa",
        [((half, d), BF16), ((k, d), BF16), ((k, half),)],
        [pltpu.VMEM((d, k), BF16), pltpu.SemaphoreType.DMA((blocks,)), pltpu.SemaphoreType.DMA],
        mm,
        2 * half * d,
    )(delta, omega)
    received = swap(to_send, "col", n_col, 1)
    held_own, kept = call(
        keep_half_body,
        "av",
        [((half, d), BF16), ((k, half),)],
        [pltpu.SemaphoreType.DMA((blocks,))],
        mm,
        2 * half * d,
    )(delta, omega_t)
    partial = call(add_chunks_body, "vv", [((width, half),)] * CHUNKS, (), k * half, 12 * k * half)(kept, received)
    owns, others = [], []
    terms = []
    bit = 2
    while bit < n_col:
        moved = [swap(x, "col", n_col, bit) for x in partial]
        partial = [call(add_body, "vv", [((width, half),)], (), width * half, 12 * width * half)(a, b)[0] for a, b in zip(partial, moved)]
        bit *= 2
    for own in partial:
        other = swap(own, "col", n_col, 1)
        owns.append(own)
        others.append(other)
        send, keep = call(
            corange_body,
            "vvvv",
            [((width // 2, d),), ((width // 2, d),)],
            (),
            4 * half * d * width,
            4 * half * d,
        )(own, other, held_own, held_other)
        got = swap(send, "row", n_row, 1)
        if piece % 8 == 0:
            parts = call(
                functools.partial(split_high_body, n_high),
                "vv",
                [((piece, d),)] * n_high,
                (),
                width * d,
                6 * width * d,
            )(keep, got)
        else:
            total = keep + got
            high = lax.axis_index("row") // 2
            parts = [lax.dynamic_slice_in_dim(total, lax.rem(high + i, n_high) * piece, piece, 0) for i in range(n_high)]
        parts = list(parts)
        for shift in range(1, n_high):
            pairs = [(r, 2 * ((r // 2 + shift) % n_high) + r % 2) for r in range(n_row)]
            parts[shift] = lax.ppermute(parts[shift], "row", pairs)
        terms.append(parts)

    if piece % 8 == 0:
        flat = [x for parts in terms for x in parts]
        corange = pl.pallas_call(
            functools.partial(final_corange_body, CHUNKS),
            out_shape=jax.ShapeDtypeStruct((k // n_row, d), F32),
        )(*flat)
        sketch = pl.pallas_call(
            functools.partial(final_sketch_body, CHUNKS, n_row),
            out_shape=jax.ShapeDtypeStruct((rows, k), F32),
        )(*owns, *others)
    else:
        corange = jnp.concatenate([functools.reduce(jnp.add, parts) for parts in terms], axis=0)
        parity = lax.rem(lax.axis_index("col"), 2)

        def columns(parts):
            stacked = jnp.stack(parts).reshape(CHUNKS, 2, n_high, piece, half)
            return stacked.transpose(4, 2, 1, 0, 3).reshape(half, k)

        own, other = columns(owns), columns(others)
        sketch = jnp.where(parity == 0, jnp.concatenate([own, other]), jnp.concatenate([other, own]))
    return sketch, corange.T


def solution(mesh):
    body = functools.partial(shards, mesh.shape["row"], mesh.shape["col"])
    in_specs = (P("row", "col"), P("col", None))
    out_specs = (P("row", None), P("col", "row"))
    return jax.shard_map(body, mesh=mesh, in_specs=in_specs, out_specs=out_specs, check_vma=False)
```

time: 151 us -> 84.3 us (0.56)
  waiting for transfers between devices: 121 us -> 25.4 us
  starting transfers between devices: 0.08 us -> 32.9 us
  Pallas kernels: 0 us -> 19 us
  matrix products: 13.7 us -> 0 us
  between operations: 14 us -> 1.04 us
  local copies, waits for them, and re-layouts: 2.45 us -> 5.53 us
    reduce_scatter x1 -> x0, waiting for transfers between devices: 66.6 us -> none  [shards(): lax.psum_scatter(local_terms, 'row', scatter_dimension=1, tiled=True)]
    psum x1 -> x0, waiting for transfers between devices: 54.2 us -> none  [shards(): sketch = lax.psum(partial_value, 'col')]
    ppermute x0 -> x25, starting transfers between devices: none -> 32.9 us  [the longest x12 23.1 us: shards(): parts[shift] = lax.ppermute(parts[shift], 'row', pairs)]
    ppermute x0 -> x25, waiting for transfers between devices: none -> 25.4 us  [the longest x13 25.4 us: swap(): return lax.ppermute(x, axis, [(i, i ^ bit) for i in range(size)])]
    pallas_call x0 -> x17, Pallas kernels: none -> 19 us  [the longest x4 5.5 us: shards(): call(corange_body, 'vvvv', [((width // 2, d),), ((width // 2, d),)], (),...]
    dot_general x2 -> x0, matrix products: 13.7 us -> none  [the longest x1 7.19 us: shards(): lax.dot_general(delta, sketch_half, (((0,), (0,)), ((), ())), preferred_e...]
    unnamed x5 -> x52, local copies, waits for them, and re-layouts: 2.45 us -> 5.53 us
  transfers between devices with their start and end apart: 2 -> 25, of which waited for: 2 -> 7; matrix products, arithmetic and copies ran while one was open for 0% -> 0% of each run, Pallas kernels for 0% -> 15%
where the time goes in v1:
time: 84.3 us; the launch traced here: 84 us
  starting transfers between devices  32.9 us (39%)
  waiting for transfers between devices  25.4 us (30%)
  Pallas kernels  19 us (23%)
  local copies, waits for them, and re-layouts  5.53 us (7%)
  between operations  1.04 us (1%)
    ppermute x13, waiting for transfers between devices, swap(): return lax.ppermute(x, axis, [(i, i ^ bit) for i in range(size)])  25.4 us
    ppermute x12, starting transfers between devices, shards(): parts[shift] = lax.ppermute(parts[shift], 'row', pairs)  23.1 us
    ppermute x13, starting transfers between devices, swap(): return lax.ppermute(x, axis, [(i, i ^ bit) for i in range(size)])  9.8 us
    unnamed x52, local copies, waits for them, and re-layouts  5.53 us
    pallas_call x4, Pallas kernels, shards(): call(corange_body, 'vvvv', [((width // 2, d),), ((width // 2, d),)], (),...  5.5 us
    pallas_call x1, Pallas kernels, shards(): call(functools.partial(send_half_body, n_row), 'aa', [((half, d), BF16),...  4.32 us
    pallas_call x1, Pallas kernels, shards(): call(keep_half_body, 'av', [((half, d), BF16), ((k, half),)], [pltpu.Sema...  3.54 us
    pallas_call x1, Pallas kernels, shards(): pl.pallas_call(functools.partial(final_sketch_body, CHUNKS, n_row), out_s...  3.43 us
  transfers between devices with their start and end apart: 25, of which 7 were waited for; matrix products, arithmetic and copies ran while one was open for 0% of the time, Pallas kernels for 15%

profile of v1, /device:TPU:0, one launch (start us, length us, event | category | flops | bytes accessed | tf_op | source)
XLA Modules:
  0.0 84.0 jit_solution(8325484615585880256)
XLA Ops:
  0.6 3.1 %copy-done = bf16[2048,1792]{1,0:T(8,128)(2,1)S(1)} copy-done((bf16[2048,1792]{1,0:T(8,128)(2,1)S(1)}, bf16[2048,1792]{1,0:T(8,128)(2,1)}, u32[]{:S(2)}) %copy-start) | copy-done | bytes 7340056
  3.7 1.2 %copy-done.9 = bf16[1792,256]{1,0:T(8,128)(2,1)S(1)} copy-done((bf16[1792,256]{1,0:T(8,128)(2,1)S(1)}, bf16[1792,256]{1,0:T(8,128)(2,1)}, u32[]{:S(2)}) %copy-start.9) | copy-done | bytes 917528
  4.9 4.3 %shard_map.41 = (bf16[1024,1792]{1,0:T(8,128)(2,1)S(1)}, bf16[256,1792]{1,0:T(8,128)(2,1)S(1)}, f32[256,1024]{1,0:T(8,128)S(1)}) custom-call(bf16[2048,1792]{1,0:T(8,128)(2,1)S(1)} %copy-done, bf16[1792,256]{1,0:T(8,128)(2,1)S(1)} %copy-done.9), custom_call_target="tpu_custom_call" | custom-call | flops 939524096 | bytes 3670016 | tf_op jit(solution)/shard_map/pallas_call | solution.py:165
  9.7 3.5 %shard_map.42 = (bf16[1024,1792]{1,0:T(8,128)(2,1)S(1)}, f32[256,1024]{1,0:T(8,128)S(1)}) custom-call(bf16[2048,1792]{1,0:T(8,128)(2,1)S(1)} %copy-done, bf16[256,1792]{1,0:T(8,128)(2,1)S(1)} %get-tuple-element.35.omega_t), custom_call_target="tpu_custom_call" | custom-call | flops 939524096 | bytes 3670016 | tf_op jit(solution)/shard_map/pallas_call | solution.py:174
  13.4 2.6 %collective-permute-start.4 = (f32[64,1024]{1,0:T(8,128)S(1)}, f32[64,1024]{1,0:T(8,128)S(1)}, u32[]{:S(2)}, u32[]{:S(2)}) collective-permute-start(f32[64,1024]{1,0:T(8,128)S(1)} %get-tuple-element.41.a), channel_id=1, source_target_pairs={{0,2},{1,3},{2,0},{3,1},{4,6},{5,7},{6,4},{7,5},{8,10},{9,11},{10,... | collective-permute-start | bytes 786440 | tf_op jit(solution)/shard_map/ppermute | solution.py:152
  16.1 1.9 %collective-permute-start.2 = (f32[64,1024]{1,0:T(8,128)S(1)}, f32[64,1024]{1,0:T(8,128)S(1)}, u32[]{:S(2)}, u32[]{:S(2)}) collective-permute-start(f32[64,1024]{1,0:T(8,128)S(1)} %get-tuple-element.39.a), channel_id=1, source_target_pairs={{0,2},{1,3},{2,0},{3,1},{4,6},{5,7},{6,4},{7,5},{8,10},{9,11},{10,... | collective-permute-start | bytes 786440 | tf_op jit(solution)/shard_map/ppermute | solution.py:152
  18.1 5.1 %collective-permute-done.4.b = f32[64,1024]{1,0:T(8,128)S(1)} collective-permute-done((f32[64,1024]{1,0:T(8,128)S(1)}, f32[64,1024]{1,0:T(8,128)S(1)}, u32[]{:S(2)}, u32[]{:S(2)}) %collective-permute-start.4) | collective-permute-done | bytes 262176 | tf_op jit(solution)/shard_map/ppermute | solution.py:152
  23.3 5.5 %collective-permute-done.3.b = f32[64,1024]{1,0:T(8,128)S(1)} collective-permute-done((f32[64,1024]{1,0:T(8,128)S(1)}, f32[64,1024]{1,0:T(8,128)S(1)}, u32[]{:S(2)}, u32[]{:S(2)}) %collective-permute-start.3) | collective-permute-done | bytes 262176 | tf_op jit(solution)/shard_map/ppermute | solution.py:152
  28.9 5.5 %collective-permute-done.2.b = f32[64,1024]{1,0:T(8,128)S(1)} collective-permute-done((f32[64,1024]{1,0:T(8,128)S(1)}, f32[64,1024]{1,0:T(8,128)S(1)}, u32[]{:S(2)}, u32[]{:S(2)}) %collective-permute-start.2) | collective-permute-done | bytes 262176 | tf_op jit(solution)/shard_map/ppermute | solution.py:152
  34.5 5.3 %collective-permute-done.1.b = f32[64,1024]{1,0:T(8,128)S(1)} collective-permute-done((f32[64,1024]{1,0:T(8,128)S(1)}, f32[64,1024]{1,0:T(8,128)S(1)}, u32[]{:S(2)}, u32[]{:S(2)}) %collective-permute-start.1) | collective-permute-done | bytes 262176 | tf_op jit(solution)/shard_map/ppermute | solution.py:152
  39.9 1.4 %shard_map.55 = (f32[32,1792]{1,0:T(8,128)S(1)}, f32[32,1792]{1,0:T(8,128)S(1)}) custom-call(f32[64,1024]{1,0:T(8,128)S(1)} %shard_map.47.refs_3_.own, f32[64,1024]{1,0:T(8,128)S(1)} %collective-permute-done.8.refs_7_.other, bf16[1024,1792]{1,0:T(8,128)(2,1)S(1)} %get-tuple-element.42.held_own, bf16[1024,1792]{1,0:T(8,128)(2,1)S(1)} %get-tuple-element.43.held_other), custom_call_target="tpu_custom_call" | custom-call | flops 469762048 | bytes 7340032 | tf_op jit(solution)/shard_map/pallas_call | solution.py:194
  41.3 1.8 %collective-permute-start.21 = (f32[32,1792]{1,0:T(8,128)S(1)}, f32[32,1792]{1,0:T(8,128)S(1)}, u32[]{:S(2)}, u32[]{:S(2)}) collective-permute-start(f32[32,1792]{1,0:T(8,128)S(1)} %get-tuple-element.63), channel_id=1, source_target_pairs={{0,4},{4,0},{8,12},{12,8},{16,20},{20,16},{24,28},{28,24},{1,5},{5... | collective-permute-start | bytes 688136 | tf_op jit(solution)/shard_map/ppermute | solution.py:152
  43.2 1.4 %shard_map.53 = (f32[32,1792]{1,0:T(8,128)S(1)}, f32[32,1792]{1,0:T(8,128)S(1)}) custom-call(f32[64,1024]{1,0:T(8,128)S(1)} %shard_map.46.refs_2_.own, f32[64,1024]{1,0:T(8,128)S(1)} %collective-permute-done.7.refs_6_.other, bf16[1024,1792]{1,0:T(8,128)(2,1)S(1)} %get-tuple-element.42.held_own, bf16[1024,1792]{1,0:T(8,128)(2,1)S(1)} %get-tuple-element.43.held_other), custom_call_target="tpu_custom_call" | custom-call | flops 469762048 | bytes 7340032 | tf_op jit(solution)/shard_map/pallas_call | solution.py:194
  44.9 1.4 %shard_map.51 = (f32[32,1792]{1,0:T(8,128)S(1)}, f32[32,1792]{1,0:T(8,128)S(1)}) custom-call(f32[64,1024]{1,0:T(8,128)S(1)} %shard_map.45.refs_1_.own, f32[64,1024]{1,0:T(8,128)S(1)} %collective-permute-done.6.refs_5_.other, bf16[1024,1792]{1,0:T(8,128)(2,1)S(1)} %get-tuple-element.42.held_own, bf16[1024,1792]{1,0:T(8,128)(2,1)S(1)} %get-tuple-element.43.held_other), custom_call_target="tpu_custom_call" | custom-call | flops 469762048 | bytes 7340032 | tf_op jit(solution)/shard_map/pallas_call | solution.py:194
  46.3 1.8 %collective-permute-start.13 = (f32[32,1792]{1,0:T(8,128)S(1)}, f32[32,1792]{1,0:T(8,128)S(1)}, u32[]{:S(2)}, u32[]{:S(2)}) collective-permute-start(f32[32,1792]{1,0:T(8,128)S(1)} %get-tuple-element.51), channel_id=1, source_target_pairs={{0,4},{4,0},{8,12},{12,8},{16,20},{20,16},{24,28},{28,24},{1,5},{5... | collective-permute-start | bytes 688136 | tf_op jit(solution)/shard_map/ppermute | solution.py:152
  48.2 1.4 %shard_map.49 = (f32[32,1792]{1,0:T(8,128)S(1)}, f32[32,1792]{1,0:T(8,128)S(1)}) custom-call(f32[64,1024]{1,0:T(8,128)S(1)} %shard_map.44.refs_0_.own, f32[64,1024]{1,0:T(8,128)S(1)} %collective-permute-done.5.refs_4_.other, bf16[1024,1792]{1,0:T(8,128)(2,1)S(1)} %get-tuple-element.42.held_own, bf16[1024,1792]{1,0:T(8,128)(2,1)S(1)} %get-tuple-element.43.held_other), custom_call_target="tpu_custom_call" | custom-call | flops 469762048 | bytes 7340032 | tf_op jit(solution)/shard_map/pallas_call | solution.py:194
  49.9 1.9 %collective-permute-start.22 = (f32[8,1792]{1,0:T(8,128)S(1)}, f32[8,1792]{1,0:T(8,128)S(1)}, u32[]{:S(2)}, u32[]{:S(2)}) collective-permute-start(f32[8,1792]{1,0:T(8,128)S(1)} %get-tuple-element.65), channel_id=1, source_target_pairs={{0,8},{4,12},{8,16},{12,20},{16,24},{20,28},{24,0},{28,4},{1,9},{5... | collective-permute-start | bytes 172040 | tf_op jit(solution)/shard_map/ppermute | solution.py:219
  51.8 2.6 %collective-permute-start.23 = (f32[8,1792]{1,0:T(8,128)S(1)}, f32[8,1792]{1,0:T(8,128)S(1)}, u32[]{:S(2)}, u32[]{:S(2)}) collective-permute-start(f32[8,1792]{1,0:T(8,128)S(1)} %get-tuple-element.66), channel_id=1, source_target_pairs={{0,16},{4,20},{8,24},{12,28},{16,0},{20,4},{24,8},{28,12},{1,17},{... | collective-permute-start | bytes 172040 | tf_op jit(solution)/shard_map/ppermute | solution.py:219
  54.7 3.9 %collective-permute-start.24 = (f32[8,1792]{1,0:T(8,128)S(1)}, f32[8,1792]{1,0:T(8,128)S(1)}, u32[]{:S(2)}, u32[]{:S(2)}) collective-permute-start(f32[8,1792]{1,0:T(8,128)S(1)} %get-tuple-element.67), channel_id=1, source_target_pairs={{0,24},{4,28},{8,0},{12,4},{16,8},{20,12},{24,16},{28,20},{1,25},{... | collective-permute-start | bytes 172040 | tf_op jit(solution)/shard_map/ppermute | solution.py:219
  58.6 1.0 %collective-permute-done.13.received = f32[32,1792]{1,0:T(8,128)S(1)} collective-permute-done((f32[32,1792]{1,0:T(8,128)S(1)}, f32[32,1792]{1,0:T(8,128)S(1)}, u32[]{:S(2)}, u32[]{:S(2)}) %collective-permute-start.13) | collective-permute-done | bytes 229408 | tf_op jit(solution)/shard_map/ppermute | solution.py:152
  59.6 1.8 %collective-permute-start.18 = (f32[8,1792]{1,0:T(8,128)S(1)}, f32[8,1792]{1,0:T(8,128)S(1)}, u32[]{:S(2)}, u32[]{:S(2)}) collective-permute-start(f32[8,1792]{1,0:T(8,128)S(1)} %get-tuple-element.59), channel_id=1, source_target_pairs={{0,8},{4,12},{8,16},{12,20},{16,24},{20,28},{24,0},{28,4},{1,9},{5... | collective-permute-start | bytes 172040 | tf_op jit(solution)/shard_map/ppermute | solution.py:219
  61.5 2.7 %collective-permute-done.9.received = f32[32,1792]{1,0:T(8,128)S(1)} collective-permute-done((f32[32,1792]{1,0:T(8,128)S(1)}, f32[32,1792]{1,0:T(8,128)S(1)}, u32[]{:S(2)}, u32[]{:S(2)}) %collective-permute-start.9) | collective-permute-done | bytes 229408 | tf_op jit(solution)/shard_map/ppermute | solution.py:152
  64.2 2.8 %collective-permute-start.19 = (f32[8,1792]{1,0:T(8,128)S(1)}, f32[8,1792]{1,0:T(8,128)S(1)}, u32[]{:S(2)}, u32[]{:S(2)}) collective-permute-start(f32[8,1792]{1,0:T(8,128)S(1)} %get-tuple-element.60), channel_id=1, source_target_pairs={{0,16},{4,20},{8,24},{12,28},{16,0},{20,4},{24,8},{28,12},{1,17},{... | collective-permute-start | bytes 172040 | tf_op jit(solution)/shard_map/ppermute | solution.py:219
  67.0 1.3 %collective-permute-start.20 = (f32[8,1792]{1,0:T(8,128)S(1)}, f32[8,1792]{1,0:T(8,128)S(1)}, u32[]{:S(2)}, u32[]{:S(2)}) collective-permute-start(f32[8,1792]{1,0:T(8,128)S(1)} %get-tuple-element.61), channel_id=1, source_target_pairs={{0,24},{4,28},{8,0},{12,4},{16,8},{20,12},{24,16},{28,20},{1,25},{... | collective-permute-start | bytes 172040 | tf_op jit(solution)/shard_map/ppermute | solution.py:219
  68.3 0.7 collective-permute-start.14
  69.1 0.6 copy-done.13
  69.7 1.1 %collective-permute-start.15 = (f32[8,1792]{1,0:T(8,128)S(1)}, f32[8,1792]{1,0:T(8,128)S(1)}, u32[]{:S(2)}, u32[]{:S(2)}) collective-permute-start(f32[8,1792]{1,0:T(8,128)S(1)} %get-tuple-element.54), channel_id=1, source_target_pairs={{0,16},{4,20},{8,24},{12,28},{16,0},{20,4},{24,8},{28,12},{1,17},{... | collective-permute-start | bytes 172040 | tf_op jit(solution)/shard_map/ppermute | solution.py:219
  70.8 2.9 %collective-permute-start.16 = (f32[8,1792]{1,0:T(8,128)S(1)}, f32[8,1792]{1,0:T(8,128)S(1)}, u32[]{:S(2)}, u32[]{:S(2)}) collective-permute-start(f32[8,1792]{1,0:T(8,128)S(1)} %get-tuple-element.55), channel_id=1, source_target_pairs={{0,24},{4,28},{8,0},{12,4},{16,8},{20,12},{24,16},{28,20},{1,25},{... | collective-permute-start | bytes 172040 | tf_op jit(solution)/shard_map/ppermute | solution.py:219
  73.7 2.7 %collective-permute-start.11 = (f32[8,1792]{1,0:T(8,128)S(1)}, f32[8,1792]{1,0:T(8,128)S(1)}, u32[]{:S(2)}, u32[]{:S(2)}) collective-permute-start(f32[8,1792]{1,0:T(8,128)S(1)} %get-tuple-element.48), channel_id=1, source_target_pairs={{0,16},{4,20},{8,24},{12,28},{16,0},{20,4},{24,8},{28,12},{1,17},{... | collective-permute-start | bytes 172040 | tf_op jit(solution)/shard_map/ppermute | solution.py:219
  76.5 1.4 %collective-permute-start.12 = (f32[8,1792]{1,0:T(8,128)S(1)}, f32[8,1792]{1,0:T(8,128)S(1)}, u32[]{:S(2)}, u32[]{:S(2)}) collective-permute-start(f32[8,1792]{1,0:T(8,128)S(1)} %get-tuple-element.49), channel_id=1, source_target_pairs={{0,24},{4,28},{8,0},{12,4},{16,8},{20,12},{24,16},{28,20},{1,25},{... | collective-permute-start | bytes 172040 | tf_op jit(solution)/shard_map/ppermute | solution.py:219
  77.9 3.4 %shard_map.48 = f32[2048,256]{1,0:T(8,128)} custom-call(f32[64,1024]{1,0:T(8,128)} %copy-done.4, f32[64,1024]{1,0:T(8,128)} %copy-done.3, f32[64,1024]{1,0:T(8,128)} %copy-done.2, f32[64,1024]{1,0:T(8,128)} %copy-done.1, f32[64,1024]{1,0:T(8,128)} %copy-done.8, f32[64,1024]{1,0:T(8,128)} %copy-done.7, f32[64,1024]{1,0:T(8,128)} %copy-done.6, ...), custom_call_target="tpu_custom_call" | custom-call | tf_op jit(solution)/shard_map/pallas_call | solution.py:228
  82.1 1.9 %shard_map.57 = f32[32,1792]{1,0:T(8,128)} custom-call(f32[8,1792]{1,0:T(8,128)} %copy-done.13, f32[8,1792]{1,0:T(8,128)} %copy-done.23, f32[8,1792]{1,0:T(8,128)} %copy-done.24, f32[8,1792]{1,0:T(8,128)} %copy-done.25, f32[8,1792]{1,0:T(8,128)} %copy-done.12, f32[8,1792]{1,0:T(8,128)} %copy-done.20, f32[8,1792]{1,0:T(8,128)} %copy-done.21, ...), custom_call_target="tpu_custom_call" | custom-call | tf_op jit(solution)/shard_map/pallas_call | solution.py:224
  (87 shorter events, 3.0 us)
Async XLA Ops:
  9.2 4.1 %collective-permute-start = (f32[256,1024]{1,0:T(8,128)S(1)}, f32[256,1024]{1,0:T(8,128)S(1)}, u32[]{:S(2)}, u32[]{:S(2)}) collective-permute-start(f32[256,1024]{1,0:T(8,128)S(1)} %get-tuple-element.37), channel_id=1, source_target_pairs={{0,1},{1,0},{2,3},{3,2},{4,5},{5,4},{6,7},{7,6},{8,9},{9,8},{10,11... | collective-permute-start | bytes 3145736 | tf_op jit(solution)/shard_map/ppermute | solution.py:152
  13.4 9.7 %collective-permute-start.4 = (f32[64,1024]{1,0:T(8,128)S(1)}, f32[64,1024]{1,0:T(8,128)S(1)}, u32[]{:S(2)}, u32[]{:S(2)}) collective-permute-start(f32[64,1024]{1,0:T(8,128)S(1)} %get-tuple-element.41.a), channel_id=1, source_target_pairs={{0,2},{1,3},{2,0},{3,1},{4,6},{5,7},{6,4},{7,5},{8,10},{9,11},{10,... | collective-permute-start | bytes 786440 | tf_op jit(solution)/shard_map/ppermute | solution.py:152
  16.0 12.8 %collective-permute-start.3 = (f32[64,1024]{1,0:T(8,128)S(1)}, f32[64,1024]{1,0:T(8,128)S(1)}, u32[]{:S(2)}, u32[]{:S(2)}) collective-permute-start(f32[64,1024]{1,0:T(8,128)S(1)} %get-tuple-element.40.a), channel_id=1, source_target_pairs={{0,2},{1,3},{2,0},{3,1},{4,6},{5,7},{6,4},{7,5},{8,10},{9,11},{10,... | collective-permute-start | bytes 786440 | tf_op jit(solution)/shard_map/ppermute | solution.py:152
  16.1 18.3 %collective-permute-start.2 = (f32[64,1024]{1,0:T(8,128)S(1)}, f32[64,1024]{1,0:T(8,128)S(1)}, u32[]{:S(2)}, u32[]{:S(2)}) collective-permute-start(f32[64,1024]{1,0:T(8,128)S(1)} %get-tuple-element.39.a), channel_id=1, source_target_pairs={{0,2},{1,3},{2,0},{3,1},{4,6},{5,7},{6,4},{7,5},{8,10},{9,11},{10,... | collective-permute-start | bytes 786440 | tf_op jit(solution)/shard_map/ppermute | solution.py:152
  18.0 21.8 %collective-permute-start.1 = (f32[64,1024]{1,0:T(8,128)S(1)}, f32[64,1024]{1,0:T(8,128)S(1)}, u32[]{:S(2)}, u32[]{:S(2)}) collective-permute-start(f32[64,1024]{1,0:T(8,128)S(1)} %get-tuple-element.38.a), channel_id=1, source_target_pairs={{0,2},{1,3},{2,0},{3,1},{4,6},{5,7},{6,4},{7,5},{8,10},{9,11},{10,... | collective-permute-start | bytes 786440 | tf_op jit(solution)/shard_map/ppermute | solution.py:152
  23.2 18.1 %copy-start.1 = (f32[64,1024]{1,0:T(8,128)}, f32[64,1024]{1,0:T(8,128)S(1)}, u32[]{:S(2)}) copy-start(f32[64,1024]{1,0:T(8,128)S(1)} %shard_map.47.refs_3_.own) | copy-start | bytes 786436
  23.2 16.7 %collective-permute-start.8 = (f32[64,1024]{1,0:T(8,128)S(1)}, f32[64,1024]{1,0:T(8,128)S(1)}, u32[]{:S(2)}, u32[]{:S(2)}) collective-permute-start(f32[64,1024]{1,0:T(8,128)S(1)} %shard_map.47.refs_3_.own), channel_id=1, source_target_pairs={{0,1},{1,0},{2,3},{3,2},{4,5},{5,4},{6,7},{7,6},{8,9},{9,8},{10,11... | collective-permute-start | bytes 786440 | tf_op jit(solution)/shard_map/ppermute | solution.py:152
  28.8 14.4 %copy-start.2 = (f32[64,1024]{1,0:T(8,128)}, f32[64,1024]{1,0:T(8,128)S(1)}, u32[]{:S(2)}) copy-start(f32[64,1024]{1,0:T(8,128)S(1)} %shard_map.46.refs_2_.own) | copy-start | bytes 786436
  28.8 14.4 %collective-permute-start.7 = (f32[64,1024]{1,0:T(8,128)S(1)}, f32[64,1024]{1,0:T(8,128)S(1)}, u32[]{:S(2)}, u32[]{:S(2)}) collective-permute-start(f32[64,1024]{1,0:T(8,128)S(1)} %shard_map.46.refs_2_.own), channel_id=1, source_target_pairs={{0,1},{1,0},{2,3},{3,2},{4,5},{5,4},{6,7},{7,6},{8,9},{9,8},{10,11... | collective-permute-start | bytes 786440 | tf_op jit(solution)/shard_map/ppermute | solution.py:152
  34.4 10.5 %collective-permute-start.6 = (f32[64,1024]{1,0:T(8,128)S(1)}, f32[64,1024]{1,0:T(8,128)S(1)}, u32[]{:S(2)}, u32[]{:S(2)}) collective-permute-start(f32[64,1024]{1,0:T(8,128)S(1)} %shard_map.45.refs_1_.own), channel_id=1, source_target_pairs={{0,1},{1,0},{2,3},{3,2},{4,5},{5,4},{6,7},{7,6},{8,9},{9,8},{10,11... | collective-permute-start | bytes 786440 | tf_op jit(solution)/shard_map/ppermute | solution.py:152
  39.8 8.3 %collective-permute-start.5 = (f32[64,1024]{1,0:T(8,128)S(1)}, f32[64,1024]{1,0:T(8,128)S(1)}, u32[]{:S(2)}, u32[]{:S(2)}) collective-permute-start(f32[64,1024]{1,0:T(8,128)S(1)} %shard_map.44.refs_0_.own), channel_id=1, source_target_pairs={{0,1},{1,0},{2,3},{3,2},{4,5},{5,4},{6,7},{7,6},{8,9},{9,8},{10,11... | collective-permute-start | bytes 786440 | tf_op jit(solution)/shard_map/ppermute | solution.py:152
  41.3 8.5 %collective-permute-start.21 = (f32[32,1792]{1,0:T(8,128)S(1)}, f32[32,1792]{1,0:T(8,128)S(1)}, u32[]{:S(2)}, u32[]{:S(2)}) collective-permute-start(f32[32,1792]{1,0:T(8,128)S(1)} %get-tuple-element.63), channel_id=1, source_target_pairs={{0,4},{4,0},{8,12},{12,8},{16,20},{20,16},{24,28},{28,24},{1,5},{5... | collective-permute-start | bytes 688136 | tf_op jit(solution)/shard_map/ppermute | solution.py:152
  44.6 10.1 %collective-permute-start.17 = (f32[32,1792]{1,0:T(8,128)S(1)}, f32[32,1792]{1,0:T(8,128)S(1)}, u32[]{:S(2)}, u32[]{:S(2)}) collective-permute-start(f32[32,1792]{1,0:T(8,128)S(1)} %get-tuple-element.57), channel_id=1, source_target_pairs={{0,4},{4,0},{8,12},{12,8},{16,20},{20,16},{24,28},{28,24},{1,5},{5... | collective-permute-start | bytes 688136 | tf_op jit(solution)/shard_map/ppermute | solution.py:152
  46.3 13.3 %collective-permute-start.13 = (f32[32,1792]{1,0:T(8,128)S(1)}, f32[32,1792]{1,0:T(8,128)S(1)}, u32[]{:S(2)}, u32[]{:S(2)}) collective-permute-start(f32[32,1792]{1,0:T(8,128)S(1)} %get-tuple-element.51), channel_id=1, source_target_pairs={{0,4},{4,0},{8,12},{12,8},{16,20},{20,16},{24,28},{28,24},{1,5},{5... | collective-permute-start | bytes 688136 | tf_op jit(solution)/shard_map/ppermute | solution.py:152
  49.5 14.6 %collective-permute-start.9 = (f32[32,1792]{1,0:T(8,128)S(1)}, f32[32,1792]{1,0:T(8,128)S(1)}, u32[]{:S(2)}, u32[]{:S(2)}) collective-permute-start(f32[32,1792]{1,0:T(8,128)S(1)} %get-tuple-element.45), channel_id=1, source_target_pairs={{0,4},{4,0},{8,12},{12,8},{16,20},{20,16},{24,28},{28,24},{1,5},{5... | collective-permute-start | bytes 688136 | tf_op jit(solution)/shard_map/ppermute | solution.py:152
  49.9 19.2 %copy-start.10 = (f32[8,1792]{1,0:T(8,128)}, f32[8,1792]{1,0:T(8,128)S(1)}, u32[]{:S(2)}) copy-start(f32[8,1792]{1,0:T(8,128)S(1)} %get-tuple-element.64.refs_12_) | copy-start | bytes 172036
  49.9 17.1 %collective-permute-start.22 = (f32[8,1792]{1,0:T(8,128)S(1)}, f32[8,1792]{1,0:T(8,128)S(1)}, u32[]{:S(2)}, u32[]{:S(2)}) collective-permute-start(f32[8,1792]{1,0:T(8,128)S(1)} %get-tuple-element.65), channel_id=1, source_target_pairs={{0,8},{4,12},{8,16},{12,20},{16,24},{20,28},{24,0},{28,4},{1,9},{5... | collective-permute-start | bytes 172040 | tf_op jit(solution)/shard_map/ppermute | solution.py:219
  51.8 16.6 %collective-permute-start.23 = (f32[8,1792]{1,0:T(8,128)S(1)}, f32[8,1792]{1,0:T(8,128)S(1)}, u32[]{:S(2)}, u32[]{:S(2)}) collective-permute-start(f32[8,1792]{1,0:T(8,128)S(1)} %get-tuple-element.66), channel_id=1, source_target_pairs={{0,16},{4,20},{8,24},{12,28},{16,0},{20,4},{24,8},{28,12},{1,17},{... | collective-permute-start | bytes 172040 | tf_op jit(solution)/shard_map/ppermute | solution.py:219
  54.7 15.0 %collective-permute-start.24 = (f32[8,1792]{1,0:T(8,128)S(1)}, f32[8,1792]{1,0:T(8,128)S(1)}, u32[]{:S(2)}, u32[]{:S(2)}) collective-permute-start(f32[8,1792]{1,0:T(8,128)S(1)} %get-tuple-element.67), channel_id=1, source_target_pairs={{0,24},{4,28},{8,0},{12,4},{16,8},{20,12},{24,16},{28,20},{1,25},{... | collective-permute-start | bytes 172040 | tf_op jit(solution)/shard_map/ppermute | solution.py:219
  58.6 11.1 %copy-start.11 = (f32[8,1792]{1,0:T(8,128)}, f32[8,1792]{1,0:T(8,128)S(1)}, u32[]{:S(2)}) copy-start(f32[8,1792]{1,0:T(8,128)S(1)} %get-tuple-element.58.refs_8_) | copy-start | bytes 172036
  59.6 11.2 %collective-permute-start.18 = (f32[8,1792]{1,0:T(8,128)S(1)}, f32[8,1792]{1,0:T(8,128)S(1)}, u32[]{:S(2)}, u32[]{:S(2)}) collective-permute-start(f32[8,1792]{1,0:T(8,128)S(1)} %get-tuple-element.59), channel_id=1, source_target_pairs={{0,8},{4,12},{8,16},{12,20},{16,24},{20,28},{24,0},{28,4},{1,9},{5... | collective-permute-start | bytes 172040 | tf_op jit(solution)/shard_map/ppermute | solution.py:219
  64.2 9.5 %collective-permute-start.19 = (f32[8,1792]{1,0:T(8,128)S(1)}, f32[8,1792]{1,0:T(8,128)S(1)}, u32[]{:S(2)}, u32[]{:S(2)}) collective-permute-start(f32[8,1792]{1,0:T(8,128)S(1)} %get-tuple-element.60), channel_id=1, source_target_pairs={{0,16},{4,20},{8,24},{12,28},{16,0},{20,4},{24,8},{28,12},{1,17},{... | collective-permute-start | bytes 172040 | tf_op jit(solution)/shard_map/ppermute | solution.py:219
  67.0 14.4 %copy-start.14 = (f32[8,1792]{1,0:T(8,128)}, f32[8,1792]{1,0:T(8,128)S(1)}, u32[]{:S(2)}) copy-start(f32[8,1792]{1,0:T(8,128)S(1)} %collective-permute-done.22.refs_13_) | copy-start | bytes 172036
  67.0 6.7 %collective-permute-start.20 = (f32[8,1792]{1,0:T(8,128)S(1)}, f32[8,1792]{1,0:T(8,128)S(1)}, u32[]{:S(2)}, u32[]{:S(2)}) collective-permute-start(f32[8,1792]{1,0:T(8,128)S(1)} %get-tuple-element.61), channel_id=1, source_target_pairs={{0,24},{4,28},{8,0},{12,4},{16,8},{20,12},{24,16},{28,20},{1,25},{... | collective-permute-start | bytes 172040 | tf_op jit(solution)/shard_map/ppermute | solution.py:219
  68.3 13.1 %copy-start.15 = (f32[8,1792]{1,0:T(8,128)}, f32[8,1792]{1,0:T(8,128)S(1)}, u32[]{:S(2)}) copy-start(f32[8,1792]{1,0:T(8,128)S(1)} %collective-permute-done.23.refs_14_) | copy-start | bytes 172036
  68.3 8.1 %collective-permute-start.14 = (f32[8,1792]{1,0:T(8,128)S(1)}, f32[8,1792]{1,0:T(8,128)S(1)}, u32[]{:S(2)}, u32[]{:S(2)}) collective-permute-start(f32[8,1792]{1,0:T(8,128)S(1)} %get-tuple-element.53), channel_id=1, source_target_pairs={{0,8},{4,12},{8,16},{12,20},{16,24},{20,28},{24,0},{28,4},{1,9},{5... | collective-permute-start | bytes 172040 | tf_op jit(solution)/shard_map/ppermute | solution.py:219
  69.7 11.7 %copy-start.16 = (f32[8,1792]{1,0:T(8,128)}, f32[8,1792]{1,0:T(8,128)S(1)}, u32[]{:S(2)}) copy-start(f32[8,1792]{1,0:T(8,128)S(1)} %collective-permute-done.24.refs_15_) | copy-start | bytes 172036
  69.7 11.6 %collective-permute-start.15 = (f32[8,1792]{1,0:T(8,128)S(1)}, f32[8,1792]{1,0:T(8,128)S(1)}, u32[]{:S(2)}, u32[]{:S(2)}) collective-permute-start(f32[8,1792]{1,0:T(8,128)S(1)} %get-tuple-element.54), channel_id=1, source_target_pairs={{0,16},{4,20},{8,24},{12,28},{16,0},{20,4},{24,8},{28,12},{1,17},{... | collective-permute-start | bytes 172040 | tf_op jit(solution)/shard_map/ppermute | solution.py:219
  70.8 10.5 %collective-permute-start.16 = (f32[8,1792]{1,0:T(8,128)S(1)}, f32[8,1792]{1,0:T(8,128)S(1)}, u32[]{:S(2)}, u32[]{:S(2)}) collective-permute-start(f32[8,1792]{1,0:T(8,128)S(1)} %get-tuple-element.55), channel_id=1, source_target_pairs={{0,24},{4,28},{8,0},{12,4},{16,8},{20,12},{24,16},{28,20},{1,25},{... | collective-permute-start | bytes 172040 | tf_op jit(solution)/shard_map/ppermute | solution.py:219
  73.7 7.6 %collective-permute-start.10 = (f32[8,1792]{1,0:T(8,128)S(1)}, f32[8,1792]{1,0:T(8,128)S(1)}, u32[]{:S(2)}, u32[]{:S(2)}) collective-permute-start(f32[8,1792]{1,0:T(8,128)S(1)} %get-tuple-element.47), channel_id=1, source_target_pairs={{0,8},{4,12},{8,16},{12,20},{16,24},{20,28},{24,0},{28,4},{1,9},{5... | collective-permute-start | bytes 172040 | tf_op jit(solution)/shard_map/ppermute | solution.py:219
  73.7 7.6 %collective-permute-start.11 = (f32[8,1792]{1,0:T(8,128)S(1)}, f32[8,1792]{1,0:T(8,128)S(1)}, u32[]{:S(2)}, u32[]{:S(2)}) collective-permute-start(f32[8,1792]{1,0:T(8,128)S(1)} %get-tuple-element.48), channel_id=1, source_target_pairs={{0,16},{4,20},{8,24},{12,28},{16,0},{20,4},{24,8},{28,12},{1,17},{... | collective-permute-start | bytes 172040 | tf_op jit(solution)/shard_map/ppermute | solution.py:219
  76.5 4.9 %collective-permute-start.12 = (f32[8,1792]{1,0:T(8,128)S(1)}, f32[8,1792]{1,0:T(8,128)S(1)}, u32[]{:S(2)}, u32[]{:S(2)}) collective-permute-start(f32[8,1792]{1,0:T(8,128)S(1)} %get-tuple-element.49), channel_id=1, source_target_pairs={{0,24},{4,28},{8,0},{12,4},{16,8},{20,12},{24,16},{28,20},{1,25},{... | collective-permute-start | bytes 172040 | tf_op jit(solution)/shard_map/ppermute | solution.py:219
  (19 other events, 71.8 us)

commit v2 on v0

v2 whole, which is shorter than its diff:
```python
import functools

import jax
import jax.numpy as jnp
from jax import lax
from jax.experimental import pallas as pl
from jax.experimental.pallas import tpu as pltpu
from jax.sharding import PartitionSpec as P

CHUNKS = 4
WEIGHTS = (20000000000, 2000000000, 4000000000, 4000000000, 4000000000, 100000000, 2000000000, 1000000000, 10000000000)
BLOCK = 256
F32 = jnp.float32
BF16 = jnp.bfloat16
SPECS = {
    "v": pl.BlockSpec(memory_space=pltpu.VMEM),
    "h": pl.BlockSpec(memory_space=pltpu.HBM),
    "a": pl.BlockSpec(memory_space=pl.ANY),
}


def call(body, args, outs, kinds=None, after=(), scratch=(), results=0, weight=0):
    n = len(args)
    kinds = (kinds or "v" * n) + "a" * len(after)

    def run(*refs):
        body(*refs[:n], *refs[len(kinds) :])

    return pl.pallas_call(
        run,
        out_shape=[pltpu.VMEM(*o) if i >= results else jax.ShapeDtypeStruct(*o) for i, o in enumerate(outs)],
        in_specs=[SPECS[kind] for kind in kinds],
        out_specs=[SPECS["v"]] * len(outs),
        scratch_shapes=list(scratch),
        cost_estimate=pl.CostEstimate(flops=weight, bytes_accessed=0, transcendentals=0),
        compiler_params=pltpu.CompilerParams(vmem_limit_bytes=16 << 20),
    )(*args, *after)


def owner_at(index, n_row):
    owner, bit = 0, 1
    while bit < n_row:
        owner = 2 * owner + index % 2
        index //= 2
        bit *= 2
    return owner


def sketch_half_body(n_row, mine, delta, omega, held, out, omega_v, sem, omega_sem):
    rows, k = held.shape[0], out.shape[0]
    parity = lax.rem(lax.axis_index("col"), 2)
    first = (parity if mine else 1 - parity) * rows
    fetch = pltpu.make_async_copy(omega, omega_v, omega_sem)
    fetch.start()
    copies = []
    for b in range(rows // BLOCK):
        source = delta.at[pl.ds(pl.multiple_of(first + b * BLOCK, BLOCK), BLOCK), :]
        copies.append(pltpu.make_async_copy(source, held.at[pl.ds(b * BLOCK, BLOCK), :], sem.at[b]))
        copies[-1].start()
    fetch.wait()
    per_owner = k // n_row
    piece = per_owner // CHUNKS
    for b, copy in enumerate(copies):
        copy.wait()
        lanes = pl.ds(b * BLOCK, BLOCK)
        turned = jnp.dot(held[lanes, :], omega_v[...], preferred_element_type=F32).T
        for c in range(CHUNKS):
            for i in range(n_row):
                start = owner_at(i, n_row) * per_owner + c * piece
                out[pl.ds((c * n_row + i) * piece, piece), lanes] = turned[start : start + piece]


def add_chunks_body(kept, received, *outs):
    width = outs[0].shape[0]
    for c, out in enumerate(outs):
        part = pl.ds(c * width, width)
        out[...] = kept[part, :] + received[part, :]


def add_body(a, b, out):
    out[...] = a[...] + b[...]


def product_body(n_row, sketch, held, out):
    out[...] = jnp.dot(sketch[...].astype(BF16), held[...], preferred_element_type=F32)


def halves(bit, ref):
    half = ref.shape[0] // 2
    own = lax.rem(lax.axis_index("row") // bit, 2)
    if half % 8:
        low, high = ref[:half, :], ref[half:, :]
        return jnp.where(own == 0, high, low), jnp.where(own == 0, low, high)
    theirs = pl.ds(pl.multiple_of((1 - own) * half, half), half)
    mine = pl.ds(pl.multiple_of(own * half, half), half)
    return ref[theirs, :], ref[mine, :]


def product_send_body(sketch, held, before, send, keep):
    half = send.shape[0]
    ordered = jnp.concatenate(halves(1, sketch), axis=0).astype(BF16)
    total = jnp.dot(ordered, held[...], preferred_element_type=F32)
    theirs, mine = halves(1, before)
    send[...] = total[:half] + theirs
    keep[...] = total[half:] + mine


def add_send_body(bit, kept, received, send, keep):
    for out, a, b in zip((send, keep), halves(bit, kept), halves(bit, received)):
        out[...] = a + b


def final_corange_body(*refs):
    out = refs[-1]
    width = refs[0].shape[0]
    for c in range(len(refs) // 2):
        out[pl.ds(c * width, width), :] = refs[2 * c][...] + refs[2 * c + 1][...]


def final_sketch_body(n_row, *refs):
    out, done = refs[-2:]
    width, rows = refs[0].shape
    piece = width // n_row
    parity = lax.rem(lax.axis_index("col"), 2)
    for side in range(2):
        parts = refs[side * CHUNKS : (side + 1) * CHUNKS]
        first = (parity if side == 0 else 1 - parity) * rows
        for b in range(rows // 128):
            lanes = pl.ds(b * 128, 128)
            pieces = []
            for r in range(n_row):
                start = owner_at(r, n_row) * piece
                pieces.extend(part[pl.ds(start, piece), lanes] for part in parts)
            block = jnp.concatenate(pieces, axis=0)
            out[pl.ds(pl.multiple_of(first + b * 128, 128), 128), :] = block.T
    done[...] = jnp.zeros_like(done)


def swap(x, axis, size, bit):
    return lax.ppermute(x, axis, [(i, i ^ bit) for i in range(size)])


def shards(n_row, n_col, delta, omega):
    rows, d = delta.shape
    k = omega.shape[1]
    half = rows // 2
    width = k // CHUNKS
    piece = width // n_row

    def sketch_half(mine, after):
        return call(
            functools.partial(sketch_half_body, n_row, mine),
            (pltpu.with_memory_space_constraint(delta, pltpu.HBM), pltpu.with_memory_space_constraint(omega, pltpu.HBM)),
            [((half, d), BF16), ((k, half), F32)],
            "hh",
            after,
            [pltpu.VMEM((d, k), BF16), pltpu.SemaphoreType.DMA((half // BLOCK,)), pltpu.SemaphoreType.DMA],
            weight=WEIGHTS[0],
        )

    held_other, to_send = sketch_half(False, ())
    received = swap(to_send, "col", n_col, 1)
    held_own, kept = sketch_half(True, (to_send,))
    partial = call(add_chunks_body, (kept, received), [((width, half), F32)] * CHUNKS, weight=WEIGHTS[1])
    bit = 2
    while bit < n_col // 2:
        moved = [swap(x, "col", n_col, bit) for x in partial]
        partial = [call(add_body, pair, [((width, half), F32)])[0] for pair in zip(partial, moved)]
        bit *= 2
    moved = [swap(x, "col", n_col, bit) for x in partial]

    bits = [1 << i for i in range(n_row.bit_length() - 1)]
    stages = len(bits)
    owns, others = [], []
    pending = {}
    last = ()

    def reduce_step(c, s):
        nonlocal last
        kept, got = pending[c]
        wide = width >> (s + 2)
        send, keep = call(
            functools.partial(add_send_body, bits[s + 1]), (kept, got), [((wide, d), F32)] * 2, after=last, weight=WEIGHTS[5 + min(s, 1)]
        )
        last = (keep,)
        pending[c] = keep, swap(send, "row", n_row, bits[s + 1])

    for c in range(CHUNKS + stages - 1):
        if c < CHUNKS:
            own = call(add_body, (partial[c], moved[c]), [((width, half), F32)], after=last, weight=WEIGHTS[2])[0]
            other = swap(own, "col", n_col, 1)
            owns.append(own)
            others.append(other)
            before = call(functools.partial(product_body, n_row), (own, held_own), [((width, d), F32)], weight=WEIGHTS[3])[0]
            send, keep = call(product_send_body, (other, held_other, before), [((width // 2, d), F32)] * 2, weight=WEIGHTS[4])
            pending[c] = keep, swap(send, "row", n_row, bits[0])
            last = (keep,)
        if c == CHUNKS - 1:
            sketch, done = finish_sketch(n_row, k, owns, others, last)
            last = (done,)
        for s in range(stages - 1):
            if 0 <= c - 1 - s < CHUNKS:
                reduce_step(c - 1 - s, s)
    if piece % 8 == 0:
        flat = [x for c in range(CHUNKS) for x in pending[c]]
        corange = call(final_corange_body, flat, [((k // n_row, d), F32)], results=1, weight=WEIGHTS[8])[0]
    else:
        corange = jnp.concatenate([kept + got for kept, got in (pending[c] for c in range(CHUNKS))], axis=0)
    return sketch, corange.T


def finish_sketch(n_row, k, owns, others, after):
    width, half = owns[0].shape
    piece = width // n_row
    if piece % 8 == 0:
        body = functools.partial(final_sketch_body, n_row)
        return call(body, (*owns, *others), [((2 * half, k), F32), ((8, 128), F32)], after=after, results=1, weight=WEIGHTS[7])
    places = [owner_at(r, n_row) for r in range(n_row)]

    def columns(parts):
        stacked = jnp.stack(parts).reshape(CHUNKS, n_row, piece, half)[:, jnp.array(places)]
        return stacked.transpose(3, 1, 0, 2).reshape(half, k)

    own, other = columns(owns), columns(others)
    first = lax.rem(lax.axis_index("col"), 2) == 0
    return jnp.where(first, jnp.concatenate([own, other]), jnp.concatenate([other, own])), after[0]


def solution(mesh):
    body = functools.partial(shards, mesh.shape["row"], mesh.shape["col"])
    in_specs = (P("row", "col"), P("col", None))
    out_specs = (P("row", None), P("col", "row"))
    return jax.shard_map(body, mesh=mesh, in_specs=in_specs, out_specs=out_specs, check_vma=False)
```

time: 151 us -> 68.1 us (0.45)
  waiting for transfers between devices: 121 us -> 24.8 us
  starting transfers between devices: 0.08 us -> 24.7 us
  Pallas kernels: 0 us -> 17.5 us
  matrix products: 13.7 us -> 0 us
  between operations: 14 us -> 0.88 us
  local copies, waits for them, and re-layouts: 2.45 us -> 0 us
    reduce_scatter x1 -> x0, waiting for transfers between devices: 66.6 us -> none  [shards(): lax.psum_scatter(local_terms, 'row', scatter_dimension=1, tiled=True)]
    psum x1 -> x0, waiting for transfers between devices: 54.2 us -> none  [shards(): sketch = lax.psum(partial_value, 'col')]
    ppermute x0 -> x21, waiting for transfers between devices: none -> 24.8 us  [swap(): return lax.ppermute(x, axis, [(i, i ^ bit) for i in range(size)])]
    ppermute x0 -> x21, starting transfers between devices: none -> 24.7 us  [swap(): return lax.ppermute(x, axis, [(i, i ^ bit) for i in range(size)])]
    pallas_call x0 -> x25, Pallas kernels: none -> 17.5 us  [call(): pl.pallas_call(run, out_shape=[pltpu.VMEM(*o) if i >= results else jax.Sh...]
    dot_general x2 -> x0, matrix products: 13.7 us -> none  [the longest x1 7.19 us: shards(): lax.dot_general(delta, sketch_half, (((0,), (0,)), ((), ())), preferred_e...]
    unnamed x5 -> x0, local copies, waits for them, and re-layouts: 2.45 us -> none
  transfers between devices with their start and end apart: 2 -> 21, of which waited for: 2 -> 8; matrix products, arithmetic and copies ran while one was open for 0% -> 0% of each run, Pallas kernels for 0% -> 18%
where the time goes in v2:
time: 68.1 us; the launch traced here: 68 us
  waiting for transfers between devices  24.8 us (36%)
  starting transfers between devices  24.7 us (36%)
  Pallas kernels  17.5 us (26%)
  between operations  0.88 us (1%)
    ppermute x21, waiting for transfers between devices, swap(): return lax.ppermute(x, axis, [(i, i ^ bit) for i in range(size)])  24.8 us
    ppermute x21, starting transfers between devices, swap(): return lax.ppermute(x, axis, [(i, i ^ bit) for i in range(size)])  24.7 us
    pallas_call x25, Pallas kernels, call(): pl.pallas_call(run, out_shape=[pltpu.VMEM(*o) if i >= results else jax.Sh...  17.5 us
  transfers between devices with their start and end apart: 21, of which 8 were waited for; matrix products, arithmetic and copies ran while one was open for 0% of the time, Pallas kernels for 18%

profile of v2, /device:TPU:0, one launch (start us, length us, event | category | flops | bytes accessed | tf_op | source)
XLA Modules:
  0.0 68.0 jit_solution(16722191995810349233)
XLA Ops:
  0.6 4.3 %shard_map.41 = (bf16[1024,1792]{1,0:T(8,128)(2,1)S(1)}, f32[256,1024]{1,0:T(8,128)S(1)}) custom-call(bf16[2048,1792]{1,0:T(8,128)(2,1)} %refs_0_.3, bf16[1792,256]{1,0:T(8,128)(2,1)} %refs_1_.3), custom_call_target="tpu_custom_call" | custom-call | flops 20000000000 | tf_op jit(solution)/shard_map/pallas_call | solution.py:29
  5.4 4.3 %shard_map.42 = (bf16[1024,1792]{1,0:T(8,128)(2,1)S(1)}, f32[256,1024]{1,0:T(8,128)S(1)}) custom-call(bf16[2048,1792]{1,0:T(8,128)(2,1)} %refs_0_.3, bf16[1792,256]{1,0:T(8,128)(2,1)} %refs_1_.3, f32[256,1024]{1,0:T(8,128)S(1)} %get-tuple-element.36.refs_2_), custom_call_target="tpu_custom_call" | custom-call | flops 20000000000 | tf_op jit(solution)/shard_map/pallas_call | solution.py:29
  9.8 2.6 %collective-permute-start.1 = (f32[64,1024]{1,0:T(8,128)S(1)}, f32[64,1024]{1,0:T(8,128)S(1)}, u32[]{:S(2)}, u32[]{:S(2)}) collective-permute-start(f32[64,1024]{1,0:T(8,128)S(1)} %get-tuple-element.38.refs_0_), channel_id=1, source_target_pairs={{0,2},{1,3},{2,0},{3,1},{4,6},{5,7},{6,4},{7,5},{8,10},{9,11},{10,... | collective-permute-start | bytes 786440 | tf_op jit(solution)/shard_map/ppermute | solution.py:140
  12.5 1.9 %collective-permute-start.4 = (f32[64,1024]{1,0:T(8,128)S(1)}, f32[64,1024]{1,0:T(8,128)S(1)}, u32[]{:S(2)}, u32[]{:S(2)}) collective-permute-start(f32[64,1024]{1,0:T(8,128)S(1)} %get-tuple-element.43.refs_0_), channel_id=1, source_target_pairs={{0,2},{1,3},{2,0},{3,1},{4,6},{5,7},{6,4},{7,5},{8,10},{9,11},{10,... | collective-permute-start | bytes 786440 | tf_op jit(solution)/shard_map/ppermute | solution.py:140
  14.5 5.1 %collective-permute-done.1.refs_1_ = f32[64,1024]{1,0:T(8,128)S(1)} collective-permute-done((f32[64,1024]{1,0:T(8,128)S(1)}, f32[64,1024]{1,0:T(8,128)S(1)}, u32[]{:S(2)}, u32[]{:S(2)}) %collective-permute-start.1) | collective-permute-done | bytes 262176 | tf_op jit(solution)/shard_map/ppermute | solution.py:140
  19.6 0.7 %shard_map.45.refs_2_ = f32[64,1792]{1,0:T(8,128)S(1)} custom-call(f32[64,1024]{1,0:T(8,128)S(1)} %shard_map.44.refs_0_, bf16[1024,1792]{1,0:T(8,128)(2,1)S(1)} %get-tuple-element.41.refs_1_), custom_call_target="tpu_custom_call" | custom-call | flops 4000000000 | tf_op jit(solution)/shard_map/pallas_call | solution.py:29
  20.4 0.8 %collective-permute-done.3.refs_0_.refs_4_ = f32[64,1024]{1,0:T(8,128)S(1)} collective-permute-done((f32[64,1024]{1,0:T(8,128)S(1)}, f32[64,1024]{1,0:T(8,128)S(1)}, u32[]{:S(2)}, u32[]{:S(2)}) %collective-permute-start.3) | collective-permute-done | bytes 262176 | tf_op jit(solution)/shard_map/ppermute | solution.py:140
  21.2 0.7 %shard_map.46 = (f32[32,1792]{1,0:T(8,128)S(1)}, f32[32,1792]{1,0:T(8,128)S(1)}) custom-call(f32[64,1024]{1,0:T(8,128)S(1)} %collective-permute-done.3.refs_0_.refs_4_, bf16[1024,1792]{1,0:T(8,128)(2,1)S(1)} %get-tuple-element.40.refs_1_, f32[64,1792]{1,0:T(8,128)S(1)} %shard_map.45.refs_2_), custom_call_target="tpu_custom_call" | custom-call | flops 4000000000 | tf_op jit(solution)/shard_map/pallas_call | solution.py:29
  21.9 3.2 %collective-permute-done.2.refs_1_ = f32[64,1024]{1,0:T(8,128)S(1)} collective-permute-done((f32[64,1024]{1,0:T(8,128)S(1)}, f32[64,1024]{1,0:T(8,128)S(1)}, u32[]{:S(2)}, u32[]{:S(2)}) %collective-permute-start.2) | collective-permute-done | bytes 262176 | tf_op jit(solution)/shard_map/ppermute | solution.py:140
  25.3 2.0 %collective-permute-start.5 = (f32[32,1792]{1,0:T(8,128)S(1)}, f32[32,1792]{1,0:T(8,128)S(1)}, u32[]{:S(2)}, u32[]{:S(2)}) collective-permute-start(f32[32,1792]{1,0:T(8,128)S(1)} %get-tuple-element.44), channel_id=1, source_target_pairs={{0,4},{4,0},{8,12},{12,8},{16,20},{20,16},{24,28},{28,24},{1,5},{5... | collective-permute-start | bytes 688136 | tf_op jit(solution)/shard_map/ppermute | solution.py:140
  27.3 0.7 %shard_map.48.refs_2_ = f32[64,1792]{1,0:T(8,128)S(1)} custom-call(f32[64,1024]{1,0:T(8,128)S(1)} %shard_map.47.refs_0_.refs_1_, bf16[1024,1792]{1,0:T(8,128)(2,1)S(1)} %get-tuple-element.41.refs_1_), custom_call_target="tpu_custom_call" | custom-call | flops 4000000000 | tf_op jit(solution)/shard_map/pallas_call | solution.py:29
  28.1 0.7 %shard_map.49 = (f32[32,1792]{1,0:T(8,128)S(1)}, f32[32,1792]{1,0:T(8,128)S(1)}) custom-call(f32[64,1024]{1,0:T(8,128)S(1)} %collective-permute-done.6.refs_0_.refs_5_, bf16[1024,1792]{1,0:T(8,128)(2,1)S(1)} %get-tuple-element.40.refs_1_, f32[64,1792]{1,0:T(8,128)S(1)} %shard_map.48.refs_2_), custom_call_target="tpu_custom_call" | custom-call | flops 4000000000 | tf_op jit(solution)/shard_map/pallas_call | solution.py:29
  28.8 4.7 %collective-permute-done.5.refs_1_ = f32[32,1792]{1,0:T(8,128)S(1)} collective-permute-done((f32[32,1792]{1,0:T(8,128)S(1)}, f32[32,1792]{1,0:T(8,128)S(1)}, u32[]{:S(2)}, u32[]{:S(2)}) %collective-permute-start.5) | collective-permute-done | bytes 229408 | tf_op jit(solution)/shard_map/ppermute | solution.py:140
  33.7 1.8 %collective-permute-start.9 = (f32[32,1792]{1,0:T(8,128)S(1)}, f32[32,1792]{1,0:T(8,128)S(1)}, u32[]{:S(2)}, u32[]{:S(2)}) collective-permute-start(f32[32,1792]{1,0:T(8,128)S(1)} %get-tuple-element.49), channel_id=1, source_target_pairs={{0,4},{4,0},{8,12},{12,8},{16,20},{20,16},{24,28},{28,24},{1,5},{5... | collective-permute-start | bytes 688136 | tf_op jit(solution)/shard_map/ppermute | solution.py:140
  35.5 1.6 %collective-permute-start.8 = (f32[16,1792]{1,0:T(8,128)S(1)}, f32[16,1792]{1,0:T(8,128)S(1)}, u32[]{:S(2)}, u32[]{:S(2)}) collective-permute-start(f32[16,1792]{1,0:T(8,128)S(1)} %get-tuple-element.48), channel_id=1, source_target_pairs={{0,8},{4,12},{8,0},{12,4},{16,24},{20,28},{24,16},{28,20},{1,9},{5... | collective-permute-start | bytes 344072 | tf_op jit(solution)/shard_map/ppermute | solution.py:140
  37.1 0.7 %shard_map.52.refs_2_ = f32[64,1792]{1,0:T(8,128)S(1)} custom-call(f32[64,1024]{1,0:T(8,128)S(1)} %shard_map.51.refs_0_.refs_2_, bf16[1024,1792]{1,0:T(8,128)(2,1)S(1)} %get-tuple-element.41.refs_1_), custom_call_target="tpu_custom_call" | custom-call | flops 4000000000 | tf_op jit(solution)/shard_map/pallas_call | solution.py:29
  37.8 0.7 %shard_map.53 = (f32[32,1792]{1,0:T(8,128)S(1)}, f32[32,1792]{1,0:T(8,128)S(1)}) custom-call(f32[64,1024]{1,0:T(8,128)S(1)} %collective-permute-done.10.refs_0_.refs_6_, bf16[1024,1792]{1,0:T(8,128)(2,1)S(1)} %get-tuple-element.40.refs_1_, f32[64,1792]{1,0:T(8,128)S(1)} %shard_map.52.refs_2_), custom_call_target="tpu_custom_call" | custom-call | flops 4000000000 | tf_op jit(solution)/shard_map/pallas_call | solution.py:29
  38.6 3.1 %collective-permute-done.9.refs_1_ = f32[32,1792]{1,0:T(8,128)S(1)} collective-permute-done((f32[32,1792]{1,0:T(8,128)S(1)}, f32[32,1792]{1,0:T(8,128)S(1)}, u32[]{:S(2)}, u32[]{:S(2)}) %collective-permute-start.9) | collective-permute-done | bytes 229408 | tf_op jit(solution)/shard_map/ppermute | solution.py:140
  41.9 1.8 %collective-permute-start.14 = (f32[32,1792]{1,0:T(8,128)S(1)}, f32[32,1792]{1,0:T(8,128)S(1)}, u32[]{:S(2)}, u32[]{:S(2)}) collective-permute-start(f32[32,1792]{1,0:T(8,128)S(1)} %get-tuple-element.57), channel_id=1, source_target_pairs={{0,4},{4,0},{8,12},{12,8},{16,20},{20,16},{24,28},{28,24},{1,5},{5... | collective-permute-start | bytes 688136 | tf_op jit(solution)/shard_map/ppermute | solution.py:140
  43.7 1.6 %collective-permute-start.13 = (f32[16,1792]{1,0:T(8,128)S(1)}, f32[16,1792]{1,0:T(8,128)S(1)}, u32[]{:S(2)}, u32[]{:S(2)}) collective-permute-start(f32[16,1792]{1,0:T(8,128)S(1)} %get-tuple-element.56), channel_id=1, source_target_pairs={{0,8},{4,12},{8,0},{12,4},{16,24},{20,28},{24,16},{28,20},{1,9},{5... | collective-permute-start | bytes 344072 | tf_op jit(solution)/shard_map/ppermute | solution.py:140
  45.3 2.6 %collective-permute-start.12 = (f32[8,1792]{1,0:T(8,128)S(1)}, f32[8,1792]{1,0:T(8,128)S(1)}, u32[]{:S(2)}, u32[]{:S(2)}) collective-permute-start(f32[8,1792]{1,0:T(8,128)S(1)} %get-tuple-element.55), channel_id=1, source_target_pairs={{0,16},{4,20},{8,24},{12,28},{16,0},{20,4},{24,8},{28,12},{1,17},{... | collective-permute-start | bytes 172040 | tf_op jit(solution)/shard_map/ppermute | solution.py:140
  47.9 0.7 %shard_map.57.refs_2_ = f32[64,1792]{1,0:T(8,128)S(1)} custom-call(f32[64,1024]{1,0:T(8,128)S(1)} %shard_map.56.refs_0_.refs_3_, bf16[1024,1792]{1,0:T(8,128)(2,1)S(1)} %get-tuple-element.41.refs_1_), custom_call_target="tpu_custom_call" | custom-call | flops 4000000000 | tf_op jit(solution)/shard_map/pallas_call | solution.py:29
  48.6 0.7 %shard_map.58 = (f32[32,1792]{1,0:T(8,128)S(1)}, f32[32,1792]{1,0:T(8,128)S(1)}) custom-call(f32[64,1024]{1,0:T(8,128)S(1)} %collective-permute-done.11.refs_0_.refs_7_, bf16[1024,1792]{1,0:T(8,128)(2,1)S(1)} %get-tuple-element.40.refs_1_, f32[64,1792]{1,0:T(8,128)S(1)} %shard_map.57.refs_2_), custom_call_target="tpu_custom_call" | custom-call | flops 4000000000 | tf_op jit(solution)/shard_map/pallas_call | solution.py:29
  49.4 0.6 collective-permute-start.17
  50.0 1.9 %shard_map.59 = (f32[2048,256]{1,0:T(8,128)}, f32[8,128]{1,0:T(8,128)S(1)}) custom-call(f32[64,1024]{1,0:T(8,128)S(1)} %shard_map.44.refs_0_, f32[64,1024]{1,0:T(8,128)S(1)} %shard_map.47.refs_0_.refs_1_, f32[64,1024]{1,0:T(8,128)S(1)} %shard_map.51.refs_0_.refs_2_, f32[64,1024]{1,0:T(8,128)S(1)} %shard_map.56.refs_0_.refs_3_, ...), custom_call_target="tpu_custom_call" | custom-call | flops 1000000000 | tf_op jit(solution)/shard_map/pallas_call | solution.py:29
  52.5 2.5 %collective-permute-start.15 = (f32[8,1792]{1,0:T(8,128)S(1)}, f32[8,1792]{1,0:T(8,128)S(1)}, u32[]{:S(2)}, u32[]{:S(2)}) collective-permute-start(f32[8,1792]{1,0:T(8,128)S(1)} %get-tuple-element.61), channel_id=1, source_target_pairs={{0,16},{4,20},{8,24},{12,28},{16,0},{20,4},{24,8},{28,12},{1,17},{... | collective-permute-start | bytes 172040 | tf_op jit(solution)/shard_map/ppermute | solution.py:140
  54.9 1.6 %collective-permute-done.17.refs_1_ = f32[32,1792]{1,0:T(8,128)S(1)} collective-permute-done((f32[32,1792]{1,0:T(8,128)S(1)}, f32[32,1792]{1,0:T(8,128)S(1)}, u32[]{:S(2)}, u32[]{:S(2)}) %collective-permute-start.17) | collective-permute-done | bytes 229408 | tf_op jit(solution)/shard_map/ppermute | solution.py:140
  57.1 2.3 %collective-permute-start.18 = (f32[8,1792]{1,0:T(8,128)S(1)}, f32[8,1792]{1,0:T(8,128)S(1)}, u32[]{:S(2)}, u32[]{:S(2)}) collective-permute-start(f32[8,1792]{1,0:T(8,128)S(1)} %get-tuple-element.66), channel_id=1, source_target_pairs={{0,16},{4,20},{8,24},{12,28},{16,0},{20,4},{24,8},{28,12},{1,17},{... | collective-permute-start | bytes 172040 | tf_op jit(solution)/shard_map/ppermute | solution.py:140
  59.4 2.1 %collective-permute-done.19.refs_1_ = f32[16,1792]{1,0:T(8,128)S(1)} collective-permute-done((f32[16,1792]{1,0:T(8,128)S(1)}, f32[16,1792]{1,0:T(8,128)S(1)}, u32[]{:S(2)}, u32[]{:S(2)}) %collective-permute-start.19) | collective-permute-done | bytes 114720 | tf_op jit(solution)/shard_map/ppermute | solution.py:140
  61.5 1.5 %collective-permute-start.20 = (f32[8,1792]{1,0:T(8,128)S(1)}, f32[8,1792]{1,0:T(8,128)S(1)}, u32[]{:S(2)}, u32[]{:S(2)}) collective-permute-start(f32[8,1792]{1,0:T(8,128)S(1)} %get-tuple-element.69), channel_id=1, source_target_pairs={{0,16},{4,20},{8,24},{12,28},{16,0},{20,4},{24,8},{28,12},{1,17},{... | collective-permute-start | bytes 172040 | tf_op jit(solution)/shard_map/ppermute | solution.py:140
  63.0 4.3 %collective-permute-done.20.refs_7_ = f32[8,1792]{1,0:T(8,128)S(1)} collective-permute-done((f32[8,1792]{1,0:T(8,128)S(1)}, f32[8,1792]{1,0:T(8,128)S(1)}, u32[]{:S(2)}, u32[]{:S(2)}) %collective-permute-start.20) | collective-permute-done | bytes 57376 | tf_op jit(solution)/shard_map/ppermute | solution.py:140
  67.3 0.7 %shard_map.65 = f32[32,1792]{1,0:T(8,128)} custom-call(f32[8,1792]{1,0:T(8,128)S(1)} %get-tuple-element.52.refs_2_.refs_0_, f32[8,1792]{1,0:T(8,128)S(1)} %collective-permute-done.12.refs_1_, f32[8,1792]{1,0:T(8,128)S(1)} %get-tuple-element.60.refs_2_, f32[8,1792]{1,0:T(8,128)S(1)} %collective-permute-done.15.refs_3_, ...), custom_call_target="tpu_custom_call" | custom-call | flops 10000000000 | tf_op jit(solution)/shard_map/pallas_call | solution.py:29
  (35 shorter events, 2.4 us)
Async XLA Ops:
  4.9 4.8 %collective-permute-start = (f32[256,1024]{1,0:T(8,128)S(1)}, f32[256,1024]{1,0:T(8,128)S(1)}, u32[]{:S(2)}, u32[]{:S(2)}) collective-permute-start(f32[256,1024]{1,0:T(8,128)S(1)} %get-tuple-element.36.refs_2_), channel_id=1, source_target_pairs={{0,1},{1,0},{2,3},{3,2},{4,5},{5,4},{6,7},{7,6},{8,9},{9,8},{10,11... | collective-permute-start | bytes 3145736 | tf_op jit(solution)/shard_map/ppermute | solution.py:140
  9.8 9.7 %collective-permute-start.1 = (f32[64,1024]{1,0:T(8,128)S(1)}, f32[64,1024]{1,0:T(8,128)S(1)}, u32[]{:S(2)}, u32[]{:S(2)}) collective-permute-start(f32[64,1024]{1,0:T(8,128)S(1)} %get-tuple-element.38.refs_0_), channel_id=1, source_target_pairs={{0,2},{1,3},{2,0},{3,1},{4,6},{5,7},{6,4},{7,5},{8,10},{9,11},{10,... | collective-permute-start | bytes 786440 | tf_op jit(solution)/shard_map/ppermute | solution.py:140
  12.4 12.8 %collective-permute-start.2 = (f32[64,1024]{1,0:T(8,128)S(1)}, f32[64,1024]{1,0:T(8,128)S(1)}, u32[]{:S(2)}, u32[]{:S(2)}) collective-permute-start(f32[64,1024]{1,0:T(8,128)S(1)} %get-tuple-element.39.refs_0_), channel_id=1, source_target_pairs={{0,2},{1,3},{2,0},{3,1},{4,6},{5,7},{6,4},{7,5},{8,10},{9,11},{10,... | collective-permute-start | bytes 786440 | tf_op jit(solution)/shard_map/ppermute | solution.py:140
  12.5 21.1 %collective-permute-start.4 = (f32[64,1024]{1,0:T(8,128)S(1)}, f32[64,1024]{1,0:T(8,128)S(1)}, u32[]{:S(2)}, u32[]{:S(2)}) collective-permute-start(f32[64,1024]{1,0:T(8,128)S(1)} %get-tuple-element.43.refs_0_), channel_id=1, source_target_pairs={{0,2},{1,3},{2,0},{3,1},{4,6},{5,7},{6,4},{7,5},{8,10},{9,11},{10,... | collective-permute-start | bytes 786440 | tf_op jit(solution)/shard_map/ppermute | solution.py:140
  14.4 27.4 %collective-permute-start.7 = (f32[64,1024]{1,0:T(8,128)S(1)}, f32[64,1024]{1,0:T(8,128)S(1)}, u32[]{:S(2)}, u32[]{:S(2)}) collective-permute-start(f32[64,1024]{1,0:T(8,128)S(1)} %get-tuple-element.47.refs_0_), channel_id=1, source_target_pairs={{0,2},{1,3},{2,0},{3,1},{4,6},{5,7},{6,4},{7,5},{8,10},{9,11},{10,... | collective-permute-start | bytes 786440 | tf_op jit(solution)/shard_map/ppermute | solution.py:140
  19.6 1.6 %collective-permute-start.3 = (f32[64,1024]{1,0:T(8,128)S(1)}, f32[64,1024]{1,0:T(8,128)S(1)}, u32[]{:S(2)}, u32[]{:S(2)}) collective-permute-start(f32[64,1024]{1,0:T(8,128)S(1)} %shard_map.44.refs_0_), channel_id=1, source_target_pairs={{0,1},{1,0},{2,3},{3,2},{4,5},{5,4},{6,7},{7,6},{8,9},{9,8},{10,11... | collective-permute-start | bytes 786440 | tf_op jit(solution)/shard_map/ppermute | solution.py:140
  25.2 2.9 %collective-permute-start.6 = (f32[64,1024]{1,0:T(8,128)S(1)}, f32[64,1024]{1,0:T(8,128)S(1)}, u32[]{:S(2)}, u32[]{:S(2)}) collective-permute-start(f32[64,1024]{1,0:T(8,128)S(1)} %shard_map.47.refs_0_.refs_1_), channel_id=1, source_target_pairs={{0,1},{1,0},{2,3},{3,2},{4,5},{5,4},{6,7},{7,6},{8,9},{9,8},{10,11... | collective-permute-start | bytes 786440 | tf_op jit(solution)/shard_map/ppermute | solution.py:140
  25.3 8.2 %collective-permute-start.5 = (f32[32,1792]{1,0:T(8,128)S(1)}, f32[32,1792]{1,0:T(8,128)S(1)}, u32[]{:S(2)}, u32[]{:S(2)}) collective-permute-start(f32[32,1792]{1,0:T(8,128)S(1)} %get-tuple-element.44), channel_id=1, source_target_pairs={{0,4},{4,0},{8,12},{12,8},{16,20},{20,16},{24,28},{28,24},{1,5},{5... | collective-permute-start | bytes 688136 | tf_op jit(solution)/shard_map/ppermute | solution.py:140
  33.6 4.2 %collective-permute-start.10 = (f32[64,1024]{1,0:T(8,128)S(1)}, f32[64,1024]{1,0:T(8,128)S(1)}, u32[]{:S(2)}, u32[]{:S(2)}) collective-permute-start(f32[64,1024]{1,0:T(8,128)S(1)} %shard_map.51.refs_0_.refs_2_), channel_id=1, source_target_pairs={{0,1},{1,0},{2,3},{3,2},{4,5},{5,4},{6,7},{7,6},{8,9},{9,8},{10,11... | collective-permute-start | bytes 786440 | tf_op jit(solution)/shard_map/ppermute | solution.py:140
  33.7 8.0 %collective-permute-start.9 = (f32[32,1792]{1,0:T(8,128)S(1)}, f32[32,1792]{1,0:T(8,128)S(1)}, u32[]{:S(2)}, u32[]{:S(2)}) collective-permute-start(f32[32,1792]{1,0:T(8,128)S(1)} %get-tuple-element.49), channel_id=1, source_target_pairs={{0,4},{4,0},{8,12},{12,8},{16,20},{20,16},{24,28},{28,24},{1,5},{5... | collective-permute-start | bytes 688136 | tf_op jit(solution)/shard_map/ppermute | solution.py:140
  35.5 6.2 %collective-permute-start.8 = (f32[16,1792]{1,0:T(8,128)S(1)}, f32[16,1792]{1,0:T(8,128)S(1)}, u32[]{:S(2)}, u32[]{:S(2)}) collective-permute-start(f32[16,1792]{1,0:T(8,128)S(1)} %get-tuple-element.48), channel_id=1, source_target_pairs={{0,8},{4,12},{8,0},{12,4},{16,24},{20,28},{24,16},{28,20},{1,9},{5... | collective-permute-start | bytes 344072 | tf_op jit(solution)/shard_map/ppermute | solution.py:140
  41.8 6.8 %collective-permute-start.11 = (f32[64,1024]{1,0:T(8,128)S(1)}, f32[64,1024]{1,0:T(8,128)S(1)}, u32[]{:S(2)}, u32[]{:S(2)}) collective-permute-start(f32[64,1024]{1,0:T(8,128)S(1)} %shard_map.56.refs_0_.refs_3_), channel_id=1, source_target_pairs={{0,1},{1,0},{2,3},{3,2},{4,5},{5,4},{6,7},{7,6},{8,9},{9,8},{10,11... | collective-permute-start | bytes 786440 | tf_op jit(solution)/shard_map/ppermute | solution.py:140
  41.9 10.0 %collective-permute-start.14 = (f32[32,1792]{1,0:T(8,128)S(1)}, f32[32,1792]{1,0:T(8,128)S(1)}, u32[]{:S(2)}, u32[]{:S(2)}) collective-permute-start(f32[32,1792]{1,0:T(8,128)S(1)} %get-tuple-element.57), channel_id=1, source_target_pairs={{0,4},{4,0},{8,12},{12,8},{16,20},{20,16},{24,28},{28,24},{1,5},{5... | collective-permute-start | bytes 688136 | tf_op jit(solution)/shard_map/ppermute | solution.py:140
  43.7 8.7 %collective-permute-start.13 = (f32[16,1792]{1,0:T(8,128)S(1)}, f32[16,1792]{1,0:T(8,128)S(1)}, u32[]{:S(2)}, u32[]{:S(2)}) collective-permute-start(f32[16,1792]{1,0:T(8,128)S(1)} %get-tuple-element.56), channel_id=1, source_target_pairs={{0,8},{4,12},{8,0},{12,4},{16,24},{20,28},{24,16},{28,20},{1,9},{5... | collective-permute-start | bytes 344072 | tf_op jit(solution)/shard_map/ppermute | solution.py:140
  45.3 17.7 %collective-permute-start.12 = (f32[8,1792]{1,0:T(8,128)S(1)}, f32[8,1792]{1,0:T(8,128)S(1)}, u32[]{:S(2)}, u32[]{:S(2)}) collective-permute-start(f32[8,1792]{1,0:T(8,128)S(1)} %get-tuple-element.55), channel_id=1, source_target_pairs={{0,16},{4,20},{8,24},{12,28},{16,0},{20,4},{24,8},{28,12},{1,17},{... | collective-permute-start | bytes 172040 | tf_op jit(solution)/shard_map/ppermute | solution.py:140
  49.4 7.2 %collective-permute-start.17 = (f32[32,1792]{1,0:T(8,128)S(1)}, f32[32,1792]{1,0:T(8,128)S(1)}, u32[]{:S(2)}, u32[]{:S(2)}) collective-permute-start(f32[32,1792]{1,0:T(8,128)S(1)} %get-tuple-element.63), channel_id=1, source_target_pairs={{0,4},{4,0},{8,12},{12,8},{16,20},{20,16},{24,28},{28,24},{1,5},{5... | collective-permute-start | bytes 688136 | tf_op jit(solution)/shard_map/ppermute | solution.py:140
  51.9 5.2 %collective-permute-start.16 = (f32[16,1792]{1,0:T(8,128)S(1)}, f32[16,1792]{1,0:T(8,128)S(1)}, u32[]{:S(2)}, u32[]{:S(2)}) collective-permute-start(f32[16,1792]{1,0:T(8,128)S(1)} %get-tuple-element.62), channel_id=1, source_target_pairs={{0,8},{4,12},{8,0},{12,4},{16,24},{20,28},{24,16},{28,20},{1,9},{5... | collective-permute-start | bytes 344072 | tf_op jit(solution)/shard_map/ppermute | solution.py:140
  52.5 10.5 %collective-permute-start.15 = (f32[8,1792]{1,0:T(8,128)S(1)}, f32[8,1792]{1,0:T(8,128)S(1)}, u32[]{:S(2)}, u32[]{:S(2)}) collective-permute-start(f32[8,1792]{1,0:T(8,128)S(1)} %get-tuple-element.61), channel_id=1, source_target_pairs={{0,16},{4,20},{8,24},{12,28},{16,0},{20,4},{24,8},{28,12},{1,17},{... | collective-permute-start | bytes 172040 | tf_op jit(solution)/shard_map/ppermute | solution.py:140
  56.6 4.9 %collective-permute-start.19 = (f32[16,1792]{1,0:T(8,128)S(1)}, f32[16,1792]{1,0:T(8,128)S(1)}, u32[]{:S(2)}, u32[]{:S(2)}) collective-permute-start(f32[16,1792]{1,0:T(8,128)S(1)} %get-tuple-element.67), channel_id=1, source_target_pairs={{0,8},{4,12},{8,0},{12,4},{16,24},{20,28},{24,16},{28,20},{1,9},{5... | collective-permute-start | bytes 344072 | tf_op jit(solution)/shard_map/ppermute | solution.py:140
  57.1 5.9 %collective-permute-start.18 = (f32[8,1792]{1,0:T(8,128)S(1)}, f32[8,1792]{1,0:T(8,128)S(1)}, u32[]{:S(2)}, u32[]{:S(2)}) collective-permute-start(f32[8,1792]{1,0:T(8,128)S(1)} %get-tuple-element.66), channel_id=1, source_target_pairs={{0,16},{4,20},{8,24},{12,28},{16,0},{20,4},{24,8},{28,12},{1,17},{... | collective-permute-start | bytes 172040 | tf_op jit(solution)/shard_map/ppermute | solution.py:140
  61.5 5.8 %collective-permute-start.20 = (f32[8,1792]{1,0:T(8,128)S(1)}, f32[8,1792]{1,0:T(8,128)S(1)}, u32[]{:S(2)}, u32[]{:S(2)}) collective-permute-start(f32[8,1792]{1,0:T(8,128)S(1)} %get-tuple-element.69), channel_id=1, source_target_pairs={{0,16},{4,20},{8,24},{12,28},{16,0},{20,4},{24,8},{28,12},{1,17},{... | collective-permute-start | bytes 172040 | tf_op jit(solution)/shard_map/ppermute | solution.py:140

commit v3 on v2

--- a/solution.py
+++ b/solution.py
@@ -8,7 +8,7 @@
 from jax.sharding import PartitionSpec as P
 
 CHUNKS = 4
-WEIGHTS = (20000000000, 2000000000, 4000000000, 4000000000, 4000000000, 100000000, 2000000000, 1000000000, 10000000000)
+LAG = 2
 BLOCK = 256
 F32 = jnp.float32
 BF16 = jnp.bfloat16
@@ -19,7 +19,7 @@
 }
 
 
-def call(body, args, outs, kinds=None, after=(), scratch=(), results=0, weight=0):
+def call(body, args, outs, kinds=None, after=(), scratch=(), results=0):
     n = len(args)
     kinds = (kinds or "v" * n) + "a" * len(after)
 
@@ -32,7 +32,7 @@
         in_specs=[SPECS[kind] for kind in kinds],
         out_specs=[SPECS["v"]] * len(outs),
         scratch_shapes=list(scratch),
-        cost_estimate=pl.CostEstimate(flops=weight, bytes_accessed=0, transcendentals=0),
+        cost_estimate=pl.CostEstimate(flops=10**10, bytes_accessed=0, transcendentals=0),
         compiler_params=pltpu.CompilerParams(vmem_limit_bytes=16 << 20),
     )(*args, *after)
 
@@ -155,13 +155,12 @@
             "hh",
             after,
             [pltpu.VMEM((d, k), BF16), pltpu.SemaphoreType.DMA((half // BLOCK,)), pltpu.SemaphoreType.DMA],
-            weight=WEIGHTS[0],
         )
 
     held_other, to_send = sketch_half(False, ())
     received = swap(to_send, "col", n_col, 1)
     held_own, kept = sketch_half(True, (to_send,))
-    partial = call(add_chunks_body, (kept, received), [((width, half), F32)] * CHUNKS, weight=WEIGHTS[1])
+    partial = call(add_chunks_body, (kept, received), [((width, half), F32)] * CHUNKS)
     bit = 2
     while bit < n_col // 2:
         moved = [swap(x, "col", n_col, bit) for x in partial]
@@ -180,30 +179,30 @@
         kept, got = pending[c]
         wide = width >> (s + 2)
         send, keep = call(
-            functools.partial(add_send_body, bits[s + 1]), (kept, got), [((wide, d), F32)] * 2, after=last, weight=WEIGHTS[5 + min(s, 1)]
+            functools.partial(add_send_body, bits[s + 1]), (kept, got), [((wide, d), F32)] * 2, after=last
         )
         last = (keep,)
         pending[c] = keep, swap(send, "row", n_row, bits[s + 1])
 
-    for c in range(CHUNKS + stages - 1):
+    for c in range(CHUNKS + stages - 2 + LAG):
         if c < CHUNKS:
-            own = call(add_body, (partial[c], moved[c]), [((width, half), F32)], after=last, weight=WEIGHTS[2])[0]
+            own = call(add_body, (partial[c], moved[c]), [((width, half), F32)], after=last)[0]
             other = swap(own, "col", n_col, 1)
             owns.append(own)
             others.append(other)
-            before = call(functools.partial(product_body, n_row), (own, held_own), [((width, d), F32)], weight=WEIGHTS[3])[0]
-            send, keep = call(product_send_body, (other, held_other, before), [((width // 2, d), F32)] * 2, weight=WEIGHTS[4])
+            before = call(functools.partial(product_body, n_row), (own, held_own), [((width, d), F32)])[0]
+            send, keep = call(product_send_body, (other, held_other, before), [((width // 2, d), F32)] * 2)
             pending[c] = keep, swap(send, "row", n_row, bits[0])
             last = (keep,)
         if c == CHUNKS - 1:
             sketch, done = finish_sketch(n_row, k, owns, others, last)
             last = (done,)
         for s in range(stages - 1):
-            if 0 <= c - 1 - s < CHUNKS:
-                reduce_step(c - 1 - s, s)
+            if 0 <= c - LAG - s < CHUNKS:
+                reduce_step(c - LAG - s, s)
     if piece % 8 == 0:
         flat = [x for c in range(CHUNKS) for x in pending[c]]
-        corange = call(final_corange_body, flat, [((k // n_row, d), F32)], results=1, weight=WEIGHTS[8])[0]
+        corange = call(final_corange_body, flat, [((k // n_row, d), F32)], results=1)[0]
     else:
         corange = jnp.concatenate([kept + got for kept, got in (pending[c] for c in range(CHUNKS))], axis=0)
     return sketch, corange.T
@@ -214,7 +213,7 @@
     piece = width // n_row
     if piece % 8 == 0:
         body = functools.partial(final_sketch_body, n_row)
-        return call(body, (*owns, *others), [((2 * half, k), F32), ((8, 128), F32)], after=after, results=1, weight=WEIGHTS[7])
+        return call(body, (*owns, *others), [((2 * half, k), F32), ((8, 128), F32)], after=after, results=1)
     places = [owner_at(r, n_row) for r in range(n_row)]
 
     def columns(parts):

time: 68.1 us -> 64.8 us (0.952)
  starting transfers between devices: 24.7 us -> 22.8 us
  waiting for transfers between devices: 24.8 us -> 23.5 us
    ppermute x21, starting transfers between devices: 24.7 us -> 22.8 us  [swap(): return lax.ppermute(x, axis, [(i, i ^ bit) for i in range(size)])]
    ppermute x21, waiting for transfers between devices: 24.8 us -> 23.5 us  [swap(): return lax.ppermute(x, axis, [(i, i ^ bit) for i in range(size)])]
  transfers between devices with their start and end apart: 21 -> 21, of which waited for: 8 -> 9; matrix products, arithmetic and copies ran while one was open for 0% -> 0% of each run, Pallas kernels for 18% -> 19%
where the time goes in v3:
time: 64.8 us; the launch traced here: 64.6 us
  waiting for transfers between devices  23.5 us (36%)
  starting transfers between devices  22.8 us (35%)
  Pallas kernels  17.5 us (27%)
  between operations  0.84 us (1%)
    ppermute x21, waiting for transfers between devices, swap(): return lax.ppermute(x, axis, [(i, i ^ bit) for i in range(size)])  23.5 us
    ppermute x21, starting transfers between devices, swap(): return lax.ppermute(x, axis, [(i, i ^ bit) for i in range(size)])  22.8 us
    pallas_call x25, Pallas kernels, call(): pl.pallas_call(run, out_shape=[pltpu.VMEM(*o) if i >= results else jax.Sh...  17.5 us
  transfers between devices with their start and end apart: 21, of which 9 were waited for; matrix products, arithmetic and copies ran while one was open for 0% of the time, Pallas kernels for 19%

profile of v3, /device:TPU:0, one launch (start us, length us, event | category | flops | bytes accessed | tf_op | source)
XLA Modules:
  0.0 64.6 jit_solution(13397863924925545629)
XLA Ops:
  0.6 4.3 %shard_map.41 = (bf16[1024,1792]{1,0:T(8,128)(2,1)S(1)}, f32[256,1024]{1,0:T(8,128)S(1)}) custom-call(bf16[2048,1792]{1,0:T(8,128)(2,1)} %refs_0_.3, bf16[1792,256]{1,0:T(8,128)(2,1)} %refs_1_.3), custom_call_target="tpu_custom_call" | custom-call | flops 10000000000 | tf_op jit(solution)/shard_map/pallas_call | solution.py:29
  5.4 4.3 %shard_map.42 = (bf16[1024,1792]{1,0:T(8,128)(2,1)S(1)}, f32[256,1024]{1,0:T(8,128)S(1)}) custom-call(bf16[2048,1792]{1,0:T(8,128)(2,1)} %refs_0_.3, bf16[1792,256]{1,0:T(8,128)(2,1)} %refs_1_.3, f32[256,1024]{1,0:T(8,128)S(1)} %get-tuple-element.36.refs_2_), custom_call_target="tpu_custom_call" | custom-call | flops 10000000000 | tf_op jit(solution)/shard_map/pallas_call | solution.py:29
  9.8 2.6 %collective-permute-start.1 = (f32[64,1024]{1,0:T(8,128)S(1)}, f32[64,1024]{1,0:T(8,128)S(1)}, u32[]{:S(2)}, u32[]{:S(2)}) collective-permute-start(f32[64,1024]{1,0:T(8,128)S(1)} %get-tuple-element.38.refs_0_), channel_id=1, source_target_pairs={{0,2},{1,3},{2,0},{3,1},{4,6},{5,7},{6,4},{7,5},{8,10},{9,11},{10,... | collective-permute-start | bytes 786440 | tf_op jit(solution)/shard_map/ppermute | solution.py:140
  12.5 1.9 %collective-permute-start.4 = (f32[64,1024]{1,0:T(8,128)S(1)}, f32[64,1024]{1,0:T(8,128)S(1)}, u32[]{:S(2)}, u32[]{:S(2)}) collective-permute-start(f32[64,1024]{1,0:T(8,128)S(1)} %get-tuple-element.43.refs_0_), channel_id=1, source_target_pairs={{0,2},{1,3},{2,0},{3,1},{4,6},{5,7},{6,4},{7,5},{8,10},{9,11},{10,... | collective-permute-start | bytes 786440 | tf_op jit(solution)/shard_map/ppermute | solution.py:140
  14.5 5.1 %collective-permute-done.1.refs_1_ = f32[64,1024]{1,0:T(8,128)S(1)} collective-permute-done((f32[64,1024]{1,0:T(8,128)S(1)}, f32[64,1024]{1,0:T(8,128)S(1)}, u32[]{:S(2)}, u32[]{:S(2)}) %collective-permute-start.1) | collective-permute-done | bytes 262176 | tf_op jit(solution)/shard_map/ppermute | solution.py:140
  19.6 0.7 %shard_map.45.refs_2_ = f32[64,1792]{1,0:T(8,128)S(1)} custom-call(f32[64,1024]{1,0:T(8,128)S(1)} %shard_map.44.refs_0_, bf16[1024,1792]{1,0:T(8,128)(2,1)S(1)} %get-tuple-element.41.refs_1_), custom_call_target="tpu_custom_call" | custom-call | flops 10000000000 | tf_op jit(solution)/shard_map/pallas_call | solution.py:29
  20.4 0.8 %collective-permute-done.3.refs_0_.refs_4_ = f32[64,1024]{1,0:T(8,128)S(1)} collective-permute-done((f32[64,1024]{1,0:T(8,128)S(1)}, f32[64,1024]{1,0:T(8,128)S(1)}, u32[]{:S(2)}, u32[]{:S(2)}) %collective-permute-start.3) | collective-permute-done | bytes 262176 | tf_op jit(solution)/shard_map/ppermute | solution.py:140
  21.2 0.7 %shard_map.46 = (f32[32,1792]{1,0:T(8,128)S(1)}, f32[32,1792]{1,0:T(8,128)S(1)}) custom-call(f32[64,1024]{1,0:T(8,128)S(1)} %collective-permute-done.3.refs_0_.refs_4_, bf16[1024,1792]{1,0:T(8,128)(2,1)S(1)} %get-tuple-element.40.refs_1_, f32[64,1792]{1,0:T(8,128)S(1)} %shard_map.45.refs_2_), custom_call_target="tpu_custom_call" | custom-call | flops 10000000000 | tf_op jit(solution)/shard_map/pallas_call | solution.py:29
  21.9 3.2 %collective-permute-done.2.refs_1_ = f32[64,1024]{1,0:T(8,128)S(1)} collective-permute-done((f32[64,1024]{1,0:T(8,128)S(1)}, f32[64,1024]{1,0:T(8,128)S(1)}, u32[]{:S(2)}, u32[]{:S(2)}) %collective-permute-start.2) | collective-permute-done | bytes 262176 | tf_op jit(solution)/shard_map/ppermute | solution.py:140
  25.3 0.7 %shard_map.48.refs_2_ = f32[64,1792]{1,0:T(8,128)S(1)} custom-call(f32[64,1024]{1,0:T(8,128)S(1)} %shard_map.47.refs_0_.refs_1_, bf16[1024,1792]{1,0:T(8,128)(2,1)S(1)} %get-tuple-element.41.refs_1_), custom_call_target="tpu_custom_call" | custom-call | flops 10000000000 | tf_op jit(solution)/shard_map/pallas_call | solution.py:29
  26.0 2.0 %collective-permute-start.7 = (f32[32,1792]{1,0:T(8,128)S(1)}, f32[32,1792]{1,0:T(8,128)S(1)}, u32[]{:S(2)}, u32[]{:S(2)}) collective-permute-start(f32[32,1792]{1,0:T(8,128)S(1)} %get-tuple-element.46), channel_id=1, source_target_pairs={{0,4},{4,0},{8,12},{12,8},{16,20},{20,16},{24,28},{28,24},{1,5},{5... | collective-permute-start | bytes 688136 | tf_op jit(solution)/shard_map/ppermute | solution.py:140
  28.1 0.7 %shard_map.49 = (f32[32,1792]{1,0:T(8,128)S(1)}, f32[32,1792]{1,0:T(8,128)S(1)}) custom-call(f32[64,1024]{1,0:T(8,128)S(1)} %collective-permute-done.5.refs_0_.refs_5_, bf16[1024,1792]{1,0:T(8,128)(2,1)S(1)} %get-tuple-element.40.refs_1_, f32[64,1792]{1,0:T(8,128)S(1)} %shard_map.48.refs_2_), custom_call_target="tpu_custom_call" | custom-call | flops 10000000000 | tf_op jit(solution)/shard_map/pallas_call | solution.py:29
  28.8 2.0 %collective-permute-done.4.refs_1_ = f32[64,1024]{1,0:T(8,128)S(1)} collective-permute-done((f32[64,1024]{1,0:T(8,128)S(1)}, f32[64,1024]{1,0:T(8,128)S(1)}, u32[]{:S(2)}, u32[]{:S(2)}) %collective-permute-start.4) | collective-permute-done | bytes 262176 | tf_op jit(solution)/shard_map/ppermute | solution.py:140
  30.9 0.7 %shard_map.51.refs_2_ = f32[64,1792]{1,0:T(8,128)S(1)} custom-call(f32[64,1024]{1,0:T(8,128)S(1)} %shard_map.50.refs_0_.refs_2_, bf16[1024,1792]{1,0:T(8,128)(2,1)S(1)} %get-tuple-element.41.refs_1_), custom_call_target="tpu_custom_call" | custom-call | flops 10000000000 | tf_op jit(solution)/shard_map/pallas_call | solution.py:29
  31.6 2.0 %collective-permute-start.11 = (f32[32,1792]{1,0:T(8,128)S(1)}, f32[32,1792]{1,0:T(8,128)S(1)}, u32[]{:S(2)}, u32[]{:S(2)}) collective-permute-start(f32[32,1792]{1,0:T(8,128)S(1)} %get-tuple-element.52), channel_id=1, source_target_pairs={{0,4},{4,0},{8,12},{12,8},{16,20},{20,16},{24,28},{28,24},{1,5},{5... | collective-permute-start | bytes 688136 | tf_op jit(solution)/shard_map/ppermute | solution.py:140
  33.7 0.7 %shard_map.52 = (f32[32,1792]{1,0:T(8,128)S(1)}, f32[32,1792]{1,0:T(8,128)S(1)}) custom-call(f32[64,1024]{1,0:T(8,128)S(1)} %collective-permute-done.8.refs_0_.refs_6_, bf16[1024,1792]{1,0:T(8,128)(2,1)S(1)} %get-tuple-element.40.refs_1_, f32[64,1792]{1,0:T(8,128)S(1)} %shard_map.51.refs_2_), custom_call_target="tpu_custom_call" | custom-call | flops 10000000000 | tf_op jit(solution)/shard_map/pallas_call | solution.py:29
  34.5 1.7 %collective-permute-done.6.refs_1_ = f32[64,1024]{1,0:T(8,128)S(1)} collective-permute-done((f32[64,1024]{1,0:T(8,128)S(1)}, f32[64,1024]{1,0:T(8,128)S(1)}, u32[]{:S(2)}, u32[]{:S(2)}) %collective-permute-start.6) | collective-permute-done | bytes 262176 | tf_op jit(solution)/shard_map/ppermute | solution.py:140
  36.3 0.7 %shard_map.55.refs_2_ = f32[64,1792]{1,0:T(8,128)S(1)} custom-call(f32[64,1024]{1,0:T(8,128)S(1)} %shard_map.54.refs_0_.refs_3_, bf16[1024,1792]{1,0:T(8,128)(2,1)S(1)} %get-tuple-element.41.refs_1_), custom_call_target="tpu_custom_call" | custom-call | flops 10000000000 | tf_op jit(solution)/shard_map/pallas_call | solution.py:29
  37.1 1.9 %collective-permute-start.10 = (f32[16,1792]{1,0:T(8,128)S(1)}, f32[16,1792]{1,0:T(8,128)S(1)}, u32[]{:S(2)}, u32[]{:S(2)}) collective-permute-start(f32[16,1792]{1,0:T(8,128)S(1)} %get-tuple-element.51), channel_id=1, source_target_pairs={{0,8},{4,12},{8,0},{12,4},{16,24},{20,28},{24,16},{28,20},{1,9},{5... | collective-permute-start | bytes 344072 | tf_op jit(solution)/shard_map/ppermute | solution.py:140
  38.9 1.5 %collective-permute-start.14 = (f32[32,1792]{1,0:T(8,128)S(1)}, f32[32,1792]{1,0:T(8,128)S(1)}, u32[]{:S(2)}, u32[]{:S(2)}) collective-permute-start(f32[32,1792]{1,0:T(8,128)S(1)} %get-tuple-element.58), channel_id=1, source_target_pairs={{0,4},{4,0},{8,12},{12,8},{16,20},{20,16},{24,28},{28,24},{1,5},{5... | collective-permute-start | bytes 688136 | tf_op jit(solution)/shard_map/ppermute | solution.py:140
  40.5 0.7 %shard_map.56 = (f32[32,1792]{1,0:T(8,128)S(1)}, f32[32,1792]{1,0:T(8,128)S(1)}) custom-call(f32[64,1024]{1,0:T(8,128)S(1)} %collective-permute-done.9.refs_0_.refs_7_, bf16[1024,1792]{1,0:T(8,128)(2,1)S(1)} %get-tuple-element.40.refs_1_, f32[64,1792]{1,0:T(8,128)S(1)} %shard_map.55.refs_2_), custom_call_target="tpu_custom_call" | custom-call | flops 10000000000 | tf_op jit(solution)/shard_map/pallas_call | solution.py:29
  41.2 1.9 %shard_map.57 = (f32[2048,256]{1,0:T(8,128)}, f32[8,128]{1,0:T(8,128)S(1)}) custom-call(f32[64,1024]{1,0:T(8,128)S(1)} %shard_map.44.refs_0_, f32[64,1024]{1,0:T(8,128)S(1)} %shard_map.47.refs_0_.refs_1_, f32[64,1024]{1,0:T(8,128)S(1)} %shard_map.50.refs_0_.refs_2_, f32[64,1024]{1,0:T(8,128)S(1)} %shard_map.54.refs_0_.refs_3_, ...), custom_call_target="tpu_custom_call" | custom-call | flops 10000000000 | tf_op jit(solution)/shard_map/pallas_call | solution.py:29
  44.0 3.4 %collective-permute-done.14.refs_1_ = f32[32,1792]{1,0:T(8,128)S(1)} collective-permute-done((f32[32,1792]{1,0:T(8,128)S(1)}, f32[32,1792]{1,0:T(8,128)S(1)}, u32[]{:S(2)}, u32[]{:S(2)}) %collective-permute-start.14) | collective-permute-done | bytes 229408 | tf_op jit(solution)/shard_map/ppermute | solution.py:140
  47.5 2.7 %collective-permute-start.12 = (f32[8,1792]{1,0:T(8,128)S(1)}, f32[8,1792]{1,0:T(8,128)S(1)}, u32[]{:S(2)}, u32[]{:S(2)}) collective-permute-start(f32[8,1792]{1,0:T(8,128)S(1)} %get-tuple-element.56), channel_id=1, source_target_pairs={{0,16},{4,20},{8,24},{12,28},{16,0},{20,4},{24,8},{28,12},{1,17},{... | collective-permute-start | bytes 172040 | tf_op jit(solution)/shard_map/ppermute | solution.py:140
  50.2 0.7 %collective-permute-start.15 = (f32[8,1792]{1,0:T(8,128)S(1)}, f32[8,1792]{1,0:T(8,128)S(1)}, u32[]{:S(2)}, u32[]{:S(2)}) collective-permute-start(f32[8,1792]{1,0:T(8,128)S(1)} %get-tuple-element.61), channel_id=1, source_target_pairs={{0,16},{4,20},{8,24},{12,28},{16,0},{20,4},{24,8},{28,12},{1,17},{... | collective-permute-start | bytes 172040 | tf_op jit(solution)/shard_map/ppermute | solution.py:140
  50.9 0.7 %collective-permute-done.17.refs_1_ = f32[32,1792]{1,0:T(8,128)S(1)} collective-permute-done((f32[32,1792]{1,0:T(8,128)S(1)}, f32[32,1792]{1,0:T(8,128)S(1)}, u32[]{:S(2)}, u32[]{:S(2)}) %collective-permute-start.17) | collective-permute-done | bytes 229408 | tf_op jit(solution)/shard_map/ppermute | solution.py:140
  51.6 1.0 %collective-permute-start.19 = (f32[16,1792]{1,0:T(8,128)S(1)}, f32[16,1792]{1,0:T(8,128)S(1)}, u32[]{:S(2)}, u32[]{:S(2)}) collective-permute-start(f32[16,1792]{1,0:T(8,128)S(1)} %get-tuple-element.67), channel_id=1, source_target_pairs={{0,8},{4,12},{8,0},{12,4},{16,24},{20,28},{24,16},{28,20},{1,9},{5... | collective-permute-start | bytes 344072 | tf_op jit(solution)/shard_map/ppermute | solution.py:140
  52.6 2.9 %collective-permute-start.18 = (f32[8,1792]{1,0:T(8,128)S(1)}, f32[8,1792]{1,0:T(8,128)S(1)}, u32[]{:S(2)}, u32[]{:S(2)}) collective-permute-start(f32[8,1792]{1,0:T(8,128)S(1)} %get-tuple-element.66), channel_id=1, source_target_pairs={{0,16},{4,20},{8,24},{12,28},{16,0},{20,4},{24,8},{28,12},{1,17},{... | collective-permute-start | bytes 172040 | tf_op jit(solution)/shard_map/ppermute | solution.py:140
  55.6 2.8 %collective-permute-done.19.refs_1_ = f32[16,1792]{1,0:T(8,128)S(1)} collective-permute-done((f32[16,1792]{1,0:T(8,128)S(1)}, f32[16,1792]{1,0:T(8,128)S(1)}, u32[]{:S(2)}, u32[]{:S(2)}) %collective-permute-start.19) | collective-permute-done | bytes 114720 | tf_op jit(solution)/shard_map/ppermute | solution.py:140
  58.4 1.6 %collective-permute-start.20 = (f32[8,1792]{1,0:T(8,128)S(1)}, f32[8,1792]{1,0:T(8,128)S(1)}, u32[]{:S(2)}, u32[]{:S(2)}) collective-permute-start(f32[8,1792]{1,0:T(8,128)S(1)} %get-tuple-element.69), channel_id=1, source_target_pairs={{0,16},{4,20},{8,24},{12,28},{16,0},{20,4},{24,8},{28,12},{1,17},{... | collective-permute-start | bytes 172040 | tf_op jit(solution)/shard_map/ppermute | solution.py:140
  60.0 3.9 %collective-permute-done.20.refs_7_ = f32[8,1792]{1,0:T(8,128)S(1)} collective-permute-done((f32[8,1792]{1,0:T(8,128)S(1)}, f32[8,1792]{1,0:T(8,128)S(1)}, u32[]{:S(2)}, u32[]{:S(2)}) %collective-permute-start.20) | collective-permute-done | bytes 57376 | tf_op jit(solution)/shard_map/ppermute | solution.py:140
  63.9 0.7 %shard_map.65 = f32[32,1792]{1,0:T(8,128)} custom-call(f32[8,1792]{1,0:T(8,128)S(1)} %get-tuple-element.55.refs_2_.refs_0_, f32[8,1792]{1,0:T(8,128)S(1)} %collective-permute-done.12.refs_1_, f32[8,1792]{1,0:T(8,128)S(1)} %get-tuple-element.60.refs_2_, f32[8,1792]{1,0:T(8,128)S(1)} %collective-permute-done.15.refs_3_, ...), custom_call_target="tpu_custom_call" | custom-call | flops 10000000000 | tf_op jit(solution)/shard_map/pallas_call | solution.py:29
  (35 shorter events, 2.3 us)
Async XLA Ops:
  4.9 4.8 %collective-permute-start = (f32[256,1024]{1,0:T(8,128)S(1)}, f32[256,1024]{1,0:T(8,128)S(1)}, u32[]{:S(2)}, u32[]{:S(2)}) collective-permute-start(f32[256,1024]{1,0:T(8,128)S(1)} %get-tuple-element.36.refs_2_), channel_id=1, source_target_pairs={{0,1},{1,0},{2,3},{3,2},{4,5},{5,4},{6,7},{7,6},{8,9},{9,8},{10,11... | collective-permute-start | bytes 3145736 | tf_op jit(solution)/shard_map/ppermute | solution.py:140
  9.8 9.7 %collective-permute-start.1 = (f32[64,1024]{1,0:T(8,128)S(1)}, f32[64,1024]{1,0:T(8,128)S(1)}, u32[]{:S(2)}, u32[]{:S(2)}) collective-permute-start(f32[64,1024]{1,0:T(8,128)S(1)} %get-tuple-element.38.refs_0_), channel_id=1, source_target_pairs={{0,2},{1,3},{2,0},{3,1},{4,6},{5,7},{6,4},{7,5},{8,10},{9,11},{10,... | collective-permute-start | bytes 786440 | tf_op jit(solution)/shard_map/ppermute | solution.py:140
  12.4 12.8 %collective-permute-start.2 = (f32[64,1024]{1,0:T(8,128)S(1)}, f32[64,1024]{1,0:T(8,128)S(1)}, u32[]{:S(2)}, u32[]{:S(2)}) collective-permute-start(f32[64,1024]{1,0:T(8,128)S(1)} %get-tuple-element.39.refs_0_), channel_id=1, source_target_pairs={{0,2},{1,3},{2,0},{3,1},{4,6},{5,7},{6,4},{7,5},{8,10},{9,11},{10,... | collective-permute-start | bytes 786440 | tf_op jit(solution)/shard_map/ppermute | solution.py:140
  12.5 18.3 %collective-permute-start.4 = (f32[64,1024]{1,0:T(8,128)S(1)}, f32[64,1024]{1,0:T(8,128)S(1)}, u32[]{:S(2)}, u32[]{:S(2)}) collective-permute-start(f32[64,1024]{1,0:T(8,128)S(1)} %get-tuple-element.43.refs_0_), channel_id=1, source_target_pairs={{0,2},{1,3},{2,0},{3,1},{4,6},{5,7},{6,4},{7,5},{8,10},{9,11},{10,... | collective-permute-start | bytes 786440 | tf_op jit(solution)/shard_map/ppermute | solution.py:140
  14.4 21.8 %collective-permute-start.6 = (f32[64,1024]{1,0:T(8,128)S(1)}, f32[64,1024]{1,0:T(8,128)S(1)}, u32[]{:S(2)}, u32[]{:S(2)}) collective-permute-start(f32[64,1024]{1,0:T(8,128)S(1)} %get-tuple-element.45.refs_0_), channel_id=1, source_target_pairs={{0,2},{1,3},{2,0},{3,1},{4,6},{5,7},{6,4},{7,5},{8,10},{9,11},{10,... | collective-permute-start | bytes 786440 | tf_op jit(solution)/shard_map/ppermute | solution.py:140
  19.6 1.6 %collective-permute-start.3 = (f32[64,1024]{1,0:T(8,128)S(1)}, f32[64,1024]{1,0:T(8,128)S(1)}, u32[]{:S(2)}, u32[]{:S(2)}) collective-permute-start(f32[64,1024]{1,0:T(8,128)S(1)} %shard_map.44.refs_0_), channel_id=1, source_target_pairs={{0,1},{1,0},{2,3},{3,2},{4,5},{5,4},{6,7},{7,6},{8,9},{9,8},{10,11... | collective-permute-start | bytes 786440 | tf_op jit(solution)/shard_map/ppermute | solution.py:140
  25.2 2.9 %collective-permute-start.5 = (f32[64,1024]{1,0:T(8,128)S(1)}, f32[64,1024]{1,0:T(8,128)S(1)}, u32[]{:S(2)}, u32[]{:S(2)}) collective-permute-start(f32[64,1024]{1,0:T(8,128)S(1)} %shard_map.47.refs_0_.refs_1_), channel_id=1, source_target_pairs={{0,1},{1,0},{2,3},{3,2},{4,5},{5,4},{6,7},{7,6},{8,9},{9,8},{10,11... | collective-permute-start | bytes 786440 | tf_op jit(solution)/shard_map/ppermute | solution.py:140
  26.0 8.4 %collective-permute-start.7 = (f32[32,1792]{1,0:T(8,128)S(1)}, f32[32,1792]{1,0:T(8,128)S(1)}, u32[]{:S(2)}, u32[]{:S(2)}) collective-permute-start(f32[32,1792]{1,0:T(8,128)S(1)} %get-tuple-element.46), channel_id=1, source_target_pairs={{0,4},{4,0},{8,12},{12,8},{16,20},{20,16},{24,28},{28,24},{1,5},{5... | collective-permute-start | bytes 688136 | tf_op jit(solution)/shard_map/ppermute | solution.py:140
  30.8 2.9 %collective-permute-start.8 = (f32[64,1024]{1,0:T(8,128)S(1)}, f32[64,1024]{1,0:T(8,128)S(1)}, u32[]{:S(2)}, u32[]{:S(2)}) collective-permute-start(f32[64,1024]{1,0:T(8,128)S(1)} %shard_map.50.refs_0_.refs_2_), channel_id=1, source_target_pairs={{0,1},{1,0},{2,3},{3,2},{4,5},{5,4},{6,7},{7,6},{8,9},{9,8},{10,11... | collective-permute-start | bytes 786440 | tf_op jit(solution)/shard_map/ppermute | solution.py:140
  31.6 11.5 %collective-permute-start.11 = (f32[32,1792]{1,0:T(8,128)S(1)}, f32[32,1792]{1,0:T(8,128)S(1)}, u32[]{:S(2)}, u32[]{:S(2)}) collective-permute-start(f32[32,1792]{1,0:T(8,128)S(1)} %get-tuple-element.52), channel_id=1, source_target_pairs={{0,4},{4,0},{8,12},{12,8},{16,20},{20,16},{24,28},{28,24},{1,5},{5... | collective-permute-start | bytes 688136 | tf_op jit(solution)/shard_map/ppermute | solution.py:140
  36.2 4.2 %collective-permute-start.9 = (f32[64,1024]{1,0:T(8,128)S(1)}, f32[64,1024]{1,0:T(8,128)S(1)}, u32[]{:S(2)}, u32[]{:S(2)}) collective-permute-start(f32[64,1024]{1,0:T(8,128)S(1)} %shard_map.54.refs_0_.refs_3_), channel_id=1, source_target_pairs={{0,1},{1,0},{2,3},{3,2},{4,5},{5,4},{6,7},{7,6},{8,9},{9,8},{10,11... | collective-permute-start | bytes 786440 | tf_op jit(solution)/shard_map/ppermute | solution.py:140
  37.1 6.9 %collective-permute-start.10 = (f32[16,1792]{1,0:T(8,128)S(1)}, f32[16,1792]{1,0:T(8,128)S(1)}, u32[]{:S(2)}, u32[]{:S(2)}) collective-permute-start(f32[16,1792]{1,0:T(8,128)S(1)} %get-tuple-element.51), channel_id=1, source_target_pairs={{0,8},{4,12},{8,0},{12,4},{16,24},{20,28},{24,16},{28,20},{1,9},{5... | collective-permute-start | bytes 344072 | tf_op jit(solution)/shard_map/ppermute | solution.py:140
  38.9 8.4 %collective-permute-start.14 = (f32[32,1792]{1,0:T(8,128)S(1)}, f32[32,1792]{1,0:T(8,128)S(1)}, u32[]{:S(2)}, u32[]{:S(2)}) collective-permute-start(f32[32,1792]{1,0:T(8,128)S(1)} %get-tuple-element.58), channel_id=1, source_target_pairs={{0,4},{4,0},{8,12},{12,8},{16,20},{20,16},{24,28},{28,24},{1,5},{5... | collective-permute-start | bytes 688136 | tf_op jit(solution)/shard_map/ppermute | solution.py:140
  43.2 7.0 %collective-permute-start.13 = (f32[16,1792]{1,0:T(8,128)S(1)}, f32[16,1792]{1,0:T(8,128)S(1)}, u32[]{:S(2)}, u32[]{:S(2)}) collective-permute-start(f32[16,1792]{1,0:T(8,128)S(1)} %get-tuple-element.57), channel_id=1, source_target_pairs={{0,8},{4,12},{8,0},{12,4},{16,24},{20,28},{24,16},{28,20},{1,9},{5... | collective-permute-start | bytes 344072 | tf_op jit(solution)/shard_map/ppermute | solution.py:140
  43.7 7.9 %collective-permute-start.17 = (f32[32,1792]{1,0:T(8,128)S(1)}, f32[32,1792]{1,0:T(8,128)S(1)}, u32[]{:S(2)}, u32[]{:S(2)}) collective-permute-start(f32[32,1792]{1,0:T(8,128)S(1)} %get-tuple-element.63), channel_id=1, source_target_pairs={{0,4},{4,0},{8,12},{12,8},{16,20},{20,16},{24,28},{28,24},{1,5},{5... | collective-permute-start | bytes 688136 | tf_op jit(solution)/shard_map/ppermute | solution.py:140
  47.4 5.2 %collective-permute-start.16 = (f32[16,1792]{1,0:T(8,128)S(1)}, f32[16,1792]{1,0:T(8,128)S(1)}, u32[]{:S(2)}, u32[]{:S(2)}) collective-permute-start(f32[16,1792]{1,0:T(8,128)S(1)} %get-tuple-element.62), channel_id=1, source_target_pairs={{0,8},{4,12},{8,0},{12,4},{16,24},{20,28},{24,16},{28,20},{1,9},{5... | collective-permute-start | bytes 344072 | tf_op jit(solution)/shard_map/ppermute | solution.py:140
  47.5 12.5 %collective-permute-start.12 = (f32[8,1792]{1,0:T(8,128)S(1)}, f32[8,1792]{1,0:T(8,128)S(1)}, u32[]{:S(2)}, u32[]{:S(2)}) collective-permute-start(f32[8,1792]{1,0:T(8,128)S(1)} %get-tuple-element.56), channel_id=1, source_target_pairs={{0,16},{4,20},{8,24},{12,28},{16,0},{20,4},{24,8},{28,12},{1,17},{... | collective-permute-start | bytes 172040 | tf_op jit(solution)/shard_map/ppermute | solution.py:140
  50.2 9.9 %collective-permute-start.15 = (f32[8,1792]{1,0:T(8,128)S(1)}, f32[8,1792]{1,0:T(8,128)S(1)}, u32[]{:S(2)}, u32[]{:S(2)}) collective-permute-start(f32[8,1792]{1,0:T(8,128)S(1)} %get-tuple-element.61), channel_id=1, source_target_pairs={{0,16},{4,20},{8,24},{12,28},{16,0},{20,4},{24,8},{28,12},{1,17},{... | collective-permute-start | bytes 172040 | tf_op jit(solution)/shard_map/ppermute | solution.py:140
  51.6 6.8 %collective-permute-start.19 = (f32[16,1792]{1,0:T(8,128)S(1)}, f32[16,1792]{1,0:T(8,128)S(1)}, u32[]{:S(2)}, u32[]{:S(2)}) collective-permute-start(f32[16,1792]{1,0:T(8,128)S(1)} %get-tuple-element.67), channel_id=1, source_target_pairs={{0,8},{4,12},{8,0},{12,4},{16,24},{20,28},{24,16},{28,20},{1,9},{5... | collective-permute-start | bytes 344072 | tf_op jit(solution)/shard_map/ppermute | solution.py:140
  52.6 7.4 %collective-permute-start.18 = (f32[8,1792]{1,0:T(8,128)S(1)}, f32[8,1792]{1,0:T(8,128)S(1)}, u32[]{:S(2)}, u32[]{:S(2)}) collective-permute-start(f32[8,1792]{1,0:T(8,128)S(1)} %get-tuple-element.66), channel_id=1, source_target_pairs={{0,16},{4,20},{8,24},{12,28},{16,0},{20,4},{24,8},{28,12},{1,17},{... | collective-permute-start | bytes 172040 | tf_op jit(solution)/shard_map/ppermute | solution.py:140
  58.4 5.5 %collective-permute-start.20 = (f32[8,1792]{1,0:T(8,128)S(1)}, f32[8,1792]{1,0:T(8,128)S(1)}, u32[]{:S(2)}, u32[]{:S(2)}) collective-permute-start(f32[8,1792]{1,0:T(8,128)S(1)} %get-tuple-element.69), channel_id=1, source_target_pairs={{0,16},{4,20},{8,24},{12,28},{16,0},{20,4},{24,8},{28,12},{1,17},{... | collective-permute-start | bytes 172040 | tf_op jit(solution)/shard_map/ppermute | solution.py:140

commit v4 on v0

v4 whole, which is shorter than its diff:
```python
import functools

import jax
import jax.numpy as jnp
from jax import lax
from jax.experimental import pallas as pl
from jax.experimental.pallas import tpu as pltpu
from jax.sharding import PartitionSpec as P

EIGHTHS = (2, 2, 2, 2)
BLOCK = 512
F32 = jnp.float32
BF16 = jnp.bfloat16
NT = (((1,), (1,)), ((), ()))
SPECS = {"v": pl.BlockSpec(memory_space=pltpu.VMEM), "a": pl.BlockSpec(memory_space=pl.ANY)}
E0 = 19.5
DE = 10
GT = 12.4
WEIGHT = 0
WQ = 0
WE = 5*10**8
WC = 0
WP = 0
SPLIT = 2
DIRECT = 1


def call(body, args, outs, kinds=None, after=(), scratch=(), results=0, weight=None):
    n = len(args)
    kinds = (kinds or "v" * n) + "a" * len(after)

    def run(*refs):
        body(*refs[:n], *refs[len(kinds) :])

    return pl.pallas_call(
        run,
        out_shape=[pltpu.VMEM(*o) if i >= results else jax.ShapeDtypeStruct(*o) for i, o in enumerate(outs)],
        in_specs=[SPECS[kind] for kind in kinds],
        out_specs=[SPECS["v"]] * len(outs),
        scratch_shapes=list(scratch),
        cost_estimate=pl.CostEstimate(flops=WEIGHT if weight is None else weight, bytes_accessed=0, transcendentals=0),
        compiler_params=pltpu.CompilerParams(vmem_limit_bytes=16 << 20),
    )(*args, *after)


def owner_at(index, n_row):
    owner, bit = index * 0, 1
    while bit < n_row:
        owner = 2 * owner + index % 2
        index = index // 2
        bit *= 2
    return owner


def column_of(position, k, n_row, pieces):
    column, first, done = position * 0, 0, 0
    for piece in pieces:
        rest = position - first
        found = owner_at(rest // piece, n_row) * (k // n_row) + done + rest % piece
        column = jnp.where((rest >= 0) & (rest < piece * n_row), found, column)
        first += piece * n_row
        done += piece
    return column


def stream_half(delta, held, sem, mine):
    rows = held.shape[0]
    parity = lax.rem(lax.axis_index("col"), 2)
    first = (parity if mine else 1 - parity) * rows
    copies = []
    for b in range(rows // BLOCK):
        source = delta.at[pl.ds(pl.multiple_of(first + b * BLOCK, BLOCK), BLOCK), :]
        copies.append(pltpu.make_async_copy(source, held.at[pl.ds(b * BLOCK, BLOCK), :], sem.at[b]))
        copies[-1].start()
    return copies


def sketch_half(omega_t, held, copies, out):
    for b, copy in enumerate(copies):
        copy.wait()
        block = pl.ds(b * BLOCK, BLOCK)
        out[:, block] = lax.dot_general(omega_t[...], held[block, :], NT, preferred_element_type=F32)


def first_half_body(n_row, pieces, delta, omega, held, omega_t, out, omega_v, sem, omega_sem):
    k = out.shape[0]
    fetch = pltpu.make_async_copy(omega, omega_v, omega_sem)
    fetch.start()
    copies = stream_half(delta, held, sem, False)
    position = lax.broadcasted_iota(jnp.int32, (k, k), 0)
    column = lax.broadcasted_iota(jnp.int32, (k, k), 1)
    pick = jnp.where(column_of(position, k, n_row, pieces) == column, 1.0, 0.0).astype(BF16)
    fetch.wait()
    omega_t[...] = lax.dot_general(pick, omega_v[...], NT, preferred_element_type=F32).astype(BF16)
    sketch_half(omega_t, held, copies, out)


def second_half_body(delta, omega_t, held, out, sem):
    sketch_half(omega_t, held, stream_half(delta, held, sem, True), out)


def add_chunks_body(kept, received, *outs):
    first = 0
    for out in outs:
        part = pl.ds(first, out.shape[0])
        out[...] = kept[part, :] + received[part, :]
        first += out.shape[0]


def add_body(a, b, *outs):
    first = 0
    for out in outs:
        part = pl.ds(first, out.shape[0])
        out[...] = a[part, :] + b[part, :]
        first += out.shape[0]


def joined(refs):
    return jnp.concatenate([ref[...] for ref in refs], axis=0)


def product_body(*refs):
    *sketch, held, out = refs
    out[...] = jnp.dot(joined(sketch).astype(BF16), held[...], preferred_element_type=F32)


def halves(bit, ref):
    half = ref.shape[0] // 2
    own = lax.rem(lax.axis_index("row") // bit, 2)
    if half % 8:
        low, high = ref[:half, :], ref[half:, :]
        return jnp.where(own == 0, high, low), jnp.where(own == 0, low, high)
    theirs = pl.ds(pl.multiple_of((1 - own) * half, half), half)
    mine = pl.ds(pl.multiple_of(own * half, half), half)
    return ref[theirs, :], ref[mine, :]


def product_send_body(*refs):
    *sketch, held, before, send, keep, total = refs
    total[...] = before[...] + jnp.dot(joined(sketch).astype(BF16), held[...], preferred_element_type=F32)
    send[...], keep[...] = halves(1, total)


def add_send_body(bit, kept, received, send, keep):
    for out, a, b in zip((send, keep), halves(bit, kept), halves(bit, received)):
        out[...] = a + b


def add_spread_body(n_high, kept, received, *outs):
    piece = outs[0].shape[0]
    place = owner_at(lax.axis_index("row") // 2, n_high)
    for flip, out in enumerate(outs):
        part = pl.ds(pl.multiple_of(lax.bitwise_xor(place, flip) * piece, piece), piece)
        out[...] = kept[part, :] + received[part, :]


def final_corange_body(counts, *refs):
    out = refs[-1]
    first, used = 0, 0
    for count in counts:
        terms = refs[used : used + count]
        piece = terms[0].shape[0]
        out[pl.ds(first, piece), :] = functools.reduce(jnp.add, [term[...] for term in terms])
        first += piece
        used += count


def final_sketch_body(n_row, pieces, *refs):
    out, done = refs[-2:]
    n, rows = len(refs) // 2 - 1, refs[0].shape[1]
    parity = lax.rem(lax.axis_index("col"), 2)
    per_part = n_row // SPLIT
    for side in range(2):
        parts = refs[side * n : (side + 1) * n]
        first = (parity if side == 0 else 1 - parity) * rows
        for b in range(rows // 128):
            lanes = pl.ds(b * 128, 128)
            found = []
            for r in range(n_row):
                place = owner_at(r, n_row)
                for c, piece in enumerate(pieces):
                    part = parts[c * SPLIT + place // per_part]
                    found.append(part[pl.ds(place % per_part * piece, piece), lanes])
            block = jnp.concatenate(found, axis=0)
            out[pl.ds(pl.multiple_of(first + b * 128, 128), 128), :] = block.T
    done[...] = jnp.zeros_like(done)


def swap(x, axis, size, bit):
    return lax.ppermute(x, axis, [(i, i ^ bit) for i in range(size)])


def shards(n_row, n_col, delta, omega):
    rows, d = delta.shape
    k = omega.shape[1]
    half = rows // 2
    per_owner = k // n_row
    pieces = [per_owner * part // sum(EIGHTHS) for part in EIGHTHS] if per_owner % 8 == 0 else [1] * per_owner
    widths = [piece * n_row for piece in pieces]
    n = len(pieces)
    bits = [1 << i for i in range(n_row.bit_length() - 1)]

    in_hbm = pltpu.with_memory_space_constraint(delta, pltpu.HBM)
    sems = pltpu.SemaphoreType.DMA((half // BLOCK,))
    held_other, omega_t, to_send = call(
        functools.partial(first_half_body, n_row, pieces),
        (in_hbm, pltpu.with_memory_space_constraint(omega, pltpu.HBM)),
        [((half, d), BF16), ((k, d), BF16), ((k, half), F32)],
        "aa",
        scratch=[pltpu.VMEM((d, k), BF16), sems, pltpu.SemaphoreType.DMA],
    )
    received = swap(to_send, "col", n_col, 1)
    held_own, kept = call(second_half_body, (in_hbm, omega_t), [((half, d), BF16), ((k, half), F32)], "av", scratch=[sems])
    partial = call(add_chunks_body, (kept, received), [((width, half), F32) for width in widths])
    bit = 2
    while bit < n_col // 2:
        moved = [swap(x, "col", n_col, bit) for x in partial]
        partial = [call(add_body, pair, [(pair[0].shape, F32)])[0] for pair in zip(partial, moved)]
        bit *= 2
    moved = [swap(x, "col", n_col, bit) for x in partial]

    owns, others, befores, pending = {}, {}, {}, {}
    sketch = None
    last = ()
    steps = []
    direct = [len(bits) == 3 and pieces[c] % 8 == 0 and c >= n - DIRECT for c in range(n)]
    for c in range(n):
        steps += [(10 * c, "own", c, 0), (10 * c + 1, "before", c, 0), (10 * c + 2, "send", c, 0)]
        steps += [(10 * c + E0 + DE * s, "add", c, s + 1) for s in range(1 if direct[c] else len(bits) - 1)]
    steps.append((10 * (n - 1) + GT, "sketch", 0, 0))
    for _, step, c, s in sorted(steps):
        width = widths[c]
        if step == "own":
            outs = [((width // SPLIT, half), F32)] * SPLIT
            owns[c] = call(add_body, (partial[c], moved[c]), outs, after=last, weight=WC)
            others[c] = [swap(x, "col", n_col, 1) for x in owns[c]]
            last = (owns[c][0],)
        elif step == "before":
            befores[c] = call(product_body, (*owns[c], held_own), [((width, d), F32)], after=last, weight=WP)[0]
            last = (befores[c],)
        elif step == "send":
            outs = [((width // 2, d), F32)] * 2
            total = pltpu.VMEM((width, d), F32)
            args = (*others[c], held_other, befores[c])
            send, keep = call(product_send_body, args, outs, after=last, scratch=[total], weight=WQ)
            pending[c] = keep, swap(send, "row", n_row, bits[0])
            last = (keep,)
        elif step == "add" and direct[c]:
            outs = [((pieces[c], d), F32)] * (n_row // 2)
            own, *sends = call(functools.partial(add_spread_body, n_row // 2), pending[c], outs, after=last, weight=WE)
            flips = [2 * owner_at(flip, n_row // 2) for flip in range(1, n_row // 2)]
            pending[c] = own, *[swap(x, "row", n_row, flip) for x, flip in zip(sends, flips)]
            last = (own,)
        elif step == "add":
            outs = [((width >> (s + 1), d), F32)] * 2
            send, keep = call(functools.partial(add_send_body, bits[s]), pending[c], outs, after=last, weight=WE)
            pending[c] = keep, swap(send, "row", n_row, bits[s])
            last = (keep,)
        else:
            parts = [[x for group in groups.values() for x in group] for groups in (owns, others)]
            sketch, done = finish_sketch(n_row, k, pieces, *parts, last)
            last = (done,)
    flat = [x for c in range(n) for x in pending[c]]
    if per_owner % 8 == 0:
        body = functools.partial(final_corange_body, [len(pending[c]) for c in range(n)])
        corange = call(body, flat, [((per_owner, d), F32)], results=1)[0]
    else:
        corange = jnp.concatenate([functools.reduce(jnp.add, pending[c]) for c in range(n)], axis=0)
    return sketch, corange.T


def finish_sketch(n_row, k, pieces, owns, others, after):
    half = owns[0].shape[1]
    if k // n_row % 8 == 0:
        body = functools.partial(final_sketch_body, n_row, pieces)
        return call(body, (*owns, *others), [((2 * half, k), F32), ((8, 128), F32)], after=after, results=1)
    places = jnp.array([owner_at(r, n_row) for r in range(n_row)])

    def columns(parts):
        parts = [jnp.concatenate(parts[c : c + SPLIT], axis=0) for c in range(0, len(parts), SPLIT)]
        found = [part.reshape(n_row, piece, half)[places] for part, piece in zip(parts, pieces)]
        return jnp.concatenate(found, axis=1).reshape(k, half).T

    own, other = columns(owns), columns(others)
    first = lax.rem(lax.axis_index("col"), 2) == 0
    return jnp.where(first, jnp.concatenate([own, other]), jnp.concatenate([other, own])), after[0]


def solution(mesh):
    body = functools.partial(shards, mesh.shape["row"], mesh.shape["col"])
    in_specs = (P("row", "col"), P("col", None))
    out_specs = (P("row", None), P("col", "row"))
    return jax.shard_map(body, mesh=mesh, in_specs=in_specs, out_specs=out_specs, check_vma=False)
```

time: 151 us -> 59.2 us (0.39)
  waiting for transfers between devices: 121 us -> 15.9 us
  starting transfers between devices: 0.08 us -> 27.1 us
  Pallas kernels: 0 us -> 15.2 us
  matrix products: 13.7 us -> 0 us
  between operations: 14 us -> 0.87 us
  local copies, waits for them, and re-layouts: 2.45 us -> 0 us
    reduce_scatter x1 -> x0, waiting for transfers between devices: 66.6 us -> none  [shards(): lax.psum_scatter(local_terms, 'row', scatter_dimension=1, tiled=True)]
    psum x1 -> x0, waiting for transfers between devices: 54.2 us -> none  [shards(): sketch = lax.psum(partial_value, 'col')]
    ppermute x0 -> x26, starting transfers between devices: none -> 27.1 us  [swap(): return lax.ppermute(x, axis, [(i, i ^ bit) for i in range(size)])]
    ppermute x0 -> x26, waiting for transfers between devices: none -> 15.9 us  [swap(): return lax.ppermute(x, axis, [(i, i ^ bit) for i in range(size)])]
    pallas_call x0 -> x24, Pallas kernels: none -> 15.2 us  [call(): pl.pallas_call(run, out_shape=[pltpu.VMEM(*o) if i >= results else jax.Sh...]
    dot_general x2 -> x0, matrix products: 13.7 us -> none  [the longest x1 7.19 us: shards(): lax.dot_general(delta, sketch_half, (((0,), (0,)), ((), ())), preferred_e...]
    unnamed x5 -> x0, local copies, waits for them, and re-layouts: 2.45 us -> none
  transfers between devices with their start and end apart: 2 -> 26, of which waited for: 2 -> 10; matrix products, arithmetic and copies ran while one was open for 0% -> 0% of each run, Pallas kernels for 0% -> 19%
where the time goes in v4:
time: 59.2 us; the launch traced here: 59.1 us
  starting transfers between devices  27.1 us (46%)
  waiting for transfers between devices  15.9 us (27%)
  Pallas kernels  15.2 us (26%)
  between operations  0.87 us (1%)
    ppermute x26, starting transfers between devices, swap(): return lax.ppermute(x, axis, [(i, i ^ bit) for i in range(size)])  27.1 us
    ppermute x26, waiting for transfers between devices, swap(): return lax.ppermute(x, axis, [(i, i ^ bit) for i in range(size)])  15.9 us
    pallas_call x24, Pallas kernels, call(): pl.pallas_call(run, out_shape=[pltpu.VMEM(*o) if i >= results else jax.Sh...  15.2 us
  transfers between devices with their start and end apart: 26, of which 10 were waited for; matrix products, arithmetic and copies ran while one was open for 0% of the time, Pallas kernels for 19%

profile of v4, /device:TPU:0, one launch (start us, length us, event | category | flops | bytes accessed | tf_op | source)
XLA Modules:
  0.0 59.1 jit_solution(3267297351481601481)
XLA Ops:
  0.6 3.2 %shard_map.41 = (bf16[1024,1792]{1,0:T(8,128)(2,1)S(1)}, bf16[256,1792]{1,0:T(8,128)(2,1)S(1)}, f32[256,1024]{1,0:T(8,128)S(1)}) custom-call(bf16[2048,1792]{1,0:T(8,128)(2,1)} %refs_0_.3, bf16[1792,256]{1,0:T(8,128)(2,1)} %refs_1_.1), custom_call_target="tpu_custom_call" | custom-call | tf_op jit(solution)/shard_map/pallas_call | solution.py:35
  3.8 0.5 collective-permute-start
  4.3 2.9 %shard_map.42 = (bf16[1024,1792]{1,0:T(8,128)(2,1)S(1)}, f32[256,1024]{1,0:T(8,128)S(1)}) custom-call(bf16[2048,1792]{1,0:T(8,128)(2,1)} %refs_0_.3, bf16[256,1792]{1,0:T(8,128)(2,1)S(1)} %get-tuple-element.45.refs_1_), custom_call_target="tpu_custom_call" | custom-call | tf_op jit(solution)/shard_map/pallas_call | solution.py:35
  7.3 2.6 %collective-permute-start.1 = (f32[64,1024]{1,0:T(8,128)S(1)}, f32[64,1024]{1,0:T(8,128)S(1)}, u32[]{:S(2)}, u32[]{:S(2)}) collective-permute-start(f32[64,1024]{1,0:T(8,128)S(1)} %get-tuple-element.48.refs_0_), channel_id=1, source_target_pairs={{0,2},{1,3},{2,0},{3,1},{4,6},{5,7},{6,4},{7,5},{8,10},{9,11},{10,... | collective-permute-start | bytes 786440 | tf_op jit(solution)/shard_map/ppermute | solution.py:190
  10.0 7.1 %collective-permute-done.1.refs_1_ = f32[64,1024]{1,0:T(8,128)S(1)} collective-permute-done((f32[64,1024]{1,0:T(8,128)S(1)}, f32[64,1024]{1,0:T(8,128)S(1)}, u32[]{:S(2)}, u32[]{:S(2)}) %collective-permute-start.1) | collective-permute-done | bytes 262176 | tf_op jit(solution)/shard_map/ppermute | solution.py:190
  17.2 0.5 collective-permute-start.4
  17.7 0.7 %shard_map.45.refs_3_.refs_4_ = f32[64,1792]{1,0:T(8,128)S(1)} custom-call(f32[32,1024]{1,0:T(8,128)S(1)} %get-tuple-element.49.refs_0_.refs_3_, f32[32,1024]{1,0:T(8,128)S(1)} %get-tuple-element.50.refs_1_, bf16[1024,1792]{1,0:T(8,128)(2,1)S(1)} %get-tuple-element.53.refs_2_, f32[32,1024]{1,0:T(8,128)S(1)} %get-tuple-element.49.refs_0_.refs_3_), custom_call_target="tpu_custom_call" | custom-call | tf_op jit(solution)/shard_map/pallas_call | solution.py:35
  18.7 0.8 %shard_map.46 = (f32[32,1792]{1,0:T(8,128)S(1)}, f32[32,1792]{1,0:T(8,128)S(1)}) custom-call(f32[32,1024]{1,0:T(8,128)S(1)} %collective-permute-done.3.refs_0_.refs_8_, f32[32,1024]{1,0:T(8,128)S(1)} %collective-permute-done.4.refs_1_.refs_9_, bf16[1024,1792]{1,0:T(8,128)(2,1)S(1)} %get-tuple-element.52.refs_2_, f32[64,1792]{1,0:T(8,128)S(1)} %shard_map.45.refs_3_.refs_4_, ...), custom_call_target="tpu_custom_call" | custom-call | tf_op jit(solution)/shard_map/pallas_call | solution.py:35
  19.5 2.0 %collective-permute-start.6 = (f32[32,1792]{1,0:T(8,128)S(1)}, f32[32,1792]{1,0:T(8,128)S(1)}, u32[]{:S(2)}, u32[]{:S(2)}) collective-permute-start(f32[32,1792]{1,0:T(8,128)S(1)} %get-tuple-element.58), channel_id=1, source_target_pairs={{0,4},{4,0},{8,12},{12,8},{16,20},{20,16},{24,28},{28,24},{1,5},{5... | collective-permute-start | bytes 688136 | tf_op jit(solution)/shard_map/ppermute | solution.py:190
  21.5 1.5 %collective-permute-start.5 = (f32[64,1024]{1,0:T(8,128)S(1)}, f32[64,1024]{1,0:T(8,128)S(1)}, u32[]{:S(2)}, u32[]{:S(2)}) collective-permute-start(f32[64,1024]{1,0:T(8,128)S(1)} %get-tuple-element.57.refs_0_), channel_id=1, source_target_pairs={{0,2},{1,3},{2,0},{3,1},{4,6},{5,7},{6,4},{7,5},{8,10},{9,11},{10,... | collective-permute-start | bytes 786440 | tf_op jit(solution)/shard_map/ppermute | solution.py:190
  23.6 0.7 %shard_map.48.refs_3_.refs_4_ = f32[64,1792]{1,0:T(8,128)S(1)} custom-call(f32[32,1024]{1,0:T(8,128)S(1)} %get-tuple-element.55.refs_0_.refs_3_.refs_2_, f32[32,1024]{1,0:T(8,128)S(1)} %get-tuple-element.56.refs_1_.refs_3_, bf16[1024,1792]{1,0:T(8,128)(2,1)S(1)} %get-tuple-element.53.refs_2_, f32[32,1024]{1,0:T(8,128)S(1)} %get-tuple-element.55.refs_0_.refs_3_.refs_2_), custom_call_target="tpu_custom_call" | custom-call | tf_op jit(solution)/shard_map/pallas_call | solution.py:35
  24.7 0.8 %shard_map.49 = (f32[32,1792]{1,0:T(8,128)S(1)}, f32[32,1792]{1,0:T(8,128)S(1)}) custom-call(f32[32,1024]{1,0:T(8,128)S(1)} %collective-permute-done.7.refs_0_.refs_10_, f32[32,1024]{1,0:T(8,128)S(1)} %collective-permute-done.8.refs_1_.refs_11_, bf16[1024,1792]{1,0:T(8,128)(2,1)S(1)} %get-tuple-element.52.refs_2_, f32[64,1792]{1,0:T(8,128)S(1)} %shard_map.48.refs_3_.refs_4_, ...), custom_call_target="tpu_custom_call" | custom-call | tf_op jit(solution)/shard_map/pallas_call | solution.py:35
  25.4 1.3 %collective-permute-start.10 = (f32[32,1792]{1,0:T(8,128)S(1)}, f32[32,1792]{1,0:T(8,128)S(1)}, u32[]{:S(2)}, u32[]{:S(2)}) collective-permute-start(f32[32,1792]{1,0:T(8,128)S(1)} %get-tuple-element.64), channel_id=1, source_target_pairs={{0,4},{4,0},{8,12},{12,8},{16,20},{20,16},{24,28},{28,24},{1,5},{5... | collective-permute-start | bytes 688136 | tf_op jit(solution)/shard_map/ppermute | solution.py:190
  26.7 1.5 %collective-permute-start.9 = (f32[64,1024]{1,0:T(8,128)S(1)}, f32[64,1024]{1,0:T(8,128)S(1)}, u32[]{:S(2)}, u32[]{:S(2)}) collective-permute-start(f32[64,1024]{1,0:T(8,128)S(1)} %get-tuple-element.63.refs_0_), channel_id=1, source_target_pairs={{0,2},{1,3},{2,0},{3,1},{4,6},{5,7},{6,4},{7,5},{8,10},{9,11},{10,... | collective-permute-start | bytes 786440 | tf_op jit(solution)/shard_map/ppermute | solution.py:190
  28.3 1.9 %collective-permute-done.5.refs_1_ = f32[64,1024]{1,0:T(8,128)S(1)} collective-permute-done((f32[64,1024]{1,0:T(8,128)S(1)}, f32[64,1024]{1,0:T(8,128)S(1)}, u32[]{:S(2)}, u32[]{:S(2)}) %collective-permute-start.5) | collective-permute-done | bytes 262176 | tf_op jit(solution)/shard_map/ppermute | solution.py:190
  30.8 1.6 %collective-permute-start.11 = (f32[16,1792]{1,0:T(8,128)S(1)}, f32[16,1792]{1,0:T(8,128)S(1)}, u32[]{:S(2)}, u32[]{:S(2)}) collective-permute-start(f32[16,1792]{1,0:T(8,128)S(1)} %get-tuple-element.65), channel_id=1, source_target_pairs={{0,8},{4,12},{8,0},{12,4},{16,24},{20,28},{24,16},{28,20},{1,9},{5... | collective-permute-start | bytes 344072 | tf_op jit(solution)/shard_map/ppermute | solution.py:190
  32.3 0.7 %shard_map.52.refs_3_.refs_4_ = f32[64,1792]{1,0:T(8,128)S(1)} custom-call(f32[32,1024]{1,0:T(8,128)S(1)} %get-tuple-element.61.refs_0_.refs_3_.refs_4_, f32[32,1024]{1,0:T(8,128)S(1)} %get-tuple-element.62.refs_1_.refs_5_, bf16[1024,1792]{1,0:T(8,128)(2,1)S(1)} %get-tuple-element.53.refs_2_, f32[32,1024]{1,0:T(8,128)S(1)} %get-tuple-element.61.refs_0_.refs_3_.refs_4_), custom_call_target="tpu_custom_call" | custom-call | tf_op jit(solution)/shard_map/pallas_call | solution.py:35
  33.1 0.8 %shard_map.53 = (f32[32,1792]{1,0:T(8,128)S(1)}, f32[32,1792]{1,0:T(8,128)S(1)}) custom-call(f32[32,1024]{1,0:T(8,128)S(1)} %collective-permute-done.12.refs_0_.refs_12_, f32[32,1024]{1,0:T(8,128)S(1)} %collective-permute-done.13.refs_1_.refs_13_, bf16[1024,1792]{1,0:T(8,128)(2,1)S(1)} %get-tuple-element.52.refs_2_, ...), custom_call_target="tpu_custom_call" | custom-call | tf_op jit(solution)/shard_map/pallas_call | solution.py:35
  34.1 1.7 %collective-permute-done.11.refs_1_ = f32[16,1792]{1,0:T(8,128)S(1)} collective-permute-done((f32[16,1792]{1,0:T(8,128)S(1)}, f32[16,1792]{1,0:T(8,128)S(1)}, u32[]{:S(2)}, u32[]{:S(2)}) %collective-permute-start.11) | collective-permute-done | bytes 114720 | tf_op jit(solution)/shard_map/ppermute | solution.py:190
  36.6 1.6 %collective-permute-start.17 = (f32[16,1792]{1,0:T(8,128)S(1)}, f32[16,1792]{1,0:T(8,128)S(1)}, u32[]{:S(2)}, u32[]{:S(2)}) collective-permute-start(f32[16,1792]{1,0:T(8,128)S(1)} %get-tuple-element.72), channel_id=1, source_target_pairs={{0,8},{4,12},{8,0},{12,4},{16,24},{20,28},{24,16},{28,20},{1,9},{5... | collective-permute-start | bytes 344072 | tf_op jit(solution)/shard_map/ppermute | solution.py:190
  38.1 0.7 %shard_map.57.refs_3_.refs_4_ = f32[64,1792]{1,0:T(8,128)S(1)} custom-call(f32[32,1024]{1,0:T(8,128)S(1)} %get-tuple-element.69.refs_0_.refs_3_.refs_6_, f32[32,1024]{1,0:T(8,128)S(1)} %get-tuple-element.70.refs_1_.refs_7_, bf16[1024,1792]{1,0:T(8,128)(2,1)S(1)} %get-tuple-element.53.refs_2_, f32[32,1024]{1,0:T(8,128)S(1)} %get-tuple-element.69.refs_0_.refs_3_.refs_6_), custom_call_target="tpu_custom_call" | custom-call | tf_op jit(solution)/shard_map/pallas_call | solution.py:35
  38.9 0.8 %shard_map.58 = (f32[32,1792]{1,0:T(8,128)S(1)}, f32[32,1792]{1,0:T(8,128)S(1)}) custom-call(f32[32,1024]{1,0:T(8,128)S(1)} %collective-permute-done.14.refs_0_.refs_14_, f32[32,1024]{1,0:T(8,128)S(1)} %collective-permute-done.15.refs_1_.refs_15_, bf16[1024,1792]{1,0:T(8,128)(2,1)S(1)} %get-tuple-element.52.refs_2_, ...), custom_call_target="tpu_custom_call" | custom-call | tf_op jit(solution)/shard_map/pallas_call | solution.py:35
  40.0 1.7 %collective-permute-done.17.refs_1_ = f32[16,1792]{1,0:T(8,128)S(1)} collective-permute-done((f32[16,1792]{1,0:T(8,128)S(1)}, f32[16,1792]{1,0:T(8,128)S(1)}, u32[]{:S(2)}, u32[]{:S(2)}) %collective-permute-start.17) | collective-permute-done | bytes 114720 | tf_op jit(solution)/shard_map/ppermute | solution.py:190
  41.8 1.6 %collective-permute-start.20 = (f32[16,1792]{1,0:T(8,128)S(1)}, f32[16,1792]{1,0:T(8,128)S(1)}, u32[]{:S(2)}, u32[]{:S(2)}) collective-permute-start(f32[16,1792]{1,0:T(8,128)S(1)} %get-tuple-element.79), channel_id=1, source_target_pairs={{0,8},{4,12},{8,0},{12,4},{16,24},{20,28},{24,16},{28,20},{1,9},{5... | collective-permute-start | bytes 344072 | tf_op jit(solution)/shard_map/ppermute | solution.py:190
  43.4 2.6 %collective-permute-start.18 = (f32[8,1792]{1,0:T(8,128)S(1)}, f32[8,1792]{1,0:T(8,128)S(1)}, u32[]{:S(2)}, u32[]{:S(2)}) collective-permute-start(f32[8,1792]{1,0:T(8,128)S(1)} %get-tuple-element.77), channel_id=1, source_target_pairs={{0,16},{4,20},{8,24},{12,28},{16,0},{20,4},{24,8},{28,12},{1,17},{... | collective-permute-start | bytes 172040 | tf_op jit(solution)/shard_map/ppermute | solution.py:190
  46.4 1.9 %shard_map.61 = (f32[2048,256]{1,0:T(8,128)}, f32[8,128]{1,0:T(8,128)S(1)}) custom-call(f32[32,1024]{1,0:T(8,128)S(1)} %get-tuple-element.49.refs_0_.refs_3_, f32[32,1024]{1,0:T(8,128)S(1)} %get-tuple-element.50.refs_1_, f32[32,1024]{1,0:T(8,128)S(1)} %get-tuple-element.55.refs_0_.refs_3_.refs_2_, f32[32,1024]{1,0:T(8,128)S(1)} %get-tuple-element.56.refs_1_.refs_3_, ...), custom_call_target="tpu_custom_call" | custom-call | tf_op jit(solution)/shard_map/pallas_call | solution.py:35
  48.3 2.6 %collective-permute-start.21 = (f32[8,1792]{1,0:T(8,128)S(1)}, f32[8,1792]{1,0:T(8,128)S(1)}, u32[]{:S(2)}, u32[]{:S(2)}) collective-permute-start(f32[8,1792]{1,0:T(8,128)S(1)} %get-tuple-element.82), channel_id=1, source_target_pairs={{0,16},{4,20},{8,24},{12,28},{16,0},{20,4},{24,8},{28,12},{1,17},{... | collective-permute-start | bytes 172040 | tf_op jit(solution)/shard_map/ppermute | solution.py:190
  51.4 0.6 %collective-permute-start.24 = (f32[8,1792]{1,0:T(8,128)S(1)}, f32[8,1792]{1,0:T(8,128)S(1)}, u32[]{:S(2)}, u32[]{:S(2)}) collective-permute-start(f32[8,1792]{1,0:T(8,128)S(1)} %get-tuple-element.86), channel_id=1, source_target_pairs={{0,8},{4,12},{8,0},{12,4},{16,24},{20,28},{24,16},{28,20},{1,9},{5... | collective-permute-start | bytes 172040 | tf_op jit(solution)/shard_map/ppermute | solution.py:190
  52.0 3.4 %collective-permute-start.25 = (f32[8,1792]{1,0:T(8,128)S(1)}, f32[8,1792]{1,0:T(8,128)S(1)}, u32[]{:S(2)}, u32[]{:S(2)}) collective-permute-start(f32[8,1792]{1,0:T(8,128)S(1)} %get-tuple-element.87), channel_id=1, source_target_pairs={{0,24},{4,28},{8,16},{12,20},{16,8},{20,12},{24,0},{28,4},{1,25},{... | collective-permute-start | bytes 172040 | tf_op jit(solution)/shard_map/ppermute | solution.py:190
  55.4 1.1 %collective-permute-done.21.refs_5_ = f32[8,1792]{1,0:T(8,128)S(1)} collective-permute-done((f32[8,1792]{1,0:T(8,128)S(1)}, f32[8,1792]{1,0:T(8,128)S(1)}, u32[]{:S(2)}, u32[]{:S(2)}) %collective-permute-start.21) | collective-permute-done | bytes 57376 | tf_op jit(solution)/shard_map/ppermute | solution.py:190
  56.6 1.8 %collective-permute-done.23.refs_7_ = f32[8,1792]{1,0:T(8,128)S(1)} collective-permute-done((f32[8,1792]{1,0:T(8,128)S(1)}, f32[8,1792]{1,0:T(8,128)S(1)}, u32[]{:S(2)}, u32[]{:S(2)}) %collective-permute-start.23) | collective-permute-done | bytes 57376 | tf_op jit(solution)/shard_map/ppermute | solution.py:190
  58.3 0.7 %shard_map.64 = f32[32,1792]{1,0:T(8,128)} custom-call(f32[8,1792]{1,0:T(8,128)S(1)} %get-tuple-element.67.refs_2_.refs_0_, f32[8,1792]{1,0:T(8,128)S(1)} %collective-permute-done.18.refs_1_, f32[8,1792]{1,0:T(8,128)S(1)} %get-tuple-element.74.refs_2_, f32[8,1792]{1,0:T(8,128)S(1)} %collective-permute-done.19.refs_3_, ...), custom_call_target="tpu_custom_call" | custom-call | tf_op jit(solution)/shard_map/pallas_call | solution.py:35
  (44 shorter events, 4.2 us)
Async XLA Ops:
  3.8 3.4 %collective-permute-start = (f32[256,1024]{1,0:T(8,128)S(1)}, f32[256,1024]{1,0:T(8,128)S(1)}, u32[]{:S(2)}, u32[]{:S(2)}) collective-permute-start(f32[256,1024]{1,0:T(8,128)S(1)} %get-tuple-element.47), channel_id=1, source_target_pairs={{0,1},{1,0},{2,3},{3,2},{4,5},{5,4},{6,7},{7,6},{8,9},{9,8},{10,11... | collective-permute-start | bytes 3145736 | tf_op jit(solution)/shard_map/ppermute | solution.py:190
  7.3 9.7 %collective-permute-start.1 = (f32[64,1024]{1,0:T(8,128)S(1)}, f32[64,1024]{1,0:T(8,128)S(1)}, u32[]{:S(2)}, u32[]{:S(2)}) collective-permute-start(f32[64,1024]{1,0:T(8,128)S(1)} %get-tuple-element.48.refs_0_), channel_id=1, source_target_pairs={{0,2},{1,3},{2,0},{3,1},{4,6},{5,7},{6,4},{7,5},{8,10},{9,11},{10,... | collective-permute-start | bytes 786440 | tf_op jit(solution)/shard_map/ppermute | solution.py:190
  9.9 13.1 %collective-permute-start.2 = (f32[64,1024]{1,0:T(8,128)S(1)}, f32[64,1024]{1,0:T(8,128)S(1)}, u32[]{:S(2)}, u32[]{:S(2)}) collective-permute-start(f32[64,1024]{1,0:T(8,128)S(1)} %get-tuple-element.51.refs_0_), channel_id=1, source_target_pairs={{0,2},{1,3},{2,0},{3,1},{4,6},{5,7},{6,4},{7,5},{8,10},{9,11},{10,... | collective-permute-start | bytes 786440 | tf_op jit(solution)/shard_map/ppermute | solution.py:190
  17.1 1.4 %collective-permute-start.3 = (f32[32,1024]{1,0:T(8,128)S(1)}, f32[32,1024]{1,0:T(8,128)S(1)}, u32[]{:S(2)}, u32[]{:S(2)}) collective-permute-start(f32[32,1024]{1,0:T(8,128)S(1)} %get-tuple-element.49.refs_0_.refs_3_), channel_id=1, source_target_pairs={{0,1},{1,0},{2,3},{3,2},{4,5},{5,4},{6,7},{7,6},{8,9},{9,8},{10,11... | collective-permute-start | bytes 393224 | tf_op jit(solution)/shard_map/ppermute | solution.py:190
  17.2 1.5 %collective-permute-start.4 = (f32[32,1024]{1,0:T(8,128)S(1)}, f32[32,1024]{1,0:T(8,128)S(1)}, u32[]{:S(2)}, u32[]{:S(2)}) collective-permute-start(f32[32,1024]{1,0:T(8,128)S(1)} %get-tuple-element.50.refs_1_), channel_id=1, source_target_pairs={{0,1},{1,0},{2,3},{3,2},{4,5},{5,4},{6,7},{7,6},{8,9},{9,8},{10,11... | collective-permute-start | bytes 393224 | tf_op jit(solution)/shard_map/ppermute | solution.py:190
  19.5 8.7 %collective-permute-start.6 = (f32[32,1792]{1,0:T(8,128)S(1)}, f32[32,1792]{1,0:T(8,128)S(1)}, u32[]{:S(2)}, u32[]{:S(2)}) collective-permute-start(f32[32,1792]{1,0:T(8,128)S(1)} %get-tuple-element.58), channel_id=1, source_target_pairs={{0,4},{4,0},{8,12},{12,8},{16,20},{20,16},{24,28},{28,24},{1,5},{5... | collective-permute-start | bytes 688136 | tf_op jit(solution)/shard_map/ppermute | solution.py:190
  21.5 8.6 %collective-permute-start.5 = (f32[64,1024]{1,0:T(8,128)S(1)}, f32[64,1024]{1,0:T(8,128)S(1)}, u32[]{:S(2)}, u32[]{:S(2)}) collective-permute-start(f32[64,1024]{1,0:T(8,128)S(1)} %get-tuple-element.57.refs_0_), channel_id=1, source_target_pairs={{0,2},{1,3},{2,0},{3,1},{4,6},{5,7},{6,4},{7,5},{8,10},{9,11},{10,... | collective-permute-start | bytes 786440 | tf_op jit(solution)/shard_map/ppermute | solution.py:190
  23.1 1.4 %collective-permute-start.7 = (f32[32,1024]{1,0:T(8,128)S(1)}, f32[32,1024]{1,0:T(8,128)S(1)}, u32[]{:S(2)}, u32[]{:S(2)}) collective-permute-start(f32[32,1024]{1,0:T(8,128)S(1)} %get-tuple-element.55.refs_0_.refs_3_.refs_2_), channel_id=1, source_target_pairs={{0,1},{1,0},{2,3},{3,2},{4,5},{5,4},{6,7},{7,6},{8,9},{9,8},{10,11... | collective-permute-start | bytes 393224 | tf_op jit(solution)/shard_map/ppermute | solution.py:190
  23.1 1.5 %collective-permute-start.8 = (f32[32,1024]{1,0:T(8,128)S(1)}, f32[32,1024]{1,0:T(8,128)S(1)}, u32[]{:S(2)}, u32[]{:S(2)}) collective-permute-start(f32[32,1024]{1,0:T(8,128)S(1)} %get-tuple-element.56.refs_1_.refs_3_), channel_id=1, source_target_pairs={{0,1},{1,0},{2,3},{3,2},{4,5},{5,4},{6,7},{7,6},{8,9},{9,8},{10,11... | collective-permute-start | bytes 393224 | tf_op jit(solution)/shard_map/ppermute | solution.py:190
  25.4 10.5 %collective-permute-start.10 = (f32[32,1792]{1,0:T(8,128)S(1)}, f32[32,1792]{1,0:T(8,128)S(1)}, u32[]{:S(2)}, u32[]{:S(2)}) collective-permute-start(f32[32,1792]{1,0:T(8,128)S(1)} %get-tuple-element.64), channel_id=1, source_target_pairs={{0,4},{4,0},{8,12},{12,8},{16,20},{20,16},{24,28},{28,24},{1,5},{5... | collective-permute-start | bytes 688136 | tf_op jit(solution)/shard_map/ppermute | solution.py:190
  26.7 9.2 %collective-permute-start.9 = (f32[64,1024]{1,0:T(8,128)S(1)}, f32[64,1024]{1,0:T(8,128)S(1)}, u32[]{:S(2)}, u32[]{:S(2)}) collective-permute-start(f32[64,1024]{1,0:T(8,128)S(1)} %get-tuple-element.63.refs_0_), channel_id=1, source_target_pairs={{0,2},{1,3},{2,0},{3,1},{4,6},{5,7},{6,4},{7,5},{8,10},{9,11},{10,... | collective-permute-start | bytes 786440 | tf_op jit(solution)/shard_map/ppermute | solution.py:190
  30.2 2.9 %collective-permute-start.12 = (f32[32,1024]{1,0:T(8,128)S(1)}, f32[32,1024]{1,0:T(8,128)S(1)}, u32[]{:S(2)}, u32[]{:S(2)}) collective-permute-start(f32[32,1024]{1,0:T(8,128)S(1)} %get-tuple-element.61.refs_0_.refs_3_.refs_4_), channel_id=1, source_target_pairs={{0,1},{1,0},{2,3},{3,2},{4,5},{5,4},{6,7},{7,6},{8,9},{9,8},{10,11... | collective-permute-start | bytes 393224 | tf_op jit(solution)/shard_map/ppermute | solution.py:190
  30.3 2.8 %collective-permute-start.13 = (f32[32,1024]{1,0:T(8,128)S(1)}, f32[32,1024]{1,0:T(8,128)S(1)}, u32[]{:S(2)}, u32[]{:S(2)}) collective-permute-start(f32[32,1024]{1,0:T(8,128)S(1)} %get-tuple-element.62.refs_1_.refs_5_), channel_id=1, source_target_pairs={{0,1},{1,0},{2,3},{3,2},{4,5},{5,4},{6,7},{7,6},{8,9},{9,8},{10,11... | collective-permute-start | bytes 393224 | tf_op jit(solution)/shard_map/ppermute | solution.py:190
  30.8 5.1 %collective-permute-start.11 = (f32[16,1792]{1,0:T(8,128)S(1)}, f32[16,1792]{1,0:T(8,128)S(1)}, u32[]{:S(2)}, u32[]{:S(2)}) collective-permute-start(f32[16,1792]{1,0:T(8,128)S(1)} %get-tuple-element.65), channel_id=1, source_target_pairs={{0,8},{4,12},{8,0},{12,4},{16,24},{20,28},{24,16},{28,20},{1,9},{5... | collective-permute-start | bytes 344072 | tf_op jit(solution)/shard_map/ppermute | solution.py:190
  33.9 7.9 %collective-permute-start.16 = (f32[32,1792]{1,0:T(8,128)S(1)}, f32[32,1792]{1,0:T(8,128)S(1)}, u32[]{:S(2)}, u32[]{:S(2)}) collective-permute-start(f32[32,1792]{1,0:T(8,128)S(1)} %get-tuple-element.71), channel_id=1, source_target_pairs={{0,4},{4,0},{8,12},{12,8},{16,20},{20,16},{24,28},{28,24},{1,5},{5... | collective-permute-start | bytes 688136 | tf_op jit(solution)/shard_map/ppermute | solution.py:190
  36.0 2.9 %collective-permute-start.14 = (f32[32,1024]{1,0:T(8,128)S(1)}, f32[32,1024]{1,0:T(8,128)S(1)}, u32[]{:S(2)}, u32[]{:S(2)}) collective-permute-start(f32[32,1024]{1,0:T(8,128)S(1)} %get-tuple-element.69.refs_0_.refs_3_.refs_6_), channel_id=1, source_target_pairs={{0,1},{1,0},{2,3},{3,2},{4,5},{5,4},{6,7},{7,6},{8,9},{9,8},{10,11... | collective-permute-start | bytes 393224 | tf_op jit(solution)/shard_map/ppermute | solution.py:190
  36.1 2.8 %collective-permute-start.15 = (f32[32,1024]{1,0:T(8,128)S(1)}, f32[32,1024]{1,0:T(8,128)S(1)}, u32[]{:S(2)}, u32[]{:S(2)}) collective-permute-start(f32[32,1024]{1,0:T(8,128)S(1)} %get-tuple-element.70.refs_1_.refs_7_), channel_id=1, source_target_pairs={{0,1},{1,0},{2,3},{3,2},{4,5},{5,4},{6,7},{7,6},{8,9},{9,8},{10,11... | collective-permute-start | bytes 393224 | tf_op jit(solution)/shard_map/ppermute | solution.py:190
  36.6 5.1 %collective-permute-start.17 = (f32[16,1792]{1,0:T(8,128)S(1)}, f32[16,1792]{1,0:T(8,128)S(1)}, u32[]{:S(2)}, u32[]{:S(2)}) collective-permute-start(f32[16,1792]{1,0:T(8,128)S(1)} %get-tuple-element.72), channel_id=1, source_target_pairs={{0,8},{4,12},{8,0},{12,4},{16,24},{20,28},{24,16},{28,20},{1,9},{5... | collective-permute-start | bytes 344072 | tf_op jit(solution)/shard_map/ppermute | solution.py:190
  39.7 11.3 %collective-permute-start.22 = (f32[32,1792]{1,0:T(8,128)S(1)}, f32[32,1792]{1,0:T(8,128)S(1)}, u32[]{:S(2)}, u32[]{:S(2)}) collective-permute-start(f32[32,1792]{1,0:T(8,128)S(1)} %get-tuple-element.83), channel_id=1, source_target_pairs={{0,4},{4,0},{8,12},{12,8},{16,20},{20,16},{24,28},{28,24},{1,5},{5... | collective-permute-start | bytes 688136 | tf_op jit(solution)/shard_map/ppermute | solution.py:190
  41.8 6.5 %collective-permute-start.20 = (f32[16,1792]{1,0:T(8,128)S(1)}, f32[16,1792]{1,0:T(8,128)S(1)}, u32[]{:S(2)}, u32[]{:S(2)}) collective-permute-start(f32[16,1792]{1,0:T(8,128)S(1)} %get-tuple-element.79), channel_id=1, source_target_pairs={{0,8},{4,12},{8,0},{12,4},{16,24},{20,28},{24,16},{28,20},{1,9},{5... | collective-permute-start | bytes 344072 | tf_op jit(solution)/shard_map/ppermute | solution.py:190
  43.4 8.6 %collective-permute-start.18 = (f32[8,1792]{1,0:T(8,128)S(1)}, f32[8,1792]{1,0:T(8,128)S(1)}, u32[]{:S(2)}, u32[]{:S(2)}) collective-permute-start(f32[8,1792]{1,0:T(8,128)S(1)} %get-tuple-element.77), channel_id=1, source_target_pairs={{0,16},{4,20},{8,24},{12,28},{16,0},{20,4},{24,8},{28,12},{1,17},{... | collective-permute-start | bytes 172040 | tf_op jit(solution)/shard_map/ppermute | solution.py:190
  46.0 9.4 %collective-permute-start.19 = (f32[8,1792]{1,0:T(8,128)S(1)}, f32[8,1792]{1,0:T(8,128)S(1)}, u32[]{:S(2)}, u32[]{:S(2)}) collective-permute-start(f32[8,1792]{1,0:T(8,128)S(1)} %get-tuple-element.78), channel_id=1, source_target_pairs={{0,16},{4,20},{8,24},{12,28},{16,0},{20,4},{24,8},{28,12},{1,17},{... | collective-permute-start | bytes 172040 | tf_op jit(solution)/shard_map/ppermute | solution.py:190
  48.3 8.3 %collective-permute-start.21 = (f32[8,1792]{1,0:T(8,128)S(1)}, f32[8,1792]{1,0:T(8,128)S(1)}, u32[]{:S(2)}, u32[]{:S(2)}) collective-permute-start(f32[8,1792]{1,0:T(8,128)S(1)} %get-tuple-element.82), channel_id=1, source_target_pairs={{0,16},{4,20},{8,24},{12,28},{16,0},{20,4},{24,8},{28,12},{1,17},{... | collective-permute-start | bytes 172040 | tf_op jit(solution)/shard_map/ppermute | solution.py:190
  51.0 7.3 %collective-permute-start.23 = (f32[8,1792]{1,0:T(8,128)S(1)}, f32[8,1792]{1,0:T(8,128)S(1)}, u32[]{:S(2)}, u32[]{:S(2)}) collective-permute-start(f32[8,1792]{1,0:T(8,128)S(1)} %get-tuple-element.85), channel_id=1, source_target_pairs={{0,16},{4,20},{8,24},{12,28},{16,0},{20,4},{24,8},{28,12},{1,17},{... | collective-permute-start | bytes 172040 | tf_op jit(solution)/shard_map/ppermute | solution.py:190
  51.4 6.9 %collective-permute-start.24 = (f32[8,1792]{1,0:T(8,128)S(1)}, f32[8,1792]{1,0:T(8,128)S(1)}, u32[]{:S(2)}, u32[]{:S(2)}) collective-permute-start(f32[8,1792]{1,0:T(8,128)S(1)} %get-tuple-element.86), channel_id=1, source_target_pairs={{0,8},{4,12},{8,0},{12,4},{16,24},{20,28},{24,16},{28,20},{1,9},{5... | collective-permute-start | bytes 172040 | tf_op jit(solution)/shard_map/ppermute | solution.py:190
  52.0 6.3 %collective-permute-start.25 = (f32[8,1792]{1,0:T(8,128)S(1)}, f32[8,1792]{1,0:T(8,128)S(1)}, u32[]{:S(2)}, u32[]{:S(2)}) collective-permute-start(f32[8,1792]{1,0:T(8,128)S(1)} %get-tuple-element.87), channel_id=1, source_target_pairs={{0,24},{4,28},{8,16},{12,20},{16,8},{20,12},{24,0},{28,4},{1,25},{... | collective-permute-start | bytes 172040 | tf_op jit(solution)/shard_map/ppermute | solution.py:190

commit v5 on v4

--- a/solution.py
+++ b/solution.py
@@ -13,19 +13,14 @@
 BF16 = jnp.bfloat16
 NT = (((1,), (1,)), ((), ()))
 SPECS = {"v": pl.BlockSpec(memory_space=pltpu.VMEM), "a": pl.BlockSpec(memory_space=pl.ANY)}
-E0 = 19.5
-DE = 10
-GT = 12.4
-WEIGHT = 0
-WQ = 0
-WE = 5*10**8
-WC = 0
-WP = 0
+ORDER = "own0 before0 send0 own1 before1 send1 add0.1 own2 before2 send2 add0.2 add1.1 own3 before3 send3 add2.1 add1.2 add2.2 add3.1 sketch"
+WEIGHTS = {'add2.2': 1000000000, 'send1': 200000000, 'own1': 1000000000, 'own2': 0, 'before2': 2000000000, 'before1': 500000000, 'add0.2': 0, 'sketch': 500000000, 'add3.1': 200000000}
 SPLIT = 2
 DIRECT = 1
-
-
-def call(body, args, outs, kinds=None, after=(), scratch=(), results=0, weight=None):
+GROUPS = ((0,), (1,), (2,), (3,))
+
+
+def call(body, args, outs, kinds=None, after=(), scratch=(), results=0, weight=0):
     n = len(args)
     kinds = (kinds or "v" * n) + "a" * len(after)
 
@@ -38,7 +33,7 @@
         in_specs=[SPECS[kind] for kind in kinds],
         out_specs=[SPECS["v"]] * len(outs),
         scratch_shapes=list(scratch),
-        cost_estimate=pl.CostEstimate(flops=WEIGHT if weight is None else weight, bytes_accessed=0, transcendentals=0),
+        cost_estimate=pl.CostEstimate(flops=weight, bytes_accessed=0, transcendentals=0),
         compiler_params=pltpu.CompilerParams(vmem_limit_bytes=16 << 20),
     )(*args, *after)
 
@@ -124,26 +119,40 @@
     out[...] = jnp.dot(joined(sketch).astype(BF16), held[...], preferred_element_type=F32)
 
 
-def halves(bit, ref):
-    half = ref.shape[0] // 2
+def split(bit, segments, refs, send, keep):
     own = lax.rem(lax.axis_index("row") // bit, 2)
-    if half % 8:
-        low, high = ref[:half, :], ref[half:, :]
-        return jnp.where(own == 0, high, low), jnp.where(own == 0, low, high)
-    theirs = pl.ds(pl.multiple_of((1 - own) * half, half), half)
-    mine = pl.ds(pl.multiple_of(own * half, half), half)
-    return ref[theirs, :], ref[mine, :]
+    start, first = 0, 0
+    for rows in segments:
+        half = rows // 2
+        for out, which in ((send, 1 - own), (keep, own)):
+            if half % 8:
+                low, high = (
+                    functools.reduce(jnp.add, [ref[pl.ds(start + i * half, half), :] for ref in refs]) for i in range(2)
+                )
+                value = jnp.where(which == 0, low, high)
+            else:
+                part = pl.ds(pl.multiple_of(start + which * half, 8), half)
+                value = functools.reduce(jnp.add, [ref[part, :] for ref in refs])
+            out[pl.ds(first, half), :] = value
+        start += rows
+        first += half
 
 
 def product_send_body(*refs):
     *sketch, held, before, send, keep, total = refs
     total[...] = before[...] + jnp.dot(joined(sketch).astype(BF16), held[...], preferred_element_type=F32)
-    send[...], keep[...] = halves(1, total)
-
-
-def add_send_body(bit, kept, received, send, keep):
-    for out, a, b in zip((send, keep), halves(bit, kept), halves(bit, received)):
-        out[...] = a + b
+    split(1, [total.shape[0]], [total], send, keep)
+
+
+def add_send_body(bit, segments, *refs):
+    *pairs, send, keep = refs
+    first = 0
+    for kept, got in zip(pairs[::2], pairs[1::2]):
+        mine = segments if len(pairs) == 2 else [kept.shape[0]]
+        half = kept.shape[0] // 2
+        part = pl.ds(first, half)
+        split(bit, mine, [kept, got], send.at[part, :], keep.at[part, :])
+        first += half
 
 
 def add_spread_body(n_high, kept, received, *outs):
@@ -222,50 +231,66 @@
     owns, others, befores, pending = {}, {}, {}, {}
     sketch = None
     last = ()
-    steps = []
-    direct = [len(bits) == 3 and pieces[c] % 8 == 0 and c >= n - DIRECT for c in range(n)]
-    for c in range(n):
-        steps += [(10 * c, "own", c, 0), (10 * c + 1, "before", c, 0), (10 * c + 2, "send", c, 0)]
-        steps += [(10 * c + E0 + DE * s, "add", c, s + 1) for s in range(1 if direct[c] else len(bits) - 1)]
-    steps.append((10 * (n - 1) + GT, "sketch", 0, 0))
-    for _, step, c, s in sorted(steps):
-        width = widths[c]
-        if step == "own":
-            outs = [((width // SPLIT, half), F32)] * SPLIT
-            owns[c] = call(add_body, (partial[c], moved[c]), outs, after=last, weight=WC)
+    groups = GROUPS if n == 4 else tuple((c,) for c in range(n))
+    direct = [len(bits) == 3 and len(group) == 1 and pieces[group[0]] % 8 == 0 and g >= len(groups) - DIRECT for g, group in enumerate(groups)]
+    steps = ORDER.split() if len(bits) == 3 and n == 4 else []
+    if not steps:
+        found = []
+        for c in range(n):
+            found += [(10 * c, f"own{c}"), (10 * c + 1, f"before{c}"), (10 * c + 2, f"send{c}")]
+        for g, group in enumerate(groups):
+            found += [(10 * group[-1] + 9.5 + 10 * s, f"add{g}.{s}") for s in range(1, 2 if direct[g] else len(bits))]
+        steps = [step for _, step in sorted(found)] + ["sketch"]
+
+    for step in steps:
+        weight = WEIGHTS.get(step, 0)
+        if step.startswith("own"):
+            c = int(step[3:])
+            outs = [((widths[c] // SPLIT, half), F32)] * SPLIT
+            owns[c] = call(add_body, (partial[c], moved[c]), outs, after=last, weight=weight)
             others[c] = [swap(x, "col", n_col, 1) for x in owns[c]]
             last = (owns[c][0],)
-        elif step == "before":
-            befores[c] = call(product_body, (*owns[c], held_own), [((width, d), F32)], after=last, weight=WP)[0]
+        elif step.startswith("before"):
+            c = int(step[6:])
+            befores[c] = call(product_body, (*owns[c], held_own), [((widths[c], d), F32)], after=last, weight=weight)[0]
             last = (befores[c],)
-        elif step == "send":
-            outs = [((width // 2, d), F32)] * 2
-            total = pltpu.VMEM((width, d), F32)
+        elif step.startswith("send"):
+            c = int(step[4:])
+            outs = [((widths[c] // 2, d), F32)] * 2
+            total = pltpu.VMEM((widths[c], d), F32)
             args = (*others[c], held_other, befores[c])
-            send, keep = call(product_send_body, args, outs, after=last, scratch=[total], weight=WQ)
-            pending[c] = keep, swap(send, "row", n_row, bits[0])
+            send, keep = call(product_send_body, args, outs, after=last, scratch=[total], weight=weight)
+            pending[(c,)] = keep, swap(send, "row", n_row, bits[0])
             last = (keep,)
-        elif step == "add" and direct[c]:
-            outs = [((pieces[c], d), F32)] * (n_row // 2)
-            own, *sends = call(functools.partial(add_spread_body, n_row // 2), pending[c], outs, after=last, weight=WE)
-            flips = [2 * owner_at(flip, n_row // 2) for flip in range(1, n_row // 2)]
-            pending[c] = own, *[swap(x, "row", n_row, flip) for x, flip in zip(sends, flips)]
-            last = (own,)
-        elif step == "add":
-            outs = [((width >> (s + 1), d), F32)] * 2
-            send, keep = call(functools.partial(add_send_body, bits[s]), pending[c], outs, after=last, weight=WE)
-            pending[c] = keep, swap(send, "row", n_row, bits[s])
+        elif step.startswith("add"):
+            g, s = (int(x) for x in step[3:].split("."))
+            group = groups[g]
+            if direct[g]:
+                outs = [((pieces[group[0]], d), F32)] * (n_row // 2)
+                body = functools.partial(add_spread_body, n_row // 2)
+                own, *sends = call(body, pending[group], outs, after=last, weight=weight)
+                flips = [2 * owner_at(flip, n_row // 2) for flip in range(1, n_row // 2)]
+                pending[group] = own, *[swap(x, "row", n_row, flip) for x, flip in zip(sends, flips)]
+                last = (own,)
+                continue
+            if s == 1:
+                pending[group] = [x for c in group for x in pending[(c,)]]
+            segments = [widths[c] >> s for c in group]
+            body = functools.partial(add_send_body, bits[s], segments)
+            outs = [((sum(segments) // 2, d), F32)] * 2
+            send, keep = call(body, pending[group], outs, after=last, weight=weight)
+            pending[group] = keep, swap(send, "row", n_row, bits[s])
             last = (keep,)
         else:
-            parts = [[x for group in groups.values() for x in group] for groups in (owns, others)]
+            parts = [[x for found in halves.values() for x in found] for halves in (owns, others)]
             sketch, done = finish_sketch(n_row, k, pieces, *parts, last)
             last = (done,)
-    flat = [x for c in range(n) for x in pending[c]]
+    flat = [x for group in groups for x in pending[group]]
     if per_owner % 8 == 0:
-        body = functools.partial(final_corange_body, [len(pending[c]) for c in range(n)])
-        corange = call(body, flat, [((per_owner, d), F32)], results=1)[0]
+        body = functools.partial(final_corange_body, [len(pending[group]) for group in groups])
+        corange = call(body, flat, [((per_owner, d), F32)], after=last, results=1, weight=WEIGHTS.get("F", 0))[0]
     else:
-        corange = jnp.concatenate([functools.reduce(jnp.add, pending[c]) for c in range(n)], axis=0)
+        corange = jnp.concatenate([functools.reduce(jnp.add, pending[group]) for group in groups], axis=0)
     return sketch, corange.T
 
 

time: 59.2 us -> 59.6 us (level)
  starting transfers between devices: 27.1 us -> 30.5 us
  waiting for transfers between devices: 15.9 us -> 12.8 us
    ppermute x26, starting transfers between devices: 27.1 us -> 30.5 us  [swap(): return lax.ppermute(x, axis, [(i, i ^ bit) for i in range(size)])]
    ppermute x26, waiting for transfers between devices: 15.9 us -> 12.8 us  [swap(): return lax.ppermute(x, axis, [(i, i ^ bit) for i in range(size)])]
  transfers between devices with their start and end apart: 26 -> 26, of which waited for: 10 -> 9; matrix products, arithmetic and copies ran while one was open for 0% -> 0% of each run, Pallas kernels for 19% -> 19%
where the time goes in v5:
time: 59.6 us; the launch traced here: 59.4 us
  starting transfers between devices  30.5 us (51%)
  Pallas kernels  15.2 us (26%)
  waiting for transfers between devices  12.8 us (21%)
  between operations  0.88 us (1%)
    ppermute x26, starting transfers between devices, swap(): return lax.ppermute(x, axis, [(i, i ^ bit) for i in range(size)])  30.5 us
    pallas_call x24, Pallas kernels, call(): pl.pallas_call(run, out_shape=[pltpu.VMEM(*o) if i >= results else jax.Sh...  15.2 us
    ppermute x26, waiting for transfers between devices, swap(): return lax.ppermute(x, axis, [(i, i ^ bit) for i in range(size)])  12.8 us
  transfers between devices with their start and end apart: 26, of which 9 were waited for; matrix products, arithmetic and copies ran while one was open for 0% of the time, Pallas kernels for 19%

profile of v5, /device:TPU:0, one launch (start us, length us, event | category | flops | bytes accessed | tf_op | source)
XLA Modules:
  0.0 59.4 jit_solution(172232951595689516)
XLA Ops:
  0.6 3.2 %shard_map.41 = (bf16[1024,1792]{1,0:T(8,128)(2,1)S(1)}, bf16[256,1792]{1,0:T(8,128)(2,1)S(1)}, f32[256,1024]{1,0:T(8,128)S(1)}) custom-call(bf16[2048,1792]{1,0:T(8,128)(2,1)} %refs_0_.3, bf16[1792,256]{1,0:T(8,128)(2,1)} %refs_1_.1), custom_call_target="tpu_custom_call" | custom-call | tf_op jit(solution)/shard_map/pallas_call | solution.py:30
  4.3 2.9 %shard_map.42 = (bf16[1024,1792]{1,0:T(8,128)(2,1)S(1)}, f32[256,1024]{1,0:T(8,128)S(1)}) custom-call(bf16[2048,1792]{1,0:T(8,128)(2,1)} %refs_0_.3, bf16[256,1792]{1,0:T(8,128)(2,1)S(1)} %get-tuple-element.45.refs_1_), custom_call_target="tpu_custom_call" | custom-call | tf_op jit(solution)/shard_map/pallas_call | solution.py:30
  7.3 2.6 %collective-permute-start.1 = (f32[64,1024]{1,0:T(8,128)S(1)}, f32[64,1024]{1,0:T(8,128)S(1)}, u32[]{:S(2)}, u32[]{:S(2)}) collective-permute-start(f32[64,1024]{1,0:T(8,128)S(1)} %get-tuple-element.48.refs_0_), channel_id=1, source_target_pairs={{0,2},{1,3},{2,0},{3,1},{4,6},{5,7},{6,4},{7,5},{8,10},{9,11},{10,... | collective-permute-start | bytes 786440 | tf_op jit(solution)/shard_map/ppermute | solution.py:199
  10.0 7.1 %collective-permute-done.1.refs_1_ = f32[64,1024]{1,0:T(8,128)S(1)} collective-permute-done((f32[64,1024]{1,0:T(8,128)S(1)}, f32[64,1024]{1,0:T(8,128)S(1)}, u32[]{:S(2)}, u32[]{:S(2)}) %collective-permute-start.1) | collective-permute-done | bytes 262176 | tf_op jit(solution)/shard_map/ppermute | solution.py:199
  17.7 1.9 %collective-permute-start.5 = (f32[64,1024]{1,0:T(8,128)S(1)}, f32[64,1024]{1,0:T(8,128)S(1)}, u32[]{:S(2)}, u32[]{:S(2)}) collective-permute-start(f32[64,1024]{1,0:T(8,128)S(1)} %get-tuple-element.57.refs_0_), channel_id=1, source_target_pairs={{0,2},{1,3},{2,0},{3,1},{4,6},{5,7},{6,4},{7,5},{8,10},{9,11},{10,... | collective-permute-start | bytes 786440 | tf_op jit(solution)/shard_map/ppermute | solution.py:199
  19.6 0.7 %shard_map.45.refs_3_.refs_4_ = f32[64,1792]{1,0:T(8,128)S(1)} custom-call(f32[32,1024]{1,0:T(8,128)S(1)} %get-tuple-element.49.refs_0_.refs_3_, f32[32,1024]{1,0:T(8,128)S(1)} %get-tuple-element.50.refs_1_, bf16[1024,1792]{1,0:T(8,128)(2,1)S(1)} %get-tuple-element.53.refs_2_, f32[32,1024]{1,0:T(8,128)S(1)} %get-tuple-element.49.refs_0_.refs_3_), custom_call_target="tpu_custom_call" | custom-call | tf_op jit(solution)/shard_map/pallas_call | solution.py:30
  20.4 0.8 %shard_map.46 = (f32[32,1792]{1,0:T(8,128)S(1)}, f32[32,1792]{1,0:T(8,128)S(1)}) custom-call(f32[32,1024]{1,0:T(8,128)S(1)} %collective-permute-done.3.refs_0_.refs_8_, f32[32,1024]{1,0:T(8,128)S(1)} %collective-permute-done.4.refs_1_.refs_9_, bf16[1024,1792]{1,0:T(8,128)(2,1)S(1)} %get-tuple-element.52.refs_2_, f32[64,1792]{1,0:T(8,128)S(1)} %shard_map.45.refs_3_.refs_4_, ...), custom_call_target="tpu_custom_call" | custom-call | tf_op jit(solution)/shard_map/pallas_call | solution.py:30
  21.2 1.6 %collective-permute-start.6 = (f32[32,1792]{1,0:T(8,128)S(1)}, f32[32,1792]{1,0:T(8,128)S(1)}, u32[]{:S(2)}, u32[]{:S(2)}) collective-permute-start(f32[32,1792]{1,0:T(8,128)S(1)} %get-tuple-element.58), channel_id=1, source_target_pairs={{0,4},{4,0},{8,12},{12,8},{16,20},{20,16},{24,28},{28,24},{1,5},{5... | collective-permute-start | bytes 688136 | tf_op jit(solution)/shard_map/ppermute | solution.py:199
  23.4 1.9 %collective-permute-start.9 = (f32[64,1024]{1,0:T(8,128)S(1)}, f32[64,1024]{1,0:T(8,128)S(1)}, u32[]{:S(2)}, u32[]{:S(2)}) collective-permute-start(f32[64,1024]{1,0:T(8,128)S(1)} %get-tuple-element.63.refs_0_), channel_id=1, source_target_pairs={{0,2},{1,3},{2,0},{3,1},{4,6},{5,7},{6,4},{7,5},{8,10},{9,11},{10,... | collective-permute-start | bytes 786440 | tf_op jit(solution)/shard_map/ppermute | solution.py:199
  25.3 0.7 %shard_map.48.refs_3_.refs_4_ = f32[64,1792]{1,0:T(8,128)S(1)} custom-call(f32[32,1024]{1,0:T(8,128)S(1)} %get-tuple-element.55.refs_0_.refs_3_.refs_2_, f32[32,1024]{1,0:T(8,128)S(1)} %get-tuple-element.56.refs_1_.refs_3_, bf16[1024,1792]{1,0:T(8,128)(2,1)S(1)} %get-tuple-element.53.refs_2_, f32[32,1024]{1,0:T(8,128)S(1)} %get-tuple-element.55.refs_0_.refs_3_.refs_2_), custom_call_target="tpu_custom_call" | custom-call | flops 500000000 | tf_op jit(solution)/shard_map/pallas_call | solution.py:30
  26.0 0.8 %shard_map.49 = (f32[32,1792]{1,0:T(8,128)S(1)}, f32[32,1792]{1,0:T(8,128)S(1)}) custom-call(f32[32,1024]{1,0:T(8,128)S(1)} %collective-permute-done.7.refs_0_.refs_10_, f32[32,1024]{1,0:T(8,128)S(1)} %collective-permute-done.8.refs_1_.refs_11_, bf16[1024,1792]{1,0:T(8,128)(2,1)S(1)} %get-tuple-element.52.refs_2_, f32[64,1792]{1,0:T(8,128)S(1)} %shard_map.48.refs_3_.refs_4_, ...), custom_call_target="tpu_custom_call" | custom-call | flops 200000000 | tf_op jit(solution)/shard_map/pallas_call | solution.py:30
  26.8 1.6 %collective-permute-start.10 = (f32[32,1792]{1,0:T(8,128)S(1)}, f32[32,1792]{1,0:T(8,128)S(1)}, u32[]{:S(2)}, u32[]{:S(2)}) collective-permute-start(f32[32,1792]{1,0:T(8,128)S(1)} %get-tuple-element.64), channel_id=1, source_target_pairs={{0,4},{4,0},{8,12},{12,8},{16,20},{20,16},{24,28},{28,24},{1,5},{5... | collective-permute-start | bytes 688136 | tf_op jit(solution)/shard_map/ppermute | solution.py:199
  29.2 1.7 %collective-permute-start.11 = (f32[16,1792]{1,0:T(8,128)S(1)}, f32[16,1792]{1,0:T(8,128)S(1)}, u32[]{:S(2)}, u32[]{:S(2)}) collective-permute-start(f32[16,1792]{1,0:T(8,128)S(1)} %get-tuple-element.65), channel_id=1, source_target_pairs={{0,8},{4,12},{8,0},{12,4},{16,24},{20,28},{24,16},{28,20},{1,9},{5... | collective-permute-start | bytes 344072 | tf_op jit(solution)/shard_map/ppermute | solution.py:199
  31.0 0.7 %shard_map.52.refs_3_.refs_4_ = f32[64,1792]{1,0:T(8,128)S(1)} custom-call(f32[32,1024]{1,0:T(8,128)S(1)} %get-tuple-element.61.refs_0_.refs_3_.refs_4_, f32[32,1024]{1,0:T(8,128)S(1)} %get-tuple-element.62.refs_1_.refs_5_, bf16[1024,1792]{1,0:T(8,128)(2,1)S(1)} %get-tuple-element.53.refs_2_, f32[32,1024]{1,0:T(8,128)S(1)} %get-tuple-element.61.refs_0_.refs_3_.refs_4_), custom_call_target="tpu_custom_call" | custom-call | flops 2000000000 | tf_op jit(solution)/shard_map/pallas_call | solution.py:30
  31.7 0.8 %shard_map.53 = (f32[32,1792]{1,0:T(8,128)S(1)}, f32[32,1792]{1,0:T(8,128)S(1)}) custom-call(f32[32,1024]{1,0:T(8,128)S(1)} %collective-permute-done.12.refs_0_.refs_12_, f32[32,1024]{1,0:T(8,128)S(1)} %collective-permute-done.13.refs_1_.refs_13_, bf16[1024,1792]{1,0:T(8,128)(2,1)S(1)} %get-tuple-element.52.refs_2_, ...), custom_call_target="tpu_custom_call" | custom-call | tf_op jit(solution)/shard_map/pallas_call | solution.py:30
  32.5 1.6 %collective-permute-start.17 = (f32[32,1792]{1,0:T(8,128)S(1)}, f32[32,1792]{1,0:T(8,128)S(1)}, u32[]{:S(2)}, u32[]{:S(2)}) collective-permute-start(f32[32,1792]{1,0:T(8,128)S(1)} %get-tuple-element.73), channel_id=1, source_target_pairs={{0,4},{4,0},{8,12},{12,8},{16,20},{20,16},{24,28},{28,24},{1,5},{5... | collective-permute-start | bytes 688136 | tf_op jit(solution)/shard_map/ppermute | solution.py:199
  35.1 0.7 %shard_map.57.refs_3_.refs_4_ = f32[64,1792]{1,0:T(8,128)S(1)} custom-call(f32[32,1024]{1,0:T(8,128)S(1)} %get-tuple-element.69.refs_0_.refs_3_.refs_6_, f32[32,1024]{1,0:T(8,128)S(1)} %get-tuple-element.70.refs_1_.refs_7_, bf16[1024,1792]{1,0:T(8,128)(2,1)S(1)} %get-tuple-element.53.refs_2_, f32[32,1024]{1,0:T(8,128)S(1)} %get-tuple-element.69.refs_0_.refs_3_.refs_6_), custom_call_target="tpu_custom_call" | custom-call | tf_op jit(solution)/shard_map/pallas_call | solution.py:30
  36.1 0.8 %shard_map.58 = (f32[32,1792]{1,0:T(8,128)S(1)}, f32[32,1792]{1,0:T(8,128)S(1)}) custom-call(f32[32,1024]{1,0:T(8,128)S(1)} %collective-permute-done.14.refs_0_.refs_14_, f32[32,1024]{1,0:T(8,128)S(1)} %collective-permute-done.15.refs_1_.refs_15_, bf16[1024,1792]{1,0:T(8,128)(2,1)S(1)} %get-tuple-element.52.refs_2_, ...), custom_call_target="tpu_custom_call" | custom-call | tf_op jit(solution)/shard_map/pallas_call | solution.py:30
  36.9 1.8 %collective-permute-start.16 = (f32[32,1792]{1,0:T(8,128)S(1)}, f32[32,1792]{1,0:T(8,128)S(1)}, u32[]{:S(2)}, u32[]{:S(2)}) collective-permute-start(f32[32,1792]{1,0:T(8,128)S(1)} %get-tuple-element.72), channel_id=1, source_target_pairs={{0,4},{4,0},{8,12},{12,8},{16,20},{20,16},{24,28},{28,24},{1,5},{5... | collective-permute-start | bytes 688136 | tf_op jit(solution)/shard_map/ppermute | solution.py:199
  38.6 1.6 %collective-permute-start.19 = (f32[16,1792]{1,0:T(8,128)S(1)}, f32[16,1792]{1,0:T(8,128)S(1)}, u32[]{:S(2)}, u32[]{:S(2)}) collective-permute-start(f32[16,1792]{1,0:T(8,128)S(1)} %get-tuple-element.76), channel_id=1, source_target_pairs={{0,8},{4,12},{8,0},{12,4},{16,24},{20,28},{24,16},{28,20},{1,9},{5... | collective-permute-start | bytes 344072 | tf_op jit(solution)/shard_map/ppermute | solution.py:199
  40.8 2.6 %collective-permute-start.20 = (f32[8,1792]{1,0:T(8,128)S(1)}, f32[8,1792]{1,0:T(8,128)S(1)}, u32[]{:S(2)}, u32[]{:S(2)}) collective-permute-start(f32[8,1792]{1,0:T(8,128)S(1)} %get-tuple-element.81), channel_id=1, source_target_pairs={{0,16},{4,20},{8,24},{12,28},{16,0},{20,4},{24,8},{28,12},{1,17},{... | collective-permute-start | bytes 172040 | tf_op jit(solution)/shard_map/ppermute | solution.py:199
  43.4 1.9 %collective-permute-done.19.refs_1_ = f32[16,1792]{1,0:T(8,128)S(1)} collective-permute-done((f32[16,1792]{1,0:T(8,128)S(1)}, f32[16,1792]{1,0:T(8,128)S(1)}, u32[]{:S(2)}, u32[]{:S(2)}) %collective-permute-start.19) | collective-permute-done | bytes 114720 | tf_op jit(solution)/shard_map/ppermute | solution.py:199
  45.3 2.0 %collective-permute-start.21 = (f32[8,1792]{1,0:T(8,128)S(1)}, f32[8,1792]{1,0:T(8,128)S(1)}, u32[]{:S(2)}, u32[]{:S(2)}) collective-permute-start(f32[8,1792]{1,0:T(8,128)S(1)} %get-tuple-element.82), channel_id=1, source_target_pairs={{0,16},{4,20},{8,24},{12,28},{16,0},{20,4},{24,8},{28,12},{1,17},{... | collective-permute-start | bytes 172040 | tf_op jit(solution)/shard_map/ppermute | solution.py:199
  47.3 0.7 %collective-permute-done.18.refs_1_ = f32[16,1792]{1,0:T(8,128)S(1)} collective-permute-done((f32[16,1792]{1,0:T(8,128)S(1)}, f32[16,1792]{1,0:T(8,128)S(1)}, u32[]{:S(2)}, u32[]{:S(2)}) %collective-permute-start.18) | collective-permute-done | bytes 114720 | tf_op jit(solution)/shard_map/ppermute | solution.py:199
  48.0 1.7 %collective-permute-start.22 = (f32[8,1792]{1,0:T(8,128)S(1)}, f32[8,1792]{1,0:T(8,128)S(1)}, u32[]{:S(2)}, u32[]{:S(2)}) collective-permute-start(f32[8,1792]{1,0:T(8,128)S(1)} %get-tuple-element.83), channel_id=1, source_target_pairs={{0,16},{4,20},{8,24},{12,28},{16,0},{20,4},{24,8},{28,12},{1,17},{... | collective-permute-start | bytes 172040 | tf_op jit(solution)/shard_map/ppermute | solution.py:199
  49.8 1.3 %collective-permute-start.23 = (f32[8,1792]{1,0:T(8,128)S(1)}, f32[8,1792]{1,0:T(8,128)S(1)}, u32[]{:S(2)}, u32[]{:S(2)}) collective-permute-start(f32[8,1792]{1,0:T(8,128)S(1)} %get-tuple-element.84), channel_id=1, source_target_pairs={{0,16},{4,20},{8,24},{12,28},{16,0},{20,4},{24,8},{28,12},{1,17},{... | collective-permute-start | bytes 172040 | tf_op jit(solution)/shard_map/ppermute | solution.py:199
  51.1 1.5 %collective-permute-start.24 = (f32[8,1792]{1,0:T(8,128)S(1)}, f32[8,1792]{1,0:T(8,128)S(1)}, u32[]{:S(2)}, u32[]{:S(2)}) collective-permute-start(f32[8,1792]{1,0:T(8,128)S(1)} %get-tuple-element.85), channel_id=1, source_target_pairs={{0,8},{4,12},{8,0},{12,4},{16,24},{20,28},{24,16},{28,20},{1,9},{5... | collective-permute-start | bytes 172040 | tf_op jit(solution)/shard_map/ppermute | solution.py:199
  52.6 1.7 %collective-permute-start.25 = (f32[8,1792]{1,0:T(8,128)S(1)}, f32[8,1792]{1,0:T(8,128)S(1)}, u32[]{:S(2)}, u32[]{:S(2)}) collective-permute-start(f32[8,1792]{1,0:T(8,128)S(1)} %get-tuple-element.86), channel_id=1, source_target_pairs={{0,24},{4,28},{8,16},{12,20},{16,8},{20,12},{24,0},{28,4},{1,25},{... | collective-permute-start | bytes 172040 | tf_op jit(solution)/shard_map/ppermute | solution.py:199
  54.3 1.9 %shard_map.63 = (f32[2048,256]{1,0:T(8,128)}, f32[8,128]{1,0:T(8,128)S(1)}) custom-call(f32[32,1024]{1,0:T(8,128)S(1)} %get-tuple-element.49.refs_0_.refs_3_, f32[32,1024]{1,0:T(8,128)S(1)} %get-tuple-element.50.refs_1_, f32[32,1024]{1,0:T(8,128)S(1)} %get-tuple-element.55.refs_0_.refs_3_.refs_2_, f32[32,1024]{1,0:T(8,128)S(1)} %get-tuple-element.56.refs_1_.refs_3_, ...), custom_call_target="tpu_custom_call" | custom-call | tf_op jit(solution)/shard_map/pallas_call | solution.py:30
  56.2 1.2 %collective-permute-done.23.refs_7_ = f32[8,1792]{1,0:T(8,128)S(1)} collective-permute-done((f32[8,1792]{1,0:T(8,128)S(1)}, f32[8,1792]{1,0:T(8,128)S(1)}, u32[]{:S(2)}, u32[]{:S(2)}) %collective-permute-start.23) | collective-permute-done | bytes 57376 | tf_op jit(solution)/shard_map/ppermute | solution.py:199
  57.4 1.2 %collective-permute-done.25.refs_9_ = f32[8,1792]{1,0:T(8,128)S(1)} collective-permute-done((f32[8,1792]{1,0:T(8,128)S(1)}, f32[8,1792]{1,0:T(8,128)S(1)}, u32[]{:S(2)}, u32[]{:S(2)}) %collective-permute-start.25) | collective-permute-done | bytes 57376 | tf_op jit(solution)/shard_map/ppermute | solution.py:199
  58.7 0.7 %shard_map.64 = f32[32,1792]{1,0:T(8,128)} custom-call(f32[8,1792]{1,0:T(8,128)S(1)} %get-tuple-element.67.refs_2_.refs_0_, f32[8,1792]{1,0:T(8,128)S(1)} %collective-permute-done.20.refs_1_, f32[8,1792]{1,0:T(8,128)S(1)} %get-tuple-element.77.refs_2_, f32[8,1792]{1,0:T(8,128)S(1)} %collective-permute-done.21.refs_3_, ...), custom_call_target="tpu_custom_call" | custom-call | tf_op jit(solution)/shard_map/pallas_call | solution.py:30
  (44 shorter events, 4.6 us)
Async XLA Ops:
  3.8 3.4 %collective-permute-start = (f32[256,1024]{1,0:T(8,128)S(1)}, f32[256,1024]{1,0:T(8,128)S(1)}, u32[]{:S(2)}, u32[]{:S(2)}) collective-permute-start(f32[256,1024]{1,0:T(8,128)S(1)} %get-tuple-element.47), channel_id=1, source_target_pairs={{0,1},{1,0},{2,3},{3,2},{4,5},{5,4},{6,7},{7,6},{8,9},{9,8},{10,11... | collective-permute-start | bytes 3145736 | tf_op jit(solution)/shard_map/ppermute | solution.py:199
  7.3 9.7 %collective-permute-start.1 = (f32[64,1024]{1,0:T(8,128)S(1)}, f32[64,1024]{1,0:T(8,128)S(1)}, u32[]{:S(2)}, u32[]{:S(2)}) collective-permute-start(f32[64,1024]{1,0:T(8,128)S(1)} %get-tuple-element.48.refs_0_), channel_id=1, source_target_pairs={{0,2},{1,3},{2,0},{3,1},{4,6},{5,7},{6,4},{7,5},{8,10},{9,11},{10,... | collective-permute-start | bytes 786440 | tf_op jit(solution)/shard_map/ppermute | solution.py:199
  9.9 12.9 %collective-permute-start.2 = (f32[64,1024]{1,0:T(8,128)S(1)}, f32[64,1024]{1,0:T(8,128)S(1)}, u32[]{:S(2)}, u32[]{:S(2)}) collective-permute-start(f32[64,1024]{1,0:T(8,128)S(1)} %get-tuple-element.51.refs_0_), channel_id=1, source_target_pairs={{0,2},{1,3},{2,0},{3,1},{4,6},{5,7},{6,4},{7,5},{8,10},{9,11},{10,... | collective-permute-start | bytes 786440 | tf_op jit(solution)/shard_map/ppermute | solution.py:199
  17.1 3.3 %collective-permute-start.3 = (f32[32,1024]{1,0:T(8,128)S(1)}, f32[32,1024]{1,0:T(8,128)S(1)}, u32[]{:S(2)}, u32[]{:S(2)}) collective-permute-start(f32[32,1024]{1,0:T(8,128)S(1)} %get-tuple-element.49.refs_0_.refs_3_), channel_id=1, source_target_pairs={{0,1},{1,0},{2,3},{3,2},{4,5},{5,4},{6,7},{7,6},{8,9},{9,8},{10,11... | collective-permute-start | bytes 393224 | tf_op jit(solution)/shard_map/ppermute | solution.py:199
  17.2 3.2 %collective-permute-start.4 = (f32[32,1024]{1,0:T(8,128)S(1)}, f32[32,1024]{1,0:T(8,128)S(1)}, u32[]{:S(2)}, u32[]{:S(2)}) collective-permute-start(f32[32,1024]{1,0:T(8,128)S(1)} %get-tuple-element.50.refs_1_), channel_id=1, source_target_pairs={{0,1},{1,0},{2,3},{3,2},{4,5},{5,4},{6,7},{7,6},{8,9},{9,8},{10,11... | collective-permute-start | bytes 393224 | tf_op jit(solution)/shard_map/ppermute | solution.py:199
  17.7 10.9 %collective-permute-start.5 = (f32[64,1024]{1,0:T(8,128)S(1)}, f32[64,1024]{1,0:T(8,128)S(1)}, u32[]{:S(2)}, u32[]{:S(2)}) collective-permute-start(f32[64,1024]{1,0:T(8,128)S(1)} %get-tuple-element.57.refs_0_), channel_id=1, source_target_pairs={{0,2},{1,3},{2,0},{3,1},{4,6},{5,7},{6,4},{7,5},{8,10},{9,11},{10,... | collective-permute-start | bytes 786440 | tf_op jit(solution)/shard_map/ppermute | solution.py:199
  21.2 7.4 %collective-permute-start.6 = (f32[32,1792]{1,0:T(8,128)S(1)}, f32[32,1792]{1,0:T(8,128)S(1)}, u32[]{:S(2)}, u32[]{:S(2)}) collective-permute-start(f32[32,1792]{1,0:T(8,128)S(1)} %get-tuple-element.58), channel_id=1, source_target_pairs={{0,4},{4,0},{8,12},{12,8},{16,20},{20,16},{24,28},{28,24},{1,5},{5... | collective-permute-start | bytes 688136 | tf_op jit(solution)/shard_map/ppermute | solution.py:199
  22.8 3.2 %collective-permute-start.7 = (f32[32,1024]{1,0:T(8,128)S(1)}, f32[32,1024]{1,0:T(8,128)S(1)}, u32[]{:S(2)}, u32[]{:S(2)}) collective-permute-start(f32[32,1024]{1,0:T(8,128)S(1)} %get-tuple-element.55.refs_0_.refs_3_.refs_2_), channel_id=1, source_target_pairs={{0,1},{1,0},{2,3},{3,2},{4,5},{5,4},{6,7},{7,6},{8,9},{9,8},{10,11... | collective-permute-start | bytes 393224 | tf_op jit(solution)/shard_map/ppermute | solution.py:199
  22.9 3.1 %collective-permute-start.8 = (f32[32,1024]{1,0:T(8,128)S(1)}, f32[32,1024]{1,0:T(8,128)S(1)}, u32[]{:S(2)}, u32[]{:S(2)}) collective-permute-start(f32[32,1024]{1,0:T(8,128)S(1)} %get-tuple-element.56.refs_1_.refs_3_), channel_id=1, source_target_pairs={{0,1},{1,0},{2,3},{3,2},{4,5},{5,4},{6,7},{7,6},{8,9},{9,8},{10,11... | collective-permute-start | bytes 393224 | tf_op jit(solution)/shard_map/ppermute | solution.py:199
  23.4 11.0 %collective-permute-start.9 = (f32[64,1024]{1,0:T(8,128)S(1)}, f32[64,1024]{1,0:T(8,128)S(1)}, u32[]{:S(2)}, u32[]{:S(2)}) collective-permute-start(f32[64,1024]{1,0:T(8,128)S(1)} %get-tuple-element.63.refs_0_), channel_id=1, source_target_pairs={{0,2},{1,3},{2,0},{3,1},{4,6},{5,7},{6,4},{7,5},{8,10},{9,11},{10,... | collective-permute-start | bytes 786440 | tf_op jit(solution)/shard_map/ppermute | solution.py:199
  26.8 7.6 %collective-permute-start.10 = (f32[32,1792]{1,0:T(8,128)S(1)}, f32[32,1792]{1,0:T(8,128)S(1)}, u32[]{:S(2)}, u32[]{:S(2)}) collective-permute-start(f32[32,1792]{1,0:T(8,128)S(1)} %get-tuple-element.64), channel_id=1, source_target_pairs={{0,4},{4,0},{8,12},{12,8},{16,20},{20,16},{24,28},{28,24},{1,5},{5... | collective-permute-start | bytes 688136 | tf_op jit(solution)/shard_map/ppermute | solution.py:199
  28.6 3.1 %collective-permute-start.12 = (f32[32,1024]{1,0:T(8,128)S(1)}, f32[32,1024]{1,0:T(8,128)S(1)}, u32[]{:S(2)}, u32[]{:S(2)}) collective-permute-start(f32[32,1024]{1,0:T(8,128)S(1)} %get-tuple-element.61.refs_0_.refs_3_.refs_4_), channel_id=1, source_target_pairs={{0,1},{1,0},{2,3},{3,2},{4,5},{5,4},{6,7},{7,6},{8,9},{9,8},{10,11... | collective-permute-start | bytes 393224 | tf_op jit(solution)/shard_map/ppermute | solution.py:199
  28.7 3.0 %collective-permute-start.13 = (f32[32,1024]{1,0:T(8,128)S(1)}, f32[32,1024]{1,0:T(8,128)S(1)}, u32[]{:S(2)}, u32[]{:S(2)}) collective-permute-start(f32[32,1024]{1,0:T(8,128)S(1)} %get-tuple-element.62.refs_1_.refs_5_), channel_id=1, source_target_pairs={{0,1},{1,0},{2,3},{3,2},{4,5},{5,4},{6,7},{7,6},{8,9},{9,8},{10,11... | collective-permute-start | bytes 393224 | tf_op jit(solution)/shard_map/ppermute | solution.py:199
  29.2 5.1 %collective-permute-start.11 = (f32[16,1792]{1,0:T(8,128)S(1)}, f32[16,1792]{1,0:T(8,128)S(1)}, u32[]{:S(2)}, u32[]{:S(2)}) collective-permute-start(f32[16,1792]{1,0:T(8,128)S(1)} %get-tuple-element.65), channel_id=1, source_target_pairs={{0,8},{4,12},{8,0},{12,4},{16,24},{20,28},{24,16},{28,20},{1,9},{5... | collective-permute-start | bytes 344072 | tf_op jit(solution)/shard_map/ppermute | solution.py:199
  32.5 7.7 %collective-permute-start.17 = (f32[32,1792]{1,0:T(8,128)S(1)}, f32[32,1792]{1,0:T(8,128)S(1)}, u32[]{:S(2)}, u32[]{:S(2)}) collective-permute-start(f32[32,1792]{1,0:T(8,128)S(1)} %get-tuple-element.73), channel_id=1, source_target_pairs={{0,4},{4,0},{8,12},{12,8},{16,20},{20,16},{24,28},{28,24},{1,5},{5... | collective-permute-start | bytes 688136 | tf_op jit(solution)/shard_map/ppermute | solution.py:199
  34.5 1.4 %collective-permute-start.14 = (f32[32,1024]{1,0:T(8,128)S(1)}, f32[32,1024]{1,0:T(8,128)S(1)}, u32[]{:S(2)}, u32[]{:S(2)}) collective-permute-start(f32[32,1024]{1,0:T(8,128)S(1)} %get-tuple-element.69.refs_0_.refs_3_.refs_6_), channel_id=1, source_target_pairs={{0,1},{1,0},{2,3},{3,2},{4,5},{5,4},{6,7},{7,6},{8,9},{9,8},{10,11... | collective-permute-start | bytes 393224 | tf_op jit(solution)/shard_map/ppermute | solution.py:199
  34.6 1.5 %collective-permute-start.15 = (f32[32,1024]{1,0:T(8,128)S(1)}, f32[32,1024]{1,0:T(8,128)S(1)}, u32[]{:S(2)}, u32[]{:S(2)}) collective-permute-start(f32[32,1024]{1,0:T(8,128)S(1)} %get-tuple-element.70.refs_1_.refs_7_), channel_id=1, source_target_pairs={{0,1},{1,0},{2,3},{3,2},{4,5},{5,4},{6,7},{7,6},{8,9},{9,8},{10,11... | collective-permute-start | bytes 393224 | tf_op jit(solution)/shard_map/ppermute | solution.py:199
  36.9 12.9 %collective-permute-start.16 = (f32[32,1792]{1,0:T(8,128)S(1)}, f32[32,1792]{1,0:T(8,128)S(1)}, u32[]{:S(2)}, u32[]{:S(2)}) collective-permute-start(f32[32,1792]{1,0:T(8,128)S(1)} %get-tuple-element.72), channel_id=1, source_target_pairs={{0,4},{4,0},{8,12},{12,8},{16,20},{20,16},{24,28},{28,24},{1,5},{5... | collective-permute-start | bytes 688136 | tf_op jit(solution)/shard_map/ppermute | solution.py:199
  38.6 6.6 %collective-permute-start.19 = (f32[16,1792]{1,0:T(8,128)S(1)}, f32[16,1792]{1,0:T(8,128)S(1)}, u32[]{:S(2)}, u32[]{:S(2)}) collective-permute-start(f32[16,1792]{1,0:T(8,128)S(1)} %get-tuple-element.76), channel_id=1, source_target_pairs={{0,8},{4,12},{8,0},{12,4},{16,24},{20,28},{24,16},{28,20},{1,9},{5... | collective-permute-start | bytes 344072 | tf_op jit(solution)/shard_map/ppermute | solution.py:199
  40.2 7.8 %collective-permute-start.18 = (f32[16,1792]{1,0:T(8,128)S(1)}, f32[16,1792]{1,0:T(8,128)S(1)}, u32[]{:S(2)}, u32[]{:S(2)}) collective-permute-start(f32[16,1792]{1,0:T(8,128)S(1)} %get-tuple-element.75), channel_id=1, source_target_pairs={{0,8},{4,12},{8,0},{12,4},{16,24},{20,28},{24,16},{28,20},{1,9},{5... | collective-permute-start | bytes 344072 | tf_op jit(solution)/shard_map/ppermute | solution.py:199
  40.8 11.8 %collective-permute-start.20 = (f32[8,1792]{1,0:T(8,128)S(1)}, f32[8,1792]{1,0:T(8,128)S(1)}, u32[]{:S(2)}, u32[]{:S(2)}) collective-permute-start(f32[8,1792]{1,0:T(8,128)S(1)} %get-tuple-element.81), channel_id=1, source_target_pairs={{0,16},{4,20},{8,24},{12,28},{16,0},{20,4},{24,8},{28,12},{1,17},{... | collective-permute-start | bytes 172040 | tf_op jit(solution)/shard_map/ppermute | solution.py:199
  45.3 11.0 %collective-permute-start.21 = (f32[8,1792]{1,0:T(8,128)S(1)}, f32[8,1792]{1,0:T(8,128)S(1)}, u32[]{:S(2)}, u32[]{:S(2)}) collective-permute-start(f32[8,1792]{1,0:T(8,128)S(1)} %get-tuple-element.82), channel_id=1, source_target_pairs={{0,16},{4,20},{8,24},{12,28},{16,0},{20,4},{24,8},{28,12},{1,17},{... | collective-permute-start | bytes 172040 | tf_op jit(solution)/shard_map/ppermute | solution.py:199
  48.0 8.2 %collective-permute-start.22 = (f32[8,1792]{1,0:T(8,128)S(1)}, f32[8,1792]{1,0:T(8,128)S(1)}, u32[]{:S(2)}, u32[]{:S(2)}) collective-permute-start(f32[8,1792]{1,0:T(8,128)S(1)} %get-tuple-element.83), channel_id=1, source_target_pairs={{0,16},{4,20},{8,24},{12,28},{16,0},{20,4},{24,8},{28,12},{1,17},{... | collective-permute-start | bytes 172040 | tf_op jit(solution)/shard_map/ppermute | solution.py:199
  49.8 7.7 %collective-permute-start.23 = (f32[8,1792]{1,0:T(8,128)S(1)}, f32[8,1792]{1,0:T(8,128)S(1)}, u32[]{:S(2)}, u32[]{:S(2)}) collective-permute-start(f32[8,1792]{1,0:T(8,128)S(1)} %get-tuple-element.84), channel_id=1, source_target_pairs={{0,16},{4,20},{8,24},{12,28},{16,0},{20,4},{24,8},{28,12},{1,17},{... | collective-permute-start | bytes 172040 | tf_op jit(solution)/shard_map/ppermute | solution.py:199
  51.1 6.3 %collective-permute-start.24 = (f32[8,1792]{1,0:T(8,128)S(1)}, f32[8,1792]{1,0:T(8,128)S(1)}, u32[]{:S(2)}, u32[]{:S(2)}) collective-permute-start(f32[8,1792]{1,0:T(8,128)S(1)} %get-tuple-element.85), channel_id=1, source_target_pairs={{0,8},{4,12},{8,0},{12,4},{16,24},{20,28},{24,16},{28,20},{1,9},{5... | collective-permute-start | bytes 172040 | tf_op jit(solution)/shard_map/ppermute | solution.py:199
  52.6 6.1 %collective-permute-start.25 = (f32[8,1792]{1,0:T(8,128)S(1)}, f32[8,1792]{1,0:T(8,128)S(1)}, u32[]{:S(2)}, u32[]{:S(2)}) collective-permute-start(f32[8,1792]{1,0:T(8,128)S(1)} %get-tuple-element.86), channel_id=1, source_target_pairs={{0,24},{4,28},{8,16},{12,20},{16,8},{20,12},{24,0},{28,4},{1,25},{... | collective-permute-start | bytes 172040 | tf_op jit(solution)/shard_map/ppermute | solution.py:199

commit v6 on v5

--- a/solution.py
+++ b/solution.py
@@ -13,11 +13,11 @@
 BF16 = jnp.bfloat16
 NT = (((1,), (1,)), ((), ()))
 SPECS = {"v": pl.BlockSpec(memory_space=pltpu.VMEM), "a": pl.BlockSpec(memory_space=pl.ANY)}
-ORDER = "own0 before0 send0 own1 before1 send1 add0.1 own2 before2 send2 add0.2 add1.1 own3 before3 send3 add2.1 add1.2 add2.2 add3.1 sketch"
-WEIGHTS = {'add2.2': 1000000000, 'send1': 200000000, 'own1': 1000000000, 'own2': 0, 'before2': 2000000000, 'before1': 500000000, 'add0.2': 0, 'sketch': 500000000, 'add3.1': 200000000}
+ORDER = ()
+WEIGHTS = {}
 SPLIT = 2
-DIRECT = 1
 GROUPS = ((0,), (1,), (2,), (3,))
+MODES = ("all", "all", "all", "all")
 
 
 def call(body, args, outs, kinds=None, after=(), scratch=(), results=0, weight=0):
@@ -144,6 +144,16 @@
     split(1, [total.shape[0]], [total], send, keep)
 
 
+def product_spread_body(n_row, *refs):
+    outs, total = refs[-1 - n_row : -1], refs[-1]
+    *sketch, held, before = refs[: -1 - n_row]
+    total[...] = before[...] + jnp.dot(joined(sketch).astype(BF16), held[...], preferred_element_type=F32)
+    piece = outs[0].shape[0]
+    place = owner_at(lax.axis_index("row"), n_row)
+    for flip, out in enumerate(outs):
+        out[...] = total[pl.ds(pl.multiple_of(lax.bitwise_xor(place, flip) * piece, piece), piece), :]
+
+
 def add_send_body(bit, segments, *refs):
     *pairs, send, keep = refs
     first = 0
@@ -163,13 +173,20 @@
         out[...] = kept[part, :] + received[part, :]
 
 
-def final_corange_body(counts, *refs):
+def add_all_body(n_high, kept, received, out):
+    piece = out.shape[0] // n_high
+    for high in range(n_high):
+        part = pl.ds(owner_at(high, n_high) * piece, piece)
+        out[pl.ds(high * piece, piece), :] = kept[part, :] + received[part, :]
+
+
+def final_corange_body(counts, rows, *refs):
     out = refs[-1]
     first, used = 0, 0
-    for count in counts:
+    for count, piece in zip(counts, rows):
         terms = refs[used : used + count]
-        piece = terms[0].shape[0]
-        out[pl.ds(first, piece), :] = functools.reduce(jnp.add, [term[...] for term in terms])
+        parts = [term[pl.ds(i, piece), :] for term in terms for i in range(0, term.shape[0], piece)]
+        out[pl.ds(first, piece), :] = functools.reduce(jnp.add, parts)
         first += piece
         used += count
 
@@ -231,17 +248,18 @@
     owns, others, befores, pending = {}, {}, {}, {}
     sketch = None
     last = ()
-    groups = GROUPS if n == 4 else tuple((c,) for c in range(n))
-    direct = [len(bits) == 3 and len(group) == 1 and pieces[group[0]] % 8 == 0 and g >= len(groups) - DIRECT for g, group in enumerate(groups)]
-    steps = ORDER.split() if len(bits) == 3 and n == 4 else []
+    groups = GROUPS if n == sum(len(group) for group in GROUPS) else tuple((c,) for c in range(n))
+    modes = MODES if len(groups) == len(MODES) else ("all",) * len(groups)
+    whole = [any(mode == "spread" and c in group for mode, group in zip(modes, groups)) for c in range(n)]
+    steps = ORDER
     if not steps:
         found = []
         for c in range(n):
             found += [(10 * c, f"own{c}"), (10 * c + 1, f"before{c}"), (10 * c + 2, f"send{c}")]
         for g, group in enumerate(groups):
-            found += [(10 * group[-1] + 9.5 + 10 * s, f"add{g}.{s}") for s in range(1, 2 if direct[g] else len(bits))]
+            last_step = {"all": 2, "direct": 2, "spread": 1, "pairs": len(bits)}[modes[g]]
+            found += [(10 * group[-1] + 9.5 + 10 * s, f"add{g}.{s}") for s in range(1, last_step)]
         steps = [step for _, step in sorted(found)] + ["sketch"]
-
     for step in steps:
         weight = WEIGHTS.get(step, 0)
         if step.startswith("own"):
@@ -256,6 +274,15 @@
             last = (befores[c],)
         elif step.startswith("send"):
             c = int(step[4:])
+            if whole[c]:
+                args = (*others[c], held_other, befores[c])
+                body = functools.partial(product_spread_body, n_row)
+                outs = [((pieces[c], d), F32)] * n_row
+                own, *sends = call(body, args, outs, after=last, scratch=[pltpu.VMEM((widths[c], d), F32)], weight=weight)
+                flips = [owner_at(flip, n_row) for flip in range(1, n_row)]
+                pending[(c,)] = own, *[swap(x, "row", n_row, flip) for x, flip in zip(sends, flips)]
+                last = (own,)
+                continue
             outs = [((widths[c] // 2, d), F32)] * 2
             total = pltpu.VMEM((widths[c], d), F32)
             args = (*others[c], held_other, befores[c])
@@ -265,7 +292,14 @@
         elif step.startswith("add"):
             g, s = (int(x) for x in step[3:].split("."))
             group = groups[g]
-            if direct[g]:
+            if modes[g] == "all":
+                outs = [((n_row // 2 * pieces[group[0]], d), F32)]
+                total = call(functools.partial(add_all_body, n_row // 2), pending[group], outs, after=last, weight=weight)[0]
+                across = [[2 * high + low for high in range(n_row // 2)] for low in range(2)]
+                pending[group] = (lax.all_to_all(total, "row", 0, 0, axis_index_groups=across, tiled=True),)
+                last = (total,)
+                continue
+            if modes[g] == "direct":
                 outs = [((pieces[group[0]], d), F32)] * (n_row // 2)
                 body = functools.partial(add_spread_body, n_row // 2)
                 own, *sends = call(body, pending[group], outs, after=last, weight=weight)
@@ -287,10 +321,11 @@
             last = (done,)
     flat = [x for group in groups for x in pending[group]]
     if per_owner % 8 == 0:
-        body = functools.partial(final_corange_body, [len(pending[group]) for group in groups])
+        body = functools.partial(final_corange_body, [len(pending[group]) for group in groups], [sum(pieces[c] for c in group) for group in groups])
         corange = call(body, flat, [((per_owner, d), F32)], after=last, results=1, weight=WEIGHTS.get("F", 0))[0]
     else:
-        corange = jnp.concatenate([functools.reduce(jnp.add, pending[group]) for group in groups], axis=0)
+        parts = [x for group in groups for x in pending[group]]
+        corange = jnp.concatenate([part.reshape(n_row // 2, -1, d).sum(0) for part in parts], axis=0)
     return sketch, corange.T
 
 

time: 59.6 us -> 80 us (1.34)
  waiting for transfers between devices: 12.8 us -> 22.1 us
  local copies, waits for them, and re-layouts: 0 us -> 4.09 us
  Pallas kernels: 15.2 us -> 18.6 us
  starting transfers between devices: 30.5 us -> 33.7 us
    all_to_all x0 -> x4, starting transfers between devices: none -> 19.7 us  [shards(): lax.all_to_all(total, 'row', 0, 0, axis_index_groups=across, tiled=True)]
    ppermute x26 -> x17, starting transfers between devices: 30.5 us -> 14.1 us  [swap(): return lax.ppermute(x, axis, [(i, i ^ bit) for i in range(size)])]
    all_to_all x0 -> x4, waiting for transfers between devices: none -> 5.02 us  [shards(): lax.all_to_all(total, 'row', 0, 0, axis_index_groups=across, tiled=True)]
    ppermute x26 -> x17, waiting for transfers between devices: 12.8 us -> 17.1 us  [swap(): return lax.ppermute(x, axis, [(i, i ^ bit) for i in range(size)])]
    unnamed x0 -> x12, local copies, waits for them, and re-layouts: none -> 4.09 us
    pallas_call x24 -> x21, Pallas kernels: 15.2 us -> 18.6 us  [call(): pl.pallas_call(run, out_shape=[pltpu.VMEM(*o) if i >= results else jax.Sh...]
  transfers between devices with their start and end apart: 26 -> 21, of which waited for: 9 -> 9; matrix products, arithmetic and copies ran while one was open for 0% -> 0% of each run, Pallas kernels for 19% -> 18%
where the time goes in v6:
time: 80 us; the launch traced here: 79.5 us
  starting transfers between devices  33.7 us (42%)
  waiting for transfers between devices  22.1 us (28%)
  Pallas kernels  18.6 us (23%)
  local copies, waits for them, and re-layouts  4.09 us (5%)
  between operations  0.88 us (1%)
    all_to_all x4, starting transfers between devices, shards(): lax.all_to_all(total, 'row', 0, 0, axis_index_groups=across, tiled=True)  19.7 us
    pallas_call x21, Pallas kernels, call(): pl.pallas_call(run, out_shape=[pltpu.VMEM(*o) if i >= results else jax.Sh...  18.6 us
    ppermute x17, waiting for transfers between devices, swap(): return lax.ppermute(x, axis, [(i, i ^ bit) for i in range(size)])  17.1 us
    ppermute x17, starting transfers between devices, swap(): return lax.ppermute(x, axis, [(i, i ^ bit) for i in range(size)])  14.1 us
    all_to_all x4, waiting for transfers between devices, shards(): lax.all_to_all(total, 'row', 0, 0, axis_index_groups=across, tiled=True)  5.02 us
    unnamed x12, local copies, waits for them, and re-layouts  4.09 us
  transfers between devices with their start and end apart: 21, of which 9 were waited for; matrix products, arithmetic and copies ran while one was open for 0% of the time, Pallas kernels for 18%

profile of v6, /device:TPU:0, one launch (start us, length us, event | category | flops | bytes accessed | tf_op | source)
XLA Modules:
  0.0 79.5 jit_solution(1320226727004855909)
XLA Ops:
  0.6 3.2 %shard_map.41 = (bf16[1024,1792]{1,0:T(8,128)(2,1)S(1)}, bf16[256,1792]{1,0:T(8,128)(2,1)S(1)}, f32[256,1024]{1,0:T(8,128)S(1)}) custom-call(bf16[2048,1792]{1,0:T(8,128)(2,1)} %refs_0_.3, bf16[1792,256]{1,0:T(8,128)(2,1)} %refs_1_.1), custom_call_target="tpu_custom_call" | custom-call | tf_op jit(solution)/shard_map/pallas_call | solution.py:30
  4.4 3.6 %shard_map.42 = (bf16[1024,1792]{1,0:T(8,128)(2,1)S(1)}, f32[256,1024]{1,0:T(8,128)S(1)}) custom-call(bf16[2048,1792]{1,0:T(8,128)(2,1)} %refs_0_.3, bf16[256,1792]{1,0:T(8,128)(2,1)S(1)} %get-tuple-element.29.refs_1_), custom_call_target="tpu_custom_call" | custom-call | tf_op jit(solution)/shard_map/pallas_call | solution.py:30
  8.1 3.0 %collective-permute-start.1 = (f32[64,1024]{1,0:T(8,128)S(1)}, f32[64,1024]{1,0:T(8,128)S(1)}, u32[]{:S(2)}, u32[]{:S(2)}) collective-permute-start(f32[64,1024]{1,0:T(8,128)S(1)} %get-tuple-element.32.refs_0_), channel_id=1, source_target_pairs={{0,2},{1,3},{2,0},{3,1},{4,6},{5,7},{6,4},{7,5},{8,10},{9,11},{10,... | collective-permute-start | bytes 786440 | tf_op jit(solution)/shard_map/ppermute | solution.py:216
  11.3 7.1 %collective-permute-done.1.refs_1_ = f32[64,1024]{1,0:T(8,128)S(1)} collective-permute-done((f32[64,1024]{1,0:T(8,128)S(1)}, f32[64,1024]{1,0:T(8,128)S(1)}, u32[]{:S(2)}, u32[]{:S(2)}) %collective-permute-start.1) | collective-permute-done | bytes 262176 | tf_op jit(solution)/shard_map/ppermute | solution.py:216
  18.9 0.7 shard_map.45.refs_3_.refs_4_
  20.0 0.8 shard_map.46
  20.7 2.2 %collective-permute-start.6 = (f32[32,1792]{1,0:T(8,128)S(1)}, f32[32,1792]{1,0:T(8,128)S(1)}, u32[]{:S(2)}, u32[]{:S(2)}) collective-permute-start(f32[32,1792]{1,0:T(8,128)S(1)} %get-tuple-element.42), channel_id=1, source_target_pairs={{0,4},{4,0},{8,12},{12,8},{16,20},{20,16},{24,28},{28,24},{1,5},{5... | collective-permute-start | bytes 688136 | tf_op jit(solution)/shard_map/ppermute | solution.py:216
  23.6 1.7 %collective-permute-start.5 = (f32[64,1024]{1,0:T(8,128)S(1)}, f32[64,1024]{1,0:T(8,128)S(1)}, u32[]{:S(2)}, u32[]{:S(2)}) collective-permute-start(f32[64,1024]{1,0:T(8,128)S(1)} %get-tuple-element.41.refs_0_), channel_id=1, source_target_pairs={{0,2},{1,3},{2,0},{3,1},{4,6},{5,7},{6,4},{7,5},{8,10},{9,11},{10,... | collective-permute-start | bytes 786440 | tf_op jit(solution)/shard_map/ppermute | solution.py:216
  25.4 0.7 shard_map.48.refs_3_.refs_4_
  26.2 0.8 shard_map.49
  26.9 2.0 %collective-permute-done.6.refs_1_ = f32[32,1792]{1,0:T(8,128)S(1)} collective-permute-done((f32[32,1792]{1,0:T(8,128)S(1)}, f32[32,1792]{1,0:T(8,128)S(1)}, u32[]{:S(2)}, u32[]{:S(2)}) %collective-permute-start.6) | collective-permute-done | bytes 229408 | tf_op jit(solution)/shard_map/ppermute | solution.py:216
  29.0 0.7 shard_map.50.refs_2_
  29.7 5.1 %all-to-all-start = ((f32[4,8,1792]{2,1,0:T(8,128)}), f32[4,8,1792]{2,1,0:T(8,128)S(1)}, u32[]{:S(2)}, u32[]{:S(2)}) async-start(f32[4,8,1792]{2,1,0:T(8,128)} %bitcast), calls=%async_computation | async-start | bytes 458752 | tf_op jit(solution)/shard_map/all_to_all | solution.py:299
  34.8 1.5 %collective-permute-start.10 = (f32[32,1792]{1,0:T(8,128)S(1)}, f32[32,1792]{1,0:T(8,128)S(1)}, u32[]{:S(2)}, u32[]{:S(2)}) collective-permute-start(f32[32,1792]{1,0:T(8,128)S(1)} %get-tuple-element.47), channel_id=1, source_target_pairs={{0,4},{4,0},{8,12},{12,8},{16,20},{20,16},{24,28},{28,24},{1,5},{5... | collective-permute-start | bytes 688136 | tf_op jit(solution)/shard_map/ppermute | solution.py:216
  36.9 1.5 %collective-permute-start.9 = (f32[64,1024]{1,0:T(8,128)S(1)}, f32[64,1024]{1,0:T(8,128)S(1)}, u32[]{:S(2)}, u32[]{:S(2)}) collective-permute-start(f32[64,1024]{1,0:T(8,128)S(1)} %get-tuple-element.46.refs_0_), channel_id=1, source_target_pairs={{0,2},{1,3},{2,0},{3,1},{4,6},{5,7},{6,4},{7,5},{8,10},{9,11},{10,... | collective-permute-start | bytes 786440 | tf_op jit(solution)/shard_map/ppermute | solution.py:216
  38.4 2.0 %copy-done.4 = bf16[1024,1792]{1,0:T(8,128)(2,1)S(1)} copy-done((bf16[1024,1792]{1,0:T(8,128)(2,1)S(1)}, bf16[1024,1792]{1,0:T(8,128)(2,1)}, u32[]{:S(2)}) %copy-start.4) | copy-done | bytes 3670040
  40.4 0.7 shard_map.52.refs_3_.refs_4_
  41.2 0.8 shard_map.53
  42.0 0.7 shard_map.54.refs_2_
  42.7 5.1 %all-to-all-start.1 = ((f32[4,8,1792]{2,1,0:T(8,128)}), f32[4,8,1792]{2,1,0:T(8,128)S(1)}, u32[]{:S(2)}, u32[]{:S(2)}) async-start(f32[4,8,1792]{2,1,0:T(8,128)} %bitcast.2), calls=%async_computation.1 | async-start | bytes 458752 | tf_op jit(solution)/shard_map/all_to_all | solution.py:299
  47.8 0.8 collective-permute-start.16
  49.2 2.0 %copy-done.5 = bf16[1024,1792]{1,0:T(8,128)(2,1)S(1)} copy-done((bf16[1024,1792]{1,0:T(8,128)(2,1)S(1)}, bf16[1024,1792]{1,0:T(8,128)(2,1)}, u32[]{:S(2)}) %copy-start.5) | copy-done | bytes 3670040
  51.2 0.7 shard_map.56.refs_3_.refs_4_
  52.0 0.8 shard_map.57
  52.8 2.1 %collective-permute-done.16.refs_1_ = f32[32,1792]{1,0:T(8,128)S(1)} collective-permute-done((f32[32,1792]{1,0:T(8,128)S(1)}, f32[32,1792]{1,0:T(8,128)S(1)}, u32[]{:S(2)}, u32[]{:S(2)}) %collective-permute-start.16) | collective-permute-done | bytes 229408 | tf_op jit(solution)/shard_map/ppermute | solution.py:216
  56.0 4.4 %all-to-all-start.2 = ((f32[4,8,1792]{2,1,0:T(8,128)}), f32[4,8,1792]{2,1,0:T(8,128)S(1)}, u32[]{:S(2)}, u32[]{:S(2)}) async-start(f32[4,8,1792]{2,1,0:T(8,128)} %bitcast.4), calls=%async_computation.2 | async-start | bytes 458752 | tf_op jit(solution)/shard_map/all_to_all | solution.py:299
  60.9 5.5 %collective-permute-done.15.refs_1_ = f32[32,1792]{1,0:T(8,128)S(1)} collective-permute-done((f32[32,1792]{1,0:T(8,128)S(1)}, f32[32,1792]{1,0:T(8,128)S(1)}, u32[]{:S(2)}, u32[]{:S(2)}) %collective-permute-start.15) | collective-permute-done | bytes 229408 | tf_op jit(solution)/shard_map/ppermute | solution.py:216
  66.4 0.7 shard_map.59.refs_16_
  67.1 5.1 %all-to-all-start.3 = ((f32[4,8,1792]{2,1,0:T(8,128)}), f32[4,8,1792]{2,1,0:T(8,128)S(1)}, u32[]{:S(2)}, u32[]{:S(2)}) async-start(f32[4,8,1792]{2,1,0:T(8,128)} %bitcast.6), calls=%async_computation.3 | async-start | bytes 458752 | tf_op jit(solution)/shard_map/all_to_all | solution.py:299
  72.2 1.9 %shard_map.60 = (f32[2048,256]{1,0:T(8,128)}, f32[8,128]{1,0:T(8,128)S(1)}) custom-call(f32[32,1024]{1,0:T(8,128)S(1)} %get-tuple-element.33.refs_0_.refs_3_, f32[32,1024]{1,0:T(8,128)S(1)} %get-tuple-element.34.refs_1_, f32[32,1024]{1,0:T(8,128)S(1)} %get-tuple-element.39.refs_0_.refs_3_.refs_2_, f32[32,1024]{1,0:T(8,128)S(1)} %get-tuple-element.40.refs_1_.refs_3_, ...), custom_call_target="tpu_custom_call" | custom-call | tf_op jit(solution)/shard_map/pallas_call | solution.py:30
  74.1 4.6 %all-to-all-done.3 = f32[4,8,1792]{2,1,0:T(8,128)S(1)} async-done(((f32[4,8,1792]{2,1,0:T(8,128)}), f32[4,8,1792]{2,1,0:T(8,128)S(1)}, u32[]{:S(2)}, u32[]{:S(2)}) %all-to-all-start.3) | async-done | bytes 229408 | tf_op jit(solution)/shard_map/all_to_all | solution.py:299
  78.7 0.7 shard_map.61
  (43 shorter events, 5.2 us)
Async XLA Ops:
  3.8 22.3 %copy-start = (bf16[1024,1792]{1,0:T(8,128)(2,1)}, bf16[1024,1792]{1,0:T(8,128)(2,1)S(1)}, u32[]{:S(2)}) copy-start(bf16[1024,1792]{1,0:T(8,128)(2,1)S(1)} %get-tuple-element.36.refs_2_) | copy-start | bytes 11010052
  3.8 4.2 %collective-permute-start = (f32[256,1024]{1,0:T(8,128)S(1)}, f32[256,1024]{1,0:T(8,128)S(1)}, u32[]{:S(2)}, u32[]{:S(2)}) collective-permute-start(f32[256,1024]{1,0:T(8,128)S(1)} %get-tuple-element.31), channel_id=1, source_target_pairs={{0,1},{1,0},{2,3},{3,2},{4,5},{5,4},{6,7},{7,6},{8,9},{9,8},{10,11... | collective-permute-start | bytes 3145736 | tf_op jit(solution)/shard_map/ppermute | solution.py:216
  8.0 17.4 %copy-start.3 = (bf16[1024,1792]{1,0:T(8,128)(2,1)}, bf16[1024,1792]{1,0:T(8,128)(2,1)S(1)}, u32[]{:S(2)}) copy-start(bf16[1024,1792]{1,0:T(8,128)(2,1)S(1)} %get-tuple-element.37.refs_2_) | copy-start | bytes 11010052
  8.1 10.2 %collective-permute-start.1 = (f32[64,1024]{1,0:T(8,128)S(1)}, f32[64,1024]{1,0:T(8,128)S(1)}, u32[]{:S(2)}, u32[]{:S(2)}) collective-permute-start(f32[64,1024]{1,0:T(8,128)S(1)} %get-tuple-element.32.refs_0_), channel_id=1, source_target_pairs={{0,2},{1,3},{2,0},{3,1},{4,6},{5,7},{6,4},{7,5},{8,10},{9,11},{10,... | collective-permute-start | bytes 786440 | tf_op jit(solution)/shard_map/ppermute | solution.py:216
  11.2 11.9 %collective-permute-start.2 = (f32[64,1024]{1,0:T(8,128)S(1)}, f32[64,1024]{1,0:T(8,128)S(1)}, u32[]{:S(2)}, u32[]{:S(2)}) collective-permute-start(f32[64,1024]{1,0:T(8,128)S(1)} %get-tuple-element.35.refs_0_), channel_id=1, source_target_pairs={{0,2},{1,3},{2,0},{3,1},{4,6},{5,7},{6,4},{7,5},{8,10},{9,11},{10,... | collective-permute-start | bytes 786440 | tf_op jit(solution)/shard_map/ppermute | solution.py:216
  18.4 1.4 %collective-permute-start.3 = (f32[32,1024]{1,0:T(8,128)S(1)}, f32[32,1024]{1,0:T(8,128)S(1)}, u32[]{:S(2)}, u32[]{:S(2)}) collective-permute-start(f32[32,1024]{1,0:T(8,128)S(1)} %get-tuple-element.33.refs_0_.refs_3_), channel_id=1, source_target_pairs={{0,1},{1,0},{2,3},{3,2},{4,5},{5,4},{6,7},{7,6},{8,9},{9,8},{10,11... | collective-permute-start | bytes 393224 | tf_op jit(solution)/shard_map/ppermute | solution.py:216
  18.4 1.5 %collective-permute-start.4 = (f32[32,1024]{1,0:T(8,128)S(1)}, f32[32,1024]{1,0:T(8,128)S(1)}, u32[]{:S(2)}, u32[]{:S(2)}) collective-permute-start(f32[32,1024]{1,0:T(8,128)S(1)} %get-tuple-element.34.refs_1_), channel_id=1, source_target_pairs={{0,1},{1,0},{2,3},{3,2},{4,5},{5,4},{6,7},{7,6},{8,9},{9,8},{10,11... | collective-permute-start | bytes 393224 | tf_op jit(solution)/shard_map/ppermute | solution.py:216
  20.7 8.2 %collective-permute-start.6 = (f32[32,1792]{1,0:T(8,128)S(1)}, f32[32,1792]{1,0:T(8,128)S(1)}, u32[]{:S(2)}, u32[]{:S(2)}) collective-permute-start(f32[32,1792]{1,0:T(8,128)S(1)} %get-tuple-element.42), channel_id=1, source_target_pairs={{0,4},{4,0},{8,12},{12,8},{16,20},{20,16},{24,28},{28,24},{1,5},{5... | collective-permute-start | bytes 688136 | tf_op jit(solution)/shard_map/ppermute | solution.py:216
  23.1 3.1 %collective-permute-start.7 = (f32[32,1024]{1,0:T(8,128)S(1)}, f32[32,1024]{1,0:T(8,128)S(1)}, u32[]{:S(2)}, u32[]{:S(2)}) collective-permute-start(f32[32,1024]{1,0:T(8,128)S(1)} %get-tuple-element.39.refs_0_.refs_3_.refs_2_), channel_id=1, source_target_pairs={{0,1},{1,0},{2,3},{3,2},{4,5},{5,4},{6,7},{7,6},{8,9},{9,8},{10,11... | collective-permute-start | bytes 393224 | tf_op jit(solution)/shard_map/ppermute | solution.py:216
  23.1 3.0 %collective-permute-start.8 = (f32[32,1024]{1,0:T(8,128)S(1)}, f32[32,1024]{1,0:T(8,128)S(1)}, u32[]{:S(2)}, u32[]{:S(2)}) collective-permute-start(f32[32,1024]{1,0:T(8,128)S(1)} %get-tuple-element.40.refs_1_.refs_3_), channel_id=1, source_target_pairs={{0,1},{1,0},{2,3},{3,2},{4,5},{5,4},{6,7},{7,6},{8,9},{9,8},{10,11... | collective-permute-start | bytes 393224 | tf_op jit(solution)/shard_map/ppermute | solution.py:216
  23.6 12.7 %collective-permute-start.5 = (f32[64,1024]{1,0:T(8,128)S(1)}, f32[64,1024]{1,0:T(8,128)S(1)}, u32[]{:S(2)}, u32[]{:S(2)}) collective-permute-start(f32[64,1024]{1,0:T(8,128)S(1)} %get-tuple-element.41.refs_0_), channel_id=1, source_target_pairs={{0,2},{1,3},{2,0},{3,1},{4,6},{5,7},{6,4},{7,5},{8,10},{9,11},{10,... | collective-permute-start | bytes 786440 | tf_op jit(solution)/shard_map/ppermute | solution.py:216
  29.7 13.0 %all-to-all-start = ((f32[4,8,1792]{2,1,0:T(8,128)}), f32[4,8,1792]{2,1,0:T(8,128)S(1)}, u32[]{:S(2)}, u32[]{:S(2)}) async-start(f32[4,8,1792]{2,1,0:T(8,128)} %bitcast), calls=%async_computation | async-start | bytes 458752 | tf_op jit(solution)/shard_map/all_to_all | solution.py:299
  34.8 6.4 %copy-start.1 = (bf16[1024,1792]{1,0:T(8,128)(2,1)S(1)}, bf16[1024,1792]{1,0:T(8,128)(2,1)}, u32[]{:S(2)}) copy-start(bf16[1024,1792]{1,0:T(8,128)(2,1)} %copy-done) | copy-start | bytes 11010052
  34.8 7.2 %collective-permute-start.10 = (f32[32,1792]{1,0:T(8,128)S(1)}, f32[32,1792]{1,0:T(8,128)S(1)}, u32[]{:S(2)}, u32[]{:S(2)}) collective-permute-start(f32[32,1792]{1,0:T(8,128)S(1)} %get-tuple-element.47), channel_id=1, source_target_pairs={{0,4},{4,0},{8,12},{12,8},{16,20},{20,16},{24,28},{28,24},{1,5},{5... | collective-permute-start | bytes 688136 | tf_op jit(solution)/shard_map/ppermute | solution.py:216
  36.3 4.9 %collective-permute-start.11 = (f32[32,1024]{1,0:T(8,128)S(1)}, f32[32,1024]{1,0:T(8,128)S(1)}, u32[]{:S(2)}, u32[]{:S(2)}) collective-permute-start(f32[32,1024]{1,0:T(8,128)S(1)} %get-tuple-element.44.refs_0_.refs_3_.refs_4_), channel_id=1, source_target_pairs={{0,1},{1,0},{2,3},{3,2},{4,5},{5,4},{6,7},{7,6},{8,9},{9,8},{10,11... | collective-permute-start | bytes 393224 | tf_op jit(solution)/shard_map/ppermute | solution.py:216
  36.4 4.8 %collective-permute-start.12 = (f32[32,1024]{1,0:T(8,128)S(1)}, f32[32,1024]{1,0:T(8,128)S(1)}, u32[]{:S(2)}, u32[]{:S(2)}) collective-permute-start(f32[32,1024]{1,0:T(8,128)S(1)} %get-tuple-element.45.refs_1_.refs_5_), channel_id=1, source_target_pairs={{0,1},{1,0},{2,3},{3,2},{4,5},{5,4},{6,7},{7,6},{8,9},{9,8},{10,11... | collective-permute-start | bytes 393224 | tf_op jit(solution)/shard_map/ppermute | solution.py:216
  36.9 11.7 %collective-permute-start.9 = (f32[64,1024]{1,0:T(8,128)S(1)}, f32[64,1024]{1,0:T(8,128)S(1)}, u32[]{:S(2)}, u32[]{:S(2)}) collective-permute-start(f32[64,1024]{1,0:T(8,128)S(1)} %get-tuple-element.46.refs_0_), channel_id=1, source_target_pairs={{0,2},{1,3},{2,0},{3,1},{4,6},{5,7},{6,4},{7,5},{8,10},{9,11},{10,... | collective-permute-start | bytes 786440 | tf_op jit(solution)/shard_map/ppermute | solution.py:216
  38.4 2.0 %copy-start.4 = (bf16[1024,1792]{1,0:T(8,128)(2,1)S(1)}, bf16[1024,1792]{1,0:T(8,128)(2,1)}, u32[]{:S(2)}) copy-start(bf16[1024,1792]{1,0:T(8,128)(2,1)} %copy-done.3) | copy-start | bytes 11010052
  42.7 13.3 %all-to-all-start.1 = ((f32[4,8,1792]{2,1,0:T(8,128)}), f32[4,8,1792]{2,1,0:T(8,128)S(1)}, u32[]{:S(2)}, u32[]{:S(2)}) async-start(f32[4,8,1792]{2,1,0:T(8,128)} %bitcast.2), calls=%async_computation.1 | async-start | bytes 458752 | tf_op jit(solution)/shard_map/all_to_all | solution.py:299
  47.8 4.2 %copy-start.2 = (bf16[1024,1792]{1,0:T(8,128)(2,1)S(1)}, bf16[1024,1792]{1,0:T(8,128)(2,1)}, u32[]{:S(2)}) copy-start(bf16[1024,1792]{1,0:T(8,128)(2,1)} %copy-done) | copy-start | bytes 11010052
  47.8 7.0 %collective-permute-start.16 = (f32[32,1792]{1,0:T(8,128)S(1)}, f32[32,1792]{1,0:T(8,128)S(1)}, u32[]{:S(2)}, u32[]{:S(2)}) collective-permute-start(f32[32,1792]{1,0:T(8,128)S(1)} %get-tuple-element.53), channel_id=1, source_target_pairs={{0,4},{4,0},{8,12},{12,8},{16,20},{20,16},{24,28},{28,24},{1,5},{5... | collective-permute-start | bytes 688136 | tf_op jit(solution)/shard_map/ppermute | solution.py:216
  48.6 3.4 %collective-permute-start.13 = (f32[32,1024]{1,0:T(8,128)S(1)}, f32[32,1024]{1,0:T(8,128)S(1)}, u32[]{:S(2)}, u32[]{:S(2)}) collective-permute-start(f32[32,1024]{1,0:T(8,128)S(1)} %get-tuple-element.49.refs_0_.refs_3_.refs_6_), channel_id=1, source_target_pairs={{0,1},{1,0},{2,3},{3,2},{4,5},{5,4},{6,7},{7,6},{8,9},{9,8},{10,11... | collective-permute-start | bytes 393224 | tf_op jit(solution)/shard_map/ppermute | solution.py:216
  48.7 3.3 %collective-permute-start.14 = (f32[32,1024]{1,0:T(8,128)S(1)}, f32[32,1024]{1,0:T(8,128)S(1)}, u32[]{:S(2)}, u32[]{:S(2)}) collective-permute-start(f32[32,1024]{1,0:T(8,128)S(1)} %get-tuple-element.50.refs_1_.refs_7_), channel_id=1, source_target_pairs={{0,1},{1,0},{2,3},{3,2},{4,5},{5,4},{6,7},{7,6},{8,9},{9,8},{10,11... | collective-permute-start | bytes 393224 | tf_op jit(solution)/shard_map/ppermute | solution.py:216
  49.2 2.0 %copy-start.5 = (bf16[1024,1792]{1,0:T(8,128)(2,1)S(1)}, bf16[1024,1792]{1,0:T(8,128)(2,1)}, u32[]{:S(2)}) copy-start(bf16[1024,1792]{1,0:T(8,128)(2,1)} %copy-done.3) | copy-start | bytes 11010052
  56.0 11.1 %all-to-all-start.2 = ((f32[4,8,1792]{2,1,0:T(8,128)}), f32[4,8,1792]{2,1,0:T(8,128)S(1)}, u32[]{:S(2)}, u32[]{:S(2)}) async-start(f32[4,8,1792]{2,1,0:T(8,128)} %bitcast.4), calls=%async_computation.2 | async-start | bytes 458752 | tf_op jit(solution)/shard_map/all_to_all | solution.py:299
  60.4 6.0 %collective-permute-start.15 = (f32[32,1792]{1,0:T(8,128)S(1)}, f32[32,1792]{1,0:T(8,128)S(1)}, u32[]{:S(2)}, u32[]{:S(2)}) collective-permute-start(f32[32,1792]{1,0:T(8,128)S(1)} %get-tuple-element.52), channel_id=1, source_target_pairs={{0,4},{4,0},{8,12},{12,8},{16,20},{20,16},{24,28},{28,24},{1,5},{5... | collective-permute-start | bytes 688136 | tf_op jit(solution)/shard_map/ppermute | solution.py:216
  67.1 11.6 %all-to-all-start.3 = ((f32[4,8,1792]{2,1,0:T(8,128)}), f32[4,8,1792]{2,1,0:T(8,128)S(1)}, u32[]{:S(2)}, u32[]{:S(2)}) async-start(f32[4,8,1792]{2,1,0:T(8,128)} %bitcast.6), calls=%async_computation.3 | async-start | bytes 458752 | tf_op jit(solution)/shard_map/all_to_all | solution.py:299

commit v7 on v5

--- a/solution.py
+++ b/solution.py
@@ -13,11 +13,12 @@
 BF16 = jnp.bfloat16
 NT = (((1,), (1,)), ((), ()))
 SPECS = {"v": pl.BlockSpec(memory_space=pltpu.VMEM), "a": pl.BlockSpec(memory_space=pl.ANY)}
-ORDER = "own0 before0 send0 own1 before1 send1 add0.1 own2 before2 send2 add0.2 add1.1 own3 before3 send3 add2.1 add1.2 add2.2 add3.1 sketch"
-WEIGHTS = {'add2.2': 1000000000, 'send1': 200000000, 'own1': 1000000000, 'own2': 0, 'before2': 2000000000, 'before1': 500000000, 'add0.2': 0, 'sketch': 500000000, 'add3.1': 200000000}
-SPLIT = 2
-DIRECT = 1
+ORDER = ('own0', 'before0', 'send0', 'own1', 'before1', 'send1', 'add0.1', 'own2', 'before2', 'send2', 'add1.1', 'own3', 'before3', 'send3', 'add2.1', 'add1.2', 'add0.2', 'add2.2', 'sketch', 'add3.1')
+REST_PARTS = 4
+WEIGHTS = {'add2.1': 500000000, 'F': 500000000, 'send1': 0, 'send0': 0, 'send3': 0, 'add2.2': 200000000, 'add0.2': 1000000000, 'own2': 500000000, 'before1': 500000000, 'add0.1': 500000000, 'before3': 2000000000, 'sketch': 500000000, 'send2': 0, 'add1.2': 200000000}
+SPLITS = (2, 2, 2, 2)
 GROUPS = ((0,), (1,), (2,), (3,))
+MODES = ('pairs', 'pairs', 'pairs', 'direct')
 
 
 def call(body, args, outs, kinds=None, after=(), scratch=(), results=0, weight=0):
@@ -74,11 +75,11 @@
     for b, copy in enumerate(copies):
         copy.wait()
         block = pl.ds(b * BLOCK, BLOCK)
-        out[:, block] = lax.dot_general(omega_t[...], held[block, :], NT, preferred_element_type=F32)
+        out[:, block] = lax.dot_general(omega_t[: out.shape[0], :], held[block, :], NT, preferred_element_type=F32)
 
 
 def first_half_body(n_row, pieces, delta, omega, held, omega_t, out, omega_v, sem, omega_sem):
-    k = out.shape[0]
+    k = omega_t.shape[0]
     fetch = pltpu.make_async_copy(omega, omega_v, omega_sem)
     fetch.start()
     copies = stream_half(delta, held, sem, False)
@@ -94,11 +95,23 @@
     sketch_half(omega_t, held, stream_half(delta, held, sem, True), out)
 
 
-def add_chunks_body(kept, received, *outs):
-    first = 0
-    for out in outs:
+def rest_half_body(omega_t, held, *outs):
+    rows = sum(out.shape[0] for out in outs)
+    later = omega_t[omega_t.shape[0] - rows :, :]
+    for b in range(held.shape[0] // BLOCK):
+        block = pl.ds(b * BLOCK, BLOCK)
+        found = lax.dot_general(later, held[block, :], NT, preferred_element_type=F32)
+        first = 0
+        for out in outs:
+            out[:, block] = found[first : first + out.shape[0]]
+            first += out.shape[0]
+
+
+def add_chunks_body(parts, kept, *refs):
+    received, first = joined(refs[:parts]), 0
+    for out in refs[parts:]:
         part = pl.ds(first, out.shape[0])
-        out[...] = kept[part, :] + received[part, :]
+        out[...] = kept[part, :] + received[first : first + out.shape[0]]
         first += out.shape[0]
 
 
@@ -159,26 +172,33 @@
     piece = outs[0].shape[0]
     place = owner_at(lax.axis_index("row") // 2, n_high)
     for flip, out in enumerate(outs):
-        part = pl.ds(pl.multiple_of(lax.bitwise_xor(place, flip) * piece, piece), piece)
-        out[...] = kept[part, :] + received[part, :]
-
-
-def final_corange_body(counts, *refs):
+        which = lax.bitwise_xor(place, flip)
+        if piece % 8 == 0:
+            part = pl.ds(pl.multiple_of(which * piece, piece), piece)
+            out[...] = kept[part, :] + received[part, :]
+            continue
+        found = jnp.zeros(out.shape, F32)
+        for i in range(n_high):
+            part = pl.ds(i * piece, piece)
+            found = jnp.where(which == i, kept[part, :] + received[part, :], found)
+        out[...] = found
+
+
+def final_corange_body(counts, rows, *refs):
     out = refs[-1]
     first, used = 0, 0
-    for count in counts:
+    for count, piece in zip(counts, rows):
         terms = refs[used : used + count]
-        piece = terms[0].shape[0]
-        out[pl.ds(first, piece), :] = functools.reduce(jnp.add, [term[...] for term in terms])
+        parts = [term[pl.ds(i, piece), :] for term in terms for i in range(0, term.shape[0], piece)]
+        out[pl.ds(first, piece), :] = functools.reduce(jnp.add, parts)
         first += piece
         used += count
 
 
-def final_sketch_body(n_row, pieces, *refs):
+def final_sketch_body(n_row, pieces, splits, *refs):
     out, done = refs[-2:]
-    n, rows = len(refs) // 2 - 1, refs[0].shape[1]
+    n, rows = sum(splits), refs[0].shape[1]
     parity = lax.rem(lax.axis_index("col"), 2)
-    per_part = n_row // SPLIT
     for side in range(2):
         parts = refs[side * n : (side + 1) * n]
         first = (parity if side == 0 else 1 - parity) * rows
@@ -186,10 +206,12 @@
             lanes = pl.ds(b * 128, 128)
             found = []
             for r in range(n_row):
-                place = owner_at(r, n_row)
-                for c, piece in enumerate(pieces):
-                    part = parts[c * SPLIT + place // per_part]
+                place, used = owner_at(r, n_row), 0
+                for piece, split in zip(pieces, splits):
+                    per_part = n_row // split
+                    part = parts[used + place // per_part]
                     found.append(part[pl.ds(place % per_part * piece, piece), lanes])
+                    used += split
             block = jnp.concatenate(found, axis=0)
             out[pl.ds(pl.multiple_of(first + b * 128, 128), 128), :] = block.T
     done[...] = jnp.zeros_like(done)
@@ -207,6 +229,7 @@
     pieces = [per_owner * part // sum(EIGHTHS) for part in EIGHTHS] if per_owner % 8 == 0 else [1] * per_owner
     widths = [piece * n_row for piece in pieces]
     n = len(pieces)
+    splits = SPLITS if len(SPLITS) == n else (2,) * n
     bits = [1 << i for i in range(n_row.bit_length() - 1)]
 
     in_hbm = pltpu.with_memory_space_constraint(delta, pltpu.HBM)
@@ -214,13 +237,21 @@
     held_other, omega_t, to_send = call(
         functools.partial(first_half_body, n_row, pieces),
         (in_hbm, pltpu.with_memory_space_constraint(omega, pltpu.HBM)),
-        [((half, d), BF16), ((k, d), BF16), ((k, half), F32)],
+        [((half, d), BF16), ((k, d), BF16), ((widths[0], half), F32)],
         "aa",
         scratch=[pltpu.VMEM((d, k), BF16), sems, pltpu.SemaphoreType.DMA],
     )
     received = swap(to_send, "col", n_col, 1)
-    held_own, kept = call(second_half_body, (in_hbm, omega_t), [((half, d), BF16), ((k, half), F32)], "av", scratch=[sems])
-    partial = call(add_chunks_body, (kept, received), [((width, half), F32) for width in widths])
+    outs = [((half, d), BF16), ((widths[0], half), F32)]
+    held_own, kept = call(second_half_body, (in_hbm, omega_t), outs, "av", (to_send,), [sems])
+    partial = call(add_body, (kept, received), [((widths[0], half), F32)])
+    rest = k - widths[0]
+    outs = [((rest // REST_PARTS, half), F32)] * REST_PARTS
+    to_send = call(rest_half_body, (omega_t, held_other), outs, after=partial)
+    received = [swap(x, "col", n_col, 1) for x in to_send]
+    kept = call(rest_half_body, (omega_t, held_own), [((rest, half), F32)], after=to_send[:1])
+    outs = [((width, half), F32) for width in widths[1:]]
+    partial += call(functools.partial(add_chunks_body, REST_PARTS), (*kept, *received), outs)
     bit = 2
     while bit < n_col // 2:
         moved = [swap(x, "col", n_col, bit) for x in partial]
@@ -231,22 +262,23 @@
     owns, others, befores, pending = {}, {}, {}, {}
     sketch = None
     last = ()
-    groups = GROUPS if n == 4 else tuple((c,) for c in range(n))
-    direct = [len(bits) == 3 and len(group) == 1 and pieces[group[0]] % 8 == 0 and g >= len(groups) - DIRECT for g, group in enumerate(groups)]
-    steps = ORDER.split() if len(bits) == 3 and n == 4 else []
+    planned = n == 4 and len(bits) == 3
+    groups = GROUPS if planned else tuple((c,) for c in range(n))
+    modes = MODES if planned else ("pairs",) * n
+    steps = ORDER if planned else ()
     if not steps:
         found = []
         for c in range(n):
             found += [(10 * c, f"own{c}"), (10 * c + 1, f"before{c}"), (10 * c + 2, f"send{c}")]
         for g, group in enumerate(groups):
-            found += [(10 * group[-1] + 9.5 + 10 * s, f"add{g}.{s}") for s in range(1, 2 if direct[g] else len(bits))]
+            stages = 2 if modes[g] == "direct" else len(bits)
+            found += [(10 * group[-1] + 9.5 + 10 * s, f"add{g}.{s}") for s in range(1, stages)]
         steps = [step for _, step in sorted(found)] + ["sketch"]
-
     for step in steps:
         weight = WEIGHTS.get(step, 0)
         if step.startswith("own"):
             c = int(step[3:])
-            outs = [((widths[c] // SPLIT, half), F32)] * SPLIT
+            outs = [((widths[c] // splits[c], half), F32)] * splits[c]
             owns[c] = call(add_body, (partial[c], moved[c]), outs, after=last, weight=weight)
             others[c] = [swap(x, "col", n_col, 1) for x in owns[c]]
             last = (owns[c][0],)
@@ -265,7 +297,7 @@
         elif step.startswith("add"):
             g, s = (int(x) for x in step[3:].split("."))
             group = groups[g]
-            if direct[g]:
+            if modes[g] == "direct":
                 outs = [((pieces[group[0]], d), F32)] * (n_row // 2)
                 body = functools.partial(add_spread_body, n_row // 2)
                 own, *sends = call(body, pending[group], outs, after=last, weight=weight)
@@ -283,26 +315,27 @@
             last = (keep,)
         else:
             parts = [[x for found in halves.values() for x in found] for halves in (owns, others)]
-            sketch, done = finish_sketch(n_row, k, pieces, *parts, last)
+            sketch, done = finish_sketch(n_row, k, pieces, splits, *parts, last)
             last = (done,)
     flat = [x for group in groups for x in pending[group]]
     if per_owner % 8 == 0:
-        body = functools.partial(final_corange_body, [len(pending[group]) for group in groups])
+        body = functools.partial(final_corange_body, [len(pending[group]) for group in groups], [sum(pieces[c] for c in group) for group in groups])
         corange = call(body, flat, [((per_owner, d), F32)], after=last, results=1, weight=WEIGHTS.get("F", 0))[0]
     else:
         corange = jnp.concatenate([functools.reduce(jnp.add, pending[group]) for group in groups], axis=0)
     return sketch, corange.T
 
 
-def finish_sketch(n_row, k, pieces, owns, others, after):
+def finish_sketch(n_row, k, pieces, splits, owns, others, after):
     half = owns[0].shape[1]
     if k // n_row % 8 == 0:
-        body = functools.partial(final_sketch_body, n_row, pieces)
+        body = functools.partial(final_sketch_body, n_row, pieces, splits)
         return call(body, (*owns, *others), [((2 * half, k), F32), ((8, 128), F32)], after=after, results=1)
     places = jnp.array([owner_at(r, n_row) for r in range(n_row)])
 
     def columns(parts):
-        parts = [jnp.concatenate(parts[c : c + SPLIT], axis=0) for c in range(0, len(parts), SPLIT)]
+        starts = [sum(splits[:c]) for c in range(len(splits))]
+        parts = [jnp.concatenate(parts[start : start + split], axis=0) for start, split in zip(starts, splits)]
         found = [part.reshape(n_row, piece, half)[places] for part, piece in zip(parts, pieces)]
         return jnp.concatenate(found, axis=1).reshape(k, half).T
 

time: 59.6 us -> 60.1 us (level)
  Pallas kernels: 15.2 us -> 17.9 us
  waiting for transfers between devices: 12.8 us -> 11.6 us
  starting transfers between devices: 30.5 us -> 29.5 us
    pallas_call x24 -> x27, Pallas kernels: 15.2 us -> 17.9 us  [call(): pl.pallas_call(run, out_shape=[pltpu.VMEM(*o) if i >= results else jax.Sh...]
    ppermute x26 -> x30, waiting for transfers between devices: 12.8 us -> 11.6 us  [swap(): return lax.ppermute(x, axis, [(i, i ^ bit) for i in range(size)])]
    ppermute x26 -> x30, starting transfers between devices: 30.5 us -> 29.5 us  [swap(): return lax.ppermute(x, axis, [(i, i ^ bit) for i in range(size)])]
  transfers between devices with their start and end apart: 26 -> 30, of which waited for: 9 -> 11; matrix products, arithmetic and copies ran while one was open for 0% -> 0% of each run, Pallas kernels for 19% -> 23%
where the time goes in v7:
time: 60.1 us; the launch traced here: 60 us
  starting transfers between devices  29.5 us (49%)
  Pallas kernels  17.9 us (30%)
  waiting for transfers between devices  11.6 us (19%)
  between operations  0.9 us (1%)
    ppermute x30, starting transfers between devices, swap(): return lax.ppermute(x, axis, [(i, i ^ bit) for i in range(size)])  29.5 us
    pallas_call x27, Pallas kernels, call(): pl.pallas_call(run, out_shape=[pltpu.VMEM(*o) if i >= results else jax.Sh...  17.9 us
    ppermute x30, waiting for transfers between devices, swap(): return lax.ppermute(x, axis, [(i, i ^ bit) for i in range(size)])  11.6 us
  transfers between devices with their start and end apart: 30, of which 11 were waited for; matrix products, arithmetic and copies ran while one was open for 0% of the time, Pallas kernels for 23%

profile of v7, /device:TPU:0, one launch (start us, length us, event | category | flops | bytes accessed | tf_op | source)
XLA Modules:
  0.0 60.0 jit_solution(1064646744190329807)
XLA Ops:
  0.6 3.2 %shard_map.41 = (bf16[1024,1792]{1,0:T(8,128)(2,1)S(1)}, bf16[256,1792]{1,0:T(8,128)(2,1)S(1)}, f32[64,1024]{1,0:T(8,128)S(1)}) custom-call(bf16[2048,1792]{1,0:T(8,128)(2,1)} %refs_0_.3, bf16[1792,256]{1,0:T(8,128)(2,1)} %refs_1_.1), custom_call_target="tpu_custom_call" | custom-call | tf_op jit(solution)/shard_map/pallas_call | solution.py:31
  4.4 2.9 %shard_map.42 = (bf16[1024,1792]{1,0:T(8,128)(2,1)S(1)}, f32[64,1024]{1,0:T(8,128)S(1)}) custom-call(bf16[2048,1792]{1,0:T(8,128)(2,1)} %refs_0_.3, bf16[256,1792]{1,0:T(8,128)(2,1)S(1)} %get-tuple-element.48.refs_1_.refs_0_, f32[64,1024]{1,0:T(8,128)S(1)} %get-tuple-element.49.refs_2_), custom_call_target="tpu_custom_call" | custom-call | tf_op jit(solution)/shard_map/pallas_call | solution.py:31
  7.3 2.6 %collective-permute-start.1 = (f32[64,1024]{1,0:T(8,128)S(1)}, f32[64,1024]{1,0:T(8,128)S(1)}, u32[]{:S(2)}, u32[]{:S(2)}) collective-permute-start(f32[64,1024]{1,0:T(8,128)S(1)} %shard_map.43.refs_0_.refs_2_), channel_id=1, source_target_pairs={{0,2},{1,3},{2,0},{3,1},{4,6},{5,7},{6,4},{7,5},{8,10},{9,11},{10,... | collective-permute-start | bytes 786440 | tf_op jit(solution)/shard_map/ppermute | solution.py:221
  9.9 1.3 %shard_map.45 = (f32[48,1024]{1,0:T(8,128)S(1)}, f32[48,1024]{1,0:T(8,128)S(1)}, f32[48,1024]{1,0:T(8,128)S(1)}, f32[48,1024]{1,0:T(8,128)S(1)}) custom-call(bf16[256,1792]{1,0:T(8,128)(2,1)S(1)} %get-tuple-element.48.refs_1_.refs_0_, bf16[1024,1792]{1,0:T(8,128)(2,1)S(1)} %get-tuple-element.54.refs_1_.refs_2_, f32[64,1024]{1,0:T(8,128)S(1)} %shard_map.43.refs_0_.refs_2_), custom_call_target="tpu_custom_call" | custom-call | tf_op jit(solution)/shard_map/pallas_call | solution.py:31
  12.3 1.3 %shard_map.46.refs_0_ = f32[192,1024]{1,0:T(8,128)S(1)} custom-call(bf16[256,1792]{1,0:T(8,128)(2,1)S(1)} %get-tuple-element.48.refs_1_.refs_0_, bf16[1024,1792]{1,0:T(8,128)(2,1)S(1)} %get-tuple-element.53.refs_1_.refs_2_, f32[48,1024]{1,0:T(8,128)S(1)} %get-tuple-element.55.refs_2_), custom_call_target="tpu_custom_call" | custom-call | tf_op jit(solution)/shard_map/pallas_call | solution.py:31
  13.9 3.0 %collective-permute-done.1.refs_1_ = f32[64,1024]{1,0:T(8,128)S(1)} collective-permute-done((f32[64,1024]{1,0:T(8,128)S(1)}, f32[64,1024]{1,0:T(8,128)S(1)}, u32[]{:S(2)}, u32[]{:S(2)}) %collective-permute-start.1) | collective-permute-done | bytes 262176 | tf_op jit(solution)/shard_map/ppermute | solution.py:221
  17.6 0.7 %shard_map.48.refs_3_.refs_4_ = f32[64,1792]{1,0:T(8,128)S(1)} custom-call(f32[32,1024]{1,0:T(8,128)S(1)} %get-tuple-element.51.refs_0_.refs_3_, f32[32,1024]{1,0:T(8,128)S(1)} %get-tuple-element.52.refs_1_, bf16[1024,1792]{1,0:T(8,128)(2,1)S(1)} %get-tuple-element.53.refs_1_.refs_2_, f32[32,1024]{1,0:T(8,128)S(1)} %get-tuple-element.51.refs_0_.refs_3_), custom_call_target="tpu_custom_call" | custom-call | tf_op jit(solution)/shard_map/pallas_call | solution.py:31
  18.6 0.8 %shard_map.49 = (f32[32,1792]{1,0:T(8,128)S(1)}, f32[32,1792]{1,0:T(8,128)S(1)}) custom-call(f32[32,1024]{1,0:T(8,128)S(1)} %collective-permute-done.7.refs_0_.refs_8_, f32[32,1024]{1,0:T(8,128)S(1)} %collective-permute-done.8.refs_1_.refs_9_, bf16[1024,1792]{1,0:T(8,128)(2,1)S(1)} %get-tuple-element.54.refs_1_.refs_2_, ...), custom_call_target="tpu_custom_call" | custom-call | tf_op jit(solution)/shard_map/pallas_call | solution.py:31
  19.4 2.1 %collective-permute-start.10 = (f32[32,1792]{1,0:T(8,128)S(1)}, f32[32,1792]{1,0:T(8,128)S(1)}, u32[]{:S(2)}, u32[]{:S(2)}) collective-permute-start(f32[32,1792]{1,0:T(8,128)S(1)} %get-tuple-element.64), channel_id=1, source_target_pairs={{0,4},{4,0},{8,12},{12,8},{16,20},{20,16},{24,28},{28,24},{1,5},{5... | collective-permute-start | bytes 688136 | tf_op jit(solution)/shard_map/ppermute | solution.py:221
  21.5 1.5 %collective-permute-start.9 = (f32[64,1024]{1,0:T(8,128)S(1)}, f32[64,1024]{1,0:T(8,128)S(1)}, u32[]{:S(2)}, u32[]{:S(2)}) collective-permute-start(f32[64,1024]{1,0:T(8,128)S(1)} %get-tuple-element.63.refs_0_), channel_id=1, source_target_pairs={{0,2},{1,3},{2,0},{3,1},{4,6},{5,7},{6,4},{7,5},{8,10},{9,11},{10,... | collective-permute-start | bytes 786440 | tf_op jit(solution)/shard_map/ppermute | solution.py:221
  23.6 1.2 %collective-permute-start.13 = (f32[64,1024]{1,0:T(8,128)S(1)}, f32[64,1024]{1,0:T(8,128)S(1)}, u32[]{:S(2)}, u32[]{:S(2)}) collective-permute-start(f32[64,1024]{1,0:T(8,128)S(1)} %get-tuple-element.69.refs_0_), channel_id=1, source_target_pairs={{0,2},{1,3},{2,0},{3,1},{4,6},{5,7},{6,4},{7,5},{8,10},{9,11},{10,... | collective-permute-start | bytes 786440 | tf_op jit(solution)/shard_map/ppermute | solution.py:221
  24.8 0.7 %shard_map.51.refs_3_.refs_4_ = f32[64,1792]{1,0:T(8,128)S(1)} custom-call(f32[32,1024]{1,0:T(8,128)S(1)} %get-tuple-element.61.refs_0_.refs_3_.refs_2_, f32[32,1024]{1,0:T(8,128)S(1)} %get-tuple-element.62.refs_1_.refs_3_, bf16[1024,1792]{1,0:T(8,128)(2,1)S(1)} %get-tuple-element.53.refs_1_.refs_2_, f32[32,1024]{1,0:T(8,128)S(1)} %get-tuple-element.61.refs_0_.refs_3_.refs_2_), custom_call_target="tpu_custom_call" | custom-call | flops 500000000 | tf_op jit(solution)/shard_map/pallas_call | solution.py:31
  25.6 0.8 %shard_map.52 = (f32[32,1792]{1,0:T(8,128)S(1)}, f32[32,1792]{1,0:T(8,128)S(1)}) custom-call(f32[32,1024]{1,0:T(8,128)S(1)} %collective-permute-done.11.refs_0_.refs_10_, f32[32,1024]{1,0:T(8,128)S(1)} %collective-permute-done.12.refs_1_.refs_11_, bf16[1024,1792]{1,0:T(8,128)(2,1)S(1)} %get-tuple-element.54.refs_1_.refs_2_, ...), custom_call_target="tpu_custom_call" | custom-call | tf_op jit(solution)/shard_map/pallas_call | solution.py:31
  26.4 1.6 %collective-permute-start.14 = (f32[32,1792]{1,0:T(8,128)S(1)}, f32[32,1792]{1,0:T(8,128)S(1)}, u32[]{:S(2)}, u32[]{:S(2)}) collective-permute-start(f32[32,1792]{1,0:T(8,128)S(1)} %get-tuple-element.70), channel_id=1, source_target_pairs={{0,4},{4,0},{8,12},{12,8},{16,20},{20,16},{24,28},{28,24},{1,5},{5... | collective-permute-start | bytes 688136 | tf_op jit(solution)/shard_map/ppermute | solution.py:221
  28.0 2.7 %collective-permute-done.9.refs_1_ = f32[64,1024]{1,0:T(8,128)S(1)} collective-permute-done((f32[64,1024]{1,0:T(8,128)S(1)}, f32[64,1024]{1,0:T(8,128)S(1)}, u32[]{:S(2)}, u32[]{:S(2)}) %collective-permute-start.9) | collective-permute-done | bytes 262176 | tf_op jit(solution)/shard_map/ppermute | solution.py:221
  31.3 0.7 %shard_map.55.refs_3_.refs_4_ = f32[64,1792]{1,0:T(8,128)S(1)} custom-call(f32[32,1024]{1,0:T(8,128)S(1)} %get-tuple-element.67.refs_0_.refs_3_.refs_4_, f32[32,1024]{1,0:T(8,128)S(1)} %get-tuple-element.68.refs_1_.refs_5_, bf16[1024,1792]{1,0:T(8,128)(2,1)S(1)} %get-tuple-element.53.refs_1_.refs_2_, f32[32,1024]{1,0:T(8,128)S(1)} %get-tuple-element.67.refs_0_.refs_3_.refs_4_), custom_call_target="tpu_custom_call" | custom-call | tf_op jit(solution)/shard_map/pallas_call | solution.py:31
  32.3 0.8 %shard_map.56 = (f32[32,1792]{1,0:T(8,128)S(1)}, f32[32,1792]{1,0:T(8,128)S(1)}) custom-call(f32[32,1024]{1,0:T(8,128)S(1)} %collective-permute-done.15.refs_0_.refs_12_, f32[32,1024]{1,0:T(8,128)S(1)} %collective-permute-done.16.refs_1_.refs_13_, bf16[1024,1792]{1,0:T(8,128)(2,1)S(1)} %get-tuple-element.54.refs_1_.refs_2_, ...), custom_call_target="tpu_custom_call" | custom-call | tf_op jit(solution)/shard_map/pallas_call | solution.py:31
  33.2 2.0 %collective-permute-start.21 = (f32[16,1792]{1,0:T(8,128)S(1)}, f32[16,1792]{1,0:T(8,128)S(1)}, u32[]{:S(2)}, u32[]{:S(2)}) collective-permute-start(f32[16,1792]{1,0:T(8,128)S(1)} %get-tuple-element.79), channel_id=1, source_target_pairs={{0,8},{4,12},{8,0},{12,4},{16,24},{20,28},{24,16},{28,20},{1,9},{5... | collective-permute-start | bytes 344072 | tf_op jit(solution)/shard_map/ppermute | solution.py:221
  36.0 1.6 %collective-permute-start.22 = (f32[16,1792]{1,0:T(8,128)S(1)}, f32[16,1792]{1,0:T(8,128)S(1)}, u32[]{:S(2)}, u32[]{:S(2)}) collective-permute-start(f32[16,1792]{1,0:T(8,128)S(1)} %get-tuple-element.80), channel_id=1, source_target_pairs={{0,8},{4,12},{8,0},{12,4},{16,24},{20,28},{24,16},{28,20},{1,9},{5... | collective-permute-start | bytes 344072 | tf_op jit(solution)/shard_map/ppermute | solution.py:221
  37.5 0.7 %shard_map.59.refs_3_.refs_4_ = f32[64,1792]{1,0:T(8,128)S(1)} custom-call(f32[32,1024]{1,0:T(8,128)S(1)} %get-tuple-element.73.refs_0_.refs_3_.refs_6_, f32[32,1024]{1,0:T(8,128)S(1)} %get-tuple-element.74.refs_1_.refs_7_, bf16[1024,1792]{1,0:T(8,128)(2,1)S(1)} %get-tuple-element.53.refs_1_.refs_2_, f32[32,1024]{1,0:T(8,128)S(1)} %get-tuple-element.73.refs_0_.refs_3_.refs_6_), custom_call_target="tpu_custom_call" | custom-call | flops 2000000000 | tf_op jit(solution)/shard_map/pallas_call | solution.py:31
  38.3 0.8 %shard_map.60 = (f32[32,1792]{1,0:T(8,128)S(1)}, f32[32,1792]{1,0:T(8,128)S(1)}) custom-call(f32[32,1024]{1,0:T(8,128)S(1)} %collective-permute-done.17.refs_0_.refs_14_, f32[32,1024]{1,0:T(8,128)S(1)} %collective-permute-done.18.refs_1_.refs_15_, bf16[1024,1792]{1,0:T(8,128)(2,1)S(1)} %get-tuple-element.54.refs_1_.refs_2_, ...), custom_call_target="tpu_custom_call" | custom-call | tf_op jit(solution)/shard_map/pallas_call | solution.py:31
  39.7 1.3 %collective-permute-done.19.refs_1_ = f32[32,1792]{1,0:T(8,128)S(1)} collective-permute-done((f32[32,1792]{1,0:T(8,128)S(1)}, f32[32,1792]{1,0:T(8,128)S(1)}, u32[]{:S(2)}, u32[]{:S(2)}) %collective-permute-start.19) | collective-permute-done | bytes 229408 | tf_op jit(solution)/shard_map/ppermute | solution.py:221
  41.0 1.8 %collective-permute-start.20 = (f32[16,1792]{1,0:T(8,128)S(1)}, f32[16,1792]{1,0:T(8,128)S(1)}, u32[]{:S(2)}, u32[]{:S(2)}) collective-permute-start(f32[16,1792]{1,0:T(8,128)S(1)} %get-tuple-element.78), channel_id=1, source_target_pairs={{0,8},{4,12},{8,0},{12,4},{16,24},{20,28},{24,16},{28,20},{1,9},{5... | collective-permute-start | bytes 344072 | tf_op jit(solution)/shard_map/ppermute | solution.py:221
  42.9 2.7 %collective-permute-start.23 = (f32[8,1792]{1,0:T(8,128)S(1)}, f32[8,1792]{1,0:T(8,128)S(1)}, u32[]{:S(2)}, u32[]{:S(2)}) collective-permute-start(f32[8,1792]{1,0:T(8,128)S(1)} %get-tuple-element.85), channel_id=1, source_target_pairs={{0,16},{4,20},{8,24},{12,28},{16,0},{20,4},{24,8},{28,12},{1,17},{... | collective-permute-start | bytes 172040 | tf_op jit(solution)/shard_map/ppermute | solution.py:221
  45.8 0.6 %collective-permute-done.20.refs_1_ = f32[16,1792]{1,0:T(8,128)S(1)} collective-permute-done((f32[16,1792]{1,0:T(8,128)S(1)}, f32[16,1792]{1,0:T(8,128)S(1)}, u32[]{:S(2)}, u32[]{:S(2)}) %collective-permute-start.20) | collective-permute-done | bytes 114720 | tf_op jit(solution)/shard_map/ppermute | solution.py:221
  46.5 3.0 %collective-permute-start.25 = (f32[8,1792]{1,0:T(8,128)S(1)}, f32[8,1792]{1,0:T(8,128)S(1)}, u32[]{:S(2)}, u32[]{:S(2)}) collective-permute-start(f32[8,1792]{1,0:T(8,128)S(1)} %get-tuple-element.87), channel_id=1, source_target_pairs={{0,16},{4,20},{8,24},{12,28},{16,0},{20,4},{24,8},{28,12},{1,17},{... | collective-permute-start | bytes 172040 | tf_op jit(solution)/shard_map/ppermute | solution.py:221
  49.5 1.9 %shard_map.65 = (f32[2048,256]{1,0:T(8,128)}, f32[8,128]{1,0:T(8,128)S(1)}) custom-call(f32[32,1024]{1,0:T(8,128)S(1)} %get-tuple-element.51.refs_0_.refs_3_, f32[32,1024]{1,0:T(8,128)S(1)} %get-tuple-element.52.refs_1_, f32[32,1024]{1,0:T(8,128)S(1)} %get-tuple-element.61.refs_0_.refs_3_.refs_2_, f32[32,1024]{1,0:T(8,128)S(1)} %get-tuple-element.62.refs_1_.refs_3_, ...), custom_call_target="tpu_custom_call" | custom-call | tf_op jit(solution)/shard_map/pallas_call | solution.py:31
  51.5 1.7 %collective-permute-start.28 = (f32[8,1792]{1,0:T(8,128)S(1)}, f32[8,1792]{1,0:T(8,128)S(1)}, u32[]{:S(2)}, u32[]{:S(2)}) collective-permute-start(f32[8,1792]{1,0:T(8,128)S(1)} %get-tuple-element.92), channel_id=1, source_target_pairs={{0,8},{4,12},{8,0},{12,4},{16,24},{20,28},{24,16},{28,20},{1,9},{5... | collective-permute-start | bytes 172040 | tf_op jit(solution)/shard_map/ppermute | solution.py:221
  53.2 2.7 %collective-permute-start.29 = (f32[8,1792]{1,0:T(8,128)S(1)}, f32[8,1792]{1,0:T(8,128)S(1)}, u32[]{:S(2)}, u32[]{:S(2)}) collective-permute-start(f32[8,1792]{1,0:T(8,128)S(1)} %get-tuple-element.93), channel_id=1, source_target_pairs={{0,24},{4,28},{8,16},{12,20},{16,8},{20,12},{24,0},{28,4},{1,25},{... | collective-permute-start | bytes 172040 | tf_op jit(solution)/shard_map/ppermute | solution.py:221
  55.9 0.8 %collective-permute-done.27.refs_7_ = f32[8,1792]{1,0:T(8,128)S(1)} collective-permute-done((f32[8,1792]{1,0:T(8,128)S(1)}, f32[8,1792]{1,0:T(8,128)S(1)}, u32[]{:S(2)}, u32[]{:S(2)}) %collective-permute-start.27) | collective-permute-done | bytes 57376 | tf_op jit(solution)/shard_map/ppermute | solution.py:221
  56.7 2.5 %collective-permute-done.29.refs_9_ = f32[8,1792]{1,0:T(8,128)S(1)} collective-permute-done((f32[8,1792]{1,0:T(8,128)S(1)}, f32[8,1792]{1,0:T(8,128)S(1)}, u32[]{:S(2)}, u32[]{:S(2)}) %collective-permute-start.29) | collective-permute-done | bytes 57376 | tf_op jit(solution)/shard_map/ppermute | solution.py:221
  59.2 0.7 %shard_map.67 = f32[32,1792]{1,0:T(8,128)} custom-call(f32[8,1792]{1,0:T(8,128)S(1)} %get-tuple-element.82.refs_2_.refs_0_, f32[8,1792]{1,0:T(8,128)S(1)} %collective-permute-done.23.refs_1_, f32[8,1792]{1,0:T(8,128)S(1)} %get-tuple-element.81.refs_2_, f32[8,1792]{1,0:T(8,128)S(1)} %collective-permute-done.24.refs_3_, ...), custom_call_target="tpu_custom_call" | custom-call | flops 500000000 | tf_op jit(solution)/shard_map/pallas_call | solution.py:31
  (55 shorter events, 6.2 us)
Async XLA Ops:
  3.9 3.4 %collective-permute-start = (f32[64,1024]{1,0:T(8,128)S(1)}, f32[64,1024]{1,0:T(8,128)S(1)}, u32[]{:S(2)}, u32[]{:S(2)}) collective-permute-start(f32[64,1024]{1,0:T(8,128)S(1)} %get-tuple-element.49.refs_2_), channel_id=1, source_target_pairs={{0,1},{1,0},{2,3},{3,2},{4,5},{5,4},{6,7},{7,6},{8,9},{9,8},{10,11... | collective-permute-start | bytes 786440 | tf_op jit(solution)/shard_map/ppermute | solution.py:221
  7.3 9.7 %collective-permute-start.1 = (f32[64,1024]{1,0:T(8,128)S(1)}, f32[64,1024]{1,0:T(8,128)S(1)}, u32[]{:S(2)}, u32[]{:S(2)}) collective-permute-start(f32[64,1024]{1,0:T(8,128)S(1)} %shard_map.43.refs_0_.refs_2_), channel_id=1, source_target_pairs={{0,2},{1,3},{2,0},{3,1},{4,6},{5,7},{6,4},{7,5},{8,10},{9,11},{10,... | collective-permute-start | bytes 786440 | tf_op jit(solution)/shard_map/ppermute | solution.py:221
  11.2 2.4 %collective-permute-start.2 = (f32[48,1024]{1,0:T(8,128)S(1)}, f32[48,1024]{1,0:T(8,128)S(1)}, u32[]{:S(2)}, u32[]{:S(2)}) collective-permute-start(f32[48,1024]{1,0:T(8,128)S(1)} %get-tuple-element.55.refs_2_), channel_id=1, source_target_pairs={{0,1},{1,0},{2,3},{3,2},{4,5},{5,4},{6,7},{7,6},{8,9},{9,8},{10,11... | collective-permute-start | bytes 589832 | tf_op jit(solution)/shard_map/ppermute | solution.py:221
  11.5 2.2 %collective-permute-start.3 = (f32[48,1024]{1,0:T(8,128)S(1)}, f32[48,1024]{1,0:T(8,128)S(1)}, u32[]{:S(2)}, u32[]{:S(2)}) collective-permute-start(f32[48,1024]{1,0:T(8,128)S(1)} %get-tuple-element.56), channel_id=1, source_target_pairs={{0,1},{1,0},{2,3},{3,2},{4,5},{5,4},{6,7},{7,6},{8,9},{9,8},{10,11... | collective-permute-start | bytes 589832 | tf_op jit(solution)/shard_map/ppermute | solution.py:221
  11.8 1.9 %collective-permute-start.4 = (f32[48,1024]{1,0:T(8,128)S(1)}, f32[48,1024]{1,0:T(8,128)S(1)}, u32[]{:S(2)}, u32[]{:S(2)}) collective-permute-start(f32[48,1024]{1,0:T(8,128)S(1)} %get-tuple-element.57), channel_id=1, source_target_pairs={{0,1},{1,0},{2,3},{3,2},{4,5},{5,4},{6,7},{7,6},{8,9},{9,8},{10,11... | collective-permute-start | bytes 589832 | tf_op jit(solution)/shard_map/ppermute | solution.py:221
  12.0 1.7 %collective-permute-start.5 = (f32[48,1024]{1,0:T(8,128)S(1)}, f32[48,1024]{1,0:T(8,128)S(1)}, u32[]{:S(2)}, u32[]{:S(2)}) collective-permute-start(f32[48,1024]{1,0:T(8,128)S(1)} %get-tuple-element.58), channel_id=1, source_target_pairs={{0,1},{1,0},{2,3},{3,2},{4,5},{5,4},{6,7},{7,6},{8,9},{9,8},{10,11... | collective-permute-start | bytes 589832 | tf_op jit(solution)/shard_map/ppermute | solution.py:221
  13.8 9.2 %collective-permute-start.6 = (f32[64,1024]{1,0:T(8,128)S(1)}, f32[64,1024]{1,0:T(8,128)S(1)}, u32[]{:S(2)}, u32[]{:S(2)}) collective-permute-start(f32[64,1024]{1,0:T(8,128)S(1)} %get-tuple-element.59.refs_0_), channel_id=1, source_target_pairs={{0,2},{1,3},{2,0},{3,1},{4,6},{5,7},{6,4},{7,5},{8,10},{9,11},{10,... | collective-permute-start | bytes 786440 | tf_op jit(solution)/shard_map/ppermute | solution.py:221
  17.0 1.4 %collective-permute-start.7 = (f32[32,1024]{1,0:T(8,128)S(1)}, f32[32,1024]{1,0:T(8,128)S(1)}, u32[]{:S(2)}, u32[]{:S(2)}) collective-permute-start(f32[32,1024]{1,0:T(8,128)S(1)} %get-tuple-element.51.refs_0_.refs_3_), channel_id=1, source_target_pairs={{0,1},{1,0},{2,3},{3,2},{4,5},{5,4},{6,7},{7,6},{8,9},{9,8},{10,11... | collective-permute-start | bytes 393224 | tf_op jit(solution)/shard_map/ppermute | solution.py:221
  17.1 1.5 %collective-permute-start.8 = (f32[32,1024]{1,0:T(8,128)S(1)}, f32[32,1024]{1,0:T(8,128)S(1)}, u32[]{:S(2)}, u32[]{:S(2)}) collective-permute-start(f32[32,1024]{1,0:T(8,128)S(1)} %get-tuple-element.52.refs_1_), channel_id=1, source_target_pairs={{0,1},{1,0},{2,3},{3,2},{4,5},{5,4},{6,7},{7,6},{8,9},{9,8},{10,11... | collective-permute-start | bytes 393224 | tf_op jit(solution)/shard_map/ppermute | solution.py:221
  19.4 8.6 %collective-permute-start.10 = (f32[32,1792]{1,0:T(8,128)S(1)}, f32[32,1792]{1,0:T(8,128)S(1)}, u32[]{:S(2)}, u32[]{:S(2)}) collective-permute-start(f32[32,1792]{1,0:T(8,128)S(1)} %get-tuple-element.64), channel_id=1, source_target_pairs={{0,4},{4,0},{8,12},{12,8},{16,20},{20,16},{24,28},{28,24},{1,5},{5... | collective-permute-start | bytes 688136 | tf_op jit(solution)/shard_map/ppermute | solution.py:221
  21.5 9.2 %collective-permute-start.9 = (f32[64,1024]{1,0:T(8,128)S(1)}, f32[64,1024]{1,0:T(8,128)S(1)}, u32[]{:S(2)}, u32[]{:S(2)}) collective-permute-start(f32[64,1024]{1,0:T(8,128)S(1)} %get-tuple-element.63.refs_0_), channel_id=1, source_target_pairs={{0,2},{1,3},{2,0},{3,1},{4,6},{5,7},{6,4},{7,5},{8,10},{9,11},{10,... | collective-permute-start | bytes 786440 | tf_op jit(solution)/shard_map/ppermute | solution.py:221
  23.0 2.5 %collective-permute-start.11 = (f32[32,1024]{1,0:T(8,128)S(1)}, f32[32,1024]{1,0:T(8,128)S(1)}, u32[]{:S(2)}, u32[]{:S(2)}) collective-permute-start(f32[32,1024]{1,0:T(8,128)S(1)} %get-tuple-element.61.refs_0_.refs_3_.refs_2_), channel_id=1, source_target_pairs={{0,1},{1,0},{2,3},{3,2},{4,5},{5,4},{6,7},{7,6},{8,9},{9,8},{10,11... | collective-permute-start | bytes 393224 | tf_op jit(solution)/shard_map/ppermute | solution.py:221
  23.1 2.5 %collective-permute-start.12 = (f32[32,1024]{1,0:T(8,128)S(1)}, f32[32,1024]{1,0:T(8,128)S(1)}, u32[]{:S(2)}, u32[]{:S(2)}) collective-permute-start(f32[32,1024]{1,0:T(8,128)S(1)} %get-tuple-element.62.refs_1_.refs_3_), channel_id=1, source_target_pairs={{0,1},{1,0},{2,3},{3,2},{4,5},{5,4},{6,7},{7,6},{8,9},{9,8},{10,11... | collective-permute-start | bytes 393224 | tf_op jit(solution)/shard_map/ppermute | solution.py:221
  23.6 11.8 %collective-permute-start.13 = (f32[64,1024]{1,0:T(8,128)S(1)}, f32[64,1024]{1,0:T(8,128)S(1)}, u32[]{:S(2)}, u32[]{:S(2)}) collective-permute-start(f32[64,1024]{1,0:T(8,128)S(1)} %get-tuple-element.69.refs_0_), channel_id=1, source_target_pairs={{0,2},{1,3},{2,0},{3,1},{4,6},{5,7},{6,4},{7,5},{8,10},{9,11},{10,... | collective-permute-start | bytes 786440 | tf_op jit(solution)/shard_map/ppermute | solution.py:221
  26.4 8.9 %collective-permute-start.14 = (f32[32,1792]{1,0:T(8,128)S(1)}, f32[32,1792]{1,0:T(8,128)S(1)}, u32[]{:S(2)}, u32[]{:S(2)}) collective-permute-start(f32[32,1792]{1,0:T(8,128)S(1)} %get-tuple-element.70), channel_id=1, source_target_pairs={{0,4},{4,0},{8,12},{12,8},{16,20},{20,16},{24,28},{28,24},{1,5},{5... | collective-permute-start | bytes 688136 | tf_op jit(solution)/shard_map/ppermute | solution.py:221
  30.7 1.4 %collective-permute-start.15 = (f32[32,1024]{1,0:T(8,128)S(1)}, f32[32,1024]{1,0:T(8,128)S(1)}, u32[]{:S(2)}, u32[]{:S(2)}) collective-permute-start(f32[32,1024]{1,0:T(8,128)S(1)} %get-tuple-element.67.refs_0_.refs_3_.refs_4_), channel_id=1, source_target_pairs={{0,1},{1,0},{2,3},{3,2},{4,5},{5,4},{6,7},{7,6},{8,9},{9,8},{10,11... | collective-permute-start | bytes 393224 | tf_op jit(solution)/shard_map/ppermute | solution.py:221
  30.8 1.5 %collective-permute-start.16 = (f32[32,1024]{1,0:T(8,128)S(1)}, f32[32,1024]{1,0:T(8,128)S(1)}, u32[]{:S(2)}, u32[]{:S(2)}) collective-permute-start(f32[32,1024]{1,0:T(8,128)S(1)} %get-tuple-element.68.refs_1_.refs_5_), channel_id=1, source_target_pairs={{0,1},{1,0},{2,3},{3,2},{4,5},{5,4},{6,7},{7,6},{8,9},{9,8},{10,11... | collective-permute-start | bytes 393224 | tf_op jit(solution)/shard_map/ppermute | solution.py:221
  33.1 7.9 %collective-permute-start.19 = (f32[32,1792]{1,0:T(8,128)S(1)}, f32[32,1792]{1,0:T(8,128)S(1)}, u32[]{:S(2)}, u32[]{:S(2)}) collective-permute-start(f32[32,1792]{1,0:T(8,128)S(1)} %get-tuple-element.75), channel_id=1, source_target_pairs={{0,4},{4,0},{8,12},{12,8},{16,20},{20,16},{24,28},{28,24},{1,5},{5... | collective-permute-start | bytes 688136 | tf_op jit(solution)/shard_map/ppermute | solution.py:221
  33.2 9.6 %collective-permute-start.21 = (f32[16,1792]{1,0:T(8,128)S(1)}, f32[16,1792]{1,0:T(8,128)S(1)}, u32[]{:S(2)}, u32[]{:S(2)}) collective-permute-start(f32[16,1792]{1,0:T(8,128)S(1)} %get-tuple-element.79), channel_id=1, source_target_pairs={{0,8},{4,12},{8,0},{12,4},{16,24},{20,28},{24,16},{28,20},{1,9},{5... | collective-permute-start | bytes 344072 | tf_op jit(solution)/shard_map/ppermute | solution.py:221
  35.4 2.9 %collective-permute-start.17 = (f32[32,1024]{1,0:T(8,128)S(1)}, f32[32,1024]{1,0:T(8,128)S(1)}, u32[]{:S(2)}, u32[]{:S(2)}) collective-permute-start(f32[32,1024]{1,0:T(8,128)S(1)} %get-tuple-element.73.refs_0_.refs_3_.refs_6_), channel_id=1, source_target_pairs={{0,1},{1,0},{2,3},{3,2},{4,5},{5,4},{6,7},{7,6},{8,9},{9,8},{10,11... | collective-permute-start | bytes 393224 | tf_op jit(solution)/shard_map/ppermute | solution.py:221
  35.5 2.8 %collective-permute-start.18 = (f32[32,1024]{1,0:T(8,128)S(1)}, f32[32,1024]{1,0:T(8,128)S(1)}, u32[]{:S(2)}, u32[]{:S(2)}) collective-permute-start(f32[32,1024]{1,0:T(8,128)S(1)} %get-tuple-element.74.refs_1_.refs_7_), channel_id=1, source_target_pairs={{0,1},{1,0},{2,3},{3,2},{4,5},{5,4},{6,7},{7,6},{8,9},{9,8},{10,11... | collective-permute-start | bytes 393224 | tf_op jit(solution)/shard_map/ppermute | solution.py:221
  36.0 6.8 %collective-permute-start.22 = (f32[16,1792]{1,0:T(8,128)S(1)}, f32[16,1792]{1,0:T(8,128)S(1)}, u32[]{:S(2)}, u32[]{:S(2)}) collective-permute-start(f32[16,1792]{1,0:T(8,128)S(1)} %get-tuple-element.80), channel_id=1, source_target_pairs={{0,8},{4,12},{8,0},{12,4},{16,24},{20,28},{24,16},{28,20},{1,9},{5... | collective-permute-start | bytes 344072 | tf_op jit(solution)/shard_map/ppermute | solution.py:221
  39.1 12.3 %collective-permute-start.26 = (f32[32,1792]{1,0:T(8,128)S(1)}, f32[32,1792]{1,0:T(8,128)S(1)}, u32[]{:S(2)}, u32[]{:S(2)}) collective-permute-start(f32[32,1792]{1,0:T(8,128)S(1)} %get-tuple-element.88), channel_id=1, source_target_pairs={{0,4},{4,0},{8,12},{12,8},{16,20},{20,16},{24,28},{28,24},{1,5},{5... | collective-permute-start | bytes 688136 | tf_op jit(solution)/shard_map/ppermute | solution.py:221
  41.0 5.5 %collective-permute-start.20 = (f32[16,1792]{1,0:T(8,128)S(1)}, f32[16,1792]{1,0:T(8,128)S(1)}, u32[]{:S(2)}, u32[]{:S(2)}) collective-permute-start(f32[16,1792]{1,0:T(8,128)S(1)} %get-tuple-element.78), channel_id=1, source_target_pairs={{0,8},{4,12},{8,0},{12,4},{16,24},{20,28},{24,16},{28,20},{1,9},{5... | collective-permute-start | bytes 344072 | tf_op jit(solution)/shard_map/ppermute | solution.py:221
  42.9 10.4 %collective-permute-start.23 = (f32[8,1792]{1,0:T(8,128)S(1)}, f32[8,1792]{1,0:T(8,128)S(1)}, u32[]{:S(2)}, u32[]{:S(2)}) collective-permute-start(f32[8,1792]{1,0:T(8,128)S(1)} %get-tuple-element.85), channel_id=1, source_target_pairs={{0,16},{4,20},{8,24},{12,28},{16,0},{20,4},{24,8},{28,12},{1,17},{... | collective-permute-start | bytes 172040 | tf_op jit(solution)/shard_map/ppermute | solution.py:221
  45.5 10.4 %collective-permute-start.24 = (f32[8,1792]{1,0:T(8,128)S(1)}, f32[8,1792]{1,0:T(8,128)S(1)}, u32[]{:S(2)}, u32[]{:S(2)}) collective-permute-start(f32[8,1792]{1,0:T(8,128)S(1)} %get-tuple-element.86), channel_id=1, source_target_pairs={{0,16},{4,20},{8,24},{12,28},{16,0},{20,4},{24,8},{28,12},{1,17},{... | collective-permute-start | bytes 172040 | tf_op jit(solution)/shard_map/ppermute | solution.py:221
  46.5 9.4 %collective-permute-start.25 = (f32[8,1792]{1,0:T(8,128)S(1)}, f32[8,1792]{1,0:T(8,128)S(1)}, u32[]{:S(2)}, u32[]{:S(2)}) collective-permute-start(f32[8,1792]{1,0:T(8,128)S(1)} %get-tuple-element.87), channel_id=1, source_target_pairs={{0,16},{4,20},{8,24},{12,28},{16,0},{20,4},{24,8},{28,12},{1,17},{... | collective-permute-start | bytes 172040 | tf_op jit(solution)/shard_map/ppermute | solution.py:221
  51.4 5.2 %collective-permute-start.27 = (f32[8,1792]{1,0:T(8,128)S(1)}, f32[8,1792]{1,0:T(8,128)S(1)}, u32[]{:S(2)}, u32[]{:S(2)}) collective-permute-start(f32[8,1792]{1,0:T(8,128)S(1)} %get-tuple-element.91), channel_id=1, source_target_pairs={{0,16},{4,20},{8,24},{12,28},{16,0},{20,4},{24,8},{28,12},{1,17},{... | collective-permute-start | bytes 172040 | tf_op jit(solution)/shard_map/ppermute | solution.py:221
  51.5 5.1 %collective-permute-start.28 = (f32[8,1792]{1,0:T(8,128)S(1)}, f32[8,1792]{1,0:T(8,128)S(1)}, u32[]{:S(2)}, u32[]{:S(2)}) collective-permute-start(f32[8,1792]{1,0:T(8,128)S(1)} %get-tuple-element.92), channel_id=1, source_target_pairs={{0,8},{4,12},{8,0},{12,4},{16,24},{20,28},{24,16},{28,20},{1,9},{5... | collective-permute-start | bytes 172040 | tf_op jit(solution)/shard_map/ppermute | solution.py:221
  53.2 6.0 %collective-permute-start.29 = (f32[8,1792]{1,0:T(8,128)S(1)}, f32[8,1792]{1,0:T(8,128)S(1)}, u32[]{:S(2)}, u32[]{:S(2)}) collective-permute-start(f32[8,1792]{1,0:T(8,128)S(1)} %get-tuple-element.93), channel_id=1, source_target_pairs={{0,24},{4,28},{8,16},{12,20},{16,8},{20,12},{24,0},{28,4},{1,25},{... | collective-permute-start | bytes 172040 | tf_op jit(solution)/shard_map/ppermute | solution.py:221

commit v8 on v7

--- a/solution.py
+++ b/solution.py
@@ -9,6 +9,8 @@
 
 EIGHTHS = (2, 2, 2, 2)
 BLOCK = 512
+STREAM = 128
+OMEGA_PARTS = 4
 F32 = jnp.float32
 BF16 = jnp.bfloat16
 NT = (((1,), (1,)), ((), ()))
@@ -64,29 +66,35 @@
     parity = lax.rem(lax.axis_index("col"), 2)
     first = (parity if mine else 1 - parity) * rows
     copies = []
-    for b in range(rows // BLOCK):
-        source = delta.at[pl.ds(pl.multiple_of(first + b * BLOCK, BLOCK), BLOCK), :]
-        copies.append(pltpu.make_async_copy(source, held.at[pl.ds(b * BLOCK, BLOCK), :], sem.at[b]))
+    for b in range(rows // STREAM):
+        source = delta.at[pl.ds(pl.multiple_of(first + b * STREAM, STREAM), STREAM), :]
+        copies.append(pltpu.make_async_copy(source, held.at[pl.ds(b * STREAM, STREAM), :], sem.at[b]))
         copies[-1].start()
     return copies
 
 
 def sketch_half(omega_t, held, copies, out):
-    for b, copy in enumerate(copies):
-        copy.wait()
+    each = BLOCK // STREAM
+    for b in range(held.shape[0] // BLOCK):
+        for copy in copies[b * each : (b + 1) * each]:
+            copy.wait()
         block = pl.ds(b * BLOCK, BLOCK)
         out[:, block] = lax.dot_general(omega_t[: out.shape[0], :], held[block, :], NT, preferred_element_type=F32)
 
 
 def first_half_body(n_row, pieces, delta, omega, held, omega_t, out, omega_v, sem, omega_sem):
     k = omega_t.shape[0]
-    fetch = pltpu.make_async_copy(omega, omega_v, omega_sem)
-    fetch.start()
+    fetches = []
+    for i in range(OMEGA_PARTS):
+        part = pl.ds(i * (omega.shape[0] // OMEGA_PARTS), omega.shape[0] // OMEGA_PARTS)
+        fetches.append(pltpu.make_async_copy(omega.at[part, :], omega_v.at[part, :], omega_sem.at[i]))
+        fetches[-1].start()
     copies = stream_half(delta, held, sem, False)
     position = lax.broadcasted_iota(jnp.int32, (k, k), 0)
     column = lax.broadcasted_iota(jnp.int32, (k, k), 1)
     pick = jnp.where(column_of(position, k, n_row, pieces) == column, 1.0, 0.0).astype(BF16)
-    fetch.wait()
+    for fetch in fetches:
+        fetch.wait()
     omega_t[...] = lax.dot_general(pick, omega_v[...], NT, preferred_element_type=F32).astype(BF16)
     sketch_half(omega_t, held, copies, out)
 
@@ -233,13 +241,13 @@
     bits = [1 << i for i in range(n_row.bit_length() - 1)]
 
     in_hbm = pltpu.with_memory_space_constraint(delta, pltpu.HBM)
-    sems = pltpu.SemaphoreType.DMA((half // BLOCK,))
+    sems = pltpu.SemaphoreType.DMA((half // STREAM,))
     held_other, omega_t, to_send = call(
         functools.partial(first_half_body, n_row, pieces),
         (in_hbm, pltpu.with_memory_space_constraint(omega, pltpu.HBM)),
         [((half, d), BF16), ((k, d), BF16), ((widths[0], half), F32)],
         "aa",
-        scratch=[pltpu.VMEM((d, k), BF16), sems, pltpu.SemaphoreType.DMA],
+        scratch=[pltpu.VMEM((d, k), BF16), sems, pltpu.SemaphoreType.DMA((OMEGA_PARTS,))],
     )
     received = swap(to_send, "col", n_col, 1)
     outs = [((half, d), BF16), ((widths[0], half), F32)]

time: 60.1 us -> 61 us (1.015)
  Pallas kernels: 17.9 us -> 18.8 us
    pallas_call x27, Pallas kernels: 17.9 us -> 18.8 us  [call(): pl.pallas_call(run, out_shape=[pltpu.VMEM(*o) if i >= results else jax.Sh...]
where the time goes in v8:
time: 61 us; the launch traced here: 60.9 us
  starting transfers between devices  29.5 us (48%)
  Pallas kernels  18.8 us (31%)
  waiting for transfers between devices  11.6 us (19%)
  between operations  0.9 us (1%)
    ppermute x30, starting transfers between devices, swap(): return lax.ppermute(x, axis, [(i, i ^ bit) for i in range(size)])  29.5 us
    pallas_call x27, Pallas kernels, call(): pl.pallas_call(run, out_shape=[pltpu.VMEM(*o) if i >= results else jax.Sh...  18.8 us
    ppermute x30, waiting for transfers between devices, swap(): return lax.ppermute(x, axis, [(i, i ^ bit) for i in range(size)])  11.6 us
  transfers between devices with their start and end apart: 30, of which 11 were waited for; matrix products, arithmetic and copies ran while one was open for 0% of the time, Pallas kernels for 23%

profile of v8, /device:TPU:0, one launch (start us, length us, event | category | flops | bytes accessed | tf_op | source)
XLA Modules:
  0.0 60.9 jit_solution(8014161914925636698)
XLA Ops:
  0.6 4.2 %shard_map.41 = (bf16[1024,1792]{1,0:T(8,128)(2,1)S(1)}, bf16[256,1792]{1,0:T(8,128)(2,1)S(1)}, f32[64,1024]{1,0:T(8,128)S(1)}) custom-call(bf16[2048,1792]{1,0:T(8,128)(2,1)} %refs_0_.3, bf16[1792,256]{1,0:T(8,128)(2,1)} %refs_1_.1), custom_call_target="tpu_custom_call" | custom-call | tf_op jit(solution)/shard_map/pallas_call | solution.py:33
  5.3 2.9 %shard_map.42 = (bf16[1024,1792]{1,0:T(8,128)(2,1)S(1)}, f32[64,1024]{1,0:T(8,128)S(1)}) custom-call(bf16[2048,1792]{1,0:T(8,128)(2,1)} %refs_0_.3, bf16[256,1792]{1,0:T(8,128)(2,1)S(1)} %get-tuple-element.48.refs_1_.refs_0_, f32[64,1024]{1,0:T(8,128)S(1)} %get-tuple-element.49.refs_2_), custom_call_target="tpu_custom_call" | custom-call | tf_op jit(solution)/shard_map/pallas_call | solution.py:33
  8.2 2.6 %collective-permute-start.1 = (f32[64,1024]{1,0:T(8,128)S(1)}, f32[64,1024]{1,0:T(8,128)S(1)}, u32[]{:S(2)}, u32[]{:S(2)}) collective-permute-start(f32[64,1024]{1,0:T(8,128)S(1)} %shard_map.43.refs_0_.refs_2_), channel_id=1, source_target_pairs={{0,2},{1,3},{2,0},{3,1},{4,6},{5,7},{6,4},{7,5},{8,10},{9,11},{10,... | collective-permute-start | bytes 786440 | tf_op jit(solution)/shard_map/ppermute | solution.py:229
  10.8 1.3 %shard_map.45 = (f32[48,1024]{1,0:T(8,128)S(1)}, f32[48,1024]{1,0:T(8,128)S(1)}, f32[48,1024]{1,0:T(8,128)S(1)}, f32[48,1024]{1,0:T(8,128)S(1)}) custom-call(bf16[256,1792]{1,0:T(8,128)(2,1)S(1)} %get-tuple-element.48.refs_1_.refs_0_, bf16[1024,1792]{1,0:T(8,128)(2,1)S(1)} %get-tuple-element.54.refs_1_.refs_2_, f32[64,1024]{1,0:T(8,128)S(1)} %shard_map.43.refs_0_.refs_2_), custom_call_target="tpu_custom_call" | custom-call | tf_op jit(solution)/shard_map/pallas_call | solution.py:33
  13.3 1.3 %shard_map.46.refs_0_ = f32[192,1024]{1,0:T(8,128)S(1)} custom-call(bf16[256,1792]{1,0:T(8,128)(2,1)S(1)} %get-tuple-element.48.refs_1_.refs_0_, bf16[1024,1792]{1,0:T(8,128)(2,1)S(1)} %get-tuple-element.53.refs_1_.refs_2_, f32[48,1024]{1,0:T(8,128)S(1)} %get-tuple-element.55.refs_2_), custom_call_target="tpu_custom_call" | custom-call | tf_op jit(solution)/shard_map/pallas_call | solution.py:33
  14.9 3.0 %collective-permute-done.1.refs_1_ = f32[64,1024]{1,0:T(8,128)S(1)} collective-permute-done((f32[64,1024]{1,0:T(8,128)S(1)}, f32[64,1024]{1,0:T(8,128)S(1)}, u32[]{:S(2)}, u32[]{:S(2)}) %collective-permute-start.1) | collective-permute-done | bytes 262176 | tf_op jit(solution)/shard_map/ppermute | solution.py:229
  18.5 0.7 %shard_map.48.refs_3_.refs_4_ = f32[64,1792]{1,0:T(8,128)S(1)} custom-call(f32[32,1024]{1,0:T(8,128)S(1)} %get-tuple-element.51.refs_0_.refs_3_, f32[32,1024]{1,0:T(8,128)S(1)} %get-tuple-element.52.refs_1_, bf16[1024,1792]{1,0:T(8,128)(2,1)S(1)} %get-tuple-element.53.refs_1_.refs_2_, f32[32,1024]{1,0:T(8,128)S(1)} %get-tuple-element.51.refs_0_.refs_3_), custom_call_target="tpu_custom_call" | custom-call | tf_op jit(solution)/shard_map/pallas_call | solution.py:33
  19.5 0.8 %shard_map.49 = (f32[32,1792]{1,0:T(8,128)S(1)}, f32[32,1792]{1,0:T(8,128)S(1)}) custom-call(f32[32,1024]{1,0:T(8,128)S(1)} %collective-permute-done.7.refs_0_.refs_8_, f32[32,1024]{1,0:T(8,128)S(1)} %collective-permute-done.8.refs_1_.refs_9_, bf16[1024,1792]{1,0:T(8,128)(2,1)S(1)} %get-tuple-element.54.refs_1_.refs_2_, ...), custom_call_target="tpu_custom_call" | custom-call | tf_op jit(solution)/shard_map/pallas_call | solution.py:33
  20.3 2.1 %collective-permute-start.10 = (f32[32,1792]{1,0:T(8,128)S(1)}, f32[32,1792]{1,0:T(8,128)S(1)}, u32[]{:S(2)}, u32[]{:S(2)}) collective-permute-start(f32[32,1792]{1,0:T(8,128)S(1)} %get-tuple-element.64), channel_id=1, source_target_pairs={{0,4},{4,0},{8,12},{12,8},{16,20},{20,16},{24,28},{28,24},{1,5},{5... | collective-permute-start | bytes 688136 | tf_op jit(solution)/shard_map/ppermute | solution.py:229
  22.4 1.5 %collective-permute-start.9 = (f32[64,1024]{1,0:T(8,128)S(1)}, f32[64,1024]{1,0:T(8,128)S(1)}, u32[]{:S(2)}, u32[]{:S(2)}) collective-permute-start(f32[64,1024]{1,0:T(8,128)S(1)} %get-tuple-element.63.refs_0_), channel_id=1, source_target_pairs={{0,2},{1,3},{2,0},{3,1},{4,6},{5,7},{6,4},{7,5},{8,10},{9,11},{10,... | collective-permute-start | bytes 786440 | tf_op jit(solution)/shard_map/ppermute | solution.py:229
  24.5 1.2 %collective-permute-start.13 = (f32[64,1024]{1,0:T(8,128)S(1)}, f32[64,1024]{1,0:T(8,128)S(1)}, u32[]{:S(2)}, u32[]{:S(2)}) collective-permute-start(f32[64,1024]{1,0:T(8,128)S(1)} %get-tuple-element.69.refs_0_), channel_id=1, source_target_pairs={{0,2},{1,3},{2,0},{3,1},{4,6},{5,7},{6,4},{7,5},{8,10},{9,11},{10,... | collective-permute-start | bytes 786440 | tf_op jit(solution)/shard_map/ppermute | solution.py:229
  25.7 0.7 %shard_map.51.refs_3_.refs_4_ = f32[64,1792]{1,0:T(8,128)S(1)} custom-call(f32[32,1024]{1,0:T(8,128)S(1)} %get-tuple-element.61.refs_0_.refs_3_.refs_2_, f32[32,1024]{1,0:T(8,128)S(1)} %get-tuple-element.62.refs_1_.refs_3_, bf16[1024,1792]{1,0:T(8,128)(2,1)S(1)} %get-tuple-element.53.refs_1_.refs_2_, f32[32,1024]{1,0:T(8,128)S(1)} %get-tuple-element.61.refs_0_.refs_3_.refs_2_), custom_call_target="tpu_custom_call" | custom-call | flops 500000000 | tf_op jit(solution)/shard_map/pallas_call | solution.py:33
  26.5 0.8 %shard_map.52 = (f32[32,1792]{1,0:T(8,128)S(1)}, f32[32,1792]{1,0:T(8,128)S(1)}) custom-call(f32[32,1024]{1,0:T(8,128)S(1)} %collective-permute-done.11.refs_0_.refs_10_, f32[32,1024]{1,0:T(8,128)S(1)} %collective-permute-done.12.refs_1_.refs_11_, bf16[1024,1792]{1,0:T(8,128)(2,1)S(1)} %get-tuple-element.54.refs_1_.refs_2_, ...), custom_call_target="tpu_custom_call" | custom-call | tf_op jit(solution)/shard_map/pallas_call | solution.py:33
  27.3 1.6 %collective-permute-start.14 = (f32[32,1792]{1,0:T(8,128)S(1)}, f32[32,1792]{1,0:T(8,128)S(1)}, u32[]{:S(2)}, u32[]{:S(2)}) collective-permute-start(f32[32,1792]{1,0:T(8,128)S(1)} %get-tuple-element.70), channel_id=1, source_target_pairs={{0,4},{4,0},{8,12},{12,8},{16,20},{20,16},{24,28},{28,24},{1,5},{5... | collective-permute-start | bytes 688136 | tf_op jit(solution)/shard_map/ppermute | solution.py:229
  28.9 2.7 %collective-permute-done.9.refs_1_ = f32[64,1024]{1,0:T(8,128)S(1)} collective-permute-done((f32[64,1024]{1,0:T(8,128)S(1)}, f32[64,1024]{1,0:T(8,128)S(1)}, u32[]{:S(2)}, u32[]{:S(2)}) %collective-permute-start.9) | collective-permute-done | bytes 262176 | tf_op jit(solution)/shard_map/ppermute | solution.py:229
  32.2 0.7 %shard_map.55.refs_3_.refs_4_ = f32[64,1792]{1,0:T(8,128)S(1)} custom-call(f32[32,1024]{1,0:T(8,128)S(1)} %get-tuple-element.67.refs_0_.refs_3_.refs_4_, f32[32,1024]{1,0:T(8,128)S(1)} %get-tuple-element.68.refs_1_.refs_5_, bf16[1024,1792]{1,0:T(8,128)(2,1)S(1)} %get-tuple-element.53.refs_1_.refs_2_, f32[32,1024]{1,0:T(8,128)S(1)} %get-tuple-element.67.refs_0_.refs_3_.refs_4_), custom_call_target="tpu_custom_call" | custom-call | tf_op jit(solution)/shard_map/pallas_call | solution.py:33
  33.2 0.8 %shard_map.56 = (f32[32,1792]{1,0:T(8,128)S(1)}, f32[32,1792]{1,0:T(8,128)S(1)}) custom-call(f32[32,1024]{1,0:T(8,128)S(1)} %collective-permute-done.15.refs_0_.refs_12_, f32[32,1024]{1,0:T(8,128)S(1)} %collective-permute-done.16.refs_1_.refs_13_, bf16[1024,1792]{1,0:T(8,128)(2,1)S(1)} %get-tuple-element.54.refs_1_.refs_2_, ...), custom_call_target="tpu_custom_call" | custom-call | tf_op jit(solution)/shard_map/pallas_call | solution.py:33
  34.1 2.1 %collective-permute-start.21 = (f32[16,1792]{1,0:T(8,128)S(1)}, f32[16,1792]{1,0:T(8,128)S(1)}, u32[]{:S(2)}, u32[]{:S(2)}) collective-permute-start(f32[16,1792]{1,0:T(8,128)S(1)} %get-tuple-element.79), channel_id=1, source_target_pairs={{0,8},{4,12},{8,0},{12,4},{16,24},{20,28},{24,16},{28,20},{1,9},{5... | collective-permute-start | bytes 344072 | tf_op jit(solution)/shard_map/ppermute | solution.py:229
  36.9 1.6 %collective-permute-start.22 = (f32[16,1792]{1,0:T(8,128)S(1)}, f32[16,1792]{1,0:T(8,128)S(1)}, u32[]{:S(2)}, u32[]{:S(2)}) collective-permute-start(f32[16,1792]{1,0:T(8,128)S(1)} %get-tuple-element.80), channel_id=1, source_target_pairs={{0,8},{4,12},{8,0},{12,4},{16,24},{20,28},{24,16},{28,20},{1,9},{5... | collective-permute-start | bytes 344072 | tf_op jit(solution)/shard_map/ppermute | solution.py:229
  38.5 0.7 %shard_map.59.refs_3_.refs_4_ = f32[64,1792]{1,0:T(8,128)S(1)} custom-call(f32[32,1024]{1,0:T(8,128)S(1)} %get-tuple-element.73.refs_0_.refs_3_.refs_6_, f32[32,1024]{1,0:T(8,128)S(1)} %get-tuple-element.74.refs_1_.refs_7_, bf16[1024,1792]{1,0:T(8,128)(2,1)S(1)} %get-tuple-element.53.refs_1_.refs_2_, f32[32,1024]{1,0:T(8,128)S(1)} %get-tuple-element.73.refs_0_.refs_3_.refs_6_), custom_call_target="tpu_custom_call" | custom-call | flops 2000000000 | tf_op jit(solution)/shard_map/pallas_call | solution.py:33
  39.3 0.8 %shard_map.60 = (f32[32,1792]{1,0:T(8,128)S(1)}, f32[32,1792]{1,0:T(8,128)S(1)}) custom-call(f32[32,1024]{1,0:T(8,128)S(1)} %collective-permute-done.17.refs_0_.refs_14_, f32[32,1024]{1,0:T(8,128)S(1)} %collective-permute-done.18.refs_1_.refs_15_, bf16[1024,1792]{1,0:T(8,128)(2,1)S(1)} %get-tuple-element.54.refs_1_.refs_2_, ...), custom_call_target="tpu_custom_call" | custom-call | tf_op jit(solution)/shard_map/pallas_call | solution.py:33
  40.6 1.3 %collective-permute-done.19.refs_1_ = f32[32,1792]{1,0:T(8,128)S(1)} collective-permute-done((f32[32,1792]{1,0:T(8,128)S(1)}, f32[32,1792]{1,0:T(8,128)S(1)}, u32[]{:S(2)}, u32[]{:S(2)}) %collective-permute-start.19) | collective-permute-done | bytes 229408 | tf_op jit(solution)/shard_map/ppermute | solution.py:229
  41.9 1.8 %collective-permute-start.20 = (f32[16,1792]{1,0:T(8,128)S(1)}, f32[16,1792]{1,0:T(8,128)S(1)}, u32[]{:S(2)}, u32[]{:S(2)}) collective-permute-start(f32[16,1792]{1,0:T(8,128)S(1)} %get-tuple-element.78), channel_id=1, source_target_pairs={{0,8},{4,12},{8,0},{12,4},{16,24},{20,28},{24,16},{28,20},{1,9},{5... | collective-permute-start | bytes 344072 | tf_op jit(solution)/shard_map/ppermute | solution.py:229
  43.8 2.7 %collective-permute-start.23 = (f32[8,1792]{1,0:T(8,128)S(1)}, f32[8,1792]{1,0:T(8,128)S(1)}, u32[]{:S(2)}, u32[]{:S(2)}) collective-permute-start(f32[8,1792]{1,0:T(8,128)S(1)} %get-tuple-element.85), channel_id=1, source_target_pairs={{0,16},{4,20},{8,24},{12,28},{16,0},{20,4},{24,8},{28,12},{1,17},{... | collective-permute-start | bytes 172040 | tf_op jit(solution)/shard_map/ppermute | solution.py:229
  46.8 0.6 %collective-permute-done.20.refs_1_ = f32[16,1792]{1,0:T(8,128)S(1)} collective-permute-done((f32[16,1792]{1,0:T(8,128)S(1)}, f32[16,1792]{1,0:T(8,128)S(1)}, u32[]{:S(2)}, u32[]{:S(2)}) %collective-permute-start.20) | collective-permute-done | bytes 114720 | tf_op jit(solution)/shard_map/ppermute | solution.py:229
  47.4 3.0 %collective-permute-start.25 = (f32[8,1792]{1,0:T(8,128)S(1)}, f32[8,1792]{1,0:T(8,128)S(1)}, u32[]{:S(2)}, u32[]{:S(2)}) collective-permute-start(f32[8,1792]{1,0:T(8,128)S(1)} %get-tuple-element.87), channel_id=1, source_target_pairs={{0,16},{4,20},{8,24},{12,28},{16,0},{20,4},{24,8},{28,12},{1,17},{... | collective-permute-start | bytes 172040 | tf_op jit(solution)/shard_map/ppermute | solution.py:229
  50.4 1.9 %shard_map.65 = (f32[2048,256]{1,0:T(8,128)}, f32[8,128]{1,0:T(8,128)S(1)}) custom-call(f32[32,1024]{1,0:T(8,128)S(1)} %get-tuple-element.51.refs_0_.refs_3_, f32[32,1024]{1,0:T(8,128)S(1)} %get-tuple-element.52.refs_1_, f32[32,1024]{1,0:T(8,128)S(1)} %get-tuple-element.61.refs_0_.refs_3_.refs_2_, f32[32,1024]{1,0:T(8,128)S(1)} %get-tuple-element.62.refs_1_.refs_3_, ...), custom_call_target="tpu_custom_call" | custom-call | tf_op jit(solution)/shard_map/pallas_call | solution.py:33
  52.5 1.7 %collective-permute-start.28 = (f32[8,1792]{1,0:T(8,128)S(1)}, f32[8,1792]{1,0:T(8,128)S(1)}, u32[]{:S(2)}, u32[]{:S(2)}) collective-permute-start(f32[8,1792]{1,0:T(8,128)S(1)} %get-tuple-element.92), channel_id=1, source_target_pairs={{0,8},{4,12},{8,0},{12,4},{16,24},{20,28},{24,16},{28,20},{1,9},{5... | collective-permute-start | bytes 172040 | tf_op jit(solution)/shard_map/ppermute | solution.py:229
  54.2 2.7 %collective-permute-start.29 = (f32[8,1792]{1,0:T(8,128)S(1)}, f32[8,1792]{1,0:T(8,128)S(1)}, u32[]{:S(2)}, u32[]{:S(2)}) collective-permute-start(f32[8,1792]{1,0:T(8,128)S(1)} %get-tuple-element.93), channel_id=1, source_target_pairs={{0,24},{4,28},{8,16},{12,20},{16,8},{20,12},{24,0},{28,4},{1,25},{... | collective-permute-start | bytes 172040 | tf_op jit(solution)/shard_map/ppermute | solution.py:229
  56.9 0.7 %collective-permute-done.27.refs_7_ = f32[8,1792]{1,0:T(8,128)S(1)} collective-permute-done((f32[8,1792]{1,0:T(8,128)S(1)}, f32[8,1792]{1,0:T(8,128)S(1)}, u32[]{:S(2)}, u32[]{:S(2)}) %collective-permute-start.27) | collective-permute-done | bytes 57376 | tf_op jit(solution)/shard_map/ppermute | solution.py:229
  57.6 2.6 %collective-permute-done.29.refs_9_ = f32[8,1792]{1,0:T(8,128)S(1)} collective-permute-done((f32[8,1792]{1,0:T(8,128)S(1)}, f32[8,1792]{1,0:T(8,128)S(1)}, u32[]{:S(2)}, u32[]{:S(2)}) %collective-permute-start.29) | collective-permute-done | bytes 57376 | tf_op jit(solution)/shard_map/ppermute | solution.py:229
  60.2 0.7 %shard_map.67 = f32[32,1792]{1,0:T(8,128)} custom-call(f32[8,1792]{1,0:T(8,128)S(1)} %get-tuple-element.82.refs_2_.refs_0_, f32[8,1792]{1,0:T(8,128)S(1)} %collective-permute-done.23.refs_1_, f32[8,1792]{1,0:T(8,128)S(1)} %get-tuple-element.81.refs_2_, f32[8,1792]{1,0:T(8,128)S(1)} %collective-permute-done.24.refs_3_, ...), custom_call_target="tpu_custom_call" | custom-call | flops 500000000 | tf_op jit(solution)/shard_map/pallas_call | solution.py:33
  (55 shorter events, 6.2 us)
Async XLA Ops:
  4.8 3.4 %collective-permute-start = (f32[64,1024]{1,0:T(8,128)S(1)}, f32[64,1024]{1,0:T(8,128)S(1)}, u32[]{:S(2)}, u32[]{:S(2)}) collective-permute-start(f32[64,1024]{1,0:T(8,128)S(1)} %get-tuple-element.49.refs_2_), channel_id=1, source_target_pairs={{0,1},{1,0},{2,3},{3,2},{4,5},{5,4},{6,7},{7,6},{8,9},{9,8},{10,11... | collective-permute-start | bytes 786440 | tf_op jit(solution)/shard_map/ppermute | solution.py:229
  8.2 9.7 %collective-permute-start.1 = (f32[64,1024]{1,0:T(8,128)S(1)}, f32[64,1024]{1,0:T(8,128)S(1)}, u32[]{:S(2)}, u32[]{:S(2)}) collective-permute-start(f32[64,1024]{1,0:T(8,128)S(1)} %shard_map.43.refs_0_.refs_2_), channel_id=1, source_target_pairs={{0,2},{1,3},{2,0},{3,1},{4,6},{5,7},{6,4},{7,5},{8,10},{9,11},{10,... | collective-permute-start | bytes 786440 | tf_op jit(solution)/shard_map/ppermute | solution.py:229
  12.2 2.4 %collective-permute-start.2 = (f32[48,1024]{1,0:T(8,128)S(1)}, f32[48,1024]{1,0:T(8,128)S(1)}, u32[]{:S(2)}, u32[]{:S(2)}) collective-permute-start(f32[48,1024]{1,0:T(8,128)S(1)} %get-tuple-element.55.refs_2_), channel_id=1, source_target_pairs={{0,1},{1,0},{2,3},{3,2},{4,5},{5,4},{6,7},{7,6},{8,9},{9,8},{10,11... | collective-permute-start | bytes 589832 | tf_op jit(solution)/shard_map/ppermute | solution.py:229
  12.4 2.2 %collective-permute-start.3 = (f32[48,1024]{1,0:T(8,128)S(1)}, f32[48,1024]{1,0:T(8,128)S(1)}, u32[]{:S(2)}, u32[]{:S(2)}) collective-permute-start(f32[48,1024]{1,0:T(8,128)S(1)} %get-tuple-element.56), channel_id=1, source_target_pairs={{0,1},{1,0},{2,3},{3,2},{4,5},{5,4},{6,7},{7,6},{8,9},{9,8},{10,11... | collective-permute-start | bytes 589832 | tf_op jit(solution)/shard_map/ppermute | solution.py:229
  12.7 1.9 %collective-permute-start.4 = (f32[48,1024]{1,0:T(8,128)S(1)}, f32[48,1024]{1,0:T(8,128)S(1)}, u32[]{:S(2)}, u32[]{:S(2)}) collective-permute-start(f32[48,1024]{1,0:T(8,128)S(1)} %get-tuple-element.57), channel_id=1, source_target_pairs={{0,1},{1,0},{2,3},{3,2},{4,5},{5,4},{6,7},{7,6},{8,9},{9,8},{10,11... | collective-permute-start | bytes 589832 | tf_op jit(solution)/shard_map/ppermute | solution.py:229
  12.9 1.7 %collective-permute-start.5 = (f32[48,1024]{1,0:T(8,128)S(1)}, f32[48,1024]{1,0:T(8,128)S(1)}, u32[]{:S(2)}, u32[]{:S(2)}) collective-permute-start(f32[48,1024]{1,0:T(8,128)S(1)} %get-tuple-element.58), channel_id=1, source_target_pairs={{0,1},{1,0},{2,3},{3,2},{4,5},{5,4},{6,7},{7,6},{8,9},{9,8},{10,11... | collective-permute-start | bytes 589832 | tf_op jit(solution)/shard_map/ppermute | solution.py:229
  14.7 9.2 %collective-permute-start.6 = (f32[64,1024]{1,0:T(8,128)S(1)}, f32[64,1024]{1,0:T(8,128)S(1)}, u32[]{:S(2)}, u32[]{:S(2)}) collective-permute-start(f32[64,1024]{1,0:T(8,128)S(1)} %get-tuple-element.59.refs_0_), channel_id=1, source_target_pairs={{0,2},{1,3},{2,0},{3,1},{4,6},{5,7},{6,4},{7,5},{8,10},{9,11},{10,... | collective-permute-start | bytes 786440 | tf_op jit(solution)/shard_map/ppermute | solution.py:229
  17.9 1.4 %collective-permute-start.7 = (f32[32,1024]{1,0:T(8,128)S(1)}, f32[32,1024]{1,0:T(8,128)S(1)}, u32[]{:S(2)}, u32[]{:S(2)}) collective-permute-start(f32[32,1024]{1,0:T(8,128)S(1)} %get-tuple-element.51.refs_0_.refs_3_), channel_id=1, source_target_pairs={{0,1},{1,0},{2,3},{3,2},{4,5},{5,4},{6,7},{7,6},{8,9},{9,8},{10,11... | collective-permute-start | bytes 393224 | tf_op jit(solution)/shard_map/ppermute | solution.py:229
  18.0 1.5 %collective-permute-start.8 = (f32[32,1024]{1,0:T(8,128)S(1)}, f32[32,1024]{1,0:T(8,128)S(1)}, u32[]{:S(2)}, u32[]{:S(2)}) collective-permute-start(f32[32,1024]{1,0:T(8,128)S(1)} %get-tuple-element.52.refs_1_), channel_id=1, source_target_pairs={{0,1},{1,0},{2,3},{3,2},{4,5},{5,4},{6,7},{7,6},{8,9},{9,8},{10,11... | collective-permute-start | bytes 393224 | tf_op jit(solution)/shard_map/ppermute | solution.py:229
  20.3 8.6 %collective-permute-start.10 = (f32[32,1792]{1,0:T(8,128)S(1)}, f32[32,1792]{1,0:T(8,128)S(1)}, u32[]{:S(2)}, u32[]{:S(2)}) collective-permute-start(f32[32,1792]{1,0:T(8,128)S(1)} %get-tuple-element.64), channel_id=1, source_target_pairs={{0,4},{4,0},{8,12},{12,8},{16,20},{20,16},{24,28},{28,24},{1,5},{5... | collective-permute-start | bytes 688136 | tf_op jit(solution)/shard_map/ppermute | solution.py:229
  22.4 9.2 %collective-permute-start.9 = (f32[64,1024]{1,0:T(8,128)S(1)}, f32[64,1024]{1,0:T(8,128)S(1)}, u32[]{:S(2)}, u32[]{:S(2)}) collective-permute-start(f32[64,1024]{1,0:T(8,128)S(1)} %get-tuple-element.63.refs_0_), channel_id=1, source_target_pairs={{0,2},{1,3},{2,0},{3,1},{4,6},{5,7},{6,4},{7,5},{8,10},{9,11},{10,... | collective-permute-start | bytes 786440 | tf_op jit(solution)/shard_map/ppermute | solution.py:229
  24.0 2.5 %collective-permute-start.11 = (f32[32,1024]{1,0:T(8,128)S(1)}, f32[32,1024]{1,0:T(8,128)S(1)}, u32[]{:S(2)}, u32[]{:S(2)}) collective-permute-start(f32[32,1024]{1,0:T(8,128)S(1)} %get-tuple-element.61.refs_0_.refs_3_.refs_2_), channel_id=1, source_target_pairs={{0,1},{1,0},{2,3},{3,2},{4,5},{5,4},{6,7},{7,6},{8,9},{9,8},{10,11... | collective-permute-start | bytes 393224 | tf_op jit(solution)/shard_map/ppermute | solution.py:229
  24.0 2.5 %collective-permute-start.12 = (f32[32,1024]{1,0:T(8,128)S(1)}, f32[32,1024]{1,0:T(8,128)S(1)}, u32[]{:S(2)}, u32[]{:S(2)}) collective-permute-start(f32[32,1024]{1,0:T(8,128)S(1)} %get-tuple-element.62.refs_1_.refs_3_), channel_id=1, source_target_pairs={{0,1},{1,0},{2,3},{3,2},{4,5},{5,4},{6,7},{7,6},{8,9},{9,8},{10,11... | collective-permute-start | bytes 393224 | tf_op jit(solution)/shard_map/ppermute | solution.py:229
  24.5 11.8 %collective-permute-start.13 = (f32[64,1024]{1,0:T(8,128)S(1)}, f32[64,1024]{1,0:T(8,128)S(1)}, u32[]{:S(2)}, u32[]{:S(2)}) collective-permute-start(f32[64,1024]{1,0:T(8,128)S(1)} %get-tuple-element.69.refs_0_), channel_id=1, source_target_pairs={{0,2},{1,3},{2,0},{3,1},{4,6},{5,7},{6,4},{7,5},{8,10},{9,11},{10,... | collective-permute-start | bytes 786440 | tf_op jit(solution)/shard_map/ppermute | solution.py:229
  27.3 8.9 %collective-permute-start.14 = (f32[32,1792]{1,0:T(8,128)S(1)}, f32[32,1792]{1,0:T(8,128)S(1)}, u32[]{:S(2)}, u32[]{:S(2)}) collective-permute-start(f32[32,1792]{1,0:T(8,128)S(1)} %get-tuple-element.70), channel_id=1, source_target_pairs={{0,4},{4,0},{8,12},{12,8},{16,20},{20,16},{24,28},{28,24},{1,5},{5... | collective-permute-start | bytes 688136 | tf_op jit(solution)/shard_map/ppermute | solution.py:229
  31.6 1.4 %collective-permute-start.15 = (f32[32,1024]{1,0:T(8,128)S(1)}, f32[32,1024]{1,0:T(8,128)S(1)}, u32[]{:S(2)}, u32[]{:S(2)}) collective-permute-start(f32[32,1024]{1,0:T(8,128)S(1)} %get-tuple-element.67.refs_0_.refs_3_.refs_4_), channel_id=1, source_target_pairs={{0,1},{1,0},{2,3},{3,2},{4,5},{5,4},{6,7},{7,6},{8,9},{9,8},{10,11... | collective-permute-start | bytes 393224 | tf_op jit(solution)/shard_map/ppermute | solution.py:229
  31.7 1.5 %collective-permute-start.16 = (f32[32,1024]{1,0:T(8,128)S(1)}, f32[32,1024]{1,0:T(8,128)S(1)}, u32[]{:S(2)}, u32[]{:S(2)}) collective-permute-start(f32[32,1024]{1,0:T(8,128)S(1)} %get-tuple-element.68.refs_1_.refs_5_), channel_id=1, source_target_pairs={{0,1},{1,0},{2,3},{3,2},{4,5},{5,4},{6,7},{7,6},{8,9},{9,8},{10,11... | collective-permute-start | bytes 393224 | tf_op jit(solution)/shard_map/ppermute | solution.py:229
  34.0 7.9 %collective-permute-start.19 = (f32[32,1792]{1,0:T(8,128)S(1)}, f32[32,1792]{1,0:T(8,128)S(1)}, u32[]{:S(2)}, u32[]{:S(2)}) collective-permute-start(f32[32,1792]{1,0:T(8,128)S(1)} %get-tuple-element.75), channel_id=1, source_target_pairs={{0,4},{4,0},{8,12},{12,8},{16,20},{20,16},{24,28},{28,24},{1,5},{5... | collective-permute-start | bytes 688136 | tf_op jit(solution)/shard_map/ppermute | solution.py:229
  34.1 9.6 %collective-permute-start.21 = (f32[16,1792]{1,0:T(8,128)S(1)}, f32[16,1792]{1,0:T(8,128)S(1)}, u32[]{:S(2)}, u32[]{:S(2)}) collective-permute-start(f32[16,1792]{1,0:T(8,128)S(1)} %get-tuple-element.79), channel_id=1, source_target_pairs={{0,8},{4,12},{8,0},{12,4},{16,24},{20,28},{24,16},{28,20},{1,9},{5... | collective-permute-start | bytes 344072 | tf_op jit(solution)/shard_map/ppermute | solution.py:229
  36.3 2.9 %collective-permute-start.17 = (f32[32,1024]{1,0:T(8,128)S(1)}, f32[32,1024]{1,0:T(8,128)S(1)}, u32[]{:S(2)}, u32[]{:S(2)}) collective-permute-start(f32[32,1024]{1,0:T(8,128)S(1)} %get-tuple-element.73.refs_0_.refs_3_.refs_6_), channel_id=1, source_target_pairs={{0,1},{1,0},{2,3},{3,2},{4,5},{5,4},{6,7},{7,6},{8,9},{9,8},{10,11... | collective-permute-start | bytes 393224 | tf_op jit(solution)/shard_map/ppermute | solution.py:229
  36.4 2.8 %collective-permute-start.18 = (f32[32,1024]{1,0:T(8,128)S(1)}, f32[32,1024]{1,0:T(8,128)S(1)}, u32[]{:S(2)}, u32[]{:S(2)}) collective-permute-start(f32[32,1024]{1,0:T(8,128)S(1)} %get-tuple-element.74.refs_1_.refs_7_), channel_id=1, source_target_pairs={{0,1},{1,0},{2,3},{3,2},{4,5},{5,4},{6,7},{7,6},{8,9},{9,8},{10,11... | collective-permute-start | bytes 393224 | tf_op jit(solution)/shard_map/ppermute | solution.py:229
  36.9 6.8 %collective-permute-start.22 = (f32[16,1792]{1,0:T(8,128)S(1)}, f32[16,1792]{1,0:T(8,128)S(1)}, u32[]{:S(2)}, u32[]{:S(2)}) collective-permute-start(f32[16,1792]{1,0:T(8,128)S(1)} %get-tuple-element.80), channel_id=1, source_target_pairs={{0,8},{4,12},{8,0},{12,4},{16,24},{20,28},{24,16},{28,20},{1,9},{5... | collective-permute-start | bytes 344072 | tf_op jit(solution)/shard_map/ppermute | solution.py:229
  40.1 12.3 %collective-permute-start.26 = (f32[32,1792]{1,0:T(8,128)S(1)}, f32[32,1792]{1,0:T(8,128)S(1)}, u32[]{:S(2)}, u32[]{:S(2)}) collective-permute-start(f32[32,1792]{1,0:T(8,128)S(1)} %get-tuple-element.88), channel_id=1, source_target_pairs={{0,4},{4,0},{8,12},{12,8},{16,20},{20,16},{24,28},{28,24},{1,5},{5... | collective-permute-start | bytes 688136 | tf_op jit(solution)/shard_map/ppermute | solution.py:229
  41.9 5.5 %collective-permute-start.20 = (f32[16,1792]{1,0:T(8,128)S(1)}, f32[16,1792]{1,0:T(8,128)S(1)}, u32[]{:S(2)}, u32[]{:S(2)}) collective-permute-start(f32[16,1792]{1,0:T(8,128)S(1)} %get-tuple-element.78), channel_id=1, source_target_pairs={{0,8},{4,12},{8,0},{12,4},{16,24},{20,28},{24,16},{28,20},{1,9},{5... | collective-permute-start | bytes 344072 | tf_op jit(solution)/shard_map/ppermute | solution.py:229
  43.8 10.4 %collective-permute-start.23 = (f32[8,1792]{1,0:T(8,128)S(1)}, f32[8,1792]{1,0:T(8,128)S(1)}, u32[]{:S(2)}, u32[]{:S(2)}) collective-permute-start(f32[8,1792]{1,0:T(8,128)S(1)} %get-tuple-element.85), channel_id=1, source_target_pairs={{0,16},{4,20},{8,24},{12,28},{16,0},{20,4},{24,8},{28,12},{1,17},{... | collective-permute-start | bytes 172040 | tf_op jit(solution)/shard_map/ppermute | solution.py:229
  46.5 10.4 %collective-permute-start.24 = (f32[8,1792]{1,0:T(8,128)S(1)}, f32[8,1792]{1,0:T(8,128)S(1)}, u32[]{:S(2)}, u32[]{:S(2)}) collective-permute-start(f32[8,1792]{1,0:T(8,128)S(1)} %get-tuple-element.86), channel_id=1, source_target_pairs={{0,16},{4,20},{8,24},{12,28},{16,0},{20,4},{24,8},{28,12},{1,17},{... | collective-permute-start | bytes 172040 | tf_op jit(solution)/shard_map/ppermute | solution.py:229
  47.4 9.4 %collective-permute-start.25 = (f32[8,1792]{1,0:T(8,128)S(1)}, f32[8,1792]{1,0:T(8,128)S(1)}, u32[]{:S(2)}, u32[]{:S(2)}) collective-permute-start(f32[8,1792]{1,0:T(8,128)S(1)} %get-tuple-element.87), channel_id=1, source_target_pairs={{0,16},{4,20},{8,24},{12,28},{16,0},{20,4},{24,8},{28,12},{1,17},{... | collective-permute-start | bytes 172040 | tf_op jit(solution)/shard_map/ppermute | solution.py:229
  52.4 5.2 %collective-permute-start.27 = (f32[8,1792]{1,0:T(8,128)S(1)}, f32[8,1792]{1,0:T(8,128)S(1)}, u32[]{:S(2)}, u32[]{:S(2)}) collective-permute-start(f32[8,1792]{1,0:T(8,128)S(1)} %get-tuple-element.91), channel_id=1, source_target_pairs={{0,16},{4,20},{8,24},{12,28},{16,0},{20,4},{24,8},{28,12},{1,17},{... | collective-permute-start | bytes 172040 | tf_op jit(solution)/shard_map/ppermute | solution.py:229
  52.5 5.1 %collective-permute-start.28 = (f32[8,1792]{1,0:T(8,128)S(1)}, f32[8,1792]{1,0:T(8,128)S(1)}, u32[]{:S(2)}, u32[]{:S(2)}) collective-permute-start(f32[8,1792]{1,0:T(8,128)S(1)} %get-tuple-element.92), channel_id=1, source_target_pairs={{0,8},{4,12},{8,0},{12,4},{16,24},{20,28},{24,16},{28,20},{1,9},{5... | collective-permute-start | bytes 172040 | tf_op jit(solution)/shard_map/ppermute | solution.py:229
  54.2 6.0 %collective-permute-start.29 = (f32[8,1792]{1,0:T(8,128)S(1)}, f32[8,1792]{1,0:T(8,128)S(1)}, u32[]{:S(2)}, u32[]{:S(2)}) collective-permute-start(f32[8,1792]{1,0:T(8,128)S(1)} %get-tuple-element.93), channel_id=1, source_target_pairs={{0,24},{4,28},{8,16},{12,20},{16,8},{20,12},{24,0},{28,4},{1,25},{... | collective-permute-start | bytes 172040 | tf_op jit(solution)/shard_map/ppermute | solution.py:229

commit v9 on v7

--- a/solution.py
+++ b/solution.py
@@ -9,13 +9,14 @@
 
 EIGHTHS = (2, 2, 2, 2)
 BLOCK = 512
+STREAM = 256
 F32 = jnp.float32
 BF16 = jnp.bfloat16
 NT = (((1,), (1,)), ((), ()))
 SPECS = {"v": pl.BlockSpec(memory_space=pltpu.VMEM), "a": pl.BlockSpec(memory_space=pl.ANY)}
-ORDER = ('own0', 'before0', 'send0', 'own1', 'before1', 'send1', 'add0.1', 'own2', 'before2', 'send2', 'add1.1', 'own3', 'before3', 'send3', 'add2.1', 'add1.2', 'add0.2', 'add2.2', 'sketch', 'add3.1')
+ORDER = ('own0', 'before0', 'send0', 'own1', 'before1', 'send1', 'add0.1', 'own2', 'before2', 'send2', 'own3', 'add1.1', 'add0.2', 'before3', 'send3', 'add2.1', 'add1.2', 'add2.2', 'add3.1', 'sketch')
 REST_PARTS = 4
-WEIGHTS = {'add2.1': 500000000, 'F': 500000000, 'send1': 0, 'send0': 0, 'send3': 0, 'add2.2': 200000000, 'add0.2': 1000000000, 'own2': 500000000, 'before1': 500000000, 'add0.1': 500000000, 'before3': 2000000000, 'sketch': 500000000, 'send2': 0, 'add1.2': 200000000}
+WEIGHTS = {'add2.1': 500000000, 'F': 500000000, 'send1': 0, 'send0': 0, 'send3': 0, 'add2.2': 200000000, 'add0.2': 1000000000, 'own2': 500000000, 'before1': 0, 'add0.1': 200000000}
 SPLITS = (2, 2, 2, 2)
 GROUPS = ((0,), (1,), (2,), (3,))
 MODES = ('pairs', 'pairs', 'pairs', 'direct')
@@ -59,22 +60,21 @@
     return column
 
 
-def stream_half(delta, held, sem, mine):
+def half_copies(delta, held, sem, mine):
     rows = held.shape[0]
     parity = lax.rem(lax.axis_index("col"), 2)
     first = (parity if mine else 1 - parity) * rows
     copies = []
-    for b in range(rows // BLOCK):
-        source = delta.at[pl.ds(pl.multiple_of(first + b * BLOCK, BLOCK), BLOCK), :]
-        copies.append(pltpu.make_async_copy(source, held.at[pl.ds(b * BLOCK, BLOCK), :], sem.at[b]))
-        copies[-1].start()
+    for b in range(rows // STREAM):
+        source = delta.at[pl.ds(pl.multiple_of(first + b * STREAM, STREAM), STREAM), :]
+        copies.append(pltpu.make_async_copy(source, held.at[pl.ds(b * STREAM, STREAM), :], sem.at[b]))
     return copies
 
 
 def sketch_half(omega_t, held, copies, out):
     for b, copy in enumerate(copies):
         copy.wait()
-        block = pl.ds(b * BLOCK, BLOCK)
+        block = pl.ds(b * STREAM, STREAM)
         out[:, block] = lax.dot_general(omega_t[: out.shape[0], :], held[block, :], NT, preferred_element_type=F32)
 
 
@@ -82,17 +82,23 @@
     k = omega_t.shape[0]
     fetch = pltpu.make_async_copy(omega, omega_v, omega_sem)
     fetch.start()
-    copies = stream_half(delta, held, sem, False)
+    copies = half_copies(delta, held, sem, False)
+    copies[0].start()
     position = lax.broadcasted_iota(jnp.int32, (k, k), 0)
     column = lax.broadcasted_iota(jnp.int32, (k, k), 1)
     pick = jnp.where(column_of(position, k, n_row, pieces) == column, 1.0, 0.0).astype(BF16)
     fetch.wait()
+    for copy in copies[1:]:
+        copy.start()
     omega_t[...] = lax.dot_general(pick, omega_v[...], NT, preferred_element_type=F32).astype(BF16)
     sketch_half(omega_t, held, copies, out)
 
 
 def second_half_body(delta, omega_t, held, out, sem):
-    sketch_half(omega_t, held, stream_half(delta, held, sem, True), out)
+    copies = half_copies(delta, held, sem, True)
+    for copy in copies:
+        copy.start()
+    sketch_half(omega_t, held, copies, out)
 
 
 def rest_half_body(omega_t, held, *outs):
@@ -233,7 +239,7 @@
     bits = [1 << i for i in range(n_row.bit_length() - 1)]
 
     in_hbm = pltpu.with_memory_space_constraint(delta, pltpu.HBM)
-    sems = pltpu.SemaphoreType.DMA((half // BLOCK,))
+    sems = pltpu.SemaphoreType.DMA((half // STREAM,))
     held_other, omega_t, to_send = call(
         functools.partial(first_half_body, n_row, pieces),
         (in_hbm, pltpu.with_memory_space_constraint(omega, pltpu.HBM)),

time: 60.1 us -> 60.7 us (level)
  waiting for transfers between devices: 11.6 us -> 8.77 us
  Pallas kernels: 17.9 us -> 19.8 us
  starting transfers between devices: 29.5 us -> 31.1 us
    ppermute x30, waiting for transfers between devices: 11.6 us -> 8.77 us  [swap(): return lax.ppermute(x, axis, [(i, i ^ bit) for i in range(size)])]
    pallas_call x27, Pallas kernels: 17.9 us -> 19.8 us  [call(): pl.pallas_call(run, out_shape=[pltpu.VMEM(*o) if i >= results else jax.Sh...]
    ppermute x30, starting transfers between devices: 29.5 us -> 31.1 us  [swap(): return lax.ppermute(x, axis, [(i, i ^ bit) for i in range(size)])]
  transfers between devices with their start and end apart: 30 -> 30, of which waited for: 11 -> 10; matrix products, arithmetic and copies ran while one was open for 0% -> 0% of each run, Pallas kernels for 23% -> 24%
where the time goes in v9:
time: 60.7 us; the launch traced here: 60.5 us
  starting transfers between devices  31.1 us (51%)
  Pallas kernels  19.8 us (33%)
  waiting for transfers between devices  8.77 us (14%)
  between operations  0.91 us (1%)
    ppermute x30, starting transfers between devices, swap(): return lax.ppermute(x, axis, [(i, i ^ bit) for i in range(size)])  31.1 us
    pallas_call x27, Pallas kernels, call(): pl.pallas_call(run, out_shape=[pltpu.VMEM(*o) if i >= results else jax.Sh...  19.8 us
    ppermute x30, waiting for transfers between devices, swap(): return lax.ppermute(x, axis, [(i, i ^ bit) for i in range(size)])  8.77 us
  transfers between devices with their start and end apart: 30, of which 10 were waited for; matrix products, arithmetic and copies ran while one was open for 0% of the time, Pallas kernels for 24%

profile of v9, /device:TPU:0, one launch (start us, length us, event | category | flops | bytes accessed | tf_op | source)
XLA Modules:
  0.0 60.5 jit_solution(976886481075191626)
XLA Ops:
  0.6 4.3 %shard_map.41 = (bf16[1024,1792]{1,0:T(8,128)(2,1)S(1)}, bf16[256,1792]{1,0:T(8,128)(2,1)S(1)}, f32[64,1024]{1,0:T(8,128)S(1)}) custom-call(bf16[2048,1792]{1,0:T(8,128)(2,1)} %refs_0_.3, bf16[1792,256]{1,0:T(8,128)(2,1)} %refs_1_.1), custom_call_target="tpu_custom_call" | custom-call | tf_op jit(solution)/shard_map/pallas_call | solution.py:32
  5.4 3.6 %shard_map.42 = (bf16[1024,1792]{1,0:T(8,128)(2,1)S(1)}, f32[64,1024]{1,0:T(8,128)S(1)}) custom-call(bf16[2048,1792]{1,0:T(8,128)(2,1)} %refs_0_.3, bf16[256,1792]{1,0:T(8,128)(2,1)S(1)} %get-tuple-element.48.refs_1_.refs_0_, f32[64,1024]{1,0:T(8,128)S(1)} %get-tuple-element.49.refs_2_), custom_call_target="tpu_custom_call" | custom-call | tf_op jit(solution)/shard_map/pallas_call | solution.py:32
  9.1 2.6 %collective-permute-start.1 = (f32[64,1024]{1,0:T(8,128)S(1)}, f32[64,1024]{1,0:T(8,128)S(1)}, u32[]{:S(2)}, u32[]{:S(2)}) collective-permute-start(f32[64,1024]{1,0:T(8,128)S(1)} %shard_map.43.refs_0_.refs_2_), channel_id=1, source_target_pairs={{0,2},{1,3},{2,0},{3,1},{4,6},{5,7},{6,4},{7,5},{8,10},{9,11},{10,... | collective-permute-start | bytes 786440 | tf_op jit(solution)/shard_map/ppermute | solution.py:227
  11.7 1.3 %shard_map.45 = (f32[48,1024]{1,0:T(8,128)S(1)}, f32[48,1024]{1,0:T(8,128)S(1)}, f32[48,1024]{1,0:T(8,128)S(1)}, f32[48,1024]{1,0:T(8,128)S(1)}) custom-call(bf16[256,1792]{1,0:T(8,128)(2,1)S(1)} %get-tuple-element.48.refs_1_.refs_0_, bf16[1024,1792]{1,0:T(8,128)(2,1)S(1)} %get-tuple-element.54.refs_1_.refs_2_, f32[64,1024]{1,0:T(8,128)S(1)} %shard_map.43.refs_0_.refs_2_), custom_call_target="tpu_custom_call" | custom-call | tf_op jit(solution)/shard_map/pallas_call | solution.py:32
  14.1 1.3 %shard_map.46.refs_0_ = f32[192,1024]{1,0:T(8,128)S(1)} custom-call(bf16[256,1792]{1,0:T(8,128)(2,1)S(1)} %get-tuple-element.48.refs_1_.refs_0_, bf16[1024,1792]{1,0:T(8,128)(2,1)S(1)} %get-tuple-element.53.refs_1_.refs_2_, f32[48,1024]{1,0:T(8,128)S(1)} %get-tuple-element.55.refs_2_), custom_call_target="tpu_custom_call" | custom-call | tf_op jit(solution)/shard_map/pallas_call | solution.py:32
  15.8 3.0 %collective-permute-done.1.refs_1_ = f32[64,1024]{1,0:T(8,128)S(1)} collective-permute-done((f32[64,1024]{1,0:T(8,128)S(1)}, f32[64,1024]{1,0:T(8,128)S(1)}, u32[]{:S(2)}, u32[]{:S(2)}) %collective-permute-start.1) | collective-permute-done | bytes 262176 | tf_op jit(solution)/shard_map/ppermute | solution.py:227
  19.4 2.0 %collective-permute-start.9 = (f32[64,1024]{1,0:T(8,128)S(1)}, f32[64,1024]{1,0:T(8,128)S(1)}, u32[]{:S(2)}, u32[]{:S(2)}) collective-permute-start(f32[64,1024]{1,0:T(8,128)S(1)} %get-tuple-element.63.refs_0_), channel_id=1, source_target_pairs={{0,2},{1,3},{2,0},{3,1},{4,6},{5,7},{6,4},{7,5},{8,10},{9,11},{10,... | collective-permute-start | bytes 786440 | tf_op jit(solution)/shard_map/ppermute | solution.py:227
  21.4 0.7 %shard_map.48.refs_3_.refs_4_ = f32[64,1792]{1,0:T(8,128)S(1)} custom-call(f32[32,1024]{1,0:T(8,128)S(1)} %get-tuple-element.51.refs_0_.refs_3_, f32[32,1024]{1,0:T(8,128)S(1)} %get-tuple-element.52.refs_1_, bf16[1024,1792]{1,0:T(8,128)(2,1)S(1)} %get-tuple-element.53.refs_1_.refs_2_, f32[32,1024]{1,0:T(8,128)S(1)} %get-tuple-element.51.refs_0_.refs_3_), custom_call_target="tpu_custom_call" | custom-call | tf_op jit(solution)/shard_map/pallas_call | solution.py:32
  22.2 0.8 %shard_map.49 = (f32[32,1792]{1,0:T(8,128)S(1)}, f32[32,1792]{1,0:T(8,128)S(1)}) custom-call(f32[32,1024]{1,0:T(8,128)S(1)} %collective-permute-done.7.refs_0_.refs_8_, f32[32,1024]{1,0:T(8,128)S(1)} %collective-permute-done.8.refs_1_.refs_9_, bf16[1024,1792]{1,0:T(8,128)(2,1)S(1)} %get-tuple-element.54.refs_1_.refs_2_, ...), custom_call_target="tpu_custom_call" | custom-call | tf_op jit(solution)/shard_map/pallas_call | solution.py:32
  23.0 1.6 %collective-permute-start.10 = (f32[32,1792]{1,0:T(8,128)S(1)}, f32[32,1792]{1,0:T(8,128)S(1)}, u32[]{:S(2)}, u32[]{:S(2)}) collective-permute-start(f32[32,1792]{1,0:T(8,128)S(1)} %get-tuple-element.64), channel_id=1, source_target_pairs={{0,4},{4,0},{8,12},{12,8},{16,20},{20,16},{24,28},{28,24},{1,5},{5... | collective-permute-start | bytes 688136 | tf_op jit(solution)/shard_map/ppermute | solution.py:227
  25.4 1.6 %collective-permute-start.13 = (f32[64,1024]{1,0:T(8,128)S(1)}, f32[64,1024]{1,0:T(8,128)S(1)}, u32[]{:S(2)}, u32[]{:S(2)}) collective-permute-start(f32[64,1024]{1,0:T(8,128)S(1)} %get-tuple-element.69.refs_0_), channel_id=1, source_target_pairs={{0,2},{1,3},{2,0},{3,1},{4,6},{5,7},{6,4},{7,5},{8,10},{9,11},{10,... | collective-permute-start | bytes 786440 | tf_op jit(solution)/shard_map/ppermute | solution.py:227
  27.0 0.7 %shard_map.51.refs_3_.refs_4_ = f32[64,1792]{1,0:T(8,128)S(1)} custom-call(f32[32,1024]{1,0:T(8,128)S(1)} %get-tuple-element.61.refs_0_.refs_3_.refs_2_, f32[32,1024]{1,0:T(8,128)S(1)} %get-tuple-element.62.refs_1_.refs_3_, bf16[1024,1792]{1,0:T(8,128)(2,1)S(1)} %get-tuple-element.53.refs_1_.refs_2_, f32[32,1024]{1,0:T(8,128)S(1)} %get-tuple-element.61.refs_0_.refs_3_.refs_2_), custom_call_target="tpu_custom_call" | custom-call | tf_op jit(solution)/shard_map/pallas_call | solution.py:32
  27.8 0.8 %shard_map.52 = (f32[32,1792]{1,0:T(8,128)S(1)}, f32[32,1792]{1,0:T(8,128)S(1)}) custom-call(f32[32,1024]{1,0:T(8,128)S(1)} %collective-permute-done.11.refs_0_.refs_10_, f32[32,1024]{1,0:T(8,128)S(1)} %collective-permute-done.12.refs_1_.refs_11_, bf16[1024,1792]{1,0:T(8,128)(2,1)S(1)} %get-tuple-element.54.refs_1_.refs_2_, ...), custom_call_target="tpu_custom_call" | custom-call | tf_op jit(solution)/shard_map/pallas_call | solution.py:32
  28.6 1.6 %collective-permute-start.19 = (f32[32,1792]{1,0:T(8,128)S(1)}, f32[32,1792]{1,0:T(8,128)S(1)}, u32[]{:S(2)}, u32[]{:S(2)}) collective-permute-start(f32[32,1792]{1,0:T(8,128)S(1)} %get-tuple-element.74), channel_id=1, source_target_pairs={{0,4},{4,0},{8,12},{12,8},{16,20},{20,16},{24,28},{28,24},{1,5},{5... | collective-permute-start | bytes 688136 | tf_op jit(solution)/shard_map/ppermute | solution.py:227
  31.0 1.7 %collective-permute-start.18 = (f32[16,1792]{1,0:T(8,128)S(1)}, f32[16,1792]{1,0:T(8,128)S(1)}, u32[]{:S(2)}, u32[]{:S(2)}) collective-permute-start(f32[16,1792]{1,0:T(8,128)S(1)} %get-tuple-element.73), channel_id=1, source_target_pairs={{0,8},{4,12},{8,0},{12,4},{16,24},{20,28},{24,16},{28,20},{1,9},{5... | collective-permute-start | bytes 344072 | tf_op jit(solution)/shard_map/ppermute | solution.py:227
  32.7 0.7 %shard_map.55.refs_3_.refs_4_ = f32[64,1792]{1,0:T(8,128)S(1)} custom-call(f32[32,1024]{1,0:T(8,128)S(1)} %get-tuple-element.67.refs_0_.refs_3_.refs_4_, f32[32,1024]{1,0:T(8,128)S(1)} %get-tuple-element.68.refs_1_.refs_5_, bf16[1024,1792]{1,0:T(8,128)(2,1)S(1)} %get-tuple-element.53.refs_1_.refs_2_, f32[32,1024]{1,0:T(8,128)S(1)} %get-tuple-element.67.refs_0_.refs_3_.refs_4_), custom_call_target="tpu_custom_call" | custom-call | tf_op jit(solution)/shard_map/pallas_call | solution.py:32
  33.5 0.8 %shard_map.56 = (f32[32,1792]{1,0:T(8,128)S(1)}, f32[32,1792]{1,0:T(8,128)S(1)}) custom-call(f32[32,1024]{1,0:T(8,128)S(1)} %collective-permute-done.14.refs_0_.refs_12_, f32[32,1024]{1,0:T(8,128)S(1)} %collective-permute-done.15.refs_1_.refs_13_, bf16[1024,1792]{1,0:T(8,128)(2,1)S(1)} %get-tuple-element.54.refs_1_.refs_2_, ...), custom_call_target="tpu_custom_call" | custom-call | tf_op jit(solution)/shard_map/pallas_call | solution.py:32
  34.3 1.6 %collective-permute-start.21 = (f32[32,1792]{1,0:T(8,128)S(1)}, f32[32,1792]{1,0:T(8,128)S(1)}, u32[]{:S(2)}, u32[]{:S(2)}) collective-permute-start(f32[32,1792]{1,0:T(8,128)S(1)} %get-tuple-element.79), channel_id=1, source_target_pairs={{0,4},{4,0},{8,12},{12,8},{16,20},{20,16},{24,28},{28,24},{1,5},{5... | collective-permute-start | bytes 688136 | tf_op jit(solution)/shard_map/ppermute | solution.py:227
  36.6 0.7 %shard_map.60.refs_3_.refs_4_ = f32[64,1792]{1,0:T(8,128)S(1)} custom-call(f32[32,1024]{1,0:T(8,128)S(1)} %get-tuple-element.71.refs_2_.refs_0_.refs_6_, f32[32,1024]{1,0:T(8,128)S(1)} %get-tuple-element.72.refs_1_.refs_7_, bf16[1024,1792]{1,0:T(8,128)(2,1)S(1)} %get-tuple-element.53.refs_1_.refs_2_, f32[8,1792]{1,0:T(8,128)S(1)} %get-tuple-element.76.refs_3_.refs_0_), custom_call_target="tpu_custom_call" | custom-call | tf_op jit(solution)/shard_map/pallas_call | solution.py:32
  37.5 0.8 %shard_map.61 = (f32[32,1792]{1,0:T(8,128)S(1)}, f32[32,1792]{1,0:T(8,128)S(1)}) custom-call(f32[32,1024]{1,0:T(8,128)S(1)} %collective-permute-done.16.refs_0_.refs_14_, f32[32,1024]{1,0:T(8,128)S(1)} %collective-permute-done.17.refs_1_.refs_15_, bf16[1024,1792]{1,0:T(8,128)(2,1)S(1)} %get-tuple-element.54.refs_1_.refs_2_, ...), custom_call_target="tpu_custom_call" | custom-call | tf_op jit(solution)/shard_map/pallas_call | solution.py:32
  38.3 1.5 %collective-permute-start.20 = (f32[32,1792]{1,0:T(8,128)S(1)}, f32[32,1792]{1,0:T(8,128)S(1)}, u32[]{:S(2)}, u32[]{:S(2)}) collective-permute-start(f32[32,1792]{1,0:T(8,128)S(1)} %get-tuple-element.78), channel_id=1, source_target_pairs={{0,4},{4,0},{8,12},{12,8},{16,20},{20,16},{24,28},{28,24},{1,5},{5... | collective-permute-start | bytes 688136 | tf_op jit(solution)/shard_map/ppermute | solution.py:227
  39.8 1.6 %collective-permute-start.23 = (f32[16,1792]{1,0:T(8,128)S(1)}, f32[16,1792]{1,0:T(8,128)S(1)}, u32[]{:S(2)}, u32[]{:S(2)}) collective-permute-start(f32[16,1792]{1,0:T(8,128)S(1)} %get-tuple-element.82), channel_id=1, source_target_pairs={{0,8},{4,12},{8,0},{12,4},{16,24},{20,28},{24,16},{28,20},{1,9},{5... | collective-permute-start | bytes 344072 | tf_op jit(solution)/shard_map/ppermute | solution.py:227
  42.6 2.6 %collective-permute-start.24 = (f32[8,1792]{1,0:T(8,128)S(1)}, f32[8,1792]{1,0:T(8,128)S(1)}, u32[]{:S(2)}, u32[]{:S(2)}) collective-permute-start(f32[8,1792]{1,0:T(8,128)S(1)} %get-tuple-element.87), channel_id=1, source_target_pairs={{0,16},{4,20},{8,24},{12,28},{16,0},{20,4},{24,8},{28,12},{1,17},{... | collective-permute-start | bytes 172040 | tf_op jit(solution)/shard_map/ppermute | solution.py:227
  45.2 1.2 %collective-permute-done.23.refs_1_ = f32[16,1792]{1,0:T(8,128)S(1)} collective-permute-done((f32[16,1792]{1,0:T(8,128)S(1)}, f32[16,1792]{1,0:T(8,128)S(1)}, u32[]{:S(2)}, u32[]{:S(2)}) %collective-permute-start.23) | collective-permute-done | bytes 114720 | tf_op jit(solution)/shard_map/ppermute | solution.py:227
  46.4 2.0 %collective-permute-start.25 = (f32[8,1792]{1,0:T(8,128)S(1)}, f32[8,1792]{1,0:T(8,128)S(1)}, u32[]{:S(2)}, u32[]{:S(2)}) collective-permute-start(f32[8,1792]{1,0:T(8,128)S(1)} %get-tuple-element.88), channel_id=1, source_target_pairs={{0,16},{4,20},{8,24},{12,28},{16,0},{20,4},{24,8},{28,12},{1,17},{... | collective-permute-start | bytes 172040 | tf_op jit(solution)/shard_map/ppermute | solution.py:227
  49.2 1.7 %collective-permute-start.26 = (f32[8,1792]{1,0:T(8,128)S(1)}, f32[8,1792]{1,0:T(8,128)S(1)}, u32[]{:S(2)}, u32[]{:S(2)}) collective-permute-start(f32[8,1792]{1,0:T(8,128)S(1)} %get-tuple-element.89), channel_id=1, source_target_pairs={{0,16},{4,20},{8,24},{12,28},{16,0},{20,4},{24,8},{28,12},{1,17},{... | collective-permute-start | bytes 172040 | tf_op jit(solution)/shard_map/ppermute | solution.py:227
  50.9 1.3 %collective-permute-start.27 = (f32[8,1792]{1,0:T(8,128)S(1)}, f32[8,1792]{1,0:T(8,128)S(1)}, u32[]{:S(2)}, u32[]{:S(2)}) collective-permute-start(f32[8,1792]{1,0:T(8,128)S(1)} %get-tuple-element.90), channel_id=1, source_target_pairs={{0,16},{4,20},{8,24},{12,28},{16,0},{20,4},{24,8},{28,12},{1,17},{... | collective-permute-start | bytes 172040 | tf_op jit(solution)/shard_map/ppermute | solution.py:227
  52.3 1.5 %collective-permute-start.28 = (f32[8,1792]{1,0:T(8,128)S(1)}, f32[8,1792]{1,0:T(8,128)S(1)}, u32[]{:S(2)}, u32[]{:S(2)}) collective-permute-start(f32[8,1792]{1,0:T(8,128)S(1)} %get-tuple-element.91), channel_id=1, source_target_pairs={{0,8},{4,12},{8,0},{12,4},{16,24},{20,28},{24,16},{28,20},{1,9},{5... | collective-permute-start | bytes 172040 | tf_op jit(solution)/shard_map/ppermute | solution.py:227
  53.8 1.6 %collective-permute-start.29 = (f32[8,1792]{1,0:T(8,128)S(1)}, f32[8,1792]{1,0:T(8,128)S(1)}, u32[]{:S(2)}, u32[]{:S(2)}) collective-permute-start(f32[8,1792]{1,0:T(8,128)S(1)} %get-tuple-element.92), channel_id=1, source_target_pairs={{0,24},{4,28},{8,16},{12,20},{16,8},{20,12},{24,0},{28,4},{1,25},{... | collective-permute-start | bytes 172040 | tf_op jit(solution)/shard_map/ppermute | solution.py:227
  55.4 1.9 %shard_map.66 = (f32[2048,256]{1,0:T(8,128)}, f32[8,128]{1,0:T(8,128)S(1)}) custom-call(f32[32,1024]{1,0:T(8,128)S(1)} %get-tuple-element.51.refs_0_.refs_3_, f32[32,1024]{1,0:T(8,128)S(1)} %get-tuple-element.52.refs_1_, f32[32,1024]{1,0:T(8,128)S(1)} %get-tuple-element.61.refs_0_.refs_3_.refs_2_, f32[32,1024]{1,0:T(8,128)S(1)} %get-tuple-element.62.refs_1_.refs_3_, ...), custom_call_target="tpu_custom_call" | custom-call | tf_op jit(solution)/shard_map/pallas_call | solution.py:32
  57.5 1.1 %collective-permute-done.27.refs_7_ = f32[8,1792]{1,0:T(8,128)S(1)} collective-permute-done((f32[8,1792]{1,0:T(8,128)S(1)}, f32[8,1792]{1,0:T(8,128)S(1)}, u32[]{:S(2)}, u32[]{:S(2)}) %collective-permute-start.27) | collective-permute-done | bytes 57376 | tf_op jit(solution)/shard_map/ppermute | solution.py:227
  58.6 1.2 %collective-permute-done.29.refs_9_ = f32[8,1792]{1,0:T(8,128)S(1)} collective-permute-done((f32[8,1792]{1,0:T(8,128)S(1)}, f32[8,1792]{1,0:T(8,128)S(1)}, u32[]{:S(2)}, u32[]{:S(2)}) %collective-permute-start.29) | collective-permute-done | bytes 57376 | tf_op jit(solution)/shard_map/ppermute | solution.py:227
  (55 shorter events, 7.9 us)
Async XLA Ops:
  4.9 4.2 %collective-permute-start = (f32[64,1024]{1,0:T(8,128)S(1)}, f32[64,1024]{1,0:T(8,128)S(1)}, u32[]{:S(2)}, u32[]{:S(2)}) collective-permute-start(f32[64,1024]{1,0:T(8,128)S(1)} %get-tuple-element.49.refs_2_), channel_id=1, source_target_pairs={{0,1},{1,0},{2,3},{3,2},{4,5},{5,4},{6,7},{7,6},{8,9},{9,8},{10,11... | collective-permute-start | bytes 786440 | tf_op jit(solution)/shard_map/ppermute | solution.py:227
  9.1 9.7 %collective-permute-start.1 = (f32[64,1024]{1,0:T(8,128)S(1)}, f32[64,1024]{1,0:T(8,128)S(1)}, u32[]{:S(2)}, u32[]{:S(2)}) collective-permute-start(f32[64,1024]{1,0:T(8,128)S(1)} %shard_map.43.refs_0_.refs_2_), channel_id=1, source_target_pairs={{0,2},{1,3},{2,0},{3,1},{4,6},{5,7},{6,4},{7,5},{8,10},{9,11},{10,... | collective-permute-start | bytes 786440 | tf_op jit(solution)/shard_map/ppermute | solution.py:227
  13.0 2.4 %collective-permute-start.2 = (f32[48,1024]{1,0:T(8,128)S(1)}, f32[48,1024]{1,0:T(8,128)S(1)}, u32[]{:S(2)}, u32[]{:S(2)}) collective-permute-start(f32[48,1024]{1,0:T(8,128)S(1)} %get-tuple-element.55.refs_2_), channel_id=1, source_target_pairs={{0,1},{1,0},{2,3},{3,2},{4,5},{5,4},{6,7},{7,6},{8,9},{9,8},{10,11... | collective-permute-start | bytes 589832 | tf_op jit(solution)/shard_map/ppermute | solution.py:227
  13.3 2.2 %collective-permute-start.3 = (f32[48,1024]{1,0:T(8,128)S(1)}, f32[48,1024]{1,0:T(8,128)S(1)}, u32[]{:S(2)}, u32[]{:S(2)}) collective-permute-start(f32[48,1024]{1,0:T(8,128)S(1)} %get-tuple-element.56), channel_id=1, source_target_pairs={{0,1},{1,0},{2,3},{3,2},{4,5},{5,4},{6,7},{7,6},{8,9},{9,8},{10,11... | collective-permute-start | bytes 589832 | tf_op jit(solution)/shard_map/ppermute | solution.py:227
  13.6 1.9 %collective-permute-start.4 = (f32[48,1024]{1,0:T(8,128)S(1)}, f32[48,1024]{1,0:T(8,128)S(1)}, u32[]{:S(2)}, u32[]{:S(2)}) collective-permute-start(f32[48,1024]{1,0:T(8,128)S(1)} %get-tuple-element.57), channel_id=1, source_target_pairs={{0,1},{1,0},{2,3},{3,2},{4,5},{5,4},{6,7},{7,6},{8,9},{9,8},{10,11... | collective-permute-start | bytes 589832 | tf_op jit(solution)/shard_map/ppermute | solution.py:227
  13.8 1.7 %collective-permute-start.5 = (f32[48,1024]{1,0:T(8,128)S(1)}, f32[48,1024]{1,0:T(8,128)S(1)}, u32[]{:S(2)}, u32[]{:S(2)}) collective-permute-start(f32[48,1024]{1,0:T(8,128)S(1)} %get-tuple-element.58), channel_id=1, source_target_pairs={{0,1},{1,0},{2,3},{3,2},{4,5},{5,4},{6,7},{7,6},{8,9},{9,8},{10,11... | collective-permute-start | bytes 589832 | tf_op jit(solution)/shard_map/ppermute | solution.py:227
  15.6 9.2 %collective-permute-start.6 = (f32[64,1024]{1,0:T(8,128)S(1)}, f32[64,1024]{1,0:T(8,128)S(1)}, u32[]{:S(2)}, u32[]{:S(2)}) collective-permute-start(f32[64,1024]{1,0:T(8,128)S(1)} %get-tuple-element.59.refs_0_), channel_id=1, source_target_pairs={{0,2},{1,3},{2,0},{3,1},{4,6},{5,7},{6,4},{7,5},{8,10},{9,11},{10,... | collective-permute-start | bytes 786440 | tf_op jit(solution)/shard_map/ppermute | solution.py:227
  18.8 3.4 %collective-permute-start.7 = (f32[32,1024]{1,0:T(8,128)S(1)}, f32[32,1024]{1,0:T(8,128)S(1)}, u32[]{:S(2)}, u32[]{:S(2)}) collective-permute-start(f32[32,1024]{1,0:T(8,128)S(1)} %get-tuple-element.51.refs_0_.refs_3_), channel_id=1, source_target_pairs={{0,1},{1,0},{2,3},{3,2},{4,5},{5,4},{6,7},{7,6},{8,9},{9,8},{10,11... | collective-permute-start | bytes 393224 | tf_op jit(solution)/shard_map/ppermute | solution.py:227
  18.9 3.3 %collective-permute-start.8 = (f32[32,1024]{1,0:T(8,128)S(1)}, f32[32,1024]{1,0:T(8,128)S(1)}, u32[]{:S(2)}, u32[]{:S(2)}) collective-permute-start(f32[32,1024]{1,0:T(8,128)S(1)} %get-tuple-element.52.refs_1_), channel_id=1, source_target_pairs={{0,1},{1,0},{2,3},{3,2},{4,5},{5,4},{6,7},{7,6},{8,9},{9,8},{10,11... | collective-permute-start | bytes 393224 | tf_op jit(solution)/shard_map/ppermute | solution.py:227
  19.4 11.0 %collective-permute-start.9 = (f32[64,1024]{1,0:T(8,128)S(1)}, f32[64,1024]{1,0:T(8,128)S(1)}, u32[]{:S(2)}, u32[]{:S(2)}) collective-permute-start(f32[64,1024]{1,0:T(8,128)S(1)} %get-tuple-element.63.refs_0_), channel_id=1, source_target_pairs={{0,2},{1,3},{2,0},{3,1},{4,6},{5,7},{6,4},{7,5},{8,10},{9,11},{10,... | collective-permute-start | bytes 786440 | tf_op jit(solution)/shard_map/ppermute | solution.py:227
  23.0 7.4 %collective-permute-start.10 = (f32[32,1792]{1,0:T(8,128)S(1)}, f32[32,1792]{1,0:T(8,128)S(1)}, u32[]{:S(2)}, u32[]{:S(2)}) collective-permute-start(f32[32,1792]{1,0:T(8,128)S(1)} %get-tuple-element.64), channel_id=1, source_target_pairs={{0,4},{4,0},{8,12},{12,8},{16,20},{20,16},{24,28},{28,24},{1,5},{5... | collective-permute-start | bytes 688136 | tf_op jit(solution)/shard_map/ppermute | solution.py:227
  24.9 2.9 %collective-permute-start.11 = (f32[32,1024]{1,0:T(8,128)S(1)}, f32[32,1024]{1,0:T(8,128)S(1)}, u32[]{:S(2)}, u32[]{:S(2)}) collective-permute-start(f32[32,1024]{1,0:T(8,128)S(1)} %get-tuple-element.61.refs_0_.refs_3_.refs_2_), channel_id=1, source_target_pairs={{0,1},{1,0},{2,3},{3,2},{4,5},{5,4},{6,7},{7,6},{8,9},{9,8},{10,11... | collective-permute-start | bytes 393224 | tf_op jit(solution)/shard_map/ppermute | solution.py:227
  24.9 2.9 %collective-permute-start.12 = (f32[32,1024]{1,0:T(8,128)S(1)}, f32[32,1024]{1,0:T(8,128)S(1)}, u32[]{:S(2)}, u32[]{:S(2)}) collective-permute-start(f32[32,1024]{1,0:T(8,128)S(1)} %get-tuple-element.62.refs_1_.refs_3_), channel_id=1, source_target_pairs={{0,1},{1,0},{2,3},{3,2},{4,5},{5,4},{6,7},{7,6},{8,9},{9,8},{10,11... | collective-permute-start | bytes 393224 | tf_op jit(solution)/shard_map/ppermute | solution.py:227
  25.4 10.5 %collective-permute-start.13 = (f32[64,1024]{1,0:T(8,128)S(1)}, f32[64,1024]{1,0:T(8,128)S(1)}, u32[]{:S(2)}, u32[]{:S(2)}) collective-permute-start(f32[64,1024]{1,0:T(8,128)S(1)} %get-tuple-element.69.refs_0_), channel_id=1, source_target_pairs={{0,2},{1,3},{2,0},{3,1},{4,6},{5,7},{6,4},{7,5},{8,10},{9,11},{10,... | collective-permute-start | bytes 786440 | tf_op jit(solution)/shard_map/ppermute | solution.py:227
  28.6 7.9 %collective-permute-start.19 = (f32[32,1792]{1,0:T(8,128)S(1)}, f32[32,1792]{1,0:T(8,128)S(1)}, u32[]{:S(2)}, u32[]{:S(2)}) collective-permute-start(f32[32,1792]{1,0:T(8,128)S(1)} %get-tuple-element.74), channel_id=1, source_target_pairs={{0,4},{4,0},{8,12},{12,8},{16,20},{20,16},{24,28},{28,24},{1,5},{5... | collective-permute-start | bytes 688136 | tf_op jit(solution)/shard_map/ppermute | solution.py:227
  30.5 3.0 %collective-permute-start.14 = (f32[32,1024]{1,0:T(8,128)S(1)}, f32[32,1024]{1,0:T(8,128)S(1)}, u32[]{:S(2)}, u32[]{:S(2)}) collective-permute-start(f32[32,1024]{1,0:T(8,128)S(1)} %get-tuple-element.67.refs_0_.refs_3_.refs_4_), channel_id=1, source_target_pairs={{0,1},{1,0},{2,3},{3,2},{4,5},{5,4},{6,7},{7,6},{8,9},{9,8},{10,11... | collective-permute-start | bytes 393224 | tf_op jit(solution)/shard_map/ppermute | solution.py:227
  30.5 3.0 %collective-permute-start.15 = (f32[32,1024]{1,0:T(8,128)S(1)}, f32[32,1024]{1,0:T(8,128)S(1)}, u32[]{:S(2)}, u32[]{:S(2)}) collective-permute-start(f32[32,1024]{1,0:T(8,128)S(1)} %get-tuple-element.68.refs_1_.refs_5_), channel_id=1, source_target_pairs={{0,1},{1,0},{2,3},{3,2},{4,5},{5,4},{6,7},{7,6},{8,9},{9,8},{10,11... | collective-permute-start | bytes 393224 | tf_op jit(solution)/shard_map/ppermute | solution.py:227
  31.0 5.5 %collective-permute-start.18 = (f32[16,1792]{1,0:T(8,128)S(1)}, f32[16,1792]{1,0:T(8,128)S(1)}, u32[]{:S(2)}, u32[]{:S(2)}) collective-permute-start(f32[16,1792]{1,0:T(8,128)S(1)} %get-tuple-element.73), channel_id=1, source_target_pairs={{0,8},{4,12},{8,0},{12,4},{16,24},{20,28},{24,16},{28,20},{1,9},{5... | collective-permute-start | bytes 344072 | tf_op jit(solution)/shard_map/ppermute | solution.py:227
  34.3 7.7 %collective-permute-start.21 = (f32[32,1792]{1,0:T(8,128)S(1)}, f32[32,1792]{1,0:T(8,128)S(1)}, u32[]{:S(2)}, u32[]{:S(2)}) collective-permute-start(f32[32,1792]{1,0:T(8,128)S(1)} %get-tuple-element.79), channel_id=1, source_target_pairs={{0,4},{4,0},{8,12},{12,8},{16,20},{20,16},{24,28},{28,24},{1,5},{5... | collective-permute-start | bytes 688136 | tf_op jit(solution)/shard_map/ppermute | solution.py:227
  35.9 1.4 %collective-permute-start.16 = (f32[32,1024]{1,0:T(8,128)S(1)}, f32[32,1024]{1,0:T(8,128)S(1)}, u32[]{:S(2)}, u32[]{:S(2)}) collective-permute-start(f32[32,1024]{1,0:T(8,128)S(1)} %get-tuple-element.71.refs_2_.refs_0_.refs_6_), channel_id=1, source_target_pairs={{0,1},{1,0},{2,3},{3,2},{4,5},{5,4},{6,7},{7,6},{8,9},{9,8},{10,11... | collective-permute-start | bytes 393224 | tf_op jit(solution)/shard_map/ppermute | solution.py:227
  36.0 1.5 %collective-permute-start.17 = (f32[32,1024]{1,0:T(8,128)S(1)}, f32[32,1024]{1,0:T(8,128)S(1)}, u32[]{:S(2)}, u32[]{:S(2)}) collective-permute-start(f32[32,1024]{1,0:T(8,128)S(1)} %get-tuple-element.72.refs_1_.refs_7_), channel_id=1, source_target_pairs={{0,1},{1,0},{2,3},{3,2},{4,5},{5,4},{6,7},{7,6},{8,9},{9,8},{10,11... | collective-permute-start | bytes 393224 | tf_op jit(solution)/shard_map/ppermute | solution.py:227
  38.3 12.6 %collective-permute-start.20 = (f32[32,1792]{1,0:T(8,128)S(1)}, f32[32,1792]{1,0:T(8,128)S(1)}, u32[]{:S(2)}, u32[]{:S(2)}) collective-permute-start(f32[32,1792]{1,0:T(8,128)S(1)} %get-tuple-element.78), channel_id=1, source_target_pairs={{0,4},{4,0},{8,12},{12,8},{16,20},{20,16},{24,28},{28,24},{1,5},{5... | collective-permute-start | bytes 688136 | tf_op jit(solution)/shard_map/ppermute | solution.py:227
  39.8 6.6 %collective-permute-start.23 = (f32[16,1792]{1,0:T(8,128)S(1)}, f32[16,1792]{1,0:T(8,128)S(1)}, u32[]{:S(2)}, u32[]{:S(2)}) collective-permute-start(f32[16,1792]{1,0:T(8,128)S(1)} %get-tuple-element.82), channel_id=1, source_target_pairs={{0,8},{4,12},{8,0},{12,4},{16,24},{20,28},{24,16},{28,20},{1,9},{5... | collective-permute-start | bytes 344072 | tf_op jit(solution)/shard_map/ppermute | solution.py:227
  42.0 7.1 %collective-permute-start.22 = (f32[16,1792]{1,0:T(8,128)S(1)}, f32[16,1792]{1,0:T(8,128)S(1)}, u32[]{:S(2)}, u32[]{:S(2)}) collective-permute-start(f32[16,1792]{1,0:T(8,128)S(1)} %get-tuple-element.81), channel_id=1, source_target_pairs={{0,8},{4,12},{8,0},{12,4},{16,24},{20,28},{24,16},{28,20},{1,9},{5... | collective-permute-start | bytes 344072 | tf_op jit(solution)/shard_map/ppermute | solution.py:227
  42.6 11.2 %collective-permute-start.24 = (f32[8,1792]{1,0:T(8,128)S(1)}, f32[8,1792]{1,0:T(8,128)S(1)}, u32[]{:S(2)}, u32[]{:S(2)}) collective-permute-start(f32[8,1792]{1,0:T(8,128)S(1)} %get-tuple-element.87), channel_id=1, source_target_pairs={{0,16},{4,20},{8,24},{12,28},{16,0},{20,4},{24,8},{28,12},{1,17},{... | collective-permute-start | bytes 172040 | tf_op jit(solution)/shard_map/ppermute | solution.py:227
  46.4 10.9 %collective-permute-start.25 = (f32[8,1792]{1,0:T(8,128)S(1)}, f32[8,1792]{1,0:T(8,128)S(1)}, u32[]{:S(2)}, u32[]{:S(2)}) collective-permute-start(f32[8,1792]{1,0:T(8,128)S(1)} %get-tuple-element.88), channel_id=1, source_target_pairs={{0,16},{4,20},{8,24},{12,28},{16,0},{20,4},{24,8},{28,12},{1,17},{... | collective-permute-start | bytes 172040 | tf_op jit(solution)/shard_map/ppermute | solution.py:227
  49.2 8.3 %collective-permute-start.26 = (f32[8,1792]{1,0:T(8,128)S(1)}, f32[8,1792]{1,0:T(8,128)S(1)}, u32[]{:S(2)}, u32[]{:S(2)}) collective-permute-start(f32[8,1792]{1,0:T(8,128)S(1)} %get-tuple-element.89), channel_id=1, source_target_pairs={{0,16},{4,20},{8,24},{12,28},{16,0},{20,4},{24,8},{28,12},{1,17},{... | collective-permute-start | bytes 172040 | tf_op jit(solution)/shard_map/ppermute | solution.py:227
  50.9 7.6 %collective-permute-start.27 = (f32[8,1792]{1,0:T(8,128)S(1)}, f32[8,1792]{1,0:T(8,128)S(1)}, u32[]{:S(2)}, u32[]{:S(2)}) collective-permute-start(f32[8,1792]{1,0:T(8,128)S(1)} %get-tuple-element.90), channel_id=1, source_target_pairs={{0,16},{4,20},{8,24},{12,28},{16,0},{20,4},{24,8},{28,12},{1,17},{... | collective-permute-start | bytes 172040 | tf_op jit(solution)/shard_map/ppermute | solution.py:227
  52.3 6.3 %collective-permute-start.28 = (f32[8,1792]{1,0:T(8,128)S(1)}, f32[8,1792]{1,0:T(8,128)S(1)}, u32[]{:S(2)}, u32[]{:S(2)}) collective-permute-start(f32[8,1792]{1,0:T(8,128)S(1)} %get-tuple-element.91), channel_id=1, source_target_pairs={{0,8},{4,12},{8,0},{12,4},{16,24},{20,28},{24,16},{28,20},{1,9},{5... | collective-permute-start | bytes 172040 | tf_op jit(solution)/shard_map/ppermute | solution.py:227
  53.8 6.0 %collective-permute-start.29 = (f32[8,1792]{1,0:T(8,128)S(1)}, f32[8,1792]{1,0:T(8,128)S(1)}, u32[]{:S(2)}, u32[]{:S(2)}) collective-permute-start(f32[8,1792]{1,0:T(8,128)S(1)} %get-tuple-element.92), channel_id=1, source_target_pairs={{0,24},{4,28},{8,16},{12,20},{16,8},{20,12},{24,0},{28,4},{1,25},{... | collective-permute-start | bytes 172040 | tf_op jit(solution)/shard_map/ppermute | solution.py:227

commit v10 on v7

--- a/solution.py
+++ b/solution.py
@@ -13,9 +13,8 @@
 BF16 = jnp.bfloat16
 NT = (((1,), (1,)), ((), ()))
 SPECS = {"v": pl.BlockSpec(memory_space=pltpu.VMEM), "a": pl.BlockSpec(memory_space=pl.ANY)}
-ORDER = ('own0', 'before0', 'send0', 'own1', 'before1', 'send1', 'add0.1', 'own2', 'before2', 'send2', 'add1.1', 'own3', 'before3', 'send3', 'add2.1', 'add1.2', 'add0.2', 'add2.2', 'sketch', 'add3.1')
-REST_PARTS = 4
-WEIGHTS = {'add2.1': 500000000, 'F': 500000000, 'send1': 0, 'send0': 0, 'send3': 0, 'add2.2': 200000000, 'add0.2': 1000000000, 'own2': 500000000, 'before1': 500000000, 'add0.1': 500000000, 'before3': 2000000000, 'sketch': 500000000, 'send2': 0, 'add1.2': 200000000}
+ORDER = ('own0', 'before0', 'send0', 'own1', 'before1', 'send1', 'add0.1', 'own2', 'before2', 'send2', 'own3', 'add1.1', 'add0.2', 'before3', 'send3', 'add2.1', 'add1.2', 'add2.2', 'add3.1', 'sketch')
+WEIGHTS = {'add2.1': 500000000, 'F': 500000000, 'send1': 0, 'send0': 0, 'send3': 0, 'add2.2': 200000000, 'add0.2': 1000000000, 'own2': 500000000, 'before1': 0, 'add0.1': 200000000}
 SPLITS = (2, 2, 2, 2)
 GROUPS = ((0,), (1,), (2,), (3,))
 MODES = ('pairs', 'pairs', 'pairs', 'direct')
@@ -75,11 +74,11 @@
     for b, copy in enumerate(copies):
         copy.wait()
         block = pl.ds(b * BLOCK, BLOCK)
-        out[:, block] = lax.dot_general(omega_t[: out.shape[0], :], held[block, :], NT, preferred_element_type=F32)
+        out[:, block] = lax.dot_general(omega_t[...], held[block, :], NT, preferred_element_type=F32)
 
 
 def first_half_body(n_row, pieces, delta, omega, held, omega_t, out, omega_v, sem, omega_sem):
-    k = omega_t.shape[0]
+    k = out.shape[0]
     fetch = pltpu.make_async_copy(omega, omega_v, omega_sem)
     fetch.start()
     copies = stream_half(delta, held, sem, False)
@@ -95,23 +94,11 @@
     sketch_half(omega_t, held, stream_half(delta, held, sem, True), out)
 
 
-def rest_half_body(omega_t, held, *outs):
-    rows = sum(out.shape[0] for out in outs)
-    later = omega_t[omega_t.shape[0] - rows :, :]
-    for b in range(held.shape[0] // BLOCK):
-        block = pl.ds(b * BLOCK, BLOCK)
-        found = lax.dot_general(later, held[block, :], NT, preferred_element_type=F32)
-        first = 0
-        for out in outs:
-            out[:, block] = found[first : first + out.shape[0]]
-            first += out.shape[0]
-
-
-def add_chunks_body(parts, kept, *refs):
-    received, first = joined(refs[:parts]), 0
-    for out in refs[parts:]:
+def add_chunks_body(kept, received, *outs):
+    first = 0
+    for out in outs:
         part = pl.ds(first, out.shape[0])
-        out[...] = kept[part, :] + received[first : first + out.shape[0]]
+        out[...] = kept[part, :] + received[part, :]
         first += out.shape[0]
 
 
@@ -237,21 +224,13 @@
     held_other, omega_t, to_send = call(
         functools.partial(first_half_body, n_row, pieces),
         (in_hbm, pltpu.with_memory_space_constraint(omega, pltpu.HBM)),
-        [((half, d), BF16), ((k, d), BF16), ((widths[0], half), F32)],
+        [((half, d), BF16), ((k, d), BF16), ((k, half), F32)],
         "aa",
         scratch=[pltpu.VMEM((d, k), BF16), sems, pltpu.SemaphoreType.DMA],
     )
     received = swap(to_send, "col", n_col, 1)
-    outs = [((half, d), BF16), ((widths[0], half), F32)]
-    held_own, kept = call(second_half_body, (in_hbm, omega_t), outs, "av", (to_send,), [sems])
-    partial = call(add_body, (kept, received), [((widths[0], half), F32)])
-    rest = k - widths[0]
-    outs = [((rest // REST_PARTS, half), F32)] * REST_PARTS
-    to_send = call(rest_half_body, (omega_t, held_other), outs, after=partial)
-    received = [swap(x, "col", n_col, 1) for x in to_send]
-    kept = call(rest_half_body, (omega_t, held_own), [((rest, half), F32)], after=to_send[:1])
-    outs = [((width, half), F32) for width in widths[1:]]
-    partial += call(functools.partial(add_chunks_body, REST_PARTS), (*kept, *received), outs)
+    held_own, kept = call(second_half_body, (in_hbm, omega_t), [((half, d), BF16), ((k, half), F32)], "av", scratch=[sems])
+    partial = call(add_chunks_body, (kept, received), [((width, half), F32) for width in widths])
     bit = 2
     while bit < n_col // 2:
         moved = [swap(x, "col", n_col, bit) for x in partial]
@@ -262,7 +241,7 @@
     owns, others, befores, pending = {}, {}, {}, {}
     sketch = None
     last = ()
-    planned = n == 4 and len(bits) == 3
+    planned = len(bits) == 3 and n == sum(len(group) for group in GROUPS)
     groups = GROUPS if planned else tuple((c,) for c in range(n))
     modes = MODES if planned else ("pairs",) * n
     steps = ORDER if planned else ()

time: 60.1 us -> 58.9 us (0.980)
  Pallas kernels: 17.9 us -> 15.2 us
  waiting for transfers between devices: 11.6 us -> 12.5 us
    pallas_call x27 -> x24, Pallas kernels: 17.9 us -> 15.2 us  [call(): pl.pallas_call(run, out_shape=[pltpu.VMEM(*o) if i >= results else jax.Sh...]
    ppermute x30 -> x26, waiting for transfers between devices: 11.6 us -> 12.5 us  [swap(): return lax.ppermute(x, axis, [(i, i ^ bit) for i in range(size)])]
    ppermute x30 -> x26, starting transfers between devices: 29.5 us -> 30.1 us  [swap(): return lax.ppermute(x, axis, [(i, i ^ bit) for i in range(size)])]
  transfers between devices with their start and end apart: 30 -> 26, of which waited for: 11 -> 9; matrix products, arithmetic and copies ran while one was open for 0% -> 0% of each run, Pallas kernels for 23% -> 19%
where the time goes in v10:
time: 58.9 us; the launch traced here: 58.7 us
  starting transfers between devices  30.1 us (51%)
  Pallas kernels  15.2 us (26%)
  waiting for transfers between devices  12.5 us (21%)
  between operations  0.88 us (1%)
    ppermute x26, starting transfers between devices, swap(): return lax.ppermute(x, axis, [(i, i ^ bit) for i in range(size)])  30.1 us
    pallas_call x24, Pallas kernels, call(): pl.pallas_call(run, out_shape=[pltpu.VMEM(*o) if i >= results else jax.Sh...  15.2 us
    ppermute x26, waiting for transfers between devices, swap(): return lax.ppermute(x, axis, [(i, i ^ bit) for i in range(size)])  12.5 us
  transfers between devices with their start and end apart: 26, of which 9 were waited for; matrix products, arithmetic and copies ran while one was open for 0% of the time, Pallas kernels for 19%

profile of v10, /device:TPU:0, one launch (start us, length us, event | category | flops | bytes accessed | tf_op | source)
XLA Modules:
  0.0 58.7 jit_solution(368473837006611969)
XLA Ops:
  0.6 3.2 %shard_map.41 = (bf16[1024,1792]{1,0:T(8,128)(2,1)S(1)}, bf16[256,1792]{1,0:T(8,128)(2,1)S(1)}, f32[256,1024]{1,0:T(8,128)S(1)}) custom-call(bf16[2048,1792]{1,0:T(8,128)(2,1)} %refs_0_.3, bf16[1792,256]{1,0:T(8,128)(2,1)} %refs_1_.1), custom_call_target="tpu_custom_call" | custom-call | tf_op jit(solution)/shard_map/pallas_call | solution.py:30
  4.3 2.9 %shard_map.42 = (bf16[1024,1792]{1,0:T(8,128)(2,1)S(1)}, f32[256,1024]{1,0:T(8,128)S(1)}) custom-call(bf16[2048,1792]{1,0:T(8,128)(2,1)} %refs_0_.3, bf16[256,1792]{1,0:T(8,128)(2,1)S(1)} %get-tuple-element.45.refs_1_), custom_call_target="tpu_custom_call" | custom-call | tf_op jit(solution)/shard_map/pallas_call | solution.py:30
  7.3 2.6 %collective-permute-start.1 = (f32[64,1024]{1,0:T(8,128)S(1)}, f32[64,1024]{1,0:T(8,128)S(1)}, u32[]{:S(2)}, u32[]{:S(2)}) collective-permute-start(f32[64,1024]{1,0:T(8,128)S(1)} %get-tuple-element.48.refs_0_), channel_id=1, source_target_pairs={{0,2},{1,3},{2,0},{3,1},{4,6},{5,7},{6,4},{7,5},{8,10},{9,11},{10,... | collective-permute-start | bytes 786440 | tf_op jit(solution)/shard_map/ppermute | solution.py:208
  10.0 7.1 %collective-permute-done.1.refs_1_ = f32[64,1024]{1,0:T(8,128)S(1)} collective-permute-done((f32[64,1024]{1,0:T(8,128)S(1)}, f32[64,1024]{1,0:T(8,128)S(1)}, u32[]{:S(2)}, u32[]{:S(2)}) %collective-permute-start.1) | collective-permute-done | bytes 262176 | tf_op jit(solution)/shard_map/ppermute | solution.py:208
  17.7 1.9 %collective-permute-start.5 = (f32[64,1024]{1,0:T(8,128)S(1)}, f32[64,1024]{1,0:T(8,128)S(1)}, u32[]{:S(2)}, u32[]{:S(2)}) collective-permute-start(f32[64,1024]{1,0:T(8,128)S(1)} %get-tuple-element.57.refs_0_), channel_id=1, source_target_pairs={{0,2},{1,3},{2,0},{3,1},{4,6},{5,7},{6,4},{7,5},{8,10},{9,11},{10,... | collective-permute-start | bytes 786440 | tf_op jit(solution)/shard_map/ppermute | solution.py:208
  19.6 0.7 %shard_map.45.refs_3_.refs_4_ = f32[64,1792]{1,0:T(8,128)S(1)} custom-call(f32[32,1024]{1,0:T(8,128)S(1)} %get-tuple-element.49.refs_0_.refs_3_, f32[32,1024]{1,0:T(8,128)S(1)} %get-tuple-element.50.refs_1_, bf16[1024,1792]{1,0:T(8,128)(2,1)S(1)} %get-tuple-element.53.refs_2_, f32[32,1024]{1,0:T(8,128)S(1)} %get-tuple-element.49.refs_0_.refs_3_), custom_call_target="tpu_custom_call" | custom-call | tf_op jit(solution)/shard_map/pallas_call | solution.py:30
  20.4 0.8 %shard_map.46 = (f32[32,1792]{1,0:T(8,128)S(1)}, f32[32,1792]{1,0:T(8,128)S(1)}) custom-call(f32[32,1024]{1,0:T(8,128)S(1)} %collective-permute-done.3.refs_0_.refs_8_, f32[32,1024]{1,0:T(8,128)S(1)} %collective-permute-done.4.refs_1_.refs_9_, bf16[1024,1792]{1,0:T(8,128)(2,1)S(1)} %get-tuple-element.52.refs_2_, f32[64,1792]{1,0:T(8,128)S(1)} %shard_map.45.refs_3_.refs_4_, ...), custom_call_target="tpu_custom_call" | custom-call | tf_op jit(solution)/shard_map/pallas_call | solution.py:30
  21.2 1.6 %collective-permute-start.6 = (f32[32,1792]{1,0:T(8,128)S(1)}, f32[32,1792]{1,0:T(8,128)S(1)}, u32[]{:S(2)}, u32[]{:S(2)}) collective-permute-start(f32[32,1792]{1,0:T(8,128)S(1)} %get-tuple-element.58), channel_id=1, source_target_pairs={{0,4},{4,0},{8,12},{12,8},{16,20},{20,16},{24,28},{28,24},{1,5},{5... | collective-permute-start | bytes 688136 | tf_op jit(solution)/shard_map/ppermute | solution.py:208
  23.4 1.9 %collective-permute-start.9 = (f32[64,1024]{1,0:T(8,128)S(1)}, f32[64,1024]{1,0:T(8,128)S(1)}, u32[]{:S(2)}, u32[]{:S(2)}) collective-permute-start(f32[64,1024]{1,0:T(8,128)S(1)} %get-tuple-element.63.refs_0_), channel_id=1, source_target_pairs={{0,2},{1,3},{2,0},{3,1},{4,6},{5,7},{6,4},{7,5},{8,10},{9,11},{10,... | collective-permute-start | bytes 786440 | tf_op jit(solution)/shard_map/ppermute | solution.py:208
  25.3 0.7 %shard_map.48.refs_3_.refs_4_ = f32[64,1792]{1,0:T(8,128)S(1)} custom-call(f32[32,1024]{1,0:T(8,128)S(1)} %get-tuple-element.55.refs_0_.refs_3_.refs_2_, f32[32,1024]{1,0:T(8,128)S(1)} %get-tuple-element.56.refs_1_.refs_3_, bf16[1024,1792]{1,0:T(8,128)(2,1)S(1)} %get-tuple-element.53.refs_2_, f32[32,1024]{1,0:T(8,128)S(1)} %get-tuple-element.55.refs_0_.refs_3_.refs_2_), custom_call_target="tpu_custom_call" | custom-call | tf_op jit(solution)/shard_map/pallas_call | solution.py:30
  26.0 0.8 %shard_map.49 = (f32[32,1792]{1,0:T(8,128)S(1)}, f32[32,1792]{1,0:T(8,128)S(1)}) custom-call(f32[32,1024]{1,0:T(8,128)S(1)} %collective-permute-done.7.refs_0_.refs_10_, f32[32,1024]{1,0:T(8,128)S(1)} %collective-permute-done.8.refs_1_.refs_11_, bf16[1024,1792]{1,0:T(8,128)(2,1)S(1)} %get-tuple-element.52.refs_2_, f32[64,1792]{1,0:T(8,128)S(1)} %shard_map.48.refs_3_.refs_4_, ...), custom_call_target="tpu_custom_call" | custom-call | tf_op jit(solution)/shard_map/pallas_call | solution.py:30
  26.8 1.6 %collective-permute-start.15 = (f32[32,1792]{1,0:T(8,128)S(1)}, f32[32,1792]{1,0:T(8,128)S(1)}, u32[]{:S(2)}, u32[]{:S(2)}) collective-permute-start(f32[32,1792]{1,0:T(8,128)S(1)} %get-tuple-element.68), channel_id=1, source_target_pairs={{0,4},{4,0},{8,12},{12,8},{16,20},{20,16},{24,28},{28,24},{1,5},{5... | collective-permute-start | bytes 688136 | tf_op jit(solution)/shard_map/ppermute | solution.py:208
  29.2 1.7 %collective-permute-start.14 = (f32[16,1792]{1,0:T(8,128)S(1)}, f32[16,1792]{1,0:T(8,128)S(1)}, u32[]{:S(2)}, u32[]{:S(2)}) collective-permute-start(f32[16,1792]{1,0:T(8,128)S(1)} %get-tuple-element.67), channel_id=1, source_target_pairs={{0,8},{4,12},{8,0},{12,4},{16,24},{20,28},{24,16},{28,20},{1,9},{5... | collective-permute-start | bytes 344072 | tf_op jit(solution)/shard_map/ppermute | solution.py:208
  30.9 0.7 %shard_map.52.refs_3_.refs_4_ = f32[64,1792]{1,0:T(8,128)S(1)} custom-call(f32[32,1024]{1,0:T(8,128)S(1)} %get-tuple-element.61.refs_0_.refs_3_.refs_4_, f32[32,1024]{1,0:T(8,128)S(1)} %get-tuple-element.62.refs_1_.refs_5_, bf16[1024,1792]{1,0:T(8,128)(2,1)S(1)} %get-tuple-element.53.refs_2_, f32[32,1024]{1,0:T(8,128)S(1)} %get-tuple-element.61.refs_0_.refs_3_.refs_4_), custom_call_target="tpu_custom_call" | custom-call | tf_op jit(solution)/shard_map/pallas_call | solution.py:30
  31.7 0.8 %shard_map.53 = (f32[32,1792]{1,0:T(8,128)S(1)}, f32[32,1792]{1,0:T(8,128)S(1)}) custom-call(f32[32,1024]{1,0:T(8,128)S(1)} %collective-permute-done.10.refs_0_.refs_12_, f32[32,1024]{1,0:T(8,128)S(1)} %collective-permute-done.11.refs_1_.refs_13_, bf16[1024,1792]{1,0:T(8,128)(2,1)S(1)} %get-tuple-element.52.refs_2_, ...), custom_call_target="tpu_custom_call" | custom-call | tf_op jit(solution)/shard_map/pallas_call | solution.py:30
  32.5 1.6 %collective-permute-start.17 = (f32[32,1792]{1,0:T(8,128)S(1)}, f32[32,1792]{1,0:T(8,128)S(1)}, u32[]{:S(2)}, u32[]{:S(2)}) collective-permute-start(f32[32,1792]{1,0:T(8,128)S(1)} %get-tuple-element.73), channel_id=1, source_target_pairs={{0,4},{4,0},{8,12},{12,8},{16,20},{20,16},{24,28},{28,24},{1,5},{5... | collective-permute-start | bytes 688136 | tf_op jit(solution)/shard_map/ppermute | solution.py:208
  34.8 0.7 %shard_map.57.refs_3_.refs_4_ = f32[64,1792]{1,0:T(8,128)S(1)} custom-call(f32[32,1024]{1,0:T(8,128)S(1)} %get-tuple-element.65.refs_2_.refs_0_.refs_6_, f32[32,1024]{1,0:T(8,128)S(1)} %get-tuple-element.66.refs_1_.refs_7_, bf16[1024,1792]{1,0:T(8,128)(2,1)S(1)} %get-tuple-element.53.refs_2_, f32[8,1792]{1,0:T(8,128)S(1)} %get-tuple-element.70.refs_3_.refs_0_), custom_call_target="tpu_custom_call" | custom-call | tf_op jit(solution)/shard_map/pallas_call | solution.py:30
  35.7 0.8 %shard_map.58 = (f32[32,1792]{1,0:T(8,128)S(1)}, f32[32,1792]{1,0:T(8,128)S(1)}) custom-call(f32[32,1024]{1,0:T(8,128)S(1)} %collective-permute-done.12.refs_0_.refs_14_, f32[32,1024]{1,0:T(8,128)S(1)} %collective-permute-done.13.refs_1_.refs_15_, bf16[1024,1792]{1,0:T(8,128)(2,1)S(1)} %get-tuple-element.52.refs_2_, ...), custom_call_target="tpu_custom_call" | custom-call | tf_op jit(solution)/shard_map/pallas_call | solution.py:30
  36.5 1.5 %collective-permute-start.16 = (f32[32,1792]{1,0:T(8,128)S(1)}, f32[32,1792]{1,0:T(8,128)S(1)}, u32[]{:S(2)}, u32[]{:S(2)}) collective-permute-start(f32[32,1792]{1,0:T(8,128)S(1)} %get-tuple-element.72), channel_id=1, source_target_pairs={{0,4},{4,0},{8,12},{12,8},{16,20},{20,16},{24,28},{28,24},{1,5},{5... | collective-permute-start | bytes 688136 | tf_op jit(solution)/shard_map/ppermute | solution.py:208
  38.0 1.6 %collective-permute-start.19 = (f32[16,1792]{1,0:T(8,128)S(1)}, f32[16,1792]{1,0:T(8,128)S(1)}, u32[]{:S(2)}, u32[]{:S(2)}) collective-permute-start(f32[16,1792]{1,0:T(8,128)S(1)} %get-tuple-element.76), channel_id=1, source_target_pairs={{0,8},{4,12},{8,0},{12,4},{16,24},{20,28},{24,16},{28,20},{1,9},{5... | collective-permute-start | bytes 344072 | tf_op jit(solution)/shard_map/ppermute | solution.py:208
  40.8 2.6 %collective-permute-start.20 = (f32[8,1792]{1,0:T(8,128)S(1)}, f32[8,1792]{1,0:T(8,128)S(1)}, u32[]{:S(2)}, u32[]{:S(2)}) collective-permute-start(f32[8,1792]{1,0:T(8,128)S(1)} %get-tuple-element.81), channel_id=1, source_target_pairs={{0,16},{4,20},{8,24},{12,28},{16,0},{20,4},{24,8},{28,12},{1,17},{... | collective-permute-start | bytes 172040 | tf_op jit(solution)/shard_map/ppermute | solution.py:208
  43.4 1.2 %collective-permute-done.19.refs_1_ = f32[16,1792]{1,0:T(8,128)S(1)} collective-permute-done((f32[16,1792]{1,0:T(8,128)S(1)}, f32[16,1792]{1,0:T(8,128)S(1)}, u32[]{:S(2)}, u32[]{:S(2)}) %collective-permute-start.19) | collective-permute-done | bytes 114720 | tf_op jit(solution)/shard_map/ppermute | solution.py:208
  44.6 2.0 %collective-permute-start.21 = (f32[8,1792]{1,0:T(8,128)S(1)}, f32[8,1792]{1,0:T(8,128)S(1)}, u32[]{:S(2)}, u32[]{:S(2)}) collective-permute-start(f32[8,1792]{1,0:T(8,128)S(1)} %get-tuple-element.82), channel_id=1, source_target_pairs={{0,16},{4,20},{8,24},{12,28},{16,0},{20,4},{24,8},{28,12},{1,17},{... | collective-permute-start | bytes 172040 | tf_op jit(solution)/shard_map/ppermute | solution.py:208
  46.7 0.7 %collective-permute-done.18.refs_1_ = f32[16,1792]{1,0:T(8,128)S(1)} collective-permute-done((f32[16,1792]{1,0:T(8,128)S(1)}, f32[16,1792]{1,0:T(8,128)S(1)}, u32[]{:S(2)}, u32[]{:S(2)}) %collective-permute-start.18) | collective-permute-done | bytes 114720 | tf_op jit(solution)/shard_map/ppermute | solution.py:208
  47.4 1.7 %collective-permute-start.22 = (f32[8,1792]{1,0:T(8,128)S(1)}, f32[8,1792]{1,0:T(8,128)S(1)}, u32[]{:S(2)}, u32[]{:S(2)}) collective-permute-start(f32[8,1792]{1,0:T(8,128)S(1)} %get-tuple-element.83), channel_id=1, source_target_pairs={{0,16},{4,20},{8,24},{12,28},{16,0},{20,4},{24,8},{28,12},{1,17},{... | collective-permute-start | bytes 172040 | tf_op jit(solution)/shard_map/ppermute | solution.py:208
  49.2 1.3 %collective-permute-start.23 = (f32[8,1792]{1,0:T(8,128)S(1)}, f32[8,1792]{1,0:T(8,128)S(1)}, u32[]{:S(2)}, u32[]{:S(2)}) collective-permute-start(f32[8,1792]{1,0:T(8,128)S(1)} %get-tuple-element.84), channel_id=1, source_target_pairs={{0,16},{4,20},{8,24},{12,28},{16,0},{20,4},{24,8},{28,12},{1,17},{... | collective-permute-start | bytes 172040 | tf_op jit(solution)/shard_map/ppermute | solution.py:208
  50.5 1.5 %collective-permute-start.24 = (f32[8,1792]{1,0:T(8,128)S(1)}, f32[8,1792]{1,0:T(8,128)S(1)}, u32[]{:S(2)}, u32[]{:S(2)}) collective-permute-start(f32[8,1792]{1,0:T(8,128)S(1)} %get-tuple-element.85), channel_id=1, source_target_pairs={{0,8},{4,12},{8,0},{12,4},{16,24},{20,28},{24,16},{28,20},{1,9},{5... | collective-permute-start | bytes 172040 | tf_op jit(solution)/shard_map/ppermute | solution.py:208
  52.0 1.6 %collective-permute-start.25 = (f32[8,1792]{1,0:T(8,128)S(1)}, f32[8,1792]{1,0:T(8,128)S(1)}, u32[]{:S(2)}, u32[]{:S(2)}) collective-permute-start(f32[8,1792]{1,0:T(8,128)S(1)} %get-tuple-element.86), channel_id=1, source_target_pairs={{0,24},{4,28},{8,16},{12,20},{16,8},{20,12},{24,0},{28,4},{1,25},{... | collective-permute-start | bytes 172040 | tf_op jit(solution)/shard_map/ppermute | solution.py:208
  53.6 1.9 %shard_map.63 = (f32[2048,256]{1,0:T(8,128)}, f32[8,128]{1,0:T(8,128)S(1)}) custom-call(f32[32,1024]{1,0:T(8,128)S(1)} %get-tuple-element.49.refs_0_.refs_3_, f32[32,1024]{1,0:T(8,128)S(1)} %get-tuple-element.50.refs_1_, f32[32,1024]{1,0:T(8,128)S(1)} %get-tuple-element.55.refs_0_.refs_3_.refs_2_, f32[32,1024]{1,0:T(8,128)S(1)} %get-tuple-element.56.refs_1_.refs_3_, ...), custom_call_target="tpu_custom_call" | custom-call | tf_op jit(solution)/shard_map/pallas_call | solution.py:30
  55.7 1.1 %collective-permute-done.23.refs_7_ = f32[8,1792]{1,0:T(8,128)S(1)} collective-permute-done((f32[8,1792]{1,0:T(8,128)S(1)}, f32[8,1792]{1,0:T(8,128)S(1)}, u32[]{:S(2)}, u32[]{:S(2)}) %collective-permute-start.23) | collective-permute-done | bytes 57376 | tf_op jit(solution)/shard_map/ppermute | solution.py:208
  56.8 1.2 %collective-permute-done.25.refs_9_ = f32[8,1792]{1,0:T(8,128)S(1)} collective-permute-done((f32[8,1792]{1,0:T(8,128)S(1)}, f32[8,1792]{1,0:T(8,128)S(1)}, u32[]{:S(2)}, u32[]{:S(2)}) %collective-permute-start.25) | collective-permute-done | bytes 57376 | tf_op jit(solution)/shard_map/ppermute | solution.py:208
  58.0 0.7 %shard_map.64 = f32[32,1792]{1,0:T(8,128)} custom-call(f32[8,1792]{1,0:T(8,128)S(1)} %get-tuple-element.70.refs_3_.refs_0_, f32[8,1792]{1,0:T(8,128)S(1)} %collective-permute-done.20.refs_1_, f32[8,1792]{1,0:T(8,128)S(1)} %get-tuple-element.77.refs_2_, f32[8,1792]{1,0:T(8,128)S(1)} %collective-permute-done.21.refs_3_, ...), custom_call_target="tpu_custom_call" | custom-call | flops 500000000 | tf_op jit(solution)/shard_map/pallas_call | solution.py:30
  (44 shorter events, 5.0 us)
Async XLA Ops:
  3.8 3.4 %collective-permute-start = (f32[256,1024]{1,0:T(8,128)S(1)}, f32[256,1024]{1,0:T(8,128)S(1)}, u32[]{:S(2)}, u32[]{:S(2)}) collective-permute-start(f32[256,1024]{1,0:T(8,128)S(1)} %get-tuple-element.47), channel_id=1, source_target_pairs={{0,1},{1,0},{2,3},{3,2},{4,5},{5,4},{6,7},{7,6},{8,9},{9,8},{10,11... | collective-permute-start | bytes 3145736 | tf_op jit(solution)/shard_map/ppermute | solution.py:208
  7.3 9.7 %collective-permute-start.1 = (f32[64,1024]{1,0:T(8,128)S(1)}, f32[64,1024]{1,0:T(8,128)S(1)}, u32[]{:S(2)}, u32[]{:S(2)}) collective-permute-start(f32[64,1024]{1,0:T(8,128)S(1)} %get-tuple-element.48.refs_0_), channel_id=1, source_target_pairs={{0,2},{1,3},{2,0},{3,1},{4,6},{5,7},{6,4},{7,5},{8,10},{9,11},{10,... | collective-permute-start | bytes 786440 | tf_op jit(solution)/shard_map/ppermute | solution.py:208
  9.9 12.9 %collective-permute-start.2 = (f32[64,1024]{1,0:T(8,128)S(1)}, f32[64,1024]{1,0:T(8,128)S(1)}, u32[]{:S(2)}, u32[]{:S(2)}) collective-permute-start(f32[64,1024]{1,0:T(8,128)S(1)} %get-tuple-element.51.refs_0_), channel_id=1, source_target_pairs={{0,2},{1,3},{2,0},{3,1},{4,6},{5,7},{6,4},{7,5},{8,10},{9,11},{10,... | collective-permute-start | bytes 786440 | tf_op jit(solution)/shard_map/ppermute | solution.py:208
  17.1 3.3 %collective-permute-start.3 = (f32[32,1024]{1,0:T(8,128)S(1)}, f32[32,1024]{1,0:T(8,128)S(1)}, u32[]{:S(2)}, u32[]{:S(2)}) collective-permute-start(f32[32,1024]{1,0:T(8,128)S(1)} %get-tuple-element.49.refs_0_.refs_3_), channel_id=1, source_target_pairs={{0,1},{1,0},{2,3},{3,2},{4,5},{5,4},{6,7},{7,6},{8,9},{9,8},{10,11... | collective-permute-start | bytes 393224 | tf_op jit(solution)/shard_map/ppermute | solution.py:208
  17.2 3.2 %collective-permute-start.4 = (f32[32,1024]{1,0:T(8,128)S(1)}, f32[32,1024]{1,0:T(8,128)S(1)}, u32[]{:S(2)}, u32[]{:S(2)}) collective-permute-start(f32[32,1024]{1,0:T(8,128)S(1)} %get-tuple-element.50.refs_1_), channel_id=1, source_target_pairs={{0,1},{1,0},{2,3},{3,2},{4,5},{5,4},{6,7},{7,6},{8,9},{9,8},{10,11... | collective-permute-start | bytes 393224 | tf_op jit(solution)/shard_map/ppermute | solution.py:208
  17.7 10.9 %collective-permute-start.5 = (f32[64,1024]{1,0:T(8,128)S(1)}, f32[64,1024]{1,0:T(8,128)S(1)}, u32[]{:S(2)}, u32[]{:S(2)}) collective-permute-start(f32[64,1024]{1,0:T(8,128)S(1)} %get-tuple-element.57.refs_0_), channel_id=1, source_target_pairs={{0,2},{1,3},{2,0},{3,1},{4,6},{5,7},{6,4},{7,5},{8,10},{9,11},{10,... | collective-permute-start | bytes 786440 | tf_op jit(solution)/shard_map/ppermute | solution.py:208
  21.2 7.4 %collective-permute-start.6 = (f32[32,1792]{1,0:T(8,128)S(1)}, f32[32,1792]{1,0:T(8,128)S(1)}, u32[]{:S(2)}, u32[]{:S(2)}) collective-permute-start(f32[32,1792]{1,0:T(8,128)S(1)} %get-tuple-element.58), channel_id=1, source_target_pairs={{0,4},{4,0},{8,12},{12,8},{16,20},{20,16},{24,28},{28,24},{1,5},{5... | collective-permute-start | bytes 688136 | tf_op jit(solution)/shard_map/ppermute | solution.py:208
  22.8 3.2 %collective-permute-start.7 = (f32[32,1024]{1,0:T(8,128)S(1)}, f32[32,1024]{1,0:T(8,128)S(1)}, u32[]{:S(2)}, u32[]{:S(2)}) collective-permute-start(f32[32,1024]{1,0:T(8,128)S(1)} %get-tuple-element.55.refs_0_.refs_3_.refs_2_), channel_id=1, source_target_pairs={{0,1},{1,0},{2,3},{3,2},{4,5},{5,4},{6,7},{7,6},{8,9},{9,8},{10,11... | collective-permute-start | bytes 393224 | tf_op jit(solution)/shard_map/ppermute | solution.py:208
  22.9 3.1 %collective-permute-start.8 = (f32[32,1024]{1,0:T(8,128)S(1)}, f32[32,1024]{1,0:T(8,128)S(1)}, u32[]{:S(2)}, u32[]{:S(2)}) collective-permute-start(f32[32,1024]{1,0:T(8,128)S(1)} %get-tuple-element.56.refs_1_.refs_3_), channel_id=1, source_target_pairs={{0,1},{1,0},{2,3},{3,2},{4,5},{5,4},{6,7},{7,6},{8,9},{9,8},{10,11... | collective-permute-start | bytes 393224 | tf_op jit(solution)/shard_map/ppermute | solution.py:208
  23.4 10.7 %collective-permute-start.9 = (f32[64,1024]{1,0:T(8,128)S(1)}, f32[64,1024]{1,0:T(8,128)S(1)}, u32[]{:S(2)}, u32[]{:S(2)}) collective-permute-start(f32[64,1024]{1,0:T(8,128)S(1)} %get-tuple-element.63.refs_0_), channel_id=1, source_target_pairs={{0,2},{1,3},{2,0},{3,1},{4,6},{5,7},{6,4},{7,5},{8,10},{9,11},{10,... | collective-permute-start | bytes 786440 | tf_op jit(solution)/shard_map/ppermute | solution.py:208
  26.8 7.9 %collective-permute-start.15 = (f32[32,1792]{1,0:T(8,128)S(1)}, f32[32,1792]{1,0:T(8,128)S(1)}, u32[]{:S(2)}, u32[]{:S(2)}) collective-permute-start(f32[32,1792]{1,0:T(8,128)S(1)} %get-tuple-element.68), channel_id=1, source_target_pairs={{0,4},{4,0},{8,12},{12,8},{16,20},{20,16},{24,28},{28,24},{1,5},{5... | collective-permute-start | bytes 688136 | tf_op jit(solution)/shard_map/ppermute | solution.py:208
  28.6 3.1 %collective-permute-start.10 = (f32[32,1024]{1,0:T(8,128)S(1)}, f32[32,1024]{1,0:T(8,128)S(1)}, u32[]{:S(2)}, u32[]{:S(2)}) collective-permute-start(f32[32,1024]{1,0:T(8,128)S(1)} %get-tuple-element.61.refs_0_.refs_3_.refs_4_), channel_id=1, source_target_pairs={{0,1},{1,0},{2,3},{3,2},{4,5},{5,4},{6,7},{7,6},{8,9},{9,8},{10,11... | collective-permute-start | bytes 393224 | tf_op jit(solution)/shard_map/ppermute | solution.py:208
  28.7 3.0 %collective-permute-start.11 = (f32[32,1024]{1,0:T(8,128)S(1)}, f32[32,1024]{1,0:T(8,128)S(1)}, u32[]{:S(2)}, u32[]{:S(2)}) collective-permute-start(f32[32,1024]{1,0:T(8,128)S(1)} %get-tuple-element.62.refs_1_.refs_5_), channel_id=1, source_target_pairs={{0,1},{1,0},{2,3},{3,2},{4,5},{5,4},{6,7},{7,6},{8,9},{9,8},{10,11... | collective-permute-start | bytes 393224 | tf_op jit(solution)/shard_map/ppermute | solution.py:208
  29.2 5.5 %collective-permute-start.14 = (f32[16,1792]{1,0:T(8,128)S(1)}, f32[16,1792]{1,0:T(8,128)S(1)}, u32[]{:S(2)}, u32[]{:S(2)}) collective-permute-start(f32[16,1792]{1,0:T(8,128)S(1)} %get-tuple-element.67), channel_id=1, source_target_pairs={{0,8},{4,12},{8,0},{12,4},{16,24},{20,28},{24,16},{28,20},{1,9},{5... | collective-permute-start | bytes 344072 | tf_op jit(solution)/shard_map/ppermute | solution.py:208
  32.5 7.7 %collective-permute-start.17 = (f32[32,1792]{1,0:T(8,128)S(1)}, f32[32,1792]{1,0:T(8,128)S(1)}, u32[]{:S(2)}, u32[]{:S(2)}) collective-permute-start(f32[32,1792]{1,0:T(8,128)S(1)} %get-tuple-element.73), channel_id=1, source_target_pairs={{0,4},{4,0},{8,12},{12,8},{16,20},{20,16},{24,28},{28,24},{1,5},{5... | collective-permute-start | bytes 688136 | tf_op jit(solution)/shard_map/ppermute | solution.py:208
  34.1 1.4 %collective-permute-start.12 = (f32[32,1024]{1,0:T(8,128)S(1)}, f32[32,1024]{1,0:T(8,128)S(1)}, u32[]{:S(2)}, u32[]{:S(2)}) collective-permute-start(f32[32,1024]{1,0:T(8,128)S(1)} %get-tuple-element.65.refs_2_.refs_0_.refs_6_), channel_id=1, source_target_pairs={{0,1},{1,0},{2,3},{3,2},{4,5},{5,4},{6,7},{7,6},{8,9},{9,8},{10,11... | collective-permute-start | bytes 393224 | tf_op jit(solution)/shard_map/ppermute | solution.py:208
  34.2 1.5 %collective-permute-start.13 = (f32[32,1024]{1,0:T(8,128)S(1)}, f32[32,1024]{1,0:T(8,128)S(1)}, u32[]{:S(2)}, u32[]{:S(2)}) collective-permute-start(f32[32,1024]{1,0:T(8,128)S(1)} %get-tuple-element.66.refs_1_.refs_7_), channel_id=1, source_target_pairs={{0,1},{1,0},{2,3},{3,2},{4,5},{5,4},{6,7},{7,6},{8,9},{9,8},{10,11... | collective-permute-start | bytes 393224 | tf_op jit(solution)/shard_map/ppermute | solution.py:208
  36.5 12.6 %collective-permute-start.16 = (f32[32,1792]{1,0:T(8,128)S(1)}, f32[32,1792]{1,0:T(8,128)S(1)}, u32[]{:S(2)}, u32[]{:S(2)}) collective-permute-start(f32[32,1792]{1,0:T(8,128)S(1)} %get-tuple-element.72), channel_id=1, source_target_pairs={{0,4},{4,0},{8,12},{12,8},{16,20},{20,16},{24,28},{28,24},{1,5},{5... | collective-permute-start | bytes 688136 | tf_op jit(solution)/shard_map/ppermute | solution.py:208
  38.0 6.6 %collective-permute-start.19 = (f32[16,1792]{1,0:T(8,128)S(1)}, f32[16,1792]{1,0:T(8,128)S(1)}, u32[]{:S(2)}, u32[]{:S(2)}) collective-permute-start(f32[16,1792]{1,0:T(8,128)S(1)} %get-tuple-element.76), channel_id=1, source_target_pairs={{0,8},{4,12},{8,0},{12,4},{16,24},{20,28},{24,16},{28,20},{1,9},{5... | collective-permute-start | bytes 344072 | tf_op jit(solution)/shard_map/ppermute | solution.py:208
  40.2 7.2 %collective-permute-start.18 = (f32[16,1792]{1,0:T(8,128)S(1)}, f32[16,1792]{1,0:T(8,128)S(1)}, u32[]{:S(2)}, u32[]{:S(2)}) collective-permute-start(f32[16,1792]{1,0:T(8,128)S(1)} %get-tuple-element.75), channel_id=1, source_target_pairs={{0,8},{4,12},{8,0},{12,4},{16,24},{20,28},{24,16},{28,20},{1,9},{5... | collective-permute-start | bytes 344072 | tf_op jit(solution)/shard_map/ppermute | solution.py:208
  40.8 11.2 %collective-permute-start.20 = (f32[8,1792]{1,0:T(8,128)S(1)}, f32[8,1792]{1,0:T(8,128)S(1)}, u32[]{:S(2)}, u32[]{:S(2)}) collective-permute-start(f32[8,1792]{1,0:T(8,128)S(1)} %get-tuple-element.81), channel_id=1, source_target_pairs={{0,16},{4,20},{8,24},{12,28},{16,0},{20,4},{24,8},{28,12},{1,17},{... | collective-permute-start | bytes 172040 | tf_op jit(solution)/shard_map/ppermute | solution.py:208
  44.6 10.9 %collective-permute-start.21 = (f32[8,1792]{1,0:T(8,128)S(1)}, f32[8,1792]{1,0:T(8,128)S(1)}, u32[]{:S(2)}, u32[]{:S(2)}) collective-permute-start(f32[8,1792]{1,0:T(8,128)S(1)} %get-tuple-element.82), channel_id=1, source_target_pairs={{0,16},{4,20},{8,24},{12,28},{16,0},{20,4},{24,8},{28,12},{1,17},{... | collective-permute-start | bytes 172040 | tf_op jit(solution)/shard_map/ppermute | solution.py:208
  47.4 8.3 %collective-permute-start.22 = (f32[8,1792]{1,0:T(8,128)S(1)}, f32[8,1792]{1,0:T(8,128)S(1)}, u32[]{:S(2)}, u32[]{:S(2)}) collective-permute-start(f32[8,1792]{1,0:T(8,128)S(1)} %get-tuple-element.83), channel_id=1, source_target_pairs={{0,16},{4,20},{8,24},{12,28},{16,0},{20,4},{24,8},{28,12},{1,17},{... | collective-permute-start | bytes 172040 | tf_op jit(solution)/shard_map/ppermute | solution.py:208
  49.2 7.6 %collective-permute-start.23 = (f32[8,1792]{1,0:T(8,128)S(1)}, f32[8,1792]{1,0:T(8,128)S(1)}, u32[]{:S(2)}, u32[]{:S(2)}) collective-permute-start(f32[8,1792]{1,0:T(8,128)S(1)} %get-tuple-element.84), channel_id=1, source_target_pairs={{0,16},{4,20},{8,24},{12,28},{16,0},{20,4},{24,8},{28,12},{1,17},{... | collective-permute-start | bytes 172040 | tf_op jit(solution)/shard_map/ppermute | solution.py:208
  50.5 6.3 %collective-permute-start.24 = (f32[8,1792]{1,0:T(8,128)S(1)}, f32[8,1792]{1,0:T(8,128)S(1)}, u32[]{:S(2)}, u32[]{:S(2)}) collective-permute-start(f32[8,1792]{1,0:T(8,128)S(1)} %get-tuple-element.85), channel_id=1, source_target_pairs={{0,8},{4,12},{8,0},{12,4},{16,24},{20,28},{24,16},{28,20},{1,9},{5... | collective-permute-start | bytes 172040 | tf_op jit(solution)/shard_map/ppermute | solution.py:208
  52.0 6.0 %collective-permute-start.25 = (f32[8,1792]{1,0:T(8,128)S(1)}, f32[8,1792]{1,0:T(8,128)S(1)}, u32[]{:S(2)}, u32[]{:S(2)}) collective-permute-start(f32[8,1792]{1,0:T(8,128)S(1)} %get-tuple-element.86), channel_id=1, source_target_pairs={{0,24},{4,28},{8,16},{12,20},{16,8},{20,12},{24,0},{28,4},{1,25},{... | collective-permute-start | bytes 172040 | tf_op jit(solution)/shard_map/ppermute | solution.py:208

commit v11 on v10

--- a/solution.py
+++ b/solution.py
@@ -7,17 +7,17 @@
 from jax.experimental.pallas import tpu as pltpu
 from jax.sharding import PartitionSpec as P
 
-EIGHTHS = (2, 2, 2, 2)
+EIGHTHS = (2,2,2,2)
 BLOCK = 512
 F32 = jnp.float32
 BF16 = jnp.bfloat16
 NT = (((1,), (1,)), ((), ()))
 SPECS = {"v": pl.BlockSpec(memory_space=pltpu.VMEM), "a": pl.BlockSpec(memory_space=pl.ANY)}
-ORDER = ('own0', 'before0', 'send0', 'own1', 'before1', 'send1', 'add0.1', 'own2', 'before2', 'send2', 'own3', 'add1.1', 'add0.2', 'before3', 'send3', 'add2.1', 'add1.2', 'add2.2', 'add3.1', 'sketch')
-WEIGHTS = {'add2.1': 500000000, 'F': 500000000, 'send1': 0, 'send0': 0, 'send3': 0, 'add2.2': 200000000, 'add0.2': 1000000000, 'own2': 500000000, 'before1': 0, 'add0.1': 200000000}
-SPLITS = (2, 2, 2, 2)
-GROUPS = ((0,), (1,), (2,), (3,))
-MODES = ('pairs', 'pairs', 'pairs', 'direct')
+ORDER = ('own0', 'before0', 'send0', 'own1', 'before1', 'send1', 'add0.1', 'own2', 'before2', 'send2', 'add1.1', 'own3', 'before3', 'send3', 'add2.1', 'add1.2', 'add0.2', 'add2.2', 'add3.1', 'sketch')
+WEIGHTS = {'add2.1': 500000000, 'F': 500000000, 'send1': 0, 'send0': 0, 'send3': 0, 'add2.2': 200000000, 'add0.2': 1000000000, 'own2': 500000000, 'before1': 500000000, 'add0.1': 500000000, 'before3': 2000000000, 'sketch': 500000000, 'send2': 0, 'add1.2': 200000000}
+SPLITS = (2,2,2,2)
+GROUPS = ((0,),(1,),(2,),(3,))
+MODES = ('pairs','pairs','pairs','direct')
 
 
 def call(body, args, outs, kinds=None, after=(), scratch=(), results=0, weight=0):

time: 58.9 us -> 58.6 us (level)
  starting transfers between devices: 30.1 us -> 28.3 us
  waiting for transfers between devices: 12.5 us -> 14.1 us
    ppermute x26, starting transfers between devices: 30.1 us -> 28.3 us  [swap(): return lax.ppermute(x, axis, [(i, i ^ bit) for i in range(size)])]
    ppermute x26, waiting for transfers between devices: 12.5 us -> 14.1 us  [swap(): return lax.ppermute(x, axis, [(i, i ^ bit) for i in range(size)])]
  transfers between devices with their start and end apart: 26 -> 26, of which waited for: 9 -> 10; matrix products, arithmetic and copies ran while one was open for 0% -> 0% of each run, Pallas kernels for 19% -> 19%
where the time goes in v11:
time: 58.6 us; the launch traced here: 58.5 us
  starting transfers between devices  28.3 us (48%)
  Pallas kernels  15.2 us (26%)
  waiting for transfers between devices  14.1 us (24%)
  between operations  0.86 us (1%)
    ppermute x26, starting transfers between devices, swap(): return lax.ppermute(x, axis, [(i, i ^ bit) for i in range(size)])  28.3 us
    pallas_call x24, Pallas kernels, call(): pl.pallas_call(run, out_shape=[pltpu.VMEM(*o) if i >= results else jax.Sh...  15.2 us
    ppermute x26, waiting for transfers between devices, swap(): return lax.ppermute(x, axis, [(i, i ^ bit) for i in range(size)])  14.1 us
  transfers between devices with their start and end apart: 26, of which 10 were waited for; matrix products, arithmetic and copies ran while one was open for 0% of the time, Pallas kernels for 19%

profile of v11, /device:TPU:0, one launch (start us, length us, event | category | flops | bytes accessed | tf_op | source)
XLA Modules:
  0.0 58.5 jit_solution(16557731304369943984)
XLA Ops:
  0.6 3.2 %shard_map.41 = (bf16[1024,1792]{1,0:T(8,128)(2,1)S(1)}, bf16[256,1792]{1,0:T(8,128)(2,1)S(1)}, f32[256,1024]{1,0:T(8,128)S(1)}) custom-call(bf16[2048,1792]{1,0:T(8,128)(2,1)} %refs_0_.3, bf16[1792,256]{1,0:T(8,128)(2,1)} %refs_1_.1), custom_call_target="tpu_custom_call" | custom-call | tf_op jit(solution)/shard_map/pallas_call | solution.py:30
  3.8 0.5 collective-permute-start
  4.3 2.9 %shard_map.42 = (bf16[1024,1792]{1,0:T(8,128)(2,1)S(1)}, f32[256,1024]{1,0:T(8,128)S(1)}) custom-call(bf16[2048,1792]{1,0:T(8,128)(2,1)} %refs_0_.3, bf16[256,1792]{1,0:T(8,128)(2,1)S(1)} %get-tuple-element.45.refs_1_), custom_call_target="tpu_custom_call" | custom-call | tf_op jit(solution)/shard_map/pallas_call | solution.py:30
  7.3 2.6 %collective-permute-start.1 = (f32[64,1024]{1,0:T(8,128)S(1)}, f32[64,1024]{1,0:T(8,128)S(1)}, u32[]{:S(2)}, u32[]{:S(2)}) collective-permute-start(f32[64,1024]{1,0:T(8,128)S(1)} %get-tuple-element.48.refs_0_), channel_id=1, source_target_pairs={{0,2},{1,3},{2,0},{3,1},{4,6},{5,7},{6,4},{7,5},{8,10},{9,11},{10,... | collective-permute-start | bytes 786440 | tf_op jit(solution)/shard_map/ppermute | solution.py:208
  10.0 7.1 %collective-permute-done.1.refs_1_ = f32[64,1024]{1,0:T(8,128)S(1)} collective-permute-done((f32[64,1024]{1,0:T(8,128)S(1)}, f32[64,1024]{1,0:T(8,128)S(1)}, u32[]{:S(2)}, u32[]{:S(2)}) %collective-permute-start.1) | collective-permute-done | bytes 262176 | tf_op jit(solution)/shard_map/ppermute | solution.py:208
  17.2 0.5 collective-permute-start.4
  17.7 0.7 %shard_map.45.refs_3_.refs_4_ = f32[64,1792]{1,0:T(8,128)S(1)} custom-call(f32[32,1024]{1,0:T(8,128)S(1)} %get-tuple-element.49.refs_0_.refs_3_, f32[32,1024]{1,0:T(8,128)S(1)} %get-tuple-element.50.refs_1_, bf16[1024,1792]{1,0:T(8,128)(2,1)S(1)} %get-tuple-element.53.refs_2_, f32[32,1024]{1,0:T(8,128)S(1)} %get-tuple-element.49.refs_0_.refs_3_), custom_call_target="tpu_custom_call" | custom-call | tf_op jit(solution)/shard_map/pallas_call | solution.py:30
  18.7 0.8 %shard_map.46 = (f32[32,1792]{1,0:T(8,128)S(1)}, f32[32,1792]{1,0:T(8,128)S(1)}) custom-call(f32[32,1024]{1,0:T(8,128)S(1)} %collective-permute-done.3.refs_0_.refs_8_, f32[32,1024]{1,0:T(8,128)S(1)} %collective-permute-done.4.refs_1_.refs_9_, bf16[1024,1792]{1,0:T(8,128)(2,1)S(1)} %get-tuple-element.52.refs_2_, f32[64,1792]{1,0:T(8,128)S(1)} %shard_map.45.refs_3_.refs_4_, ...), custom_call_target="tpu_custom_call" | custom-call | tf_op jit(solution)/shard_map/pallas_call | solution.py:30
  19.5 2.0 %collective-permute-start.6 = (f32[32,1792]{1,0:T(8,128)S(1)}, f32[32,1792]{1,0:T(8,128)S(1)}, u32[]{:S(2)}, u32[]{:S(2)}) collective-permute-start(f32[32,1792]{1,0:T(8,128)S(1)} %get-tuple-element.58), channel_id=1, source_target_pairs={{0,4},{4,0},{8,12},{12,8},{16,20},{20,16},{24,28},{28,24},{1,5},{5... | collective-permute-start | bytes 688136 | tf_op jit(solution)/shard_map/ppermute | solution.py:208
  21.5 1.5 %collective-permute-start.5 = (f32[64,1024]{1,0:T(8,128)S(1)}, f32[64,1024]{1,0:T(8,128)S(1)}, u32[]{:S(2)}, u32[]{:S(2)}) collective-permute-start(f32[64,1024]{1,0:T(8,128)S(1)} %get-tuple-element.57.refs_0_), channel_id=1, source_target_pairs={{0,2},{1,3},{2,0},{3,1},{4,6},{5,7},{6,4},{7,5},{8,10},{9,11},{10,... | collective-permute-start | bytes 786440 | tf_op jit(solution)/shard_map/ppermute | solution.py:208
  23.6 1.2 %collective-permute-start.9 = (f32[64,1024]{1,0:T(8,128)S(1)}, f32[64,1024]{1,0:T(8,128)S(1)}, u32[]{:S(2)}, u32[]{:S(2)}) collective-permute-start(f32[64,1024]{1,0:T(8,128)S(1)} %get-tuple-element.63.refs_0_), channel_id=1, source_target_pairs={{0,2},{1,3},{2,0},{3,1},{4,6},{5,7},{6,4},{7,5},{8,10},{9,11},{10,... | collective-permute-start | bytes 786440 | tf_op jit(solution)/shard_map/ppermute | solution.py:208
  24.9 0.7 %shard_map.48.refs_3_.refs_4_ = f32[64,1792]{1,0:T(8,128)S(1)} custom-call(f32[32,1024]{1,0:T(8,128)S(1)} %get-tuple-element.55.refs_0_.refs_3_.refs_2_, f32[32,1024]{1,0:T(8,128)S(1)} %get-tuple-element.56.refs_1_.refs_3_, bf16[1024,1792]{1,0:T(8,128)(2,1)S(1)} %get-tuple-element.53.refs_2_, f32[32,1024]{1,0:T(8,128)S(1)} %get-tuple-element.55.refs_0_.refs_3_.refs_2_), custom_call_target="tpu_custom_call" | custom-call | flops 500000000 | tf_op jit(solution)/shard_map/pallas_call | solution.py:30
  25.6 0.8 %shard_map.49 = (f32[32,1792]{1,0:T(8,128)S(1)}, f32[32,1792]{1,0:T(8,128)S(1)}) custom-call(f32[32,1024]{1,0:T(8,128)S(1)} %collective-permute-done.7.refs_0_.refs_10_, f32[32,1024]{1,0:T(8,128)S(1)} %collective-permute-done.8.refs_1_.refs_11_, bf16[1024,1792]{1,0:T(8,128)(2,1)S(1)} %get-tuple-element.52.refs_2_, f32[64,1792]{1,0:T(8,128)S(1)} %shard_map.48.refs_3_.refs_4_, ...), custom_call_target="tpu_custom_call" | custom-call | tf_op jit(solution)/shard_map/pallas_call | solution.py:30
  26.4 1.6 %collective-permute-start.10 = (f32[32,1792]{1,0:T(8,128)S(1)}, f32[32,1792]{1,0:T(8,128)S(1)}, u32[]{:S(2)}, u32[]{:S(2)}) collective-permute-start(f32[32,1792]{1,0:T(8,128)S(1)} %get-tuple-element.64), channel_id=1, source_target_pairs={{0,4},{4,0},{8,12},{12,8},{16,20},{20,16},{24,28},{28,24},{1,5},{5... | collective-permute-start | bytes 688136 | tf_op jit(solution)/shard_map/ppermute | solution.py:208
  28.0 2.7 %collective-permute-done.5.refs_1_ = f32[64,1024]{1,0:T(8,128)S(1)} collective-permute-done((f32[64,1024]{1,0:T(8,128)S(1)}, f32[64,1024]{1,0:T(8,128)S(1)}, u32[]{:S(2)}, u32[]{:S(2)}) %collective-permute-start.5) | collective-permute-done | bytes 262176 | tf_op jit(solution)/shard_map/ppermute | solution.py:208
  31.3 0.7 %shard_map.52.refs_3_.refs_4_ = f32[64,1792]{1,0:T(8,128)S(1)} custom-call(f32[32,1024]{1,0:T(8,128)S(1)} %get-tuple-element.61.refs_0_.refs_3_.refs_4_, f32[32,1024]{1,0:T(8,128)S(1)} %get-tuple-element.62.refs_1_.refs_5_, bf16[1024,1792]{1,0:T(8,128)(2,1)S(1)} %get-tuple-element.53.refs_2_, f32[32,1024]{1,0:T(8,128)S(1)} %get-tuple-element.61.refs_0_.refs_3_.refs_4_), custom_call_target="tpu_custom_call" | custom-call | tf_op jit(solution)/shard_map/pallas_call | solution.py:30
  32.3 0.8 %shard_map.53 = (f32[32,1792]{1,0:T(8,128)S(1)}, f32[32,1792]{1,0:T(8,128)S(1)}) custom-call(f32[32,1024]{1,0:T(8,128)S(1)} %collective-permute-done.11.refs_0_.refs_12_, f32[32,1024]{1,0:T(8,128)S(1)} %collective-permute-done.12.refs_1_.refs_13_, bf16[1024,1792]{1,0:T(8,128)(2,1)S(1)} %get-tuple-element.52.refs_2_, ...), custom_call_target="tpu_custom_call" | custom-call | tf_op jit(solution)/shard_map/pallas_call | solution.py:30
  33.2 2.0 %collective-permute-start.18 = (f32[16,1792]{1,0:T(8,128)S(1)}, f32[16,1792]{1,0:T(8,128)S(1)}, u32[]{:S(2)}, u32[]{:S(2)}) collective-permute-start(f32[16,1792]{1,0:T(8,128)S(1)} %get-tuple-element.74), channel_id=1, source_target_pairs={{0,8},{4,12},{8,0},{12,4},{16,24},{20,28},{24,16},{28,20},{1,9},{5... | collective-permute-start | bytes 344072 | tf_op jit(solution)/shard_map/ppermute | solution.py:208
  36.0 1.6 %collective-permute-start.19 = (f32[16,1792]{1,0:T(8,128)S(1)}, f32[16,1792]{1,0:T(8,128)S(1)}, u32[]{:S(2)}, u32[]{:S(2)}) collective-permute-start(f32[16,1792]{1,0:T(8,128)S(1)} %get-tuple-element.75), channel_id=1, source_target_pairs={{0,8},{4,12},{8,0},{12,4},{16,24},{20,28},{24,16},{28,20},{1,9},{5... | collective-permute-start | bytes 344072 | tf_op jit(solution)/shard_map/ppermute | solution.py:208
  37.6 0.7 %shard_map.56.refs_3_.refs_4_ = f32[64,1792]{1,0:T(8,128)S(1)} custom-call(f32[32,1024]{1,0:T(8,128)S(1)} %get-tuple-element.67.refs_0_.refs_3_.refs_6_, f32[32,1024]{1,0:T(8,128)S(1)} %get-tuple-element.68.refs_1_.refs_7_, bf16[1024,1792]{1,0:T(8,128)(2,1)S(1)} %get-tuple-element.53.refs_2_, f32[32,1024]{1,0:T(8,128)S(1)} %get-tuple-element.67.refs_0_.refs_3_.refs_6_), custom_call_target="tpu_custom_call" | custom-call | flops 2000000000 | tf_op jit(solution)/shard_map/pallas_call | solution.py:30
  38.4 0.8 %shard_map.57 = (f32[32,1792]{1,0:T(8,128)S(1)}, f32[32,1792]{1,0:T(8,128)S(1)}) custom-call(f32[32,1024]{1,0:T(8,128)S(1)} %collective-permute-done.13.refs_0_.refs_14_, f32[32,1024]{1,0:T(8,128)S(1)} %collective-permute-done.14.refs_1_.refs_15_, bf16[1024,1792]{1,0:T(8,128)(2,1)S(1)} %get-tuple-element.52.refs_2_, ...), custom_call_target="tpu_custom_call" | custom-call | tf_op jit(solution)/shard_map/pallas_call | solution.py:30
  39.1 0.6 collective-permute-start.15
  39.7 1.3 %collective-permute-done.16.refs_1_ = f32[32,1792]{1,0:T(8,128)S(1)} collective-permute-done((f32[32,1792]{1,0:T(8,128)S(1)}, f32[32,1792]{1,0:T(8,128)S(1)}, u32[]{:S(2)}, u32[]{:S(2)}) %collective-permute-start.16) | collective-permute-done | bytes 229408 | tf_op jit(solution)/shard_map/ppermute | solution.py:208
  41.0 1.8 %collective-permute-start.17 = (f32[16,1792]{1,0:T(8,128)S(1)}, f32[16,1792]{1,0:T(8,128)S(1)}, u32[]{:S(2)}, u32[]{:S(2)}) collective-permute-start(f32[16,1792]{1,0:T(8,128)S(1)} %get-tuple-element.73), channel_id=1, source_target_pairs={{0,8},{4,12},{8,0},{12,4},{16,24},{20,28},{24,16},{28,20},{1,9},{5... | collective-permute-start | bytes 344072 | tf_op jit(solution)/shard_map/ppermute | solution.py:208
  42.9 2.7 %collective-permute-start.20 = (f32[8,1792]{1,0:T(8,128)S(1)}, f32[8,1792]{1,0:T(8,128)S(1)}, u32[]{:S(2)}, u32[]{:S(2)}) collective-permute-start(f32[8,1792]{1,0:T(8,128)S(1)} %get-tuple-element.81), channel_id=1, source_target_pairs={{0,16},{4,20},{8,24},{12,28},{16,0},{20,4},{24,8},{28,12},{1,17},{... | collective-permute-start | bytes 172040 | tf_op jit(solution)/shard_map/ppermute | solution.py:208
  45.9 0.6 %collective-permute-done.17.refs_1_ = f32[16,1792]{1,0:T(8,128)S(1)} collective-permute-done((f32[16,1792]{1,0:T(8,128)S(1)}, f32[16,1792]{1,0:T(8,128)S(1)}, u32[]{:S(2)}, u32[]{:S(2)}) %collective-permute-start.17) | collective-permute-done | bytes 114720 | tf_op jit(solution)/shard_map/ppermute | solution.py:208
  46.5 3.0 %collective-permute-start.22 = (f32[8,1792]{1,0:T(8,128)S(1)}, f32[8,1792]{1,0:T(8,128)S(1)}, u32[]{:S(2)}, u32[]{:S(2)}) collective-permute-start(f32[8,1792]{1,0:T(8,128)S(1)} %get-tuple-element.83), channel_id=1, source_target_pairs={{0,16},{4,20},{8,24},{12,28},{16,0},{20,4},{24,8},{28,12},{1,17},{... | collective-permute-start | bytes 172040 | tf_op jit(solution)/shard_map/ppermute | solution.py:208
  49.7 1.7 %collective-permute-start.24 = (f32[8,1792]{1,0:T(8,128)S(1)}, f32[8,1792]{1,0:T(8,128)S(1)}, u32[]{:S(2)}, u32[]{:S(2)}) collective-permute-start(f32[8,1792]{1,0:T(8,128)S(1)} %get-tuple-element.85), channel_id=1, source_target_pairs={{0,8},{4,12},{8,0},{12,4},{16,24},{20,28},{24,16},{28,20},{1,9},{5... | collective-permute-start | bytes 172040 | tf_op jit(solution)/shard_map/ppermute | solution.py:208
  51.3 2.8 %collective-permute-start.25 = (f32[8,1792]{1,0:T(8,128)S(1)}, f32[8,1792]{1,0:T(8,128)S(1)}, u32[]{:S(2)}, u32[]{:S(2)}) collective-permute-start(f32[8,1792]{1,0:T(8,128)S(1)} %get-tuple-element.86), channel_id=1, source_target_pairs={{0,24},{4,28},{8,16},{12,20},{16,8},{20,12},{24,0},{28,4},{1,25},{... | collective-permute-start | bytes 172040 | tf_op jit(solution)/shard_map/ppermute | solution.py:208
  54.1 1.9 %shard_map.63 = (f32[2048,256]{1,0:T(8,128)}, f32[8,128]{1,0:T(8,128)S(1)}) custom-call(f32[32,1024]{1,0:T(8,128)S(1)} %get-tuple-element.49.refs_0_.refs_3_, f32[32,1024]{1,0:T(8,128)S(1)} %get-tuple-element.50.refs_1_, f32[32,1024]{1,0:T(8,128)S(1)} %get-tuple-element.55.refs_0_.refs_3_.refs_2_, f32[32,1024]{1,0:T(8,128)S(1)} %get-tuple-element.56.refs_1_.refs_3_, ...), custom_call_target="tpu_custom_call" | custom-call | tf_op jit(solution)/shard_map/pallas_call | solution.py:30
  56.0 1.7 %collective-permute-done.23.refs_7_ = f32[8,1792]{1,0:T(8,128)S(1)} collective-permute-done((f32[8,1792]{1,0:T(8,128)S(1)}, f32[8,1792]{1,0:T(8,128)S(1)}, u32[]{:S(2)}, u32[]{:S(2)}) %collective-permute-start.23) | collective-permute-done | bytes 57376 | tf_op jit(solution)/shard_map/ppermute | solution.py:208
  57.7 0.7 %shard_map.64 = f32[32,1792]{1,0:T(8,128)} custom-call(f32[8,1792]{1,0:T(8,128)S(1)} %get-tuple-element.77.refs_2_.refs_0_, f32[8,1792]{1,0:T(8,128)S(1)} %collective-permute-done.20.refs_1_, f32[8,1792]{1,0:T(8,128)S(1)} %get-tuple-element.76.refs_2_, f32[8,1792]{1,0:T(8,128)S(1)} %collective-permute-done.21.refs_3_, ...), custom_call_target="tpu_custom_call" | custom-call | flops 500000000 | tf_op jit(solution)/shard_map/pallas_call | solution.py:30
  (44 shorter events, 3.5 us)
Async XLA Ops:
  3.8 3.4 %collective-permute-start = (f32[256,1024]{1,0:T(8,128)S(1)}, f32[256,1024]{1,0:T(8,128)S(1)}, u32[]{:S(2)}, u32[]{:S(2)}) collective-permute-start(f32[256,1024]{1,0:T(8,128)S(1)} %get-tuple-element.47), channel_id=1, source_target_pairs={{0,1},{1,0},{2,3},{3,2},{4,5},{5,4},{6,7},{7,6},{8,9},{9,8},{10,11... | collective-permute-start | bytes 3145736 | tf_op jit(solution)/shard_map/ppermute | solution.py:208
  7.3 9.7 %collective-permute-start.1 = (f32[64,1024]{1,0:T(8,128)S(1)}, f32[64,1024]{1,0:T(8,128)S(1)}, u32[]{:S(2)}, u32[]{:S(2)}) collective-permute-start(f32[64,1024]{1,0:T(8,128)S(1)} %get-tuple-element.48.refs_0_), channel_id=1, source_target_pairs={{0,2},{1,3},{2,0},{3,1},{4,6},{5,7},{6,4},{7,5},{8,10},{9,11},{10,... | collective-permute-start | bytes 786440 | tf_op jit(solution)/shard_map/ppermute | solution.py:208
  9.9 13.1 %collective-permute-start.2 = (f32[64,1024]{1,0:T(8,128)S(1)}, f32[64,1024]{1,0:T(8,128)S(1)}, u32[]{:S(2)}, u32[]{:S(2)}) collective-permute-start(f32[64,1024]{1,0:T(8,128)S(1)} %get-tuple-element.51.refs_0_), channel_id=1, source_target_pairs={{0,2},{1,3},{2,0},{3,1},{4,6},{5,7},{6,4},{7,5},{8,10},{9,11},{10,... | collective-permute-start | bytes 786440 | tf_op jit(solution)/shard_map/ppermute | solution.py:208
  17.1 1.4 %collective-permute-start.3 = (f32[32,1024]{1,0:T(8,128)S(1)}, f32[32,1024]{1,0:T(8,128)S(1)}, u32[]{:S(2)}, u32[]{:S(2)}) collective-permute-start(f32[32,1024]{1,0:T(8,128)S(1)} %get-tuple-element.49.refs_0_.refs_3_), channel_id=1, source_target_pairs={{0,1},{1,0},{2,3},{3,2},{4,5},{5,4},{6,7},{7,6},{8,9},{9,8},{10,11... | collective-permute-start | bytes 393224 | tf_op jit(solution)/shard_map/ppermute | solution.py:208
  17.2 1.5 %collective-permute-start.4 = (f32[32,1024]{1,0:T(8,128)S(1)}, f32[32,1024]{1,0:T(8,128)S(1)}, u32[]{:S(2)}, u32[]{:S(2)}) collective-permute-start(f32[32,1024]{1,0:T(8,128)S(1)} %get-tuple-element.50.refs_1_), channel_id=1, source_target_pairs={{0,1},{1,0},{2,3},{3,2},{4,5},{5,4},{6,7},{7,6},{8,9},{9,8},{10,11... | collective-permute-start | bytes 393224 | tf_op jit(solution)/shard_map/ppermute | solution.py:208
  19.5 8.5 %collective-permute-start.6 = (f32[32,1792]{1,0:T(8,128)S(1)}, f32[32,1792]{1,0:T(8,128)S(1)}, u32[]{:S(2)}, u32[]{:S(2)}) collective-permute-start(f32[32,1792]{1,0:T(8,128)S(1)} %get-tuple-element.58), channel_id=1, source_target_pairs={{0,4},{4,0},{8,12},{12,8},{16,20},{20,16},{24,28},{28,24},{1,5},{5... | collective-permute-start | bytes 688136 | tf_op jit(solution)/shard_map/ppermute | solution.py:208
  21.5 9.2 %collective-permute-start.5 = (f32[64,1024]{1,0:T(8,128)S(1)}, f32[64,1024]{1,0:T(8,128)S(1)}, u32[]{:S(2)}, u32[]{:S(2)}) collective-permute-start(f32[64,1024]{1,0:T(8,128)S(1)} %get-tuple-element.57.refs_0_), channel_id=1, source_target_pairs={{0,2},{1,3},{2,0},{3,1},{4,6},{5,7},{6,4},{7,5},{8,10},{9,11},{10,... | collective-permute-start | bytes 786440 | tf_op jit(solution)/shard_map/ppermute | solution.py:208
  23.1 2.6 %collective-permute-start.7 = (f32[32,1024]{1,0:T(8,128)S(1)}, f32[32,1024]{1,0:T(8,128)S(1)}, u32[]{:S(2)}, u32[]{:S(2)}) collective-permute-start(f32[32,1024]{1,0:T(8,128)S(1)} %get-tuple-element.55.refs_0_.refs_3_.refs_2_), channel_id=1, source_target_pairs={{0,1},{1,0},{2,3},{3,2},{4,5},{5,4},{6,7},{7,6},{8,9},{9,8},{10,11... | collective-permute-start | bytes 393224 | tf_op jit(solution)/shard_map/ppermute | solution.py:208
  23.1 2.5 %collective-permute-start.8 = (f32[32,1024]{1,0:T(8,128)S(1)}, f32[32,1024]{1,0:T(8,128)S(1)}, u32[]{:S(2)}, u32[]{:S(2)}) collective-permute-start(f32[32,1024]{1,0:T(8,128)S(1)} %get-tuple-element.56.refs_1_.refs_3_), channel_id=1, source_target_pairs={{0,1},{1,0},{2,3},{3,2},{4,5},{5,4},{6,7},{7,6},{8,9},{9,8},{10,11... | collective-permute-start | bytes 393224 | tf_op jit(solution)/shard_map/ppermute | solution.py:208
  23.6 11.8 %collective-permute-start.9 = (f32[64,1024]{1,0:T(8,128)S(1)}, f32[64,1024]{1,0:T(8,128)S(1)}, u32[]{:S(2)}, u32[]{:S(2)}) collective-permute-start(f32[64,1024]{1,0:T(8,128)S(1)} %get-tuple-element.63.refs_0_), channel_id=1, source_target_pairs={{0,2},{1,3},{2,0},{3,1},{4,6},{5,7},{6,4},{7,5},{8,10},{9,11},{10,... | collective-permute-start | bytes 786440 | tf_op jit(solution)/shard_map/ppermute | solution.py:208
  26.4 8.8 %collective-permute-start.10 = (f32[32,1792]{1,0:T(8,128)S(1)}, f32[32,1792]{1,0:T(8,128)S(1)}, u32[]{:S(2)}, u32[]{:S(2)}) collective-permute-start(f32[32,1792]{1,0:T(8,128)S(1)} %get-tuple-element.64), channel_id=1, source_target_pairs={{0,4},{4,0},{8,12},{12,8},{16,20},{20,16},{24,28},{28,24},{1,5},{5... | collective-permute-start | bytes 688136 | tf_op jit(solution)/shard_map/ppermute | solution.py:208
  30.7 1.4 %collective-permute-start.11 = (f32[32,1024]{1,0:T(8,128)S(1)}, f32[32,1024]{1,0:T(8,128)S(1)}, u32[]{:S(2)}, u32[]{:S(2)}) collective-permute-start(f32[32,1024]{1,0:T(8,128)S(1)} %get-tuple-element.61.refs_0_.refs_3_.refs_4_), channel_id=1, source_target_pairs={{0,1},{1,0},{2,3},{3,2},{4,5},{5,4},{6,7},{7,6},{8,9},{9,8},{10,11... | collective-permute-start | bytes 393224 | tf_op jit(solution)/shard_map/ppermute | solution.py:208
  30.8 1.5 %collective-permute-start.12 = (f32[32,1024]{1,0:T(8,128)S(1)}, f32[32,1024]{1,0:T(8,128)S(1)}, u32[]{:S(2)}, u32[]{:S(2)}) collective-permute-start(f32[32,1024]{1,0:T(8,128)S(1)} %get-tuple-element.62.refs_1_.refs_5_), channel_id=1, source_target_pairs={{0,1},{1,0},{2,3},{3,2},{4,5},{5,4},{6,7},{7,6},{8,9},{9,8},{10,11... | collective-permute-start | bytes 393224 | tf_op jit(solution)/shard_map/ppermute | solution.py:208
  33.1 7.9 %collective-permute-start.16 = (f32[32,1792]{1,0:T(8,128)S(1)}, f32[32,1792]{1,0:T(8,128)S(1)}, u32[]{:S(2)}, u32[]{:S(2)}) collective-permute-start(f32[32,1792]{1,0:T(8,128)S(1)} %get-tuple-element.71), channel_id=1, source_target_pairs={{0,4},{4,0},{8,12},{12,8},{16,20},{20,16},{24,28},{28,24},{1,5},{5... | collective-permute-start | bytes 688136 | tf_op jit(solution)/shard_map/ppermute | solution.py:208
  33.2 9.6 %collective-permute-start.18 = (f32[16,1792]{1,0:T(8,128)S(1)}, f32[16,1792]{1,0:T(8,128)S(1)}, u32[]{:S(2)}, u32[]{:S(2)}) collective-permute-start(f32[16,1792]{1,0:T(8,128)S(1)} %get-tuple-element.74), channel_id=1, source_target_pairs={{0,8},{4,12},{8,0},{12,4},{16,24},{20,28},{24,16},{28,20},{1,9},{5... | collective-permute-start | bytes 344072 | tf_op jit(solution)/shard_map/ppermute | solution.py:208
  35.4 2.9 %collective-permute-start.13 = (f32[32,1024]{1,0:T(8,128)S(1)}, f32[32,1024]{1,0:T(8,128)S(1)}, u32[]{:S(2)}, u32[]{:S(2)}) collective-permute-start(f32[32,1024]{1,0:T(8,128)S(1)} %get-tuple-element.67.refs_0_.refs_3_.refs_6_), channel_id=1, source_target_pairs={{0,1},{1,0},{2,3},{3,2},{4,5},{5,4},{6,7},{7,6},{8,9},{9,8},{10,11... | collective-permute-start | bytes 393224 | tf_op jit(solution)/shard_map/ppermute | solution.py:208
  35.5 2.8 %collective-permute-start.14 = (f32[32,1024]{1,0:T(8,128)S(1)}, f32[32,1024]{1,0:T(8,128)S(1)}, u32[]{:S(2)}, u32[]{:S(2)}) collective-permute-start(f32[32,1024]{1,0:T(8,128)S(1)} %get-tuple-element.68.refs_1_.refs_7_), channel_id=1, source_target_pairs={{0,1},{1,0},{2,3},{3,2},{4,5},{5,4},{6,7},{7,6},{8,9},{9,8},{10,11... | collective-permute-start | bytes 393224 | tf_op jit(solution)/shard_map/ppermute | solution.py:208
  36.0 6.8 %collective-permute-start.19 = (f32[16,1792]{1,0:T(8,128)S(1)}, f32[16,1792]{1,0:T(8,128)S(1)}, u32[]{:S(2)}, u32[]{:S(2)}) collective-permute-start(f32[16,1792]{1,0:T(8,128)S(1)} %get-tuple-element.75), channel_id=1, source_target_pairs={{0,8},{4,12},{8,0},{12,4},{16,24},{20,28},{24,16},{28,20},{1,9},{5... | collective-permute-start | bytes 344072 | tf_op jit(solution)/shard_map/ppermute | solution.py:208
  39.1 10.4 %collective-permute-start.15 = (f32[32,1792]{1,0:T(8,128)S(1)}, f32[32,1792]{1,0:T(8,128)S(1)}, u32[]{:S(2)}, u32[]{:S(2)}) collective-permute-start(f32[32,1792]{1,0:T(8,128)S(1)} %get-tuple-element.70), channel_id=1, source_target_pairs={{0,4},{4,0},{8,12},{12,8},{16,20},{20,16},{24,28},{28,24},{1,5},{5... | collective-permute-start | bytes 688136 | tf_op jit(solution)/shard_map/ppermute | solution.py:208
  41.0 5.5 %collective-permute-start.17 = (f32[16,1792]{1,0:T(8,128)S(1)}, f32[16,1792]{1,0:T(8,128)S(1)}, u32[]{:S(2)}, u32[]{:S(2)}) collective-permute-start(f32[16,1792]{1,0:T(8,128)S(1)} %get-tuple-element.73), channel_id=1, source_target_pairs={{0,8},{4,12},{8,0},{12,4},{16,24},{20,28},{24,16},{28,20},{1,9},{5... | collective-permute-start | bytes 344072 | tf_op jit(solution)/shard_map/ppermute | solution.py:208
  42.9 8.5 %collective-permute-start.20 = (f32[8,1792]{1,0:T(8,128)S(1)}, f32[8,1792]{1,0:T(8,128)S(1)}, u32[]{:S(2)}, u32[]{:S(2)}) collective-permute-start(f32[8,1792]{1,0:T(8,128)S(1)} %get-tuple-element.81), channel_id=1, source_target_pairs={{0,16},{4,20},{8,24},{12,28},{16,0},{20,4},{24,8},{28,12},{1,17},{... | collective-permute-start | bytes 172040 | tf_op jit(solution)/shard_map/ppermute | solution.py:208
  45.5 10.5 %collective-permute-start.21 = (f32[8,1792]{1,0:T(8,128)S(1)}, f32[8,1792]{1,0:T(8,128)S(1)}, u32[]{:S(2)}, u32[]{:S(2)}) collective-permute-start(f32[8,1792]{1,0:T(8,128)S(1)} %get-tuple-element.82), channel_id=1, source_target_pairs={{0,16},{4,20},{8,24},{12,28},{16,0},{20,4},{24,8},{28,12},{1,17},{... | collective-permute-start | bytes 172040 | tf_op jit(solution)/shard_map/ppermute | solution.py:208
  46.5 9.5 %collective-permute-start.22 = (f32[8,1792]{1,0:T(8,128)S(1)}, f32[8,1792]{1,0:T(8,128)S(1)}, u32[]{:S(2)}, u32[]{:S(2)}) collective-permute-start(f32[8,1792]{1,0:T(8,128)S(1)} %get-tuple-element.83), channel_id=1, source_target_pairs={{0,16},{4,20},{8,24},{12,28},{16,0},{20,4},{24,8},{28,12},{1,17},{... | collective-permute-start | bytes 172040 | tf_op jit(solution)/shard_map/ppermute | solution.py:208
  49.5 8.2 %collective-permute-start.23 = (f32[8,1792]{1,0:T(8,128)S(1)}, f32[8,1792]{1,0:T(8,128)S(1)}, u32[]{:S(2)}, u32[]{:S(2)}) collective-permute-start(f32[8,1792]{1,0:T(8,128)S(1)} %get-tuple-element.84), channel_id=1, source_target_pairs={{0,16},{4,20},{8,24},{12,28},{16,0},{20,4},{24,8},{28,12},{1,17},{... | collective-permute-start | bytes 172040 | tf_op jit(solution)/shard_map/ppermute | solution.py:208
  49.7 8.1 %collective-permute-start.24 = (f32[8,1792]{1,0:T(8,128)S(1)}, f32[8,1792]{1,0:T(8,128)S(1)}, u32[]{:S(2)}, u32[]{:S(2)}) collective-permute-start(f32[8,1792]{1,0:T(8,128)S(1)} %get-tuple-element.85), channel_id=1, source_target_pairs={{0,8},{4,12},{8,0},{12,4},{16,24},{20,28},{24,16},{28,20},{1,9},{5... | collective-permute-start | bytes 172040 | tf_op jit(solution)/shard_map/ppermute | solution.py:208
  51.3 6.4 %collective-permute-start.25 = (f32[8,1792]{1,0:T(8,128)S(1)}, f32[8,1792]{1,0:T(8,128)S(1)}, u32[]{:S(2)}, u32[]{:S(2)}) collective-permute-start(f32[8,1792]{1,0:T(8,128)S(1)} %get-tuple-element.86), channel_id=1, source_target_pairs={{0,24},{4,28},{8,16},{12,20},{16,8},{20,12},{24,0},{28,4},{1,25},{... | collective-permute-start | bytes 172040 | tf_op jit(solution)/shard_map/ppermute | solution.py:208

commit v12 on v11

--- a/solution.py
+++ b/solution.py
@@ -9,6 +9,7 @@
 
 EIGHTHS = (2,2,2,2)
 BLOCK = 512
+FAR_FIRST = (0, 1)
 F32 = jnp.float32
 BF16 = jnp.bfloat16
 NT = (((1,), (1,)), ((), ()))
@@ -47,11 +48,19 @@
     return owner
 
 
-def column_of(position, k, n_row, pieces):
+def owner_of(place, order):
+    return sum(place // (1 << (len(order) - 1 - i)) % 2 * bit for i, bit in enumerate(order))
+
+
+def place_of(owner, order):
+    return sum(owner // bit % 2 * (1 << (len(order) - 1 - i)) for i, bit in enumerate(order))
+
+
+def column_of(position, k, n_row, pieces, orders):
     column, first, done = position * 0, 0, 0
-    for piece in pieces:
+    for piece, order in zip(pieces, orders):
         rest = position - first
-        found = owner_at(rest // piece, n_row) * (k // n_row) + done + rest % piece
+        found = owner_of(rest // piece, order) * (k // n_row) + done + rest % piece
         column = jnp.where((rest >= 0) & (rest < piece * n_row), found, column)
         first += piece * n_row
         done += piece
@@ -77,14 +86,14 @@
         out[:, block] = lax.dot_general(omega_t[...], held[block, :], NT, preferred_element_type=F32)
 
 
-def first_half_body(n_row, pieces, delta, omega, held, omega_t, out, omega_v, sem, omega_sem):
+def first_half_body(n_row, pieces, orders, delta, omega, held, omega_t, out, omega_v, sem, omega_sem):
     k = out.shape[0]
     fetch = pltpu.make_async_copy(omega, omega_v, omega_sem)
     fetch.start()
     copies = stream_half(delta, held, sem, False)
     position = lax.broadcasted_iota(jnp.int32, (k, k), 0)
     column = lax.broadcasted_iota(jnp.int32, (k, k), 1)
-    pick = jnp.where(column_of(position, k, n_row, pieces) == column, 1.0, 0.0).astype(BF16)
+    pick = jnp.where(column_of(position, k, n_row, pieces, orders) == column, 1.0, 0.0).astype(BF16)
     fetch.wait()
     omega_t[...] = lax.dot_general(pick, omega_v[...], NT, preferred_element_type=F32).astype(BF16)
     sketch_half(omega_t, held, copies, out)
@@ -182,7 +191,7 @@
         used += count
 
 
-def final_sketch_body(n_row, pieces, splits, *refs):
+def final_sketch_body(n_row, pieces, splits, orders, *refs):
     out, done = refs[-2:]
     n, rows = sum(splits), refs[0].shape[1]
     parity = lax.rem(lax.axis_index("col"), 2)
@@ -193,8 +202,9 @@
             lanes = pl.ds(b * 128, 128)
             found = []
             for r in range(n_row):
-                place, used = owner_at(r, n_row), 0
-                for piece, split in zip(pieces, splits):
+                used = 0
+                for piece, split, order in zip(pieces, splits, orders):
+                    place = place_of(r, order)
                     per_part = n_row // split
                     part = parts[used + place // per_part]
                     found.append(part[pl.ds(place % per_part * piece, piece), lanes])
@@ -218,11 +228,12 @@
     n = len(pieces)
     splits = SPLITS if len(SPLITS) == n else (2,) * n
     bits = [1 << i for i in range(n_row.bit_length() - 1)]
+    orders = [[1, 4, 2] if n == 4 and len(bits) == 3 and c in FAR_FIRST else bits for c in range(n)]
 
     in_hbm = pltpu.with_memory_space_constraint(delta, pltpu.HBM)
     sems = pltpu.SemaphoreType.DMA((half // BLOCK,))
     held_other, omega_t, to_send = call(
-        functools.partial(first_half_body, n_row, pieces),
+        functools.partial(first_half_body, n_row, pieces, orders),
         (in_hbm, pltpu.with_memory_space_constraint(omega, pltpu.HBM)),
         [((half, d), BF16), ((k, d), BF16), ((k, half), F32)],
         "aa",
@@ -287,14 +298,15 @@
             if s == 1:
                 pending[group] = [x for c in group for x in pending[(c,)]]
             segments = [widths[c] >> s for c in group]
-            body = functools.partial(add_send_body, bits[s], segments)
+            bit = orders[group[0]][s]
+            body = functools.partial(add_send_body, bit, segments)
             outs = [((sum(segments) // 2, d), F32)] * 2
             send, keep = call(body, pending[group], outs, after=last, weight=weight)
-            pending[group] = keep, swap(send, "row", n_row, bits[s])
+            pending[group] = keep, swap(send, "row", n_row, bit)
             last = (keep,)
         else:
             parts = [[x for found in halves.values() for x in found] for halves in (owns, others)]
-            sketch, done = finish_sketch(n_row, k, pieces, splits, *parts, last)
+            sketch, done = finish_sketch(n_row, k, pieces, splits, orders, *parts, last)
             last = (done,)
     flat = [x for group in groups for x in pending[group]]
     if per_owner % 8 == 0:
@@ -305,12 +317,12 @@
     return sketch, corange.T
 
 
-def finish_sketch(n_row, k, pieces, splits, owns, others, after):
+def finish_sketch(n_row, k, pieces, splits, orders, owns, others, after):
     half = owns[0].shape[1]
     if k // n_row % 8 == 0:
-        body = functools.partial(final_sketch_body, n_row, pieces, splits)
+        body = functools.partial(final_sketch_body, n_row, pieces, splits, orders)
         return call(body, (*owns, *others), [((2 * half, k), F32), ((8, 128), F32)], after=after, results=1)
-    places = jnp.array([owner_at(r, n_row) for r in range(n_row)])
+    places = jnp.array([place_of(r, orders[0]) for r in range(n_row)])
 
     def columns(parts):
         starts = [sum(splits[:c]) for c in range(len(splits))]

time: 58.6 us -> 61.1 us (1.043)
  waiting for transfers between devices: 14.1 us -> 17.3 us
    ppermute x26, waiting for transfers between devices: 14.1 us -> 17.3 us  [swap(): return lax.ppermute(x, axis, [(i, i ^ bit) for i in range(size)])]
    ppermute x26, starting transfers between devices: 28.3 us -> 27.7 us  [swap(): return lax.ppermute(x, axis, [(i, i ^ bit) for i in range(size)])]
  transfers between devices with their start and end apart: 26 -> 26, of which waited for: 10 -> 10; matrix products, arithmetic and copies ran while one was open for 0% -> 0% of each run, Pallas kernels for 19% -> 18%
where the time goes in v12:
time: 61.1 us; the launch traced here: 61 us
  starting transfers between devices  27.7 us (45%)
  waiting for transfers between devices  17.3 us (28%)
  Pallas kernels  15.2 us (25%)
  between operations  0.87 us (1%)
    ppermute x26, starting transfers between devices, swap(): return lax.ppermute(x, axis, [(i, i ^ bit) for i in range(size)])  27.7 us
    ppermute x26, waiting for transfers between devices, swap(): return lax.ppermute(x, axis, [(i, i ^ bit) for i in range(size)])  17.3 us
    pallas_call x24, Pallas kernels, call(): pl.pallas_call(run, out_shape=[pltpu.VMEM(*o) if i >= results else jax.Sh...  15.2 us
  transfers between devices with their start and end apart: 26, of which 10 were waited for; matrix products, arithmetic and copies ran while one was open for 0% of the time, Pallas kernels for 18%

profile of v12, /device:TPU:0, one launch (start us, length us, event | category | flops | bytes accessed | tf_op | source)
XLA Modules:
  0.0 61.0 jit_solution(99367647940317979)
XLA Ops:
  0.6 3.2 %shard_map.41 = (bf16[1024,1792]{1,0:T(8,128)(2,1)S(1)}, bf16[256,1792]{1,0:T(8,128)(2,1)S(1)}, f32[256,1024]{1,0:T(8,128)S(1)}) custom-call(bf16[2048,1792]{1,0:T(8,128)(2,1)} %refs_0_.3, bf16[1792,256]{1,0:T(8,128)(2,1)} %refs_1_.1), custom_call_target="tpu_custom_call" | custom-call | tf_op jit(solution)/shard_map/pallas_call | solution.py:31
  4.3 2.9 %shard_map.42 = (bf16[1024,1792]{1,0:T(8,128)(2,1)S(1)}, f32[256,1024]{1,0:T(8,128)S(1)}) custom-call(bf16[2048,1792]{1,0:T(8,128)(2,1)} %refs_0_.3, bf16[256,1792]{1,0:T(8,128)(2,1)S(1)} %get-tuple-element.45.refs_1_), custom_call_target="tpu_custom_call" | custom-call | tf_op jit(solution)/shard_map/pallas_call | solution.py:31
  7.3 2.6 %collective-permute-start.1 = (f32[64,1024]{1,0:T(8,128)S(1)}, f32[64,1024]{1,0:T(8,128)S(1)}, u32[]{:S(2)}, u32[]{:S(2)}) collective-permute-start(f32[64,1024]{1,0:T(8,128)S(1)} %get-tuple-element.48.refs_0_), channel_id=1, source_target_pairs={{0,2},{1,3},{2,0},{3,1},{4,6},{5,7},{6,4},{7,5},{8,10},{9,11},{10,... | collective-permute-start | bytes 786440 | tf_op jit(solution)/shard_map/ppermute | solution.py:218
  10.0 7.1 %collective-permute-done.1.refs_1_ = f32[64,1024]{1,0:T(8,128)S(1)} collective-permute-done((f32[64,1024]{1,0:T(8,128)S(1)}, f32[64,1024]{1,0:T(8,128)S(1)}, u32[]{:S(2)}, u32[]{:S(2)}) %collective-permute-start.1) | collective-permute-done | bytes 262176 | tf_op jit(solution)/shard_map/ppermute | solution.py:218
  17.7 0.7 %shard_map.45.refs_3_.refs_4_ = f32[64,1792]{1,0:T(8,128)S(1)} custom-call(f32[32,1024]{1,0:T(8,128)S(1)} %get-tuple-element.49.refs_0_.refs_3_, f32[32,1024]{1,0:T(8,128)S(1)} %get-tuple-element.50.refs_1_, bf16[1024,1792]{1,0:T(8,128)(2,1)S(1)} %get-tuple-element.53.refs_2_, f32[32,1024]{1,0:T(8,128)S(1)} %get-tuple-element.49.refs_0_.refs_3_), custom_call_target="tpu_custom_call" | custom-call | tf_op jit(solution)/shard_map/pallas_call | solution.py:31
  18.7 0.8 %shard_map.46 = (f32[32,1792]{1,0:T(8,128)S(1)}, f32[32,1792]{1,0:T(8,128)S(1)}) custom-call(f32[32,1024]{1,0:T(8,128)S(1)} %collective-permute-done.3.refs_0_.refs_8_, f32[32,1024]{1,0:T(8,128)S(1)} %collective-permute-done.4.refs_1_.refs_9_, bf16[1024,1792]{1,0:T(8,128)(2,1)S(1)} %get-tuple-element.52.refs_2_, f32[64,1792]{1,0:T(8,128)S(1)} %shard_map.45.refs_3_.refs_4_, ...), custom_call_target="tpu_custom_call" | custom-call | tf_op jit(solution)/shard_map/pallas_call | solution.py:31
  19.5 2.0 %collective-permute-start.6 = (f32[32,1792]{1,0:T(8,128)S(1)}, f32[32,1792]{1,0:T(8,128)S(1)}, u32[]{:S(2)}, u32[]{:S(2)}) collective-permute-start(f32[32,1792]{1,0:T(8,128)S(1)} %get-tuple-element.58), channel_id=1, source_target_pairs={{0,4},{4,0},{8,12},{12,8},{16,20},{20,16},{24,28},{28,24},{1,5},{5... | collective-permute-start | bytes 688136 | tf_op jit(solution)/shard_map/ppermute | solution.py:218
  21.5 1.5 %collective-permute-start.5 = (f32[64,1024]{1,0:T(8,128)S(1)}, f32[64,1024]{1,0:T(8,128)S(1)}, u32[]{:S(2)}, u32[]{:S(2)}) collective-permute-start(f32[64,1024]{1,0:T(8,128)S(1)} %get-tuple-element.57.refs_0_), channel_id=1, source_target_pairs={{0,2},{1,3},{2,0},{3,1},{4,6},{5,7},{6,4},{7,5},{8,10},{9,11},{10,... | collective-permute-start | bytes 786440 | tf_op jit(solution)/shard_map/ppermute | solution.py:218
  23.6 1.2 %collective-permute-start.9 = (f32[64,1024]{1,0:T(8,128)S(1)}, f32[64,1024]{1,0:T(8,128)S(1)}, u32[]{:S(2)}, u32[]{:S(2)}) collective-permute-start(f32[64,1024]{1,0:T(8,128)S(1)} %get-tuple-element.63.refs_0_), channel_id=1, source_target_pairs={{0,2},{1,3},{2,0},{3,1},{4,6},{5,7},{6,4},{7,5},{8,10},{9,11},{10,... | collective-permute-start | bytes 786440 | tf_op jit(solution)/shard_map/ppermute | solution.py:218
  24.9 0.7 %shard_map.48.refs_3_.refs_4_ = f32[64,1792]{1,0:T(8,128)S(1)} custom-call(f32[32,1024]{1,0:T(8,128)S(1)} %get-tuple-element.55.refs_0_.refs_3_.refs_2_, f32[32,1024]{1,0:T(8,128)S(1)} %get-tuple-element.56.refs_1_.refs_3_, bf16[1024,1792]{1,0:T(8,128)(2,1)S(1)} %get-tuple-element.53.refs_2_, f32[32,1024]{1,0:T(8,128)S(1)} %get-tuple-element.55.refs_0_.refs_3_.refs_2_), custom_call_target="tpu_custom_call" | custom-call | flops 500000000 | tf_op jit(solution)/shard_map/pallas_call | solution.py:31
  25.6 0.8 %shard_map.49 = (f32[32,1792]{1,0:T(8,128)S(1)}, f32[32,1792]{1,0:T(8,128)S(1)}) custom-call(f32[32,1024]{1,0:T(8,128)S(1)} %collective-permute-done.7.refs_0_.refs_10_, f32[32,1024]{1,0:T(8,128)S(1)} %collective-permute-done.8.refs_1_.refs_11_, bf16[1024,1792]{1,0:T(8,128)(2,1)S(1)} %get-tuple-element.52.refs_2_, f32[64,1792]{1,0:T(8,128)S(1)} %shard_map.48.refs_3_.refs_4_, ...), custom_call_target="tpu_custom_call" | custom-call | tf_op jit(solution)/shard_map/pallas_call | solution.py:31
  26.4 1.6 %collective-permute-start.10 = (f32[32,1792]{1,0:T(8,128)S(1)}, f32[32,1792]{1,0:T(8,128)S(1)}, u32[]{:S(2)}, u32[]{:S(2)}) collective-permute-start(f32[32,1792]{1,0:T(8,128)S(1)} %get-tuple-element.64), channel_id=1, source_target_pairs={{0,4},{4,0},{8,12},{12,8},{16,20},{20,16},{24,28},{28,24},{1,5},{5... | collective-permute-start | bytes 688136 | tf_op jit(solution)/shard_map/ppermute | solution.py:218
  28.0 2.7 %collective-permute-done.5.refs_1_ = f32[64,1024]{1,0:T(8,128)S(1)} collective-permute-done((f32[64,1024]{1,0:T(8,128)S(1)}, f32[64,1024]{1,0:T(8,128)S(1)}, u32[]{:S(2)}, u32[]{:S(2)}) %collective-permute-start.5) | collective-permute-done | bytes 262176 | tf_op jit(solution)/shard_map/ppermute | solution.py:218
  31.3 0.7 %shard_map.52.refs_3_.refs_4_ = f32[64,1792]{1,0:T(8,128)S(1)} custom-call(f32[32,1024]{1,0:T(8,128)S(1)} %get-tuple-element.61.refs_0_.refs_3_.refs_4_, f32[32,1024]{1,0:T(8,128)S(1)} %get-tuple-element.62.refs_1_.refs_5_, bf16[1024,1792]{1,0:T(8,128)(2,1)S(1)} %get-tuple-element.53.refs_2_, f32[32,1024]{1,0:T(8,128)S(1)} %get-tuple-element.61.refs_0_.refs_3_.refs_4_), custom_call_target="tpu_custom_call" | custom-call | tf_op jit(solution)/shard_map/pallas_call | solution.py:31
  32.3 0.8 %shard_map.53 = (f32[32,1792]{1,0:T(8,128)S(1)}, f32[32,1792]{1,0:T(8,128)S(1)}) custom-call(f32[32,1024]{1,0:T(8,128)S(1)} %collective-permute-done.11.refs_0_.refs_12_, f32[32,1024]{1,0:T(8,128)S(1)} %collective-permute-done.12.refs_1_.refs_13_, bf16[1024,1792]{1,0:T(8,128)(2,1)S(1)} %get-tuple-element.52.refs_2_, ...), custom_call_target="tpu_custom_call" | custom-call | tf_op jit(solution)/shard_map/pallas_call | solution.py:31
  33.2 3.0 %collective-permute-start.18 = (f32[16,1792]{1,0:T(8,128)S(1)}, f32[16,1792]{1,0:T(8,128)S(1)}, u32[]{:S(2)}, u32[]{:S(2)}) collective-permute-start(f32[16,1792]{1,0:T(8,128)S(1)} %get-tuple-element.74), channel_id=1, source_target_pairs={{0,16},{4,20},{8,24},{12,28},{16,0},{20,4},{24,8},{28,12},{1,17},{... | collective-permute-start | bytes 344072 | tf_op jit(solution)/shard_map/ppermute | solution.py:218
  36.9 1.7 %collective-permute-start.19 = (f32[16,1792]{1,0:T(8,128)S(1)}, f32[16,1792]{1,0:T(8,128)S(1)}, u32[]{:S(2)}, u32[]{:S(2)}) collective-permute-start(f32[16,1792]{1,0:T(8,128)S(1)} %get-tuple-element.75), channel_id=1, source_target_pairs={{0,16},{4,20},{8,24},{12,28},{16,0},{20,4},{24,8},{28,12},{1,17},{... | collective-permute-start | bytes 344072 | tf_op jit(solution)/shard_map/ppermute | solution.py:218
  38.6 0.7 %shard_map.56.refs_3_.refs_4_ = f32[64,1792]{1,0:T(8,128)S(1)} custom-call(f32[32,1024]{1,0:T(8,128)S(1)} %get-tuple-element.67.refs_0_.refs_3_.refs_6_, f32[32,1024]{1,0:T(8,128)S(1)} %get-tuple-element.68.refs_1_.refs_7_, bf16[1024,1792]{1,0:T(8,128)(2,1)S(1)} %get-tuple-element.53.refs_2_, f32[32,1024]{1,0:T(8,128)S(1)} %get-tuple-element.67.refs_0_.refs_3_.refs_6_), custom_call_target="tpu_custom_call" | custom-call | flops 2000000000 | tf_op jit(solution)/shard_map/pallas_call | solution.py:31
  39.4 0.8 %shard_map.57 = (f32[32,1792]{1,0:T(8,128)S(1)}, f32[32,1792]{1,0:T(8,128)S(1)}) custom-call(f32[32,1024]{1,0:T(8,128)S(1)} %collective-permute-done.13.refs_0_.refs_14_, f32[32,1024]{1,0:T(8,128)S(1)} %collective-permute-done.14.refs_1_.refs_15_, bf16[1024,1792]{1,0:T(8,128)(2,1)S(1)} %get-tuple-element.52.refs_2_, ...), custom_call_target="tpu_custom_call" | custom-call | tf_op jit(solution)/shard_map/pallas_call | solution.py:31
  40.1 0.6 collective-permute-start.15
  41.0 1.6 %collective-permute-start.17 = (f32[16,1792]{1,0:T(8,128)S(1)}, f32[16,1792]{1,0:T(8,128)S(1)}, u32[]{:S(2)}, u32[]{:S(2)}) collective-permute-start(f32[16,1792]{1,0:T(8,128)S(1)} %get-tuple-element.73), channel_id=1, source_target_pairs={{0,8},{4,12},{8,0},{12,4},{16,24},{20,28},{24,16},{28,20},{1,9},{5... | collective-permute-start | bytes 344072 | tf_op jit(solution)/shard_map/ppermute | solution.py:218
  42.7 4.4 %collective-permute-done.19.refs_1_ = f32[16,1792]{1,0:T(8,128)S(1)} collective-permute-done((f32[16,1792]{1,0:T(8,128)S(1)}, f32[16,1792]{1,0:T(8,128)S(1)}, u32[]{:S(2)}, u32[]{:S(2)}) %collective-permute-start.19) | collective-permute-done | bytes 114720 | tf_op jit(solution)/shard_map/ppermute | solution.py:218
  47.2 0.7 %collective-permute-start.20 = (f32[8,1792]{1,0:T(8,128)S(1)}, f32[8,1792]{1,0:T(8,128)S(1)}, u32[]{:S(2)}, u32[]{:S(2)}) collective-permute-start(f32[8,1792]{1,0:T(8,128)S(1)} %get-tuple-element.81), channel_id=1, source_target_pairs={{0,8},{4,12},{8,0},{12,4},{16,24},{20,28},{24,16},{28,20},{1,9},{5... | collective-permute-start | bytes 172040 | tf_op jit(solution)/shard_map/ppermute | solution.py:218
  47.9 1.4 %collective-permute-start.21 = (f32[8,1792]{1,0:T(8,128)S(1)}, f32[8,1792]{1,0:T(8,128)S(1)}, u32[]{:S(2)}, u32[]{:S(2)}) collective-permute-start(f32[8,1792]{1,0:T(8,128)S(1)} %get-tuple-element.82), channel_id=1, source_target_pairs={{0,8},{4,12},{8,0},{12,4},{16,24},{20,28},{24,16},{28,20},{1,9},{5... | collective-permute-start | bytes 172040 | tf_op jit(solution)/shard_map/ppermute | solution.py:218
  49.3 2.2 %collective-permute-start.22 = (f32[8,1792]{1,0:T(8,128)S(1)}, f32[8,1792]{1,0:T(8,128)S(1)}, u32[]{:S(2)}, u32[]{:S(2)}) collective-permute-start(f32[8,1792]{1,0:T(8,128)S(1)} %get-tuple-element.83), channel_id=1, source_target_pairs={{0,16},{4,20},{8,24},{12,28},{16,0},{20,4},{24,8},{28,12},{1,17},{... | collective-permute-start | bytes 172040 | tf_op jit(solution)/shard_map/ppermute | solution.py:218
  51.5 0.8 %collective-permute-start.23 = (f32[8,1792]{1,0:T(8,128)S(1)}, f32[8,1792]{1,0:T(8,128)S(1)}, u32[]{:S(2)}, u32[]{:S(2)}) collective-permute-start(f32[8,1792]{1,0:T(8,128)S(1)} %get-tuple-element.84), channel_id=1, source_target_pairs={{0,16},{4,20},{8,24},{12,28},{16,0},{20,4},{24,8},{28,12},{1,17},{... | collective-permute-start | bytes 172040 | tf_op jit(solution)/shard_map/ppermute | solution.py:218
  52.4 1.4 %collective-permute-start.24 = (f32[8,1792]{1,0:T(8,128)S(1)}, f32[8,1792]{1,0:T(8,128)S(1)}, u32[]{:S(2)}, u32[]{:S(2)}) collective-permute-start(f32[8,1792]{1,0:T(8,128)S(1)} %get-tuple-element.85), channel_id=1, source_target_pairs={{0,8},{4,12},{8,0},{12,4},{16,24},{20,28},{24,16},{28,20},{1,9},{5... | collective-permute-start | bytes 172040 | tf_op jit(solution)/shard_map/ppermute | solution.py:218
  53.8 2.3 %collective-permute-start.25 = (f32[8,1792]{1,0:T(8,128)S(1)}, f32[8,1792]{1,0:T(8,128)S(1)}, u32[]{:S(2)}, u32[]{:S(2)}) collective-permute-start(f32[8,1792]{1,0:T(8,128)S(1)} %get-tuple-element.86), channel_id=1, source_target_pairs={{0,24},{4,28},{8,16},{12,20},{16,8},{20,12},{24,0},{28,4},{1,25},{... | collective-permute-start | bytes 172040 | tf_op jit(solution)/shard_map/ppermute | solution.py:218
  56.1 1.9 %shard_map.63 = (f32[2048,256]{1,0:T(8,128)}, f32[8,128]{1,0:T(8,128)S(1)}) custom-call(f32[32,1024]{1,0:T(8,128)S(1)} %get-tuple-element.49.refs_0_.refs_3_, f32[32,1024]{1,0:T(8,128)S(1)} %get-tuple-element.50.refs_1_, f32[32,1024]{1,0:T(8,128)S(1)} %get-tuple-element.55.refs_0_.refs_3_.refs_2_, f32[32,1024]{1,0:T(8,128)S(1)} %get-tuple-element.56.refs_1_.refs_3_, ...), custom_call_target="tpu_custom_call" | custom-call | tf_op jit(solution)/shard_map/pallas_call | solution.py:31
  58.0 1.1 %collective-permute-done.23.refs_7_ = f32[8,1792]{1,0:T(8,128)S(1)} collective-permute-done((f32[8,1792]{1,0:T(8,128)S(1)}, f32[8,1792]{1,0:T(8,128)S(1)}, u32[]{:S(2)}, u32[]{:S(2)}) %collective-permute-start.23) | collective-permute-done | bytes 57376 | tf_op jit(solution)/shard_map/ppermute | solution.py:218
  59.1 1.1 %collective-permute-done.25.refs_9_ = f32[8,1792]{1,0:T(8,128)S(1)} collective-permute-done((f32[8,1792]{1,0:T(8,128)S(1)}, f32[8,1792]{1,0:T(8,128)S(1)}, u32[]{:S(2)}, u32[]{:S(2)}) %collective-permute-start.25) | collective-permute-done | bytes 57376 | tf_op jit(solution)/shard_map/ppermute | solution.py:218
  60.2 0.7 %shard_map.64 = f32[32,1792]{1,0:T(8,128)} custom-call(f32[8,1792]{1,0:T(8,128)S(1)} %get-tuple-element.77.refs_2_.refs_0_, f32[8,1792]{1,0:T(8,128)S(1)} %collective-permute-done.20.refs_1_, f32[8,1792]{1,0:T(8,128)S(1)} %get-tuple-element.76.refs_2_, f32[8,1792]{1,0:T(8,128)S(1)} %collective-permute-done.21.refs_3_, ...), custom_call_target="tpu_custom_call" | custom-call | flops 500000000 | tf_op jit(solution)/shard_map/pallas_call | solution.py:31
  (44 shorter events, 4.3 us)
Async XLA Ops:
  3.8 3.4 %collective-permute-start = (f32[256,1024]{1,0:T(8,128)S(1)}, f32[256,1024]{1,0:T(8,128)S(1)}, u32[]{:S(2)}, u32[]{:S(2)}) collective-permute-start(f32[256,1024]{1,0:T(8,128)S(1)} %get-tuple-element.47), channel_id=1, source_target_pairs={{0,1},{1,0},{2,3},{3,2},{4,5},{5,4},{6,7},{7,6},{8,9},{9,8},{10,11... | collective-permute-start | bytes 3145736 | tf_op jit(solution)/shard_map/ppermute | solution.py:218
  7.3 9.7 %collective-permute-start.1 = (f32[64,1024]{1,0:T(8,128)S(1)}, f32[64,1024]{1,0:T(8,128)S(1)}, u32[]{:S(2)}, u32[]{:S(2)}) collective-permute-start(f32[64,1024]{1,0:T(8,128)S(1)} %get-tuple-element.48.refs_0_), channel_id=1, source_target_pairs={{0,2},{1,3},{2,0},{3,1},{4,6},{5,7},{6,4},{7,5},{8,10},{9,11},{10,... | collective-permute-start | bytes 786440 | tf_op jit(solution)/shard_map/ppermute | solution.py:218
  9.9 13.1 %collective-permute-start.2 = (f32[64,1024]{1,0:T(8,128)S(1)}, f32[64,1024]{1,0:T(8,128)S(1)}, u32[]{:S(2)}, u32[]{:S(2)}) collective-permute-start(f32[64,1024]{1,0:T(8,128)S(1)} %get-tuple-element.51.refs_0_), channel_id=1, source_target_pairs={{0,2},{1,3},{2,0},{3,1},{4,6},{5,7},{6,4},{7,5},{8,10},{9,11},{10,... | collective-permute-start | bytes 786440 | tf_op jit(solution)/shard_map/ppermute | solution.py:218
  17.1 1.4 %collective-permute-start.3 = (f32[32,1024]{1,0:T(8,128)S(1)}, f32[32,1024]{1,0:T(8,128)S(1)}, u32[]{:S(2)}, u32[]{:S(2)}) collective-permute-start(f32[32,1024]{1,0:T(8,128)S(1)} %get-tuple-element.49.refs_0_.refs_3_), channel_id=1, source_target_pairs={{0,1},{1,0},{2,3},{3,2},{4,5},{5,4},{6,7},{7,6},{8,9},{9,8},{10,11... | collective-permute-start | bytes 393224 | tf_op jit(solution)/shard_map/ppermute | solution.py:218
  17.2 1.5 %collective-permute-start.4 = (f32[32,1024]{1,0:T(8,128)S(1)}, f32[32,1024]{1,0:T(8,128)S(1)}, u32[]{:S(2)}, u32[]{:S(2)}) collective-permute-start(f32[32,1024]{1,0:T(8,128)S(1)} %get-tuple-element.50.refs_1_), channel_id=1, source_target_pairs={{0,1},{1,0},{2,3},{3,2},{4,5},{5,4},{6,7},{7,6},{8,9},{9,8},{10,11... | collective-permute-start | bytes 393224 | tf_op jit(solution)/shard_map/ppermute | solution.py:218
  19.5 8.5 %collective-permute-start.6 = (f32[32,1792]{1,0:T(8,128)S(1)}, f32[32,1792]{1,0:T(8,128)S(1)}, u32[]{:S(2)}, u32[]{:S(2)}) collective-permute-start(f32[32,1792]{1,0:T(8,128)S(1)} %get-tuple-element.58), channel_id=1, source_target_pairs={{0,4},{4,0},{8,12},{12,8},{16,20},{20,16},{24,28},{28,24},{1,5},{5... | collective-permute-start | bytes 688136 | tf_op jit(solution)/shard_map/ppermute | solution.py:218
  21.5 9.2 %collective-permute-start.5 = (f32[64,1024]{1,0:T(8,128)S(1)}, f32[64,1024]{1,0:T(8,128)S(1)}, u32[]{:S(2)}, u32[]{:S(2)}) collective-permute-start(f32[64,1024]{1,0:T(8,128)S(1)} %get-tuple-element.57.refs_0_), channel_id=1, source_target_pairs={{0,2},{1,3},{2,0},{3,1},{4,6},{5,7},{6,4},{7,5},{8,10},{9,11},{10,... | collective-permute-start | bytes 786440 | tf_op jit(solution)/shard_map/ppermute | solution.py:218
  23.1 2.6 %collective-permute-start.7 = (f32[32,1024]{1,0:T(8,128)S(1)}, f32[32,1024]{1,0:T(8,128)S(1)}, u32[]{:S(2)}, u32[]{:S(2)}) collective-permute-start(f32[32,1024]{1,0:T(8,128)S(1)} %get-tuple-element.55.refs_0_.refs_3_.refs_2_), channel_id=1, source_target_pairs={{0,1},{1,0},{2,3},{3,2},{4,5},{5,4},{6,7},{7,6},{8,9},{9,8},{10,11... | collective-permute-start | bytes 393224 | tf_op jit(solution)/shard_map/ppermute | solution.py:218
  23.1 2.5 %collective-permute-start.8 = (f32[32,1024]{1,0:T(8,128)S(1)}, f32[32,1024]{1,0:T(8,128)S(1)}, u32[]{:S(2)}, u32[]{:S(2)}) collective-permute-start(f32[32,1024]{1,0:T(8,128)S(1)} %get-tuple-element.56.refs_1_.refs_3_), channel_id=1, source_target_pairs={{0,1},{1,0},{2,3},{3,2},{4,5},{5,4},{6,7},{7,6},{8,9},{9,8},{10,11... | collective-permute-start | bytes 393224 | tf_op jit(solution)/shard_map/ppermute | solution.py:218
  23.6 12.7 %collective-permute-start.9 = (f32[64,1024]{1,0:T(8,128)S(1)}, f32[64,1024]{1,0:T(8,128)S(1)}, u32[]{:S(2)}, u32[]{:S(2)}) collective-permute-start(f32[64,1024]{1,0:T(8,128)S(1)} %get-tuple-element.63.refs_0_), channel_id=1, source_target_pairs={{0,2},{1,3},{2,0},{3,1},{4,6},{5,7},{6,4},{7,5},{8,10},{9,11},{10,... | collective-permute-start | bytes 786440 | tf_op jit(solution)/shard_map/ppermute | solution.py:218
  26.4 9.9 %collective-permute-start.10 = (f32[32,1792]{1,0:T(8,128)S(1)}, f32[32,1792]{1,0:T(8,128)S(1)}, u32[]{:S(2)}, u32[]{:S(2)}) collective-permute-start(f32[32,1792]{1,0:T(8,128)S(1)} %get-tuple-element.64), channel_id=1, source_target_pairs={{0,4},{4,0},{8,12},{12,8},{16,20},{20,16},{24,28},{28,24},{1,5},{5... | collective-permute-start | bytes 688136 | tf_op jit(solution)/shard_map/ppermute | solution.py:218
  30.7 1.4 %collective-permute-start.11 = (f32[32,1024]{1,0:T(8,128)S(1)}, f32[32,1024]{1,0:T(8,128)S(1)}, u32[]{:S(2)}, u32[]{:S(2)}) collective-permute-start(f32[32,1024]{1,0:T(8,128)S(1)} %get-tuple-element.61.refs_0_.refs_3_.refs_4_), channel_id=1, source_target_pairs={{0,1},{1,0},{2,3},{3,2},{4,5},{5,4},{6,7},{7,6},{8,9},{9,8},{10,11... | collective-permute-start | bytes 393224 | tf_op jit(solution)/shard_map/ppermute | solution.py:218
  30.8 1.5 %collective-permute-start.12 = (f32[32,1024]{1,0:T(8,128)S(1)}, f32[32,1024]{1,0:T(8,128)S(1)}, u32[]{:S(2)}, u32[]{:S(2)}) collective-permute-start(f32[32,1024]{1,0:T(8,128)S(1)} %get-tuple-element.62.refs_1_.refs_5_), channel_id=1, source_target_pairs={{0,1},{1,0},{2,3},{3,2},{4,5},{5,4},{6,7},{7,6},{8,9},{9,8},{10,11... | collective-permute-start | bytes 393224 | tf_op jit(solution)/shard_map/ppermute | solution.py:218
  33.1 7.9 %collective-permute-start.16 = (f32[32,1792]{1,0:T(8,128)S(1)}, f32[32,1792]{1,0:T(8,128)S(1)}, u32[]{:S(2)}, u32[]{:S(2)}) collective-permute-start(f32[32,1792]{1,0:T(8,128)S(1)} %get-tuple-element.71), channel_id=1, source_target_pairs={{0,4},{4,0},{8,12},{12,8},{16,20},{20,16},{24,28},{28,24},{1,5},{5... | collective-permute-start | bytes 688136 | tf_op jit(solution)/shard_map/ppermute | solution.py:218
  33.2 13.9 %collective-permute-start.18 = (f32[16,1792]{1,0:T(8,128)S(1)}, f32[16,1792]{1,0:T(8,128)S(1)}, u32[]{:S(2)}, u32[]{:S(2)}) collective-permute-start(f32[16,1792]{1,0:T(8,128)S(1)} %get-tuple-element.74), channel_id=1, source_target_pairs={{0,16},{4,20},{8,24},{12,28},{16,0},{20,4},{24,8},{28,12},{1,17},{... | collective-permute-start | bytes 344072 | tf_op jit(solution)/shard_map/ppermute | solution.py:218
  36.4 3.0 %collective-permute-start.13 = (f32[32,1024]{1,0:T(8,128)S(1)}, f32[32,1024]{1,0:T(8,128)S(1)}, u32[]{:S(2)}, u32[]{:S(2)}) collective-permute-start(f32[32,1024]{1,0:T(8,128)S(1)} %get-tuple-element.67.refs_0_.refs_3_.refs_6_), channel_id=1, source_target_pairs={{0,1},{1,0},{2,3},{3,2},{4,5},{5,4},{6,7},{7,6},{8,9},{9,8},{10,11... | collective-permute-start | bytes 393224 | tf_op jit(solution)/shard_map/ppermute | solution.py:218
  36.4 2.9 %collective-permute-start.14 = (f32[32,1024]{1,0:T(8,128)S(1)}, f32[32,1024]{1,0:T(8,128)S(1)}, u32[]{:S(2)}, u32[]{:S(2)}) collective-permute-start(f32[32,1024]{1,0:T(8,128)S(1)} %get-tuple-element.68.refs_1_.refs_7_), channel_id=1, source_target_pairs={{0,1},{1,0},{2,3},{3,2},{4,5},{5,4},{6,7},{7,6},{8,9},{9,8},{10,11... | collective-permute-start | bytes 393224 | tf_op jit(solution)/shard_map/ppermute | solution.py:218
  36.9 10.2 %collective-permute-start.19 = (f32[16,1792]{1,0:T(8,128)S(1)}, f32[16,1792]{1,0:T(8,128)S(1)}, u32[]{:S(2)}, u32[]{:S(2)}) collective-permute-start(f32[16,1792]{1,0:T(8,128)S(1)} %get-tuple-element.75), channel_id=1, source_target_pairs={{0,16},{4,20},{8,24},{12,28},{16,0},{20,4},{24,8},{28,12},{1,17},{... | collective-permute-start | bytes 344072 | tf_op jit(solution)/shard_map/ppermute | solution.py:218
  40.1 11.4 %collective-permute-start.15 = (f32[32,1792]{1,0:T(8,128)S(1)}, f32[32,1792]{1,0:T(8,128)S(1)}, u32[]{:S(2)}, u32[]{:S(2)}) collective-permute-start(f32[32,1792]{1,0:T(8,128)S(1)} %get-tuple-element.70), channel_id=1, source_target_pairs={{0,4},{4,0},{8,12},{12,8},{16,20},{20,16},{24,28},{28,24},{1,5},{5... | collective-permute-start | bytes 688136 | tf_op jit(solution)/shard_map/ppermute | solution.py:218
  41.0 8.2 %collective-permute-start.17 = (f32[16,1792]{1,0:T(8,128)S(1)}, f32[16,1792]{1,0:T(8,128)S(1)}, u32[]{:S(2)}, u32[]{:S(2)}) collective-permute-start(f32[16,1792]{1,0:T(8,128)S(1)} %get-tuple-element.73), channel_id=1, source_target_pairs={{0,8},{4,12},{8,0},{12,4},{16,24},{20,28},{24,16},{28,20},{1,9},{5... | collective-permute-start | bytes 344072 | tf_op jit(solution)/shard_map/ppermute | solution.py:218
  47.2 6.6 %collective-permute-start.20 = (f32[8,1792]{1,0:T(8,128)S(1)}, f32[8,1792]{1,0:T(8,128)S(1)}, u32[]{:S(2)}, u32[]{:S(2)}) collective-permute-start(f32[8,1792]{1,0:T(8,128)S(1)} %get-tuple-element.81), channel_id=1, source_target_pairs={{0,8},{4,12},{8,0},{12,4},{16,24},{20,28},{24,16},{28,20},{1,9},{5... | collective-permute-start | bytes 172040 | tf_op jit(solution)/shard_map/ppermute | solution.py:218
  47.9 10.1 %collective-permute-start.21 = (f32[8,1792]{1,0:T(8,128)S(1)}, f32[8,1792]{1,0:T(8,128)S(1)}, u32[]{:S(2)}, u32[]{:S(2)}) collective-permute-start(f32[8,1792]{1,0:T(8,128)S(1)} %get-tuple-element.82), channel_id=1, source_target_pairs={{0,8},{4,12},{8,0},{12,4},{16,24},{20,28},{24,16},{28,20},{1,9},{5... | collective-permute-start | bytes 172040 | tf_op jit(solution)/shard_map/ppermute | solution.py:218
  49.3 8.8 %collective-permute-start.22 = (f32[8,1792]{1,0:T(8,128)S(1)}, f32[8,1792]{1,0:T(8,128)S(1)}, u32[]{:S(2)}, u32[]{:S(2)}) collective-permute-start(f32[8,1792]{1,0:T(8,128)S(1)} %get-tuple-element.83), channel_id=1, source_target_pairs={{0,16},{4,20},{8,24},{12,28},{16,0},{20,4},{24,8},{28,12},{1,17},{... | collective-permute-start | bytes 172040 | tf_op jit(solution)/shard_map/ppermute | solution.py:218
  51.5 7.6 %collective-permute-start.23 = (f32[8,1792]{1,0:T(8,128)S(1)}, f32[8,1792]{1,0:T(8,128)S(1)}, u32[]{:S(2)}, u32[]{:S(2)}) collective-permute-start(f32[8,1792]{1,0:T(8,128)S(1)} %get-tuple-element.84), channel_id=1, source_target_pairs={{0,16},{4,20},{8,24},{12,28},{16,0},{20,4},{24,8},{28,12},{1,17},{... | collective-permute-start | bytes 172040 | tf_op jit(solution)/shard_map/ppermute | solution.py:218
  52.4 6.7 %collective-permute-start.24 = (f32[8,1792]{1,0:T(8,128)S(1)}, f32[8,1792]{1,0:T(8,128)S(1)}, u32[]{:S(2)}, u32[]{:S(2)}) collective-permute-start(f32[8,1792]{1,0:T(8,128)S(1)} %get-tuple-element.85), channel_id=1, source_target_pairs={{0,8},{4,12},{8,0},{12,4},{16,24},{20,28},{24,16},{28,20},{1,9},{5... | collective-permute-start | bytes 172040 | tf_op jit(solution)/shard_map/ppermute | solution.py:218
  53.8 6.4 %collective-permute-start.25 = (f32[8,1792]{1,0:T(8,128)S(1)}, f32[8,1792]{1,0:T(8,128)S(1)}, u32[]{:S(2)}, u32[]{:S(2)}) collective-permute-start(f32[8,1792]{1,0:T(8,128)S(1)} %get-tuple-element.86), channel_id=1, source_target_pairs={{0,24},{4,28},{8,16},{12,20},{16,8},{20,12},{24,0},{28,4},{1,25},{... | collective-permute-start | bytes 172040 | tf_op jit(solution)/shard_map/ppermute | solution.py:218

commit v13 on v12

--- a/solution.py
+++ b/solution.py
@@ -9,7 +9,7 @@
 
 EIGHTHS = (2,2,2,2)
 BLOCK = 512
-FAR_FIRST = (0, 1)
+FAR_FIRST = (1,)
 F32 = jnp.float32
 BF16 = jnp.bfloat16
 NT = (((1,), (1,)), ((), ()))

time: 61.1 us -> 59.1 us (0.967)
  waiting for transfers between devices: 17.3 us -> 15.1 us
    ppermute x26, waiting for transfers between devices: 17.3 us -> 15.1 us  [swap(): return lax.ppermute(x, axis, [(i, i ^ bit) for i in range(size)])]
  transfers between devices with their start and end apart: 26 -> 26, of which waited for: 10 -> 10; matrix products, arithmetic and copies ran while one was open for 0% -> 0% of each run, Pallas kernels for 18% -> 19%
where the time goes in v13:
time: 59.1 us; the launch traced here: 58.9 us
  starting transfers between devices  27.8 us (47%)
  Pallas kernels  15.2 us (26%)
  waiting for transfers between devices  15.1 us (26%)
  between operations  0.86 us (1%)
    ppermute x26, starting transfers between devices, swap(): return lax.ppermute(x, axis, [(i, i ^ bit) for i in range(size)])  27.8 us
    pallas_call x24, Pallas kernels, call(): pl.pallas_call(run, out_shape=[pltpu.VMEM(*o) if i >= results else jax.Sh...  15.2 us
    ppermute x26, waiting for transfers between devices, swap(): return lax.ppermute(x, axis, [(i, i ^ bit) for i in range(size)])  15.1 us
  transfers between devices with their start and end apart: 26, of which 10 were waited for; matrix products, arithmetic and copies ran while one was open for 0% of the time, Pallas kernels for 19%

profile of v13, /device:TPU:0, one launch (start us, length us, event | category | flops | bytes accessed | tf_op | source)
XLA Modules:
  0.0 58.9 jit_solution(17854805074392106667)
XLA Ops:
  0.6 3.2 %shard_map.41 = (bf16[1024,1792]{1,0:T(8,128)(2,1)S(1)}, bf16[256,1792]{1,0:T(8,128)(2,1)S(1)}, f32[256,1024]{1,0:T(8,128)S(1)}) custom-call(bf16[2048,1792]{1,0:T(8,128)(2,1)} %refs_0_.3, bf16[1792,256]{1,0:T(8,128)(2,1)} %refs_1_.1), custom_call_target="tpu_custom_call" | custom-call | tf_op jit(solution)/shard_map/pallas_call | solution.py:31
  3.8 0.5 collective-permute-start
  4.3 2.9 %shard_map.42 = (bf16[1024,1792]{1,0:T(8,128)(2,1)S(1)}, f32[256,1024]{1,0:T(8,128)S(1)}) custom-call(bf16[2048,1792]{1,0:T(8,128)(2,1)} %refs_0_.3, bf16[256,1792]{1,0:T(8,128)(2,1)S(1)} %get-tuple-element.45.refs_1_), custom_call_target="tpu_custom_call" | custom-call | tf_op jit(solution)/shard_map/pallas_call | solution.py:31
  7.3 2.6 %collective-permute-start.1 = (f32[64,1024]{1,0:T(8,128)S(1)}, f32[64,1024]{1,0:T(8,128)S(1)}, u32[]{:S(2)}, u32[]{:S(2)}) collective-permute-start(f32[64,1024]{1,0:T(8,128)S(1)} %get-tuple-element.48.refs_0_), channel_id=1, source_target_pairs={{0,2},{1,3},{2,0},{3,1},{4,6},{5,7},{6,4},{7,5},{8,10},{9,11},{10,... | collective-permute-start | bytes 786440 | tf_op jit(solution)/shard_map/ppermute | solution.py:218
  10.0 7.1 %collective-permute-done.1.refs_1_ = f32[64,1024]{1,0:T(8,128)S(1)} collective-permute-done((f32[64,1024]{1,0:T(8,128)S(1)}, f32[64,1024]{1,0:T(8,128)S(1)}, u32[]{:S(2)}, u32[]{:S(2)}) %collective-permute-start.1) | collective-permute-done | bytes 262176 | tf_op jit(solution)/shard_map/ppermute | solution.py:218
  17.2 0.5 collective-permute-start.4
  17.7 0.7 %shard_map.45.refs_3_.refs_4_ = f32[64,1792]{1,0:T(8,128)S(1)} custom-call(f32[32,1024]{1,0:T(8,128)S(1)} %get-tuple-element.49.refs_0_.refs_3_, f32[32,1024]{1,0:T(8,128)S(1)} %get-tuple-element.50.refs_1_, bf16[1024,1792]{1,0:T(8,128)(2,1)S(1)} %get-tuple-element.53.refs_2_, f32[32,1024]{1,0:T(8,128)S(1)} %get-tuple-element.49.refs_0_.refs_3_), custom_call_target="tpu_custom_call" | custom-call | tf_op jit(solution)/shard_map/pallas_call | solution.py:31
  18.7 0.8 %shard_map.46 = (f32[32,1792]{1,0:T(8,128)S(1)}, f32[32,1792]{1,0:T(8,128)S(1)}) custom-call(f32[32,1024]{1,0:T(8,128)S(1)} %collective-permute-done.3.refs_0_.refs_8_, f32[32,1024]{1,0:T(8,128)S(1)} %collective-permute-done.4.refs_1_.refs_9_, bf16[1024,1792]{1,0:T(8,128)(2,1)S(1)} %get-tuple-element.52.refs_2_, f32[64,1792]{1,0:T(8,128)S(1)} %shard_map.45.refs_3_.refs_4_, ...), custom_call_target="tpu_custom_call" | custom-call | tf_op jit(solution)/shard_map/pallas_call | solution.py:31
  19.5 2.0 %collective-permute-start.6 = (f32[32,1792]{1,0:T(8,128)S(1)}, f32[32,1792]{1,0:T(8,128)S(1)}, u32[]{:S(2)}, u32[]{:S(2)}) collective-permute-start(f32[32,1792]{1,0:T(8,128)S(1)} %get-tuple-element.58), channel_id=1, source_target_pairs={{0,4},{4,0},{8,12},{12,8},{16,20},{20,16},{24,28},{28,24},{1,5},{5... | collective-permute-start | bytes 688136 | tf_op jit(solution)/shard_map/ppermute | solution.py:218
  21.5 1.5 %collective-permute-start.5 = (f32[64,1024]{1,0:T(8,128)S(1)}, f32[64,1024]{1,0:T(8,128)S(1)}, u32[]{:S(2)}, u32[]{:S(2)}) collective-permute-start(f32[64,1024]{1,0:T(8,128)S(1)} %get-tuple-element.57.refs_0_), channel_id=1, source_target_pairs={{0,2},{1,3},{2,0},{3,1},{4,6},{5,7},{6,4},{7,5},{8,10},{9,11},{10,... | collective-permute-start | bytes 786440 | tf_op jit(solution)/shard_map/ppermute | solution.py:218
  23.6 1.2 %collective-permute-start.9 = (f32[64,1024]{1,0:T(8,128)S(1)}, f32[64,1024]{1,0:T(8,128)S(1)}, u32[]{:S(2)}, u32[]{:S(2)}) collective-permute-start(f32[64,1024]{1,0:T(8,128)S(1)} %get-tuple-element.63.refs_0_), channel_id=1, source_target_pairs={{0,2},{1,3},{2,0},{3,1},{4,6},{5,7},{6,4},{7,5},{8,10},{9,11},{10,... | collective-permute-start | bytes 786440 | tf_op jit(solution)/shard_map/ppermute | solution.py:218
  24.9 0.7 %shard_map.48.refs_3_.refs_4_ = f32[64,1792]{1,0:T(8,128)S(1)} custom-call(f32[32,1024]{1,0:T(8,128)S(1)} %get-tuple-element.55.refs_0_.refs_3_.refs_2_, f32[32,1024]{1,0:T(8,128)S(1)} %get-tuple-element.56.refs_1_.refs_3_, bf16[1024,1792]{1,0:T(8,128)(2,1)S(1)} %get-tuple-element.53.refs_2_, f32[32,1024]{1,0:T(8,128)S(1)} %get-tuple-element.55.refs_0_.refs_3_.refs_2_), custom_call_target="tpu_custom_call" | custom-call | flops 500000000 | tf_op jit(solution)/shard_map/pallas_call | solution.py:31
  25.6 0.8 %shard_map.49 = (f32[32,1792]{1,0:T(8,128)S(1)}, f32[32,1792]{1,0:T(8,128)S(1)}) custom-call(f32[32,1024]{1,0:T(8,128)S(1)} %collective-permute-done.7.refs_0_.refs_10_, f32[32,1024]{1,0:T(8,128)S(1)} %collective-permute-done.8.refs_1_.refs_11_, bf16[1024,1792]{1,0:T(8,128)(2,1)S(1)} %get-tuple-element.52.refs_2_, f32[64,1792]{1,0:T(8,128)S(1)} %shard_map.48.refs_3_.refs_4_, ...), custom_call_target="tpu_custom_call" | custom-call | tf_op jit(solution)/shard_map/pallas_call | solution.py:31
  26.4 1.6 %collective-permute-start.10 = (f32[32,1792]{1,0:T(8,128)S(1)}, f32[32,1792]{1,0:T(8,128)S(1)}, u32[]{:S(2)}, u32[]{:S(2)}) collective-permute-start(f32[32,1792]{1,0:T(8,128)S(1)} %get-tuple-element.64), channel_id=1, source_target_pairs={{0,4},{4,0},{8,12},{12,8},{16,20},{20,16},{24,28},{28,24},{1,5},{5... | collective-permute-start | bytes 688136 | tf_op jit(solution)/shard_map/ppermute | solution.py:218
  28.0 2.7 %collective-permute-done.5.refs_1_ = f32[64,1024]{1,0:T(8,128)S(1)} collective-permute-done((f32[64,1024]{1,0:T(8,128)S(1)}, f32[64,1024]{1,0:T(8,128)S(1)}, u32[]{:S(2)}, u32[]{:S(2)}) %collective-permute-start.5) | collective-permute-done | bytes 262176 | tf_op jit(solution)/shard_map/ppermute | solution.py:218
  31.3 0.7 %shard_map.52.refs_3_.refs_4_ = f32[64,1792]{1,0:T(8,128)S(1)} custom-call(f32[32,1024]{1,0:T(8,128)S(1)} %get-tuple-element.61.refs_0_.refs_3_.refs_4_, f32[32,1024]{1,0:T(8,128)S(1)} %get-tuple-element.62.refs_1_.refs_5_, bf16[1024,1792]{1,0:T(8,128)(2,1)S(1)} %get-tuple-element.53.refs_2_, f32[32,1024]{1,0:T(8,128)S(1)} %get-tuple-element.61.refs_0_.refs_3_.refs_4_), custom_call_target="tpu_custom_call" | custom-call | tf_op jit(solution)/shard_map/pallas_call | solution.py:31
  32.3 0.8 %shard_map.53 = (f32[32,1792]{1,0:T(8,128)S(1)}, f32[32,1792]{1,0:T(8,128)S(1)}) custom-call(f32[32,1024]{1,0:T(8,128)S(1)} %collective-permute-done.11.refs_0_.refs_12_, f32[32,1024]{1,0:T(8,128)S(1)} %collective-permute-done.12.refs_1_.refs_13_, bf16[1024,1792]{1,0:T(8,128)(2,1)S(1)} %get-tuple-element.52.refs_2_, ...), custom_call_target="tpu_custom_call" | custom-call | tf_op jit(solution)/shard_map/pallas_call | solution.py:31
  33.2 2.0 %collective-permute-start.18 = (f32[16,1792]{1,0:T(8,128)S(1)}, f32[16,1792]{1,0:T(8,128)S(1)}, u32[]{:S(2)}, u32[]{:S(2)}) collective-permute-start(f32[16,1792]{1,0:T(8,128)S(1)} %get-tuple-element.74), channel_id=1, source_target_pairs={{0,8},{4,12},{8,0},{12,4},{16,24},{20,28},{24,16},{28,20},{1,9},{5... | collective-permute-start | bytes 344072 | tf_op jit(solution)/shard_map/ppermute | solution.py:218
  36.0 2.6 %collective-permute-start.19 = (f32[16,1792]{1,0:T(8,128)S(1)}, f32[16,1792]{1,0:T(8,128)S(1)}, u32[]{:S(2)}, u32[]{:S(2)}) collective-permute-start(f32[16,1792]{1,0:T(8,128)S(1)} %get-tuple-element.75), channel_id=1, source_target_pairs={{0,16},{4,20},{8,24},{12,28},{16,0},{20,4},{24,8},{28,12},{1,17},{... | collective-permute-start | bytes 344072 | tf_op jit(solution)/shard_map/ppermute | solution.py:218
  38.6 0.7 %shard_map.56.refs_3_.refs_4_ = f32[64,1792]{1,0:T(8,128)S(1)} custom-call(f32[32,1024]{1,0:T(8,128)S(1)} %get-tuple-element.67.refs_0_.refs_3_.refs_6_, f32[32,1024]{1,0:T(8,128)S(1)} %get-tuple-element.68.refs_1_.refs_7_, bf16[1024,1792]{1,0:T(8,128)(2,1)S(1)} %get-tuple-element.53.refs_2_, f32[32,1024]{1,0:T(8,128)S(1)} %get-tuple-element.67.refs_0_.refs_3_.refs_6_), custom_call_target="tpu_custom_call" | custom-call | flops 2000000000 | tf_op jit(solution)/shard_map/pallas_call | solution.py:31
  39.4 0.8 %shard_map.57 = (f32[32,1792]{1,0:T(8,128)S(1)}, f32[32,1792]{1,0:T(8,128)S(1)}) custom-call(f32[32,1024]{1,0:T(8,128)S(1)} %collective-permute-done.13.refs_0_.refs_14_, f32[32,1024]{1,0:T(8,128)S(1)} %collective-permute-done.14.refs_1_.refs_15_, bf16[1024,1792]{1,0:T(8,128)(2,1)S(1)} %get-tuple-element.52.refs_2_, ...), custom_call_target="tpu_custom_call" | custom-call | tf_op jit(solution)/shard_map/pallas_call | solution.py:31
  40.1 1.5 %collective-permute-start.15 = (f32[32,1792]{1,0:T(8,128)S(1)}, f32[32,1792]{1,0:T(8,128)S(1)}, u32[]{:S(2)}, u32[]{:S(2)}) collective-permute-start(f32[32,1792]{1,0:T(8,128)S(1)} %get-tuple-element.70), channel_id=1, source_target_pairs={{0,4},{4,0},{8,12},{12,8},{16,20},{20,16},{24,28},{28,24},{1,5},{5... | collective-permute-start | bytes 688136 | tf_op jit(solution)/shard_map/ppermute | solution.py:218
  41.7 1.0 %collective-permute-start.17 = (f32[16,1792]{1,0:T(8,128)S(1)}, f32[16,1792]{1,0:T(8,128)S(1)}, u32[]{:S(2)}, u32[]{:S(2)}) collective-permute-start(f32[16,1792]{1,0:T(8,128)S(1)} %get-tuple-element.73), channel_id=1, source_target_pairs={{0,8},{4,12},{8,0},{12,4},{16,24},{20,28},{24,16},{28,20},{1,9},{5... | collective-permute-start | bytes 344072 | tf_op jit(solution)/shard_map/ppermute | solution.py:218
  42.7 1.9 %collective-permute-done.19.refs_1_ = f32[16,1792]{1,0:T(8,128)S(1)} collective-permute-done((f32[16,1792]{1,0:T(8,128)S(1)}, f32[16,1792]{1,0:T(8,128)S(1)}, u32[]{:S(2)}, u32[]{:S(2)}) %collective-permute-start.19) | collective-permute-done | bytes 114720 | tf_op jit(solution)/shard_map/ppermute | solution.py:218
  44.6 0.9 %collective-permute-start.20 = (f32[8,1792]{1,0:T(8,128)S(1)}, f32[8,1792]{1,0:T(8,128)S(1)}, u32[]{:S(2)}, u32[]{:S(2)}) collective-permute-start(f32[8,1792]{1,0:T(8,128)S(1)} %get-tuple-element.81), channel_id=1, source_target_pairs={{0,16},{4,20},{8,24},{12,28},{16,0},{20,4},{24,8},{28,12},{1,17},{... | collective-permute-start | bytes 172040 | tf_op jit(solution)/shard_map/ppermute | solution.py:218
  45.5 3.2 %collective-permute-start.21 = (f32[8,1792]{1,0:T(8,128)S(1)}, f32[8,1792]{1,0:T(8,128)S(1)}, u32[]{:S(2)}, u32[]{:S(2)}) collective-permute-start(f32[8,1792]{1,0:T(8,128)S(1)} %get-tuple-element.82), channel_id=1, source_target_pairs={{0,8},{4,12},{8,0},{12,4},{16,24},{20,28},{24,16},{28,20},{1,9},{5... | collective-permute-start | bytes 172040 | tf_op jit(solution)/shard_map/ppermute | solution.py:218
  49.0 2.9 %collective-permute-start.23 = (f32[8,1792]{1,0:T(8,128)S(1)}, f32[8,1792]{1,0:T(8,128)S(1)}, u32[]{:S(2)}, u32[]{:S(2)}) collective-permute-start(f32[8,1792]{1,0:T(8,128)S(1)} %get-tuple-element.84), channel_id=1, source_target_pairs={{0,16},{4,20},{8,24},{12,28},{16,0},{20,4},{24,8},{28,12},{1,17},{... | collective-permute-start | bytes 172040 | tf_op jit(solution)/shard_map/ppermute | solution.py:218
  51.9 1.6 %collective-permute-start.25 = (f32[8,1792]{1,0:T(8,128)S(1)}, f32[8,1792]{1,0:T(8,128)S(1)}, u32[]{:S(2)}, u32[]{:S(2)}) collective-permute-start(f32[8,1792]{1,0:T(8,128)S(1)} %get-tuple-element.86), channel_id=1, source_target_pairs={{0,24},{4,28},{8,16},{12,20},{16,8},{20,12},{24,0},{28,4},{1,25},{... | collective-permute-start | bytes 172040 | tf_op jit(solution)/shard_map/ppermute | solution.py:218
  53.6 1.9 %shard_map.63 = (f32[2048,256]{1,0:T(8,128)}, f32[8,128]{1,0:T(8,128)S(1)}) custom-call(f32[32,1024]{1,0:T(8,128)S(1)} %get-tuple-element.49.refs_0_.refs_3_, f32[32,1024]{1,0:T(8,128)S(1)} %get-tuple-element.50.refs_1_, f32[32,1024]{1,0:T(8,128)S(1)} %get-tuple-element.55.refs_0_.refs_3_.refs_2_, f32[32,1024]{1,0:T(8,128)S(1)} %get-tuple-element.56.refs_1_.refs_3_, ...), custom_call_target="tpu_custom_call" | custom-call | tf_op jit(solution)/shard_map/pallas_call | solution.py:31
  55.5 1.1 %collective-permute-done.22.refs_5_ = f32[8,1792]{1,0:T(8,128)S(1)} collective-permute-done((f32[8,1792]{1,0:T(8,128)S(1)}, f32[8,1792]{1,0:T(8,128)S(1)}, u32[]{:S(2)}, u32[]{:S(2)}) %collective-permute-start.22) | collective-permute-done | bytes 57376 | tf_op jit(solution)/shard_map/ppermute | solution.py:218
  56.6 1.6 %collective-permute-done.23.refs_7_ = f32[8,1792]{1,0:T(8,128)S(1)} collective-permute-done((f32[8,1792]{1,0:T(8,128)S(1)}, f32[8,1792]{1,0:T(8,128)S(1)}, u32[]{:S(2)}, u32[]{:S(2)}) %collective-permute-start.23) | collective-permute-done | bytes 57376 | tf_op jit(solution)/shard_map/ppermute | solution.py:218
  58.2 0.7 %shard_map.64 = f32[32,1792]{1,0:T(8,128)} custom-call(f32[8,1792]{1,0:T(8,128)S(1)} %get-tuple-element.77.refs_2_.refs_0_, f32[8,1792]{1,0:T(8,128)S(1)} %collective-permute-done.20.refs_1_, f32[8,1792]{1,0:T(8,128)S(1)} %get-tuple-element.76.refs_2_, f32[8,1792]{1,0:T(8,128)S(1)} %collective-permute-done.21.refs_3_, ...), custom_call_target="tpu_custom_call" | custom-call | flops 500000000 | tf_op jit(solution)/shard_map/pallas_call | solution.py:31
  (44 shorter events, 3.2 us)
Async XLA Ops:
  3.8 3.4 %collective-permute-start = (f32[256,1024]{1,0:T(8,128)S(1)}, f32[256,1024]{1,0:T(8,128)S(1)}, u32[]{:S(2)}, u32[]{:S(2)}) collective-permute-start(f32[256,1024]{1,0:T(8,128)S(1)} %get-tuple-element.47), channel_id=1, source_target_pairs={{0,1},{1,0},{2,3},{3,2},{4,5},{5,4},{6,7},{7,6},{8,9},{9,8},{10,11... | collective-permute-start | bytes 3145736 | tf_op jit(solution)/shard_map/ppermute | solution.py:218
  7.3 9.7 %collective-permute-start.1 = (f32[64,1024]{1,0:T(8,128)S(1)}, f32[64,1024]{1,0:T(8,128)S(1)}, u32[]{:S(2)}, u32[]{:S(2)}) collective-permute-start(f32[64,1024]{1,0:T(8,128)S(1)} %get-tuple-element.48.refs_0_), channel_id=1, source_target_pairs={{0,2},{1,3},{2,0},{3,1},{4,6},{5,7},{6,4},{7,5},{8,10},{9,11},{10,... | collective-permute-start | bytes 786440 | tf_op jit(solution)/shard_map/ppermute | solution.py:218
  9.9 13.1 %collective-permute-start.2 = (f32[64,1024]{1,0:T(8,128)S(1)}, f32[64,1024]{1,0:T(8,128)S(1)}, u32[]{:S(2)}, u32[]{:S(2)}) collective-permute-start(f32[64,1024]{1,0:T(8,128)S(1)} %get-tuple-element.51.refs_0_), channel_id=1, source_target_pairs={{0,2},{1,3},{2,0},{3,1},{4,6},{5,7},{6,4},{7,5},{8,10},{9,11},{10,... | collective-permute-start | bytes 786440 | tf_op jit(solution)/shard_map/ppermute | solution.py:218
  17.1 1.4 %collective-permute-start.3 = (f32[32,1024]{1,0:T(8,128)S(1)}, f32[32,1024]{1,0:T(8,128)S(1)}, u32[]{:S(2)}, u32[]{:S(2)}) collective-permute-start(f32[32,1024]{1,0:T(8,128)S(1)} %get-tuple-element.49.refs_0_.refs_3_), channel_id=1, source_target_pairs={{0,1},{1,0},{2,3},{3,2},{4,5},{5,4},{6,7},{7,6},{8,9},{9,8},{10,11... | collective-permute-start | bytes 393224 | tf_op jit(solution)/shard_map/ppermute | solution.py:218
  17.2 1.5 %collective-permute-start.4 = (f32[32,1024]{1,0:T(8,128)S(1)}, f32[32,1024]{1,0:T(8,128)S(1)}, u32[]{:S(2)}, u32[]{:S(2)}) collective-permute-start(f32[32,1024]{1,0:T(8,128)S(1)} %get-tuple-element.50.refs_1_), channel_id=1, source_target_pairs={{0,1},{1,0},{2,3},{3,2},{4,5},{5,4},{6,7},{7,6},{8,9},{9,8},{10,11... | collective-permute-start | bytes 393224 | tf_op jit(solution)/shard_map/ppermute | solution.py:218
  19.5 8.5 %collective-permute-start.6 = (f32[32,1792]{1,0:T(8,128)S(1)}, f32[32,1792]{1,0:T(8,128)S(1)}, u32[]{:S(2)}, u32[]{:S(2)}) collective-permute-start(f32[32,1792]{1,0:T(8,128)S(1)} %get-tuple-element.58), channel_id=1, source_target_pairs={{0,4},{4,0},{8,12},{12,8},{16,20},{20,16},{24,28},{28,24},{1,5},{5... | collective-permute-start | bytes 688136 | tf_op jit(solution)/shard_map/ppermute | solution.py:218
  21.5 9.2 %collective-permute-start.5 = (f32[64,1024]{1,0:T(8,128)S(1)}, f32[64,1024]{1,0:T(8,128)S(1)}, u32[]{:S(2)}, u32[]{:S(2)}) collective-permute-start(f32[64,1024]{1,0:T(8,128)S(1)} %get-tuple-element.57.refs_0_), channel_id=1, source_target_pairs={{0,2},{1,3},{2,0},{3,1},{4,6},{5,7},{6,4},{7,5},{8,10},{9,11},{10,... | collective-permute-start | bytes 786440 | tf_op jit(solution)/shard_map/ppermute | solution.py:218
  23.1 2.6 %collective-permute-start.7 = (f32[32,1024]{1,0:T(8,128)S(1)}, f32[32,1024]{1,0:T(8,128)S(1)}, u32[]{:S(2)}, u32[]{:S(2)}) collective-permute-start(f32[32,1024]{1,0:T(8,128)S(1)} %get-tuple-element.55.refs_0_.refs_3_.refs_2_), channel_id=1, source_target_pairs={{0,1},{1,0},{2,3},{3,2},{4,5},{5,4},{6,7},{7,6},{8,9},{9,8},{10,11... | collective-permute-start | bytes 393224 | tf_op jit(solution)/shard_map/ppermute | solution.py:218
  23.1 2.5 %collective-permute-start.8 = (f32[32,1024]{1,0:T(8,128)S(1)}, f32[32,1024]{1,0:T(8,128)S(1)}, u32[]{:S(2)}, u32[]{:S(2)}) collective-permute-start(f32[32,1024]{1,0:T(8,128)S(1)} %get-tuple-element.56.refs_1_.refs_3_), channel_id=1, source_target_pairs={{0,1},{1,0},{2,3},{3,2},{4,5},{5,4},{6,7},{7,6},{8,9},{9,8},{10,11... | collective-permute-start | bytes 393224 | tf_op jit(solution)/shard_map/ppermute | solution.py:218
  23.6 11.8 %collective-permute-start.9 = (f32[64,1024]{1,0:T(8,128)S(1)}, f32[64,1024]{1,0:T(8,128)S(1)}, u32[]{:S(2)}, u32[]{:S(2)}) collective-permute-start(f32[64,1024]{1,0:T(8,128)S(1)} %get-tuple-element.63.refs_0_), channel_id=1, source_target_pairs={{0,2},{1,3},{2,0},{3,1},{4,6},{5,7},{6,4},{7,5},{8,10},{9,11},{10,... | collective-permute-start | bytes 786440 | tf_op jit(solution)/shard_map/ppermute | solution.py:218
  26.4 8.8 %collective-permute-start.10 = (f32[32,1792]{1,0:T(8,128)S(1)}, f32[32,1792]{1,0:T(8,128)S(1)}, u32[]{:S(2)}, u32[]{:S(2)}) collective-permute-start(f32[32,1792]{1,0:T(8,128)S(1)} %get-tuple-element.64), channel_id=1, source_target_pairs={{0,4},{4,0},{8,12},{12,8},{16,20},{20,16},{24,28},{28,24},{1,5},{5... | collective-permute-start | bytes 688136 | tf_op jit(solution)/shard_map/ppermute | solution.py:218
  30.7 1.4 %collective-permute-start.11 = (f32[32,1024]{1,0:T(8,128)S(1)}, f32[32,1024]{1,0:T(8,128)S(1)}, u32[]{:S(2)}, u32[]{:S(2)}) collective-permute-start(f32[32,1024]{1,0:T(8,128)S(1)} %get-tuple-element.61.refs_0_.refs_3_.refs_4_), channel_id=1, source_target_pairs={{0,1},{1,0},{2,3},{3,2},{4,5},{5,4},{6,7},{7,6},{8,9},{9,8},{10,11... | collective-permute-start | bytes 393224 | tf_op jit(solution)/shard_map/ppermute | solution.py:218
  30.8 1.5 %collective-permute-start.12 = (f32[32,1024]{1,0:T(8,128)S(1)}, f32[32,1024]{1,0:T(8,128)S(1)}, u32[]{:S(2)}, u32[]{:S(2)}) collective-permute-start(f32[32,1024]{1,0:T(8,128)S(1)} %get-tuple-element.62.refs_1_.refs_5_), channel_id=1, source_target_pairs={{0,1},{1,0},{2,3},{3,2},{4,5},{5,4},{6,7},{7,6},{8,9},{9,8},{10,11... | collective-permute-start | bytes 393224 | tf_op jit(solution)/shard_map/ppermute | solution.py:218
  33.1 8.5 %collective-permute-start.16 = (f32[32,1792]{1,0:T(8,128)S(1)}, f32[32,1792]{1,0:T(8,128)S(1)}, u32[]{:S(2)}, u32[]{:S(2)}) collective-permute-start(f32[32,1792]{1,0:T(8,128)S(1)} %get-tuple-element.71), channel_id=1, source_target_pairs={{0,4},{4,0},{8,12},{12,8},{16,20},{20,16},{24,28},{28,24},{1,5},{5... | collective-permute-start | bytes 688136 | tf_op jit(solution)/shard_map/ppermute | solution.py:218
  33.2 11.4 %collective-permute-start.18 = (f32[16,1792]{1,0:T(8,128)S(1)}, f32[16,1792]{1,0:T(8,128)S(1)}, u32[]{:S(2)}, u32[]{:S(2)}) collective-permute-start(f32[16,1792]{1,0:T(8,128)S(1)} %get-tuple-element.74), channel_id=1, source_target_pairs={{0,8},{4,12},{8,0},{12,4},{16,24},{20,28},{24,16},{28,20},{1,9},{5... | collective-permute-start | bytes 344072 | tf_op jit(solution)/shard_map/ppermute | solution.py:218
  35.4 3.9 %collective-permute-start.13 = (f32[32,1024]{1,0:T(8,128)S(1)}, f32[32,1024]{1,0:T(8,128)S(1)}, u32[]{:S(2)}, u32[]{:S(2)}) collective-permute-start(f32[32,1024]{1,0:T(8,128)S(1)} %get-tuple-element.67.refs_0_.refs_3_.refs_6_), channel_id=1, source_target_pairs={{0,1},{1,0},{2,3},{3,2},{4,5},{5,4},{6,7},{7,6},{8,9},{9,8},{10,11... | collective-permute-start | bytes 393224 | tf_op jit(solution)/shard_map/ppermute | solution.py:218
  35.5 3.8 %collective-permute-start.14 = (f32[32,1024]{1,0:T(8,128)S(1)}, f32[32,1024]{1,0:T(8,128)S(1)}, u32[]{:S(2)}, u32[]{:S(2)}) collective-permute-start(f32[32,1024]{1,0:T(8,128)S(1)} %get-tuple-element.68.refs_1_.refs_7_), channel_id=1, source_target_pairs={{0,1},{1,0},{2,3},{3,2},{4,5},{5,4},{6,7},{7,6},{8,9},{9,8},{10,11... | collective-permute-start | bytes 393224 | tf_op jit(solution)/shard_map/ppermute | solution.py:218
  36.0 8.6 %collective-permute-start.19 = (f32[16,1792]{1,0:T(8,128)S(1)}, f32[16,1792]{1,0:T(8,128)S(1)}, u32[]{:S(2)}, u32[]{:S(2)}) collective-permute-start(f32[16,1792]{1,0:T(8,128)S(1)} %get-tuple-element.75), channel_id=1, source_target_pairs={{0,16},{4,20},{8,24},{12,28},{16,0},{20,4},{24,8},{28,12},{1,17},{... | collective-permute-start | bytes 344072 | tf_op jit(solution)/shard_map/ppermute | solution.py:218
  40.1 8.8 %collective-permute-start.15 = (f32[32,1792]{1,0:T(8,128)S(1)}, f32[32,1792]{1,0:T(8,128)S(1)}, u32[]{:S(2)}, u32[]{:S(2)}) collective-permute-start(f32[32,1792]{1,0:T(8,128)S(1)} %get-tuple-element.70), channel_id=1, source_target_pairs={{0,4},{4,0},{8,12},{12,8},{16,20},{20,16},{24,28},{28,24},{1,5},{5... | collective-permute-start | bytes 688136 | tf_op jit(solution)/shard_map/ppermute | solution.py:218
  41.7 7.1 %collective-permute-start.17 = (f32[16,1792]{1,0:T(8,128)S(1)}, f32[16,1792]{1,0:T(8,128)S(1)}, u32[]{:S(2)}, u32[]{:S(2)}) collective-permute-start(f32[16,1792]{1,0:T(8,128)S(1)} %get-tuple-element.73), channel_id=1, source_target_pairs={{0,8},{4,12},{8,0},{12,4},{16,24},{20,28},{24,16},{28,20},{1,9},{5... | collective-permute-start | bytes 344072 | tf_op jit(solution)/shard_map/ppermute | solution.py:218
  44.6 7.3 %collective-permute-start.20 = (f32[8,1792]{1,0:T(8,128)S(1)}, f32[8,1792]{1,0:T(8,128)S(1)}, u32[]{:S(2)}, u32[]{:S(2)}) collective-permute-start(f32[8,1792]{1,0:T(8,128)S(1)} %get-tuple-element.81), channel_id=1, source_target_pairs={{0,16},{4,20},{8,24},{12,28},{16,0},{20,4},{24,8},{28,12},{1,17},{... | collective-permute-start | bytes 172040 | tf_op jit(solution)/shard_map/ppermute | solution.py:218
  45.5 9.9 %collective-permute-start.21 = (f32[8,1792]{1,0:T(8,128)S(1)}, f32[8,1792]{1,0:T(8,128)S(1)}, u32[]{:S(2)}, u32[]{:S(2)}) collective-permute-start(f32[8,1792]{1,0:T(8,128)S(1)} %get-tuple-element.82), channel_id=1, source_target_pairs={{0,8},{4,12},{8,0},{12,4},{16,24},{20,28},{24,16},{28,20},{1,9},{5... | collective-permute-start | bytes 172040 | tf_op jit(solution)/shard_map/ppermute | solution.py:218
  48.8 7.8 %collective-permute-start.22 = (f32[8,1792]{1,0:T(8,128)S(1)}, f32[8,1792]{1,0:T(8,128)S(1)}, u32[]{:S(2)}, u32[]{:S(2)}) collective-permute-start(f32[8,1792]{1,0:T(8,128)S(1)} %get-tuple-element.83), channel_id=1, source_target_pairs={{0,16},{4,20},{8,24},{12,28},{16,0},{20,4},{24,8},{28,12},{1,17},{... | collective-permute-start | bytes 172040 | tf_op jit(solution)/shard_map/ppermute | solution.py:218
  49.0 9.2 %collective-permute-start.23 = (f32[8,1792]{1,0:T(8,128)S(1)}, f32[8,1792]{1,0:T(8,128)S(1)}, u32[]{:S(2)}, u32[]{:S(2)}) collective-permute-start(f32[8,1792]{1,0:T(8,128)S(1)} %get-tuple-element.84), channel_id=1, source_target_pairs={{0,16},{4,20},{8,24},{12,28},{16,0},{20,4},{24,8},{28,12},{1,17},{... | collective-permute-start | bytes 172040 | tf_op jit(solution)/shard_map/ppermute | solution.py:218
  51.9 6.3 %collective-permute-start.24 = (f32[8,1792]{1,0:T(8,128)S(1)}, f32[8,1792]{1,0:T(8,128)S(1)}, u32[]{:S(2)}, u32[]{:S(2)}) collective-permute-start(f32[8,1792]{1,0:T(8,128)S(1)} %get-tuple-element.85), channel_id=1, source_target_pairs={{0,8},{4,12},{8,0},{12,4},{16,24},{20,28},{24,16},{28,20},{1,9},{5... | collective-permute-start | bytes 172040 | tf_op jit(solution)/shard_map/ppermute | solution.py:218
  51.9 6.3 %collective-permute-start.25 = (f32[8,1792]{1,0:T(8,128)S(1)}, f32[8,1792]{1,0:T(8,128)S(1)}, u32[]{:S(2)}, u32[]{:S(2)}) collective-permute-start(f32[8,1792]{1,0:T(8,128)S(1)} %get-tuple-element.86), channel_id=1, source_target_pairs={{0,24},{4,28},{8,16},{12,20},{16,8},{20,12},{24,0},{28,4},{1,25},{... | collective-permute-start | bytes 172040 | tf_op jit(solution)/shard_map/ppermute | solution.py:218

commit v14 on v11

--- a/solution.py
+++ b/solution.py
@@ -58,40 +58,45 @@
     return column
 
 
-def stream_half(delta, held, sem, mine):
-    rows = held.shape[0]
+def stream_half(delta, held, sem, mine, skipped=0):
+    rows = delta.shape[0] // 2
     parity = lax.rem(lax.axis_index("col"), 2)
-    first = (parity if mine else 1 - parity) * rows
+    first = (parity if mine else 1 - parity) * rows + skipped
     copies = []
-    for b in range(rows // BLOCK):
+    for b in range(held.shape[0] // BLOCK):
         source = delta.at[pl.ds(pl.multiple_of(first + b * BLOCK, BLOCK), BLOCK), :]
         copies.append(pltpu.make_async_copy(source, held.at[pl.ds(b * BLOCK, BLOCK), :], sem.at[b]))
         copies[-1].start()
     return copies
 
 
-def sketch_half(omega_t, held, copies, out):
+def sketch_half(omega_t, held, copies, out, skipped=0):
     for b, copy in enumerate(copies):
         copy.wait()
-        block = pl.ds(b * BLOCK, BLOCK)
-        out[:, block] = lax.dot_general(omega_t[...], held[block, :], NT, preferred_element_type=F32)
-
-
-def first_half_body(n_row, pieces, delta, omega, held, omega_t, out, omega_v, sem, omega_sem):
+        rows, lanes = pl.ds(b * BLOCK, BLOCK), pl.ds(skipped + b * BLOCK, BLOCK)
+        out[:, lanes] = lax.dot_general(omega_t[...], held[rows, :], NT, preferred_element_type=F32)
+
+
+def first_half_body(n_row, pieces, delta, omega, held, omega_t, out, ahead, omega_v, sem, omega_sem, ahead_sem):
     k = out.shape[0]
     fetch = pltpu.make_async_copy(omega, omega_v, omega_sem)
     fetch.start()
     copies = stream_half(delta, held, sem, False)
+    early = stream_half(delta, ahead, ahead_sem, True)
     position = lax.broadcasted_iota(jnp.int32, (k, k), 0)
     column = lax.broadcasted_iota(jnp.int32, (k, k), 1)
     pick = jnp.where(column_of(position, k, n_row, pieces) == column, 1.0, 0.0).astype(BF16)
     fetch.wait()
     omega_t[...] = lax.dot_general(pick, omega_v[...], NT, preferred_element_type=F32).astype(BF16)
     sketch_half(omega_t, held, copies, out)
-
-
-def second_half_body(delta, omega_t, held, out, sem):
-    sketch_half(omega_t, held, stream_half(delta, held, sem, True), out)
+    for copy in early:
+        copy.wait()
+
+
+def second_half_body(delta, omega_t, ahead, held, out, sem):
+    copies = stream_half(delta, held, sem, True, BLOCK)
+    out[:, pl.ds(0, BLOCK)] = lax.dot_general(omega_t[...], ahead[...], NT, preferred_element_type=F32)
+    sketch_half(omega_t, held, copies, out, BLOCK)
 
 
 def add_chunks_body(kept, received, *outs):
@@ -115,8 +120,10 @@
 
 
 def product_body(*refs):
-    *sketch, held, out = refs
-    out[...] = jnp.dot(joined(sketch).astype(BF16), held[...], preferred_element_type=F32)
+    *sketch, ahead, held, out = refs
+    rounded = joined(sketch).astype(BF16)
+    total = jnp.dot(rounded[:, :BLOCK], ahead[...], preferred_element_type=F32)
+    out[...] = total + jnp.dot(rounded[:, BLOCK:], held[...], preferred_element_type=F32)
 
 
 def split(bit, segments, refs, send, keep):
@@ -221,15 +228,15 @@
 
     in_hbm = pltpu.with_memory_space_constraint(delta, pltpu.HBM)
     sems = pltpu.SemaphoreType.DMA((half // BLOCK,))
-    held_other, omega_t, to_send = call(
+    held_other, omega_t, to_send, ahead = call(
         functools.partial(first_half_body, n_row, pieces),
         (in_hbm, pltpu.with_memory_space_constraint(omega, pltpu.HBM)),
-        [((half, d), BF16), ((k, d), BF16), ((k, half), F32)],
+        [((half, d), BF16), ((k, d), BF16), ((k, half), F32), ((BLOCK, d), BF16)],
         "aa",
-        scratch=[pltpu.VMEM((d, k), BF16), sems, pltpu.SemaphoreType.DMA],
+        scratch=[pltpu.VMEM((d, k), BF16), sems, pltpu.SemaphoreType.DMA, pltpu.SemaphoreType.DMA((1,))],
     )
     received = swap(to_send, "col", n_col, 1)
-    held_own, kept = call(second_half_body, (in_hbm, omega_t), [((half, d), BF16), ((k, half), F32)], "av", scratch=[sems])
+    held_own, kept = call(second_half_body, (in_hbm, omega_t, ahead), [((half - BLOCK, d), BF16), ((k, half), F32)], "avv", scratch=[sems])
     partial = call(add_chunks_body, (kept, received), [((width, half), F32) for width in widths])
     bit = 2
     while bit < n_col // 2:
@@ -263,7 +270,7 @@
             last = (owns[c][0],)
         elif step.startswith("before"):
             c = int(step[6:])
-            befores[c] = call(product_body, (*owns[c], held_own), [((widths[c], d), F32)], after=last, weight=weight)[0]
+            befores[c] = call(product_body, (*owns[c], ahead, held_own), [((widths[c], d), F32)], after=last, weight=weight)[0]
             last = (befores[c],)
         elif step.startswith("send"):
             c = int(step[4:])

time: 58.6 us -> 58.4 us (level)
  Pallas kernels: 15.2 us -> 14.5 us
    pallas_call x24, Pallas kernels: 15.2 us -> 14.5 us  [call(): pl.pallas_call(run, out_shape=[pltpu.VMEM(*o) if i >= results else jax.Sh...]
  transfers between devices with their start and end apart: 26 -> 26, of which waited for: 10 -> 11; matrix products, arithmetic and copies ran while one was open for 0% -> 0% of each run, Pallas kernels for 19% -> 18%
where the time goes in v14:
time: 58.4 us; the launch traced here: 58.3 us
  starting transfers between devices  28.5 us (49%)
  Pallas kernels  14.5 us (25%)
  waiting for transfers between devices  14.5 us (25%)
  between operations  0.82 us (1%)
    ppermute x26, starting transfers between devices, swap(): return lax.ppermute(x, axis, [(i, i ^ bit) for i in range(size)])  28.5 us
    pallas_call x24, Pallas kernels, call(): pl.pallas_call(run, out_shape=[pltpu.VMEM(*o) if i >= results else jax.Sh...  14.5 us
    ppermute x26, waiting for transfers between devices, swap(): return lax.ppermute(x, axis, [(i, i ^ bit) for i in range(size)])  14.5 us
  transfers between devices with their start and end apart: 26, of which 11 were waited for; matrix products, arithmetic and copies ran while one was open for 0% of the time, Pallas kernels for 18%

profile of v14, /device:TPU:0, one launch (start us, length us, event | category | flops | bytes accessed | tf_op | source)
XLA Modules:
  0.0 58.3 jit_solution(10329102634403840786)
XLA Ops:
  0.6 3.2 %shard_map.41 = (bf16[1024,1792]{1,0:T(8,128)(2,1)S(1)}, bf16[256,1792]{1,0:T(8,128)(2,1)S(1)}, f32[256,1024]{1,0:T(8,128)S(1)}, bf16[512,1792]{1,0:T(8,128)(2,1)S(1)}) custom-call(bf16[2048,1792]{1,0:T(8,128)(2,1)} %refs_0_.3, bf16[1792,256]{1,0:T(8,128)(2,1)} %refs_1_.1), custom_call_target="tpu_custom_call" | custom-call | tf_op jit(solution)/shard_map/pallas_call | solution.py:30
  3.8 0.5 collective-permute-start
  4.4 2.2 %shard_map.42 = (bf16[512,1792]{1,0:T(8,128)(2,1)S(1)}, f32[256,1024]{1,0:T(8,128)S(1)}) custom-call(bf16[2048,1792]{1,0:T(8,128)(2,1)} %refs_0_.3, bf16[256,1792]{1,0:T(8,128)(2,1)S(1)} %get-tuple-element.46.refs_1_, bf16[512,1792]{1,0:T(8,128)(2,1)S(1)} %get-tuple-element.47.refs_2_), custom_call_target="tpu_custom_call" | custom-call | tf_op jit(solution)/shard_map/pallas_call | solution.py:30
  6.8 2.9 %collective-permute-start.1 = (f32[64,1024]{1,0:T(8,128)S(1)}, f32[64,1024]{1,0:T(8,128)S(1)}, u32[]{:S(2)}, u32[]{:S(2)}) collective-permute-start(f32[64,1024]{1,0:T(8,128)S(1)} %get-tuple-element.50.refs_0_), channel_id=1, source_target_pairs={{0,2},{1,3},{2,0},{3,1},{4,6},{5,7},{6,4},{7,5},{8,10},{9,11},{10,... | collective-permute-start | bytes 786440 | tf_op jit(solution)/shard_map/ppermute | solution.py:215
  9.8 7.0 %collective-permute-done.1.refs_1_ = f32[64,1024]{1,0:T(8,128)S(1)} collective-permute-done((f32[64,1024]{1,0:T(8,128)S(1)}, f32[64,1024]{1,0:T(8,128)S(1)}, u32[]{:S(2)}, u32[]{:S(2)}) %collective-permute-start.1) | collective-permute-done | bytes 262176 | tf_op jit(solution)/shard_map/ppermute | solution.py:215
  16.9 0.5 collective-permute-start.4
  17.4 0.7 %shard_map.45.refs_3_.refs_4_ = f32[64,1792]{1,0:T(8,128)S(1)} custom-call(f32[32,1024]{1,0:T(8,128)S(1)} %get-tuple-element.51.refs_0_.refs_4_, f32[32,1024]{1,0:T(8,128)S(1)} %get-tuple-element.52.refs_1_, bf16[512,1792]{1,0:T(8,128)(2,1)S(1)} %get-tuple-element.47.refs_2_, bf16[512,1792]{1,0:T(8,128)(2,1)S(1)} %get-tuple-element.55.refs_3_, ...), custom_call_target="tpu_custom_call" | custom-call | tf_op jit(solution)/shard_map/pallas_call | solution.py:30
  18.4 0.8 %shard_map.46 = (f32[32,1792]{1,0:T(8,128)S(1)}, f32[32,1792]{1,0:T(8,128)S(1)}) custom-call(f32[32,1024]{1,0:T(8,128)S(1)} %collective-permute-done.3.refs_0_.refs_8_, f32[32,1024]{1,0:T(8,128)S(1)} %collective-permute-done.4.refs_1_.refs_9_, bf16[1024,1792]{1,0:T(8,128)(2,1)S(1)} %get-tuple-element.54.refs_2_, f32[64,1792]{1,0:T(8,128)S(1)} %shard_map.45.refs_3_.refs_4_, ...), custom_call_target="tpu_custom_call" | custom-call | tf_op jit(solution)/shard_map/pallas_call | solution.py:30
  19.2 2.1 %collective-permute-start.6 = (f32[32,1792]{1,0:T(8,128)S(1)}, f32[32,1792]{1,0:T(8,128)S(1)}, u32[]{:S(2)}, u32[]{:S(2)}) collective-permute-start(f32[32,1792]{1,0:T(8,128)S(1)} %get-tuple-element.60), channel_id=1, source_target_pairs={{0,4},{4,0},{8,12},{12,8},{16,20},{20,16},{24,28},{28,24},{1,5},{5... | collective-permute-start | bytes 688136 | tf_op jit(solution)/shard_map/ppermute | solution.py:215
  21.3 1.5 %collective-permute-start.5 = (f32[64,1024]{1,0:T(8,128)S(1)}, f32[64,1024]{1,0:T(8,128)S(1)}, u32[]{:S(2)}, u32[]{:S(2)}) collective-permute-start(f32[64,1024]{1,0:T(8,128)S(1)} %get-tuple-element.59.refs_0_), channel_id=1, source_target_pairs={{0,2},{1,3},{2,0},{3,1},{4,6},{5,7},{6,4},{7,5},{8,10},{9,11},{10,... | collective-permute-start | bytes 786440 | tf_op jit(solution)/shard_map/ppermute | solution.py:215
  23.5 0.8 %collective-permute-start.9 = (f32[64,1024]{1,0:T(8,128)S(1)}, f32[64,1024]{1,0:T(8,128)S(1)}, u32[]{:S(2)}, u32[]{:S(2)}) collective-permute-start(f32[64,1024]{1,0:T(8,128)S(1)} %get-tuple-element.65.refs_0_), channel_id=1, source_target_pairs={{0,2},{1,3},{2,0},{3,1},{4,6},{5,7},{6,4},{7,5},{8,10},{9,11},{10,... | collective-permute-start | bytes 786440 | tf_op jit(solution)/shard_map/ppermute | solution.py:215
  24.3 0.8 %shard_map.48.refs_3_.refs_4_ = f32[64,1792]{1,0:T(8,128)S(1)} custom-call(f32[32,1024]{1,0:T(8,128)S(1)} %get-tuple-element.57.refs_0_.refs_4_.refs_2_, f32[32,1024]{1,0:T(8,128)S(1)} %get-tuple-element.58.refs_1_.refs_3_, bf16[512,1792]{1,0:T(8,128)(2,1)S(1)} %get-tuple-element.47.refs_2_, bf16[512,1792]{1,0:T(8,128)(2,1)S(1)} %get-tuple-element.55.refs_3_, ...), custom_call_target="tpu_custom_call" | custom-call | flops 500000000 | tf_op jit(solution)/shard_map/pallas_call | solution.py:30
  25.0 0.8 %shard_map.49 = (f32[32,1792]{1,0:T(8,128)S(1)}, f32[32,1792]{1,0:T(8,128)S(1)}) custom-call(f32[32,1024]{1,0:T(8,128)S(1)} %collective-permute-done.7.refs_0_.refs_10_, f32[32,1024]{1,0:T(8,128)S(1)} %collective-permute-done.8.refs_1_.refs_11_, bf16[1024,1792]{1,0:T(8,128)(2,1)S(1)} %get-tuple-element.54.refs_2_, f32[64,1792]{1,0:T(8,128)S(1)} %shard_map.48.refs_3_.refs_4_, ...), custom_call_target="tpu_custom_call" | custom-call | tf_op jit(solution)/shard_map/pallas_call | solution.py:30
  25.8 1.6 %collective-permute-start.10 = (f32[32,1792]{1,0:T(8,128)S(1)}, f32[32,1792]{1,0:T(8,128)S(1)}, u32[]{:S(2)}, u32[]{:S(2)}) collective-permute-start(f32[32,1792]{1,0:T(8,128)S(1)} %get-tuple-element.66), channel_id=1, source_target_pairs={{0,4},{4,0},{8,12},{12,8},{16,20},{20,16},{24,28},{28,24},{1,5},{5... | collective-permute-start | bytes 688136 | tf_op jit(solution)/shard_map/ppermute | solution.py:215
  27.5 3.0 %collective-permute-done.5.refs_1_ = f32[64,1024]{1,0:T(8,128)S(1)} collective-permute-done((f32[64,1024]{1,0:T(8,128)S(1)}, f32[64,1024]{1,0:T(8,128)S(1)}, u32[]{:S(2)}, u32[]{:S(2)}) %collective-permute-start.5) | collective-permute-done | bytes 262176 | tf_op jit(solution)/shard_map/ppermute | solution.py:215
  31.1 0.7 %shard_map.52.refs_3_.refs_4_ = f32[64,1792]{1,0:T(8,128)S(1)} custom-call(f32[32,1024]{1,0:T(8,128)S(1)} %get-tuple-element.63.refs_0_.refs_4_, f32[32,1024]{1,0:T(8,128)S(1)} %get-tuple-element.64.refs_1_.refs_5_, bf16[512,1792]{1,0:T(8,128)(2,1)S(1)} %get-tuple-element.47.refs_2_, bf16[512,1792]{1,0:T(8,128)(2,1)S(1)} %get-tuple-element.55.refs_3_, ...), custom_call_target="tpu_custom_call" | custom-call | tf_op jit(solution)/shard_map/pallas_call | solution.py:30
  32.1 0.8 %shard_map.53 = (f32[32,1792]{1,0:T(8,128)S(1)}, f32[32,1792]{1,0:T(8,128)S(1)}) custom-call(f32[32,1024]{1,0:T(8,128)S(1)} %collective-permute-done.11.refs_0_.refs_12_, f32[32,1024]{1,0:T(8,128)S(1)} %collective-permute-done.12.refs_1_.refs_13_, bf16[1024,1792]{1,0:T(8,128)(2,1)S(1)} %get-tuple-element.54.refs_2_, ...), custom_call_target="tpu_custom_call" | custom-call | tf_op jit(solution)/shard_map/pallas_call | solution.py:30
  33.0 2.1 %collective-permute-start.18 = (f32[16,1792]{1,0:T(8,128)S(1)}, f32[16,1792]{1,0:T(8,128)S(1)}, u32[]{:S(2)}, u32[]{:S(2)}) collective-permute-start(f32[16,1792]{1,0:T(8,128)S(1)} %get-tuple-element.76), channel_id=1, source_target_pairs={{0,8},{4,12},{8,0},{12,4},{16,24},{20,28},{24,16},{28,20},{1,9},{5... | collective-permute-start | bytes 344072 | tf_op jit(solution)/shard_map/ppermute | solution.py:215
  35.8 1.6 %collective-permute-start.19 = (f32[16,1792]{1,0:T(8,128)S(1)}, f32[16,1792]{1,0:T(8,128)S(1)}, u32[]{:S(2)}, u32[]{:S(2)}) collective-permute-start(f32[16,1792]{1,0:T(8,128)S(1)} %get-tuple-element.77), channel_id=1, source_target_pairs={{0,8},{4,12},{8,0},{12,4},{16,24},{20,28},{24,16},{28,20},{1,9},{5... | collective-permute-start | bytes 344072 | tf_op jit(solution)/shard_map/ppermute | solution.py:215
  37.4 0.7 %shard_map.56.refs_3_.refs_4_ = f32[64,1792]{1,0:T(8,128)S(1)} custom-call(f32[32,1024]{1,0:T(8,128)S(1)} %get-tuple-element.69.refs_0_.refs_4_.refs_6_, f32[32,1024]{1,0:T(8,128)S(1)} %get-tuple-element.70.refs_1_.refs_7_, bf16[512,1792]{1,0:T(8,128)(2,1)S(1)} %get-tuple-element.47.refs_2_, bf16[512,1792]{1,0:T(8,128)(2,1)S(1)} %get-tuple-element.55.refs_3_, ...), custom_call_target="tpu_custom_call" | custom-call | flops 2000000000 | tf_op jit(solution)/shard_map/pallas_call | solution.py:30
  38.2 0.8 %shard_map.57 = (f32[32,1792]{1,0:T(8,128)S(1)}, f32[32,1792]{1,0:T(8,128)S(1)}) custom-call(f32[32,1024]{1,0:T(8,128)S(1)} %collective-permute-done.13.refs_0_.refs_14_, f32[32,1024]{1,0:T(8,128)S(1)} %collective-permute-done.14.refs_1_.refs_15_, bf16[1024,1792]{1,0:T(8,128)(2,1)S(1)} %get-tuple-element.54.refs_2_, ...), custom_call_target="tpu_custom_call" | custom-call | tf_op jit(solution)/shard_map/pallas_call | solution.py:30
  38.9 0.6 collective-permute-start.15
  39.5 1.3 %collective-permute-done.16.refs_1_ = f32[32,1792]{1,0:T(8,128)S(1)} collective-permute-done((f32[32,1792]{1,0:T(8,128)S(1)}, f32[32,1792]{1,0:T(8,128)S(1)}, u32[]{:S(2)}, u32[]{:S(2)}) %collective-permute-start.16) | collective-permute-done | bytes 229408 | tf_op jit(solution)/shard_map/ppermute | solution.py:215
  40.8 1.8 %collective-permute-start.17 = (f32[16,1792]{1,0:T(8,128)S(1)}, f32[16,1792]{1,0:T(8,128)S(1)}, u32[]{:S(2)}, u32[]{:S(2)}) collective-permute-start(f32[16,1792]{1,0:T(8,128)S(1)} %get-tuple-element.75), channel_id=1, source_target_pairs={{0,8},{4,12},{8,0},{12,4},{16,24},{20,28},{24,16},{28,20},{1,9},{5... | collective-permute-start | bytes 344072 | tf_op jit(solution)/shard_map/ppermute | solution.py:215
  42.7 2.7 %collective-permute-start.20 = (f32[8,1792]{1,0:T(8,128)S(1)}, f32[8,1792]{1,0:T(8,128)S(1)}, u32[]{:S(2)}, u32[]{:S(2)}) collective-permute-start(f32[8,1792]{1,0:T(8,128)S(1)} %get-tuple-element.83), channel_id=1, source_target_pairs={{0,16},{4,20},{8,24},{12,28},{16,0},{20,4},{24,8},{28,12},{1,17},{... | collective-permute-start | bytes 172040 | tf_op jit(solution)/shard_map/ppermute | solution.py:215
  45.7 0.6 %collective-permute-done.17.refs_1_ = f32[16,1792]{1,0:T(8,128)S(1)} collective-permute-done((f32[16,1792]{1,0:T(8,128)S(1)}, f32[16,1792]{1,0:T(8,128)S(1)}, u32[]{:S(2)}, u32[]{:S(2)}) %collective-permute-start.17) | collective-permute-done | bytes 114720 | tf_op jit(solution)/shard_map/ppermute | solution.py:215
  46.3 3.0 %collective-permute-start.22 = (f32[8,1792]{1,0:T(8,128)S(1)}, f32[8,1792]{1,0:T(8,128)S(1)}, u32[]{:S(2)}, u32[]{:S(2)}) collective-permute-start(f32[8,1792]{1,0:T(8,128)S(1)} %get-tuple-element.85), channel_id=1, source_target_pairs={{0,16},{4,20},{8,24},{12,28},{16,0},{20,4},{24,8},{28,12},{1,17},{... | collective-permute-start | bytes 172040 | tf_op jit(solution)/shard_map/ppermute | solution.py:215
  49.5 1.7 %collective-permute-start.24 = (f32[8,1792]{1,0:T(8,128)S(1)}, f32[8,1792]{1,0:T(8,128)S(1)}, u32[]{:S(2)}, u32[]{:S(2)}) collective-permute-start(f32[8,1792]{1,0:T(8,128)S(1)} %get-tuple-element.87), channel_id=1, source_target_pairs={{0,8},{4,12},{8,0},{12,4},{16,24},{20,28},{24,16},{28,20},{1,9},{5... | collective-permute-start | bytes 172040 | tf_op jit(solution)/shard_map/ppermute | solution.py:215
  51.2 2.8 %collective-permute-start.25 = (f32[8,1792]{1,0:T(8,128)S(1)}, f32[8,1792]{1,0:T(8,128)S(1)}, u32[]{:S(2)}, u32[]{:S(2)}) collective-permute-start(f32[8,1792]{1,0:T(8,128)S(1)} %get-tuple-element.88), channel_id=1, source_target_pairs={{0,24},{4,28},{8,16},{12,20},{16,8},{20,12},{24,0},{28,4},{1,25},{... | collective-permute-start | bytes 172040 | tf_op jit(solution)/shard_map/ppermute | solution.py:215
  53.9 1.9 %shard_map.63 = (f32[2048,256]{1,0:T(8,128)}, f32[8,128]{1,0:T(8,128)S(1)}) custom-call(f32[32,1024]{1,0:T(8,128)S(1)} %get-tuple-element.51.refs_0_.refs_4_, f32[32,1024]{1,0:T(8,128)S(1)} %get-tuple-element.52.refs_1_, f32[32,1024]{1,0:T(8,128)S(1)} %get-tuple-element.57.refs_0_.refs_4_.refs_2_, f32[32,1024]{1,0:T(8,128)S(1)} %get-tuple-element.58.refs_1_.refs_3_, ...), custom_call_target="tpu_custom_call" | custom-call | tf_op jit(solution)/shard_map/pallas_call | solution.py:30
  55.9 1.7 %collective-permute-done.23.refs_7_ = f32[8,1792]{1,0:T(8,128)S(1)} collective-permute-done((f32[8,1792]{1,0:T(8,128)S(1)}, f32[8,1792]{1,0:T(8,128)S(1)}, u32[]{:S(2)}, u32[]{:S(2)}) %collective-permute-start.23) | collective-permute-done | bytes 57376 | tf_op jit(solution)/shard_map/ppermute | solution.py:215
  57.5 0.7 %shard_map.64 = f32[32,1792]{1,0:T(8,128)} custom-call(f32[8,1792]{1,0:T(8,128)S(1)} %get-tuple-element.79.refs_2_.refs_0_, f32[8,1792]{1,0:T(8,128)S(1)} %collective-permute-done.20.refs_1_, f32[8,1792]{1,0:T(8,128)S(1)} %get-tuple-element.78.refs_2_, f32[8,1792]{1,0:T(8,128)S(1)} %collective-permute-done.21.refs_3_, ...), custom_call_target="tpu_custom_call" | custom-call | flops 500000000 | tf_op jit(solution)/shard_map/pallas_call | solution.py:30
  (44 shorter events, 3.6 us)
Async XLA Ops:
  3.8 2.8 %collective-permute-start = (f32[256,1024]{1,0:T(8,128)S(1)}, f32[256,1024]{1,0:T(8,128)S(1)}, u32[]{:S(2)}, u32[]{:S(2)}) collective-permute-start(f32[256,1024]{1,0:T(8,128)S(1)} %get-tuple-element.49), channel_id=1, source_target_pairs={{0,1},{1,0},{2,3},{3,2},{4,5},{5,4},{6,7},{7,6},{8,9},{9,8},{10,11... | collective-permute-start | bytes 3145736 | tf_op jit(solution)/shard_map/ppermute | solution.py:215
  6.8 10.0 %collective-permute-start.1 = (f32[64,1024]{1,0:T(8,128)S(1)}, f32[64,1024]{1,0:T(8,128)S(1)}, u32[]{:S(2)}, u32[]{:S(2)}) collective-permute-start(f32[64,1024]{1,0:T(8,128)S(1)} %get-tuple-element.50.refs_0_), channel_id=1, source_target_pairs={{0,2},{1,3},{2,0},{3,1},{4,6},{5,7},{6,4},{7,5},{8,10},{9,11},{10,... | collective-permute-start | bytes 786440 | tf_op jit(solution)/shard_map/ppermute | solution.py:215
  9.7 13.2 %collective-permute-start.2 = (f32[64,1024]{1,0:T(8,128)S(1)}, f32[64,1024]{1,0:T(8,128)S(1)}, u32[]{:S(2)}, u32[]{:S(2)}) collective-permute-start(f32[64,1024]{1,0:T(8,128)S(1)} %get-tuple-element.53.refs_0_), channel_id=1, source_target_pairs={{0,2},{1,3},{2,0},{3,1},{4,6},{5,7},{6,4},{7,5},{8,10},{9,11},{10,... | collective-permute-start | bytes 786440 | tf_op jit(solution)/shard_map/ppermute | solution.py:215
  16.8 1.4 %collective-permute-start.3 = (f32[32,1024]{1,0:T(8,128)S(1)}, f32[32,1024]{1,0:T(8,128)S(1)}, u32[]{:S(2)}, u32[]{:S(2)}) collective-permute-start(f32[32,1024]{1,0:T(8,128)S(1)} %get-tuple-element.51.refs_0_.refs_4_), channel_id=1, source_target_pairs={{0,1},{1,0},{2,3},{3,2},{4,5},{5,4},{6,7},{7,6},{8,9},{9,8},{10,11... | collective-permute-start | bytes 393224 | tf_op jit(solution)/shard_map/ppermute | solution.py:215
  16.9 1.5 %collective-permute-start.4 = (f32[32,1024]{1,0:T(8,128)S(1)}, f32[32,1024]{1,0:T(8,128)S(1)}, u32[]{:S(2)}, u32[]{:S(2)}) collective-permute-start(f32[32,1024]{1,0:T(8,128)S(1)} %get-tuple-element.52.refs_1_), channel_id=1, source_target_pairs={{0,1},{1,0},{2,3},{3,2},{4,5},{5,4},{6,7},{7,6},{8,9},{9,8},{10,11... | collective-permute-start | bytes 393224 | tf_op jit(solution)/shard_map/ppermute | solution.py:215
  19.2 8.2 %collective-permute-start.6 = (f32[32,1792]{1,0:T(8,128)S(1)}, f32[32,1792]{1,0:T(8,128)S(1)}, u32[]{:S(2)}, u32[]{:S(2)}) collective-permute-start(f32[32,1792]{1,0:T(8,128)S(1)} %get-tuple-element.60), channel_id=1, source_target_pairs={{0,4},{4,0},{8,12},{12,8},{16,20},{20,16},{24,28},{28,24},{1,5},{5... | collective-permute-start | bytes 688136 | tf_op jit(solution)/shard_map/ppermute | solution.py:215
  21.3 9.2 %collective-permute-start.5 = (f32[64,1024]{1,0:T(8,128)S(1)}, f32[64,1024]{1,0:T(8,128)S(1)}, u32[]{:S(2)}, u32[]{:S(2)}) collective-permute-start(f32[64,1024]{1,0:T(8,128)S(1)} %get-tuple-element.59.refs_0_), channel_id=1, source_target_pairs={{0,2},{1,3},{2,0},{3,1},{4,6},{5,7},{6,4},{7,5},{8,10},{9,11},{10,... | collective-permute-start | bytes 786440 | tf_op jit(solution)/shard_map/ppermute | solution.py:215
  22.9 2.1 %collective-permute-start.7 = (f32[32,1024]{1,0:T(8,128)S(1)}, f32[32,1024]{1,0:T(8,128)S(1)}, u32[]{:S(2)}, u32[]{:S(2)}) collective-permute-start(f32[32,1024]{1,0:T(8,128)S(1)} %get-tuple-element.57.refs_0_.refs_4_.refs_2_), channel_id=1, source_target_pairs={{0,1},{1,0},{2,3},{3,2},{4,5},{5,4},{6,7},{7,6},{8,9},{9,8},{10,11... | collective-permute-start | bytes 393224 | tf_op jit(solution)/shard_map/ppermute | solution.py:215
  23.0 2.0 %collective-permute-start.8 = (f32[32,1024]{1,0:T(8,128)S(1)}, f32[32,1024]{1,0:T(8,128)S(1)}, u32[]{:S(2)}, u32[]{:S(2)}) collective-permute-start(f32[32,1024]{1,0:T(8,128)S(1)} %get-tuple-element.58.refs_1_.refs_3_), channel_id=1, source_target_pairs={{0,1},{1,0},{2,3},{3,2},{4,5},{5,4},{6,7},{7,6},{8,9},{9,8},{10,11... | collective-permute-start | bytes 393224 | tf_op jit(solution)/shard_map/ppermute | solution.py:215
  23.5 11.7 %collective-permute-start.9 = (f32[64,1024]{1,0:T(8,128)S(1)}, f32[64,1024]{1,0:T(8,128)S(1)}, u32[]{:S(2)}, u32[]{:S(2)}) collective-permute-start(f32[64,1024]{1,0:T(8,128)S(1)} %get-tuple-element.65.refs_0_), channel_id=1, source_target_pairs={{0,2},{1,3},{2,0},{3,1},{4,6},{5,7},{6,4},{7,5},{8,10},{9,11},{10,... | collective-permute-start | bytes 786440 | tf_op jit(solution)/shard_map/ppermute | solution.py:215
  25.8 9.3 %collective-permute-start.10 = (f32[32,1792]{1,0:T(8,128)S(1)}, f32[32,1792]{1,0:T(8,128)S(1)}, u32[]{:S(2)}, u32[]{:S(2)}) collective-permute-start(f32[32,1792]{1,0:T(8,128)S(1)} %get-tuple-element.66), channel_id=1, source_target_pairs={{0,4},{4,0},{8,12},{12,8},{16,20},{20,16},{24,28},{28,24},{1,5},{5... | collective-permute-start | bytes 688136 | tf_op jit(solution)/shard_map/ppermute | solution.py:215
  30.5 1.4 %collective-permute-start.11 = (f32[32,1024]{1,0:T(8,128)S(1)}, f32[32,1024]{1,0:T(8,128)S(1)}, u32[]{:S(2)}, u32[]{:S(2)}) collective-permute-start(f32[32,1024]{1,0:T(8,128)S(1)} %get-tuple-element.63.refs_0_.refs_4_), channel_id=1, source_target_pairs={{0,1},{1,0},{2,3},{3,2},{4,5},{5,4},{6,7},{7,6},{8,9},{9,8},{10,11... | collective-permute-start | bytes 393224 | tf_op jit(solution)/shard_map/ppermute | solution.py:215
  30.6 1.5 %collective-permute-start.12 = (f32[32,1024]{1,0:T(8,128)S(1)}, f32[32,1024]{1,0:T(8,128)S(1)}, u32[]{:S(2)}, u32[]{:S(2)}) collective-permute-start(f32[32,1024]{1,0:T(8,128)S(1)} %get-tuple-element.64.refs_1_.refs_5_), channel_id=1, source_target_pairs={{0,1},{1,0},{2,3},{3,2},{4,5},{5,4},{6,7},{7,6},{8,9},{9,8},{10,11... | collective-permute-start | bytes 393224 | tf_op jit(solution)/shard_map/ppermute | solution.py:215
  32.9 7.9 %collective-permute-start.16 = (f32[32,1792]{1,0:T(8,128)S(1)}, f32[32,1792]{1,0:T(8,128)S(1)}, u32[]{:S(2)}, u32[]{:S(2)}) collective-permute-start(f32[32,1792]{1,0:T(8,128)S(1)} %get-tuple-element.73), channel_id=1, source_target_pairs={{0,4},{4,0},{8,12},{12,8},{16,20},{20,16},{24,28},{28,24},{1,5},{5... | collective-permute-start | bytes 688136 | tf_op jit(solution)/shard_map/ppermute | solution.py:215
  33.0 9.6 %collective-permute-start.18 = (f32[16,1792]{1,0:T(8,128)S(1)}, f32[16,1792]{1,0:T(8,128)S(1)}, u32[]{:S(2)}, u32[]{:S(2)}) collective-permute-start(f32[16,1792]{1,0:T(8,128)S(1)} %get-tuple-element.76), channel_id=1, source_target_pairs={{0,8},{4,12},{8,0},{12,4},{16,24},{20,28},{24,16},{28,20},{1,9},{5... | collective-permute-start | bytes 344072 | tf_op jit(solution)/shard_map/ppermute | solution.py:215
  35.2 2.9 %collective-permute-start.13 = (f32[32,1024]{1,0:T(8,128)S(1)}, f32[32,1024]{1,0:T(8,128)S(1)}, u32[]{:S(2)}, u32[]{:S(2)}) collective-permute-start(f32[32,1024]{1,0:T(8,128)S(1)} %get-tuple-element.69.refs_0_.refs_4_.refs_6_), channel_id=1, source_target_pairs={{0,1},{1,0},{2,3},{3,2},{4,5},{5,4},{6,7},{7,6},{8,9},{9,8},{10,11... | collective-permute-start | bytes 393224 | tf_op jit(solution)/shard_map/ppermute | solution.py:215
  35.3 2.8 %collective-permute-start.14 = (f32[32,1024]{1,0:T(8,128)S(1)}, f32[32,1024]{1,0:T(8,128)S(1)}, u32[]{:S(2)}, u32[]{:S(2)}) collective-permute-start(f32[32,1024]{1,0:T(8,128)S(1)} %get-tuple-element.70.refs_1_.refs_7_), channel_id=1, source_target_pairs={{0,1},{1,0},{2,3},{3,2},{4,5},{5,4},{6,7},{7,6},{8,9},{9,8},{10,11... | collective-permute-start | bytes 393224 | tf_op jit(solution)/shard_map/ppermute | solution.py:215
  35.8 6.8 %collective-permute-start.19 = (f32[16,1792]{1,0:T(8,128)S(1)}, f32[16,1792]{1,0:T(8,128)S(1)}, u32[]{:S(2)}, u32[]{:S(2)}) collective-permute-start(f32[16,1792]{1,0:T(8,128)S(1)} %get-tuple-element.77), channel_id=1, source_target_pairs={{0,8},{4,12},{8,0},{12,4},{16,24},{20,28},{24,16},{28,20},{1,9},{5... | collective-permute-start | bytes 344072 | tf_op jit(solution)/shard_map/ppermute | solution.py:215
  38.9 10.4 %collective-permute-start.15 = (f32[32,1792]{1,0:T(8,128)S(1)}, f32[32,1792]{1,0:T(8,128)S(1)}, u32[]{:S(2)}, u32[]{:S(2)}) collective-permute-start(f32[32,1792]{1,0:T(8,128)S(1)} %get-tuple-element.72), channel_id=1, source_target_pairs={{0,4},{4,0},{8,12},{12,8},{16,20},{20,16},{24,28},{28,24},{1,5},{5... | collective-permute-start | bytes 688136 | tf_op jit(solution)/shard_map/ppermute | solution.py:215
  40.8 5.5 %collective-permute-start.17 = (f32[16,1792]{1,0:T(8,128)S(1)}, f32[16,1792]{1,0:T(8,128)S(1)}, u32[]{:S(2)}, u32[]{:S(2)}) collective-permute-start(f32[16,1792]{1,0:T(8,128)S(1)} %get-tuple-element.75), channel_id=1, source_target_pairs={{0,8},{4,12},{8,0},{12,4},{16,24},{20,28},{24,16},{28,20},{1,9},{5... | collective-permute-start | bytes 344072 | tf_op jit(solution)/shard_map/ppermute | solution.py:215
  42.7 8.5 %collective-permute-start.20 = (f32[8,1792]{1,0:T(8,128)S(1)}, f32[8,1792]{1,0:T(8,128)S(1)}, u32[]{:S(2)}, u32[]{:S(2)}) collective-permute-start(f32[8,1792]{1,0:T(8,128)S(1)} %get-tuple-element.83), channel_id=1, source_target_pairs={{0,16},{4,20},{8,24},{12,28},{16,0},{20,4},{24,8},{28,12},{1,17},{... | collective-permute-start | bytes 172040 | tf_op jit(solution)/shard_map/ppermute | solution.py:215
  45.4 10.5 %collective-permute-start.21 = (f32[8,1792]{1,0:T(8,128)S(1)}, f32[8,1792]{1,0:T(8,128)S(1)}, u32[]{:S(2)}, u32[]{:S(2)}) collective-permute-start(f32[8,1792]{1,0:T(8,128)S(1)} %get-tuple-element.84), channel_id=1, source_target_pairs={{0,16},{4,20},{8,24},{12,28},{16,0},{20,4},{24,8},{28,12},{1,17},{... | collective-permute-start | bytes 172040 | tf_op jit(solution)/shard_map/ppermute | solution.py:215
  46.3 9.5 %collective-permute-start.22 = (f32[8,1792]{1,0:T(8,128)S(1)}, f32[8,1792]{1,0:T(8,128)S(1)}, u32[]{:S(2)}, u32[]{:S(2)}) collective-permute-start(f32[8,1792]{1,0:T(8,128)S(1)} %get-tuple-element.85), channel_id=1, source_target_pairs={{0,16},{4,20},{8,24},{12,28},{16,0},{20,4},{24,8},{28,12},{1,17},{... | collective-permute-start | bytes 172040 | tf_op jit(solution)/shard_map/ppermute | solution.py:215
  49.4 8.2 %collective-permute-start.23 = (f32[8,1792]{1,0:T(8,128)S(1)}, f32[8,1792]{1,0:T(8,128)S(1)}, u32[]{:S(2)}, u32[]{:S(2)}) collective-permute-start(f32[8,1792]{1,0:T(8,128)S(1)} %get-tuple-element.86), channel_id=1, source_target_pairs={{0,16},{4,20},{8,24},{12,28},{16,0},{20,4},{24,8},{28,12},{1,17},{... | collective-permute-start | bytes 172040 | tf_op jit(solution)/shard_map/ppermute | solution.py:215
  49.5 8.1 %collective-permute-start.24 = (f32[8,1792]{1,0:T(8,128)S(1)}, f32[8,1792]{1,0:T(8,128)S(1)}, u32[]{:S(2)}, u32[]{:S(2)}) collective-permute-start(f32[8,1792]{1,0:T(8,128)S(1)} %get-tuple-element.87), channel_id=1, source_target_pairs={{0,8},{4,12},{8,0},{12,4},{16,24},{20,28},{24,16},{28,20},{1,9},{5... | collective-permute-start | bytes 172040 | tf_op jit(solution)/shard_map/ppermute | solution.py:215
  51.2 6.4 %collective-permute-start.25 = (f32[8,1792]{1,0:T(8,128)S(1)}, f32[8,1792]{1,0:T(8,128)S(1)}, u32[]{:S(2)}, u32[]{:S(2)}) collective-permute-start(f32[8,1792]{1,0:T(8,128)S(1)} %get-tuple-element.88), channel_id=1, source_target_pairs={{0,24},{4,28},{8,16},{12,20},{16,8},{20,12},{24,0},{28,4},{1,25},{... | collective-permute-start | bytes 172040 | tf_op jit(solution)/shard_map/ppermute | solution.py:215

commit v15 on v14

--- a/solution.py
+++ b/solution.py
@@ -77,7 +77,7 @@
         out[:, lanes] = lax.dot_general(omega_t[...], held[rows, :], NT, preferred_element_type=F32)
 
 
-def first_half_body(n_row, pieces, delta, omega, held, omega_t, out, ahead, omega_v, sem, omega_sem, ahead_sem):
+def first_half_body(n_row, pieces, delta, omega, held, omega_t, out, ahead, head, omega_v, sem, omega_sem, ahead_sem):
     k = out.shape[0]
     fetch = pltpu.make_async_copy(omega, omega_v, omega_sem)
     fetch.start()
@@ -89,6 +89,7 @@
     fetch.wait()
     omega_t[...] = lax.dot_general(pick, omega_v[...], NT, preferred_element_type=F32).astype(BF16)
     sketch_half(omega_t, held, copies, out)
+    head[...] = out[pl.ds(0, head.shape[0]), :]
     for copy in early:
         copy.wait()
 
@@ -99,12 +100,16 @@
     sketch_half(omega_t, held, copies, out, BLOCK)
 
 
-def add_chunks_body(kept, received, *outs):
+def add_head_body(kept, received, out):
+    out[...] = kept[pl.ds(0, out.shape[0]), :] + received[...]
+
+
+def add_chunks_body(skipped, kept, received, *outs):
     first = 0
     for out in outs:
-        part = pl.ds(first, out.shape[0])
-        out[...] = kept[part, :] + received[part, :]
-        first += out.shape[0]
+        rows = out.shape[0]
+        out[...] = kept[pl.ds(skipped + first, rows), :] + received[pl.ds(first, rows), :]
+        first += rows
 
 
 def add_body(a, b, *outs):
@@ -228,16 +233,19 @@
 
     in_hbm = pltpu.with_memory_space_constraint(delta, pltpu.HBM)
     sems = pltpu.SemaphoreType.DMA((half // BLOCK,))
-    held_other, omega_t, to_send, ahead = call(
+    held_other, omega_t, to_send, ahead, head = call(
         functools.partial(first_half_body, n_row, pieces),
         (in_hbm, pltpu.with_memory_space_constraint(omega, pltpu.HBM)),
-        [((half, d), BF16), ((k, d), BF16), ((k, half), F32), ((BLOCK, d), BF16)],
+        [((half, d), BF16), ((k, d), BF16), ((k, half), F32), ((BLOCK, d), BF16), ((widths[0], half), F32)],
         "aa",
         scratch=[pltpu.VMEM((d, k), BF16), sems, pltpu.SemaphoreType.DMA, pltpu.SemaphoreType.DMA((1,))],
     )
-    received = swap(to_send, "col", n_col, 1)
+    received_head = swap(head, "col", n_col, 1)
+    received = swap(to_send[widths[0] :], "col", n_col, 1)
     held_own, kept = call(second_half_body, (in_hbm, omega_t, ahead), [((half - BLOCK, d), BF16), ((k, half), F32)], "avv", scratch=[sems])
-    partial = call(add_chunks_body, (kept, received), [((width, half), F32) for width in widths])
+    partial = call(add_head_body, (kept, received_head), [((widths[0], half), F32)])
+    outs = [((width, half), F32) for width in widths[1:]]
+    partial += call(functools.partial(add_chunks_body, widths[0]), (kept, received), outs, after=partial)
     bit = 2
     while bit < n_col // 2:
         moved = [swap(x, "col", n_col, bit) for x in partial]

time: 58.4 us -> 58.5 us (level)
    ppermute x26 -> x27, waiting for transfers between devices: 14.5 us -> 14.7 us  [swap(): return lax.ppermute(x, axis, [(i, i ^ bit) for i in range(size)])]
    ppermute x26 -> x27, starting transfers between devices: 28.5 us -> 28.2 us  [swap(): return lax.ppermute(x, axis, [(i, i ^ bit) for i in range(size)])]
    pallas_call x24 -> x25, Pallas kernels: 14.5 us -> 14.6 us  [call(): pl.pallas_call(run, out_shape=[pltpu.VMEM(*o) if i >= results else jax.Sh...]
  transfers between devices with their start and end apart: 26 -> 27, of which waited for: 11 -> 12; matrix products, arithmetic and copies ran while one was open for 0% -> 0% of each run, Pallas kernels for 18% -> 18%
where the time goes in v15:
time: 58.5 us; the launch traced here: 58.4 us
  starting transfers between devices  28.2 us (48%)
  waiting for transfers between devices  14.7 us (25%)
  Pallas kernels  14.6 us (25%)
  between operations  0.83 us (1%)
    ppermute x27, starting transfers between devices, swap(): return lax.ppermute(x, axis, [(i, i ^ bit) for i in range(size)])  28.2 us
    ppermute x27, waiting for transfers between devices, swap(): return lax.ppermute(x, axis, [(i, i ^ bit) for i in range(size)])  14.7 us
    pallas_call x25, Pallas kernels, call(): pl.pallas_call(run, out_shape=[pltpu.VMEM(*o) if i >= results else jax.Sh...  14.6 us
  transfers between devices with their start and end apart: 27, of which 12 were waited for; matrix products, arithmetic and copies ran while one was open for 0% of the time, Pallas kernels for 18%

profile of v15, /device:TPU:0, one launch (start us, length us, event | category | flops | bytes accessed | tf_op | source)
XLA Modules:
  0.0 58.4 jit_solution(9815213945888244450)
XLA Ops:
  0.6 3.2 %shard_map.41 = (bf16[1024,1792]{1,0:T(8,128)(2,1)S(1)}, bf16[256,1792]{1,0:T(8,128)(2,1)S(1)}, f32[256,1024]{1,0:T(8,128)S(1)}, bf16[512,1792]{1,0:T(8,128)(2,1)S(1)}, f32[64,1024]{1,0:T(8,128)S(1)}) custom-call(bf16[2048,1792]{1,0:T(8,128)(2,1)} %refs_0_.3, bf16[1792,256]{1,0:T(8,128)(2,1)} %refs_1_.1), custom_call_target="tpu_custom_call" | custom-call | tf_op jit(solution)/shard_map/pallas_call | solution.py:30
  3.9 0.5 collective-permute-start.2
  4.5 2.2 %shard_map.42 = (bf16[512,1792]{1,0:T(8,128)(2,1)S(1)}, f32[256,1024]{1,0:T(8,128)S(1)}) custom-call(bf16[2048,1792]{1,0:T(8,128)(2,1)} %refs_0_.3, bf16[256,1792]{1,0:T(8,128)(2,1)S(1)} %get-tuple-element.46.refs_1_, bf16[512,1792]{1,0:T(8,128)(2,1)S(1)} %get-tuple-element.47.refs_2_), custom_call_target="tpu_custom_call" | custom-call | tf_op jit(solution)/shard_map/pallas_call | solution.py:30
  6.8 3.0 %collective-permute-start.1 = (f32[64,1024]{1,0:T(8,128)S(1)}, f32[64,1024]{1,0:T(8,128)S(1)}, u32[]{:S(2)}, u32[]{:S(2)}) collective-permute-start(f32[64,1024]{1,0:T(8,128)S(1)} %shard_map.43.refs_0_.refs_2_), channel_id=1, source_target_pairs={{0,2},{1,3},{2,0},{3,1},{4,6},{5,7},{6,4},{7,5},{8,10},{9,11},{10,... | collective-permute-start | bytes 786440 | tf_op jit(solution)/shard_map/ppermute | solution.py:220
  9.9 6.9 %collective-permute-done.1.refs_1_ = f32[64,1024]{1,0:T(8,128)S(1)} collective-permute-done((f32[64,1024]{1,0:T(8,128)S(1)}, f32[64,1024]{1,0:T(8,128)S(1)}, u32[]{:S(2)}, u32[]{:S(2)}) %collective-permute-start.1) | collective-permute-done | bytes 262176 | tf_op jit(solution)/shard_map/ppermute | solution.py:220
  17.0 0.5 collective-permute-start.5
  17.5 0.7 %shard_map.46.refs_3_.refs_4_ = f32[64,1792]{1,0:T(8,128)S(1)} custom-call(f32[32,1024]{1,0:T(8,128)S(1)} %get-tuple-element.50.refs_0_.refs_4_, f32[32,1024]{1,0:T(8,128)S(1)} %get-tuple-element.51.refs_1_, bf16[512,1792]{1,0:T(8,128)(2,1)S(1)} %get-tuple-element.47.refs_2_, bf16[512,1792]{1,0:T(8,128)(2,1)S(1)} %get-tuple-element.55.refs_3_, ...), custom_call_target="tpu_custom_call" | custom-call | tf_op jit(solution)/shard_map/pallas_call | solution.py:30
  18.5 0.8 %shard_map.47 = (f32[32,1792]{1,0:T(8,128)S(1)}, f32[32,1792]{1,0:T(8,128)S(1)}) custom-call(f32[32,1024]{1,0:T(8,128)S(1)} %collective-permute-done.4.refs_0_.refs_8_, f32[32,1024]{1,0:T(8,128)S(1)} %collective-permute-done.5.refs_1_.refs_9_, bf16[1024,1792]{1,0:T(8,128)(2,1)S(1)} %get-tuple-element.54.refs_2_, f32[64,1792]{1,0:T(8,128)S(1)} %shard_map.46.refs_3_.refs_4_, ...), custom_call_target="tpu_custom_call" | custom-call | tf_op jit(solution)/shard_map/pallas_call | solution.py:30
  19.3 2.2 %collective-permute-start.7 = (f32[32,1792]{1,0:T(8,128)S(1)}, f32[32,1792]{1,0:T(8,128)S(1)}, u32[]{:S(2)}, u32[]{:S(2)}) collective-permute-start(f32[32,1792]{1,0:T(8,128)S(1)} %get-tuple-element.60), channel_id=1, source_target_pairs={{0,4},{4,0},{8,12},{12,8},{16,20},{20,16},{24,28},{28,24},{1,5},{5... | collective-permute-start | bytes 688136 | tf_op jit(solution)/shard_map/ppermute | solution.py:220
  21.4 1.5 %collective-permute-start.6 = (f32[64,1024]{1,0:T(8,128)S(1)}, f32[64,1024]{1,0:T(8,128)S(1)}, u32[]{:S(2)}, u32[]{:S(2)}) collective-permute-start(f32[64,1024]{1,0:T(8,128)S(1)} %get-tuple-element.59.refs_0_), channel_id=1, source_target_pairs={{0,2},{1,3},{2,0},{3,1},{4,6},{5,7},{6,4},{7,5},{8,10},{9,11},{10,... | collective-permute-start | bytes 786440 | tf_op jit(solution)/shard_map/ppermute | solution.py:220
  23.5 0.7 %collective-permute-start.10 = (f32[64,1024]{1,0:T(8,128)S(1)}, f32[64,1024]{1,0:T(8,128)S(1)}, u32[]{:S(2)}, u32[]{:S(2)}) collective-permute-start(f32[64,1024]{1,0:T(8,128)S(1)} %get-tuple-element.65.refs_0_), channel_id=1, source_target_pairs={{0,2},{1,3},{2,0},{3,1},{4,6},{5,7},{6,4},{7,5},{8,10},{9,11},{10,... | collective-permute-start | bytes 786440 | tf_op jit(solution)/shard_map/ppermute | solution.py:220
  24.3 0.8 %shard_map.49.refs_3_.refs_4_ = f32[64,1792]{1,0:T(8,128)S(1)} custom-call(f32[32,1024]{1,0:T(8,128)S(1)} %get-tuple-element.57.refs_0_.refs_4_.refs_2_, f32[32,1024]{1,0:T(8,128)S(1)} %get-tuple-element.58.refs_1_.refs_3_, bf16[512,1792]{1,0:T(8,128)(2,1)S(1)} %get-tuple-element.47.refs_2_, bf16[512,1792]{1,0:T(8,128)(2,1)S(1)} %get-tuple-element.55.refs_3_, ...), custom_call_target="tpu_custom_call" | custom-call | flops 500000000 | tf_op jit(solution)/shard_map/pallas_call | solution.py:30
  25.1 0.8 %shard_map.50 = (f32[32,1792]{1,0:T(8,128)S(1)}, f32[32,1792]{1,0:T(8,128)S(1)}) custom-call(f32[32,1024]{1,0:T(8,128)S(1)} %collective-permute-done.8.refs_0_.refs_10_, f32[32,1024]{1,0:T(8,128)S(1)} %collective-permute-done.9.refs_1_.refs_11_, bf16[1024,1792]{1,0:T(8,128)(2,1)S(1)} %get-tuple-element.54.refs_2_, f32[64,1792]{1,0:T(8,128)S(1)} %shard_map.49.refs_3_.refs_4_, ...), custom_call_target="tpu_custom_call" | custom-call | tf_op jit(solution)/shard_map/pallas_call | solution.py:30
  25.8 1.6 %collective-permute-start.11 = (f32[32,1792]{1,0:T(8,128)S(1)}, f32[32,1792]{1,0:T(8,128)S(1)}, u32[]{:S(2)}, u32[]{:S(2)}) collective-permute-start(f32[32,1792]{1,0:T(8,128)S(1)} %get-tuple-element.66), channel_id=1, source_target_pairs={{0,4},{4,0},{8,12},{12,8},{16,20},{20,16},{24,28},{28,24},{1,5},{5... | collective-permute-start | bytes 688136 | tf_op jit(solution)/shard_map/ppermute | solution.py:220
  27.6 3.0 %collective-permute-done.6.refs_1_ = f32[64,1024]{1,0:T(8,128)S(1)} collective-permute-done((f32[64,1024]{1,0:T(8,128)S(1)}, f32[64,1024]{1,0:T(8,128)S(1)}, u32[]{:S(2)}, u32[]{:S(2)}) %collective-permute-start.6) | collective-permute-done | bytes 262176 | tf_op jit(solution)/shard_map/ppermute | solution.py:220
  31.2 0.7 %shard_map.53.refs_3_.refs_4_ = f32[64,1792]{1,0:T(8,128)S(1)} custom-call(f32[32,1024]{1,0:T(8,128)S(1)} %get-tuple-element.63.refs_0_.refs_4_, f32[32,1024]{1,0:T(8,128)S(1)} %get-tuple-element.64.refs_1_.refs_5_, bf16[512,1792]{1,0:T(8,128)(2,1)S(1)} %get-tuple-element.47.refs_2_, bf16[512,1792]{1,0:T(8,128)(2,1)S(1)} %get-tuple-element.55.refs_3_, ...), custom_call_target="tpu_custom_call" | custom-call | tf_op jit(solution)/shard_map/pallas_call | solution.py:30
  32.2 0.8 %shard_map.54 = (f32[32,1792]{1,0:T(8,128)S(1)}, f32[32,1792]{1,0:T(8,128)S(1)}) custom-call(f32[32,1024]{1,0:T(8,128)S(1)} %collective-permute-done.12.refs_0_.refs_12_, f32[32,1024]{1,0:T(8,128)S(1)} %collective-permute-done.13.refs_1_.refs_13_, bf16[1024,1792]{1,0:T(8,128)(2,1)S(1)} %get-tuple-element.54.refs_2_, ...), custom_call_target="tpu_custom_call" | custom-call | tf_op jit(solution)/shard_map/pallas_call | solution.py:30
  33.1 2.0 %collective-permute-start.19 = (f32[16,1792]{1,0:T(8,128)S(1)}, f32[16,1792]{1,0:T(8,128)S(1)}, u32[]{:S(2)}, u32[]{:S(2)}) collective-permute-start(f32[16,1792]{1,0:T(8,128)S(1)} %get-tuple-element.76), channel_id=1, source_target_pairs={{0,8},{4,12},{8,0},{12,4},{16,24},{20,28},{24,16},{28,20},{1,9},{5... | collective-permute-start | bytes 344072 | tf_op jit(solution)/shard_map/ppermute | solution.py:220
  35.4 0.5 collective-permute-start.15
  35.9 0.7 %shard_map.57.refs_3_.refs_4_ = f32[64,1792]{1,0:T(8,128)S(1)} custom-call(f32[32,1024]{1,0:T(8,128)S(1)} %get-tuple-element.69.refs_0_.refs_4_.refs_6_, f32[32,1024]{1,0:T(8,128)S(1)} %get-tuple-element.70.refs_1_.refs_7_, bf16[512,1792]{1,0:T(8,128)(2,1)S(1)} %get-tuple-element.47.refs_2_, bf16[512,1792]{1,0:T(8,128)(2,1)S(1)} %get-tuple-element.55.refs_3_, ...), custom_call_target="tpu_custom_call" | custom-call | flops 2000000000 | tf_op jit(solution)/shard_map/pallas_call | solution.py:30
  36.9 0.8 %shard_map.58 = (f32[32,1792]{1,0:T(8,128)S(1)}, f32[32,1792]{1,0:T(8,128)S(1)}) custom-call(f32[32,1024]{1,0:T(8,128)S(1)} %collective-permute-done.14.refs_0_.refs_14_, f32[32,1024]{1,0:T(8,128)S(1)} %collective-permute-done.15.refs_1_.refs_15_, bf16[1024,1792]{1,0:T(8,128)(2,1)S(1)} %get-tuple-element.54.refs_2_, ...), custom_call_target="tpu_custom_call" | custom-call | tf_op jit(solution)/shard_map/pallas_call | solution.py:30
  37.7 2.0 %collective-permute-start.16 = (f32[32,1792]{1,0:T(8,128)S(1)}, f32[32,1792]{1,0:T(8,128)S(1)}, u32[]{:S(2)}, u32[]{:S(2)}) collective-permute-start(f32[32,1792]{1,0:T(8,128)S(1)} %get-tuple-element.72), channel_id=1, source_target_pairs={{0,4},{4,0},{8,12},{12,8},{16,20},{20,16},{24,28},{28,24},{1,5},{5... | collective-permute-start | bytes 688136 | tf_op jit(solution)/shard_map/ppermute | solution.py:220
  39.7 1.2 %collective-permute-done.17.refs_1_ = f32[32,1792]{1,0:T(8,128)S(1)} collective-permute-done((f32[32,1792]{1,0:T(8,128)S(1)}, f32[32,1792]{1,0:T(8,128)S(1)}, u32[]{:S(2)}, u32[]{:S(2)}) %collective-permute-start.17) | collective-permute-done | bytes 229408 | tf_op jit(solution)/shard_map/ppermute | solution.py:220
  40.9 1.6 %collective-permute-start.18 = (f32[16,1792]{1,0:T(8,128)S(1)}, f32[16,1792]{1,0:T(8,128)S(1)}, u32[]{:S(2)}, u32[]{:S(2)}) collective-permute-start(f32[16,1792]{1,0:T(8,128)S(1)} %get-tuple-element.75), channel_id=1, source_target_pairs={{0,8},{4,12},{8,0},{12,4},{16,24},{20,28},{24,16},{28,20},{1,9},{5... | collective-permute-start | bytes 344072 | tf_op jit(solution)/shard_map/ppermute | solution.py:220
  42.7 2.7 %collective-permute-start.21 = (f32[8,1792]{1,0:T(8,128)S(1)}, f32[8,1792]{1,0:T(8,128)S(1)}, u32[]{:S(2)}, u32[]{:S(2)}) collective-permute-start(f32[8,1792]{1,0:T(8,128)S(1)} %get-tuple-element.83), channel_id=1, source_target_pairs={{0,16},{4,20},{8,24},{12,28},{16,0},{20,4},{24,8},{28,12},{1,17},{... | collective-permute-start | bytes 172040 | tf_op jit(solution)/shard_map/ppermute | solution.py:220
  45.7 0.8 %collective-permute-done.18.refs_1_ = f32[16,1792]{1,0:T(8,128)S(1)} collective-permute-done((f32[16,1792]{1,0:T(8,128)S(1)}, f32[16,1792]{1,0:T(8,128)S(1)}, u32[]{:S(2)}, u32[]{:S(2)}) %collective-permute-start.18) | collective-permute-done | bytes 114720 | tf_op jit(solution)/shard_map/ppermute | solution.py:220
  46.4 3.0 %collective-permute-start.23 = (f32[8,1792]{1,0:T(8,128)S(1)}, f32[8,1792]{1,0:T(8,128)S(1)}, u32[]{:S(2)}, u32[]{:S(2)}) collective-permute-start(f32[8,1792]{1,0:T(8,128)S(1)} %get-tuple-element.85), channel_id=1, source_target_pairs={{0,16},{4,20},{8,24},{12,28},{16,0},{20,4},{24,8},{28,12},{1,17},{... | collective-permute-start | bytes 172040 | tf_op jit(solution)/shard_map/ppermute | solution.py:220
  49.6 1.7 %collective-permute-start.25 = (f32[8,1792]{1,0:T(8,128)S(1)}, f32[8,1792]{1,0:T(8,128)S(1)}, u32[]{:S(2)}, u32[]{:S(2)}) collective-permute-start(f32[8,1792]{1,0:T(8,128)S(1)} %get-tuple-element.87), channel_id=1, source_target_pairs={{0,8},{4,12},{8,0},{12,4},{16,24},{20,28},{24,16},{28,20},{1,9},{5... | collective-permute-start | bytes 172040 | tf_op jit(solution)/shard_map/ppermute | solution.py:220
  51.2 2.7 %collective-permute-start.26 = (f32[8,1792]{1,0:T(8,128)S(1)}, f32[8,1792]{1,0:T(8,128)S(1)}, u32[]{:S(2)}, u32[]{:S(2)}) collective-permute-start(f32[8,1792]{1,0:T(8,128)S(1)} %get-tuple-element.88), channel_id=1, source_target_pairs={{0,24},{4,28},{8,16},{12,20},{16,8},{20,12},{24,0},{28,4},{1,25},{... | collective-permute-start | bytes 172040 | tf_op jit(solution)/shard_map/ppermute | solution.py:220
  53.9 1.9 %shard_map.64 = (f32[2048,256]{1,0:T(8,128)}, f32[8,128]{1,0:T(8,128)S(1)}) custom-call(f32[32,1024]{1,0:T(8,128)S(1)} %get-tuple-element.50.refs_0_.refs_4_, f32[32,1024]{1,0:T(8,128)S(1)} %get-tuple-element.51.refs_1_, f32[32,1024]{1,0:T(8,128)S(1)} %get-tuple-element.57.refs_0_.refs_4_.refs_2_, f32[32,1024]{1,0:T(8,128)S(1)} %get-tuple-element.58.refs_1_.refs_3_, ...), custom_call_target="tpu_custom_call" | custom-call | tf_op jit(solution)/shard_map/pallas_call | solution.py:30
  55.9 1.8 %collective-permute-done.24.refs_7_ = f32[8,1792]{1,0:T(8,128)S(1)} collective-permute-done((f32[8,1792]{1,0:T(8,128)S(1)}, f32[8,1792]{1,0:T(8,128)S(1)}, u32[]{:S(2)}, u32[]{:S(2)}) %collective-permute-start.24) | collective-permute-done | bytes 57376 | tf_op jit(solution)/shard_map/ppermute | solution.py:220
  57.6 0.7 %shard_map.65 = f32[32,1792]{1,0:T(8,128)} custom-call(f32[8,1792]{1,0:T(8,128)S(1)} %get-tuple-element.79.refs_2_.refs_0_, f32[8,1792]{1,0:T(8,128)S(1)} %collective-permute-done.21.refs_1_, f32[8,1792]{1,0:T(8,128)S(1)} %get-tuple-element.78.refs_2_, f32[8,1792]{1,0:T(8,128)S(1)} %collective-permute-done.22.refs_3_, ...), custom_call_target="tpu_custom_call" | custom-call | flops 500000000 | tf_op jit(solution)/shard_map/pallas_call | solution.py:30
  (48 shorter events, 3.5 us)
Async XLA Ops:
  3.9 5.8 %collective-permute-start.2 = (f32[192,1024]{1,0:T(8,128)S(1)}, f32[192,1024]{1,0:T(8,128)S(1)}, u32[]{:S(2)}, u32[]{:S(2)}) collective-permute-start(f32[192,1024]{1,0:T(8,128)S(1)} %slice.3), channel_id=1, source_target_pairs={{0,1},{1,0},{2,3},{3,2},{4,5},{5,4},{6,7},{7,6},{8,9},{9,8},{10,11... | collective-permute-start | bytes 2359304 | tf_op jit(solution)/shard_map/ppermute | solution.py:220
  4.4 2.3 %collective-permute-start = (f32[64,1024]{1,0:T(8,128)S(1)}, f32[64,1024]{1,0:T(8,128)S(1)}, u32[]{:S(2)}, u32[]{:S(2)}) collective-permute-start(f32[64,1024]{1,0:T(8,128)S(1)} %get-tuple-element.49), channel_id=1, source_target_pairs={{0,1},{1,0},{2,3},{3,2},{4,5},{5,4},{6,7},{7,6},{8,9},{9,8},{10,11... | collective-permute-start | bytes 786440 | tf_op jit(solution)/shard_map/ppermute | solution.py:220
  6.8 10.1 %collective-permute-start.1 = (f32[64,1024]{1,0:T(8,128)S(1)}, f32[64,1024]{1,0:T(8,128)S(1)}, u32[]{:S(2)}, u32[]{:S(2)}) collective-permute-start(f32[64,1024]{1,0:T(8,128)S(1)} %shard_map.43.refs_0_.refs_2_), channel_id=1, source_target_pairs={{0,2},{1,3},{2,0},{3,1},{4,6},{5,7},{6,4},{7,5},{8,10},{9,11},{10,... | collective-permute-start | bytes 786440 | tf_op jit(solution)/shard_map/ppermute | solution.py:220
  9.9 13.1 %collective-permute-start.3 = (f32[64,1024]{1,0:T(8,128)S(1)}, f32[64,1024]{1,0:T(8,128)S(1)}, u32[]{:S(2)}, u32[]{:S(2)}) collective-permute-start(f32[64,1024]{1,0:T(8,128)S(1)} %get-tuple-element.53.refs_0_), channel_id=1, source_target_pairs={{0,2},{1,3},{2,0},{3,1},{4,6},{5,7},{6,4},{7,5},{8,10},{9,11},{10,... | collective-permute-start | bytes 786440 | tf_op jit(solution)/shard_map/ppermute | solution.py:220
  16.9 1.4 %collective-permute-start.4 = (f32[32,1024]{1,0:T(8,128)S(1)}, f32[32,1024]{1,0:T(8,128)S(1)}, u32[]{:S(2)}, u32[]{:S(2)}) collective-permute-start(f32[32,1024]{1,0:T(8,128)S(1)} %get-tuple-element.50.refs_0_.refs_4_), channel_id=1, source_target_pairs={{0,1},{1,0},{2,3},{3,2},{4,5},{5,4},{6,7},{7,6},{8,9},{9,8},{10,11... | collective-permute-start | bytes 393224 | tf_op jit(solution)/shard_map/ppermute | solution.py:220
  17.0 1.5 %collective-permute-start.5 = (f32[32,1024]{1,0:T(8,128)S(1)}, f32[32,1024]{1,0:T(8,128)S(1)}, u32[]{:S(2)}, u32[]{:S(2)}) collective-permute-start(f32[32,1024]{1,0:T(8,128)S(1)} %get-tuple-element.51.refs_1_), channel_id=1, source_target_pairs={{0,1},{1,0},{2,3},{3,2},{4,5},{5,4},{6,7},{7,6},{8,9},{9,8},{10,11... | collective-permute-start | bytes 393224 | tf_op jit(solution)/shard_map/ppermute | solution.py:220
  19.3 8.2 %collective-permute-start.7 = (f32[32,1792]{1,0:T(8,128)S(1)}, f32[32,1792]{1,0:T(8,128)S(1)}, u32[]{:S(2)}, u32[]{:S(2)}) collective-permute-start(f32[32,1792]{1,0:T(8,128)S(1)} %get-tuple-element.60), channel_id=1, source_target_pairs={{0,4},{4,0},{8,12},{12,8},{16,20},{20,16},{24,28},{28,24},{1,5},{5... | collective-permute-start | bytes 688136 | tf_op jit(solution)/shard_map/ppermute | solution.py:220
  21.4 9.2 %collective-permute-start.6 = (f32[64,1024]{1,0:T(8,128)S(1)}, f32[64,1024]{1,0:T(8,128)S(1)}, u32[]{:S(2)}, u32[]{:S(2)}) collective-permute-start(f32[64,1024]{1,0:T(8,128)S(1)} %get-tuple-element.59.refs_0_), channel_id=1, source_target_pairs={{0,2},{1,3},{2,0},{3,1},{4,6},{5,7},{6,4},{7,5},{8,10},{9,11},{10,... | collective-permute-start | bytes 786440 | tf_op jit(solution)/shard_map/ppermute | solution.py:220
  23.0 2.1 %collective-permute-start.8 = (f32[32,1024]{1,0:T(8,128)S(1)}, f32[32,1024]{1,0:T(8,128)S(1)}, u32[]{:S(2)}, u32[]{:S(2)}) collective-permute-start(f32[32,1024]{1,0:T(8,128)S(1)} %get-tuple-element.57.refs_0_.refs_4_.refs_2_), channel_id=1, source_target_pairs={{0,1},{1,0},{2,3},{3,2},{4,5},{5,4},{6,7},{7,6},{8,9},{9,8},{10,11... | collective-permute-start | bytes 393224 | tf_op jit(solution)/shard_map/ppermute | solution.py:220
  23.0 2.0 %collective-permute-start.9 = (f32[32,1024]{1,0:T(8,128)S(1)}, f32[32,1024]{1,0:T(8,128)S(1)}, u32[]{:S(2)}, u32[]{:S(2)}) collective-permute-start(f32[32,1024]{1,0:T(8,128)S(1)} %get-tuple-element.58.refs_1_.refs_3_), channel_id=1, source_target_pairs={{0,1},{1,0},{2,3},{3,2},{4,5},{5,4},{6,7},{7,6},{8,9},{9,8},{10,11... | collective-permute-start | bytes 393224 | tf_op jit(solution)/shard_map/ppermute | solution.py:220
  23.5 11.8 %collective-permute-start.10 = (f32[64,1024]{1,0:T(8,128)S(1)}, f32[64,1024]{1,0:T(8,128)S(1)}, u32[]{:S(2)}, u32[]{:S(2)}) collective-permute-start(f32[64,1024]{1,0:T(8,128)S(1)} %get-tuple-element.65.refs_0_), channel_id=1, source_target_pairs={{0,2},{1,3},{2,0},{3,1},{4,6},{5,7},{6,4},{7,5},{8,10},{9,11},{10,... | collective-permute-start | bytes 786440 | tf_op jit(solution)/shard_map/ppermute | solution.py:220
  25.8 9.3 %collective-permute-start.11 = (f32[32,1792]{1,0:T(8,128)S(1)}, f32[32,1792]{1,0:T(8,128)S(1)}, u32[]{:S(2)}, u32[]{:S(2)}) collective-permute-start(f32[32,1792]{1,0:T(8,128)S(1)} %get-tuple-element.66), channel_id=1, source_target_pairs={{0,4},{4,0},{8,12},{12,8},{16,20},{20,16},{24,28},{28,24},{1,5},{5... | collective-permute-start | bytes 688136 | tf_op jit(solution)/shard_map/ppermute | solution.py:220
  30.6 1.4 %collective-permute-start.12 = (f32[32,1024]{1,0:T(8,128)S(1)}, f32[32,1024]{1,0:T(8,128)S(1)}, u32[]{:S(2)}, u32[]{:S(2)}) collective-permute-start(f32[32,1024]{1,0:T(8,128)S(1)} %get-tuple-element.63.refs_0_.refs_4_), channel_id=1, source_target_pairs={{0,1},{1,0},{2,3},{3,2},{4,5},{5,4},{6,7},{7,6},{8,9},{9,8},{10,11... | collective-permute-start | bytes 393224 | tf_op jit(solution)/shard_map/ppermute | solution.py:220
  30.7 1.5 %collective-permute-start.13 = (f32[32,1024]{1,0:T(8,128)S(1)}, f32[32,1024]{1,0:T(8,128)S(1)}, u32[]{:S(2)}, u32[]{:S(2)}) collective-permute-start(f32[32,1024]{1,0:T(8,128)S(1)} %get-tuple-element.64.refs_1_.refs_5_), channel_id=1, source_target_pairs={{0,1},{1,0},{2,3},{3,2},{4,5},{5,4},{6,7},{7,6},{8,9},{9,8},{10,11... | collective-permute-start | bytes 393224 | tf_op jit(solution)/shard_map/ppermute | solution.py:220
  33.0 7.9 %collective-permute-start.17 = (f32[32,1792]{1,0:T(8,128)S(1)}, f32[32,1792]{1,0:T(8,128)S(1)}, u32[]{:S(2)}, u32[]{:S(2)}) collective-permute-start(f32[32,1792]{1,0:T(8,128)S(1)} %get-tuple-element.73), channel_id=1, source_target_pairs={{0,4},{4,0},{8,12},{12,8},{16,20},{20,16},{24,28},{28,24},{1,5},{5... | collective-permute-start | bytes 688136 | tf_op jit(solution)/shard_map/ppermute | solution.py:220
  33.1 9.5 %collective-permute-start.19 = (f32[16,1792]{1,0:T(8,128)S(1)}, f32[16,1792]{1,0:T(8,128)S(1)}, u32[]{:S(2)}, u32[]{:S(2)}) collective-permute-start(f32[16,1792]{1,0:T(8,128)S(1)} %get-tuple-element.76), channel_id=1, source_target_pairs={{0,8},{4,12},{8,0},{12,4},{16,24},{20,28},{24,16},{28,20},{1,9},{5... | collective-permute-start | bytes 344072 | tf_op jit(solution)/shard_map/ppermute | solution.py:220
  35.2 7.4 %collective-permute-start.20 = (f32[16,1792]{1,0:T(8,128)S(1)}, f32[16,1792]{1,0:T(8,128)S(1)}, u32[]{:S(2)}, u32[]{:S(2)}) collective-permute-start(f32[16,1792]{1,0:T(8,128)S(1)} %get-tuple-element.77), channel_id=1, source_target_pairs={{0,8},{4,12},{8,0},{12,4},{16,24},{20,28},{24,16},{28,20},{1,9},{5... | collective-permute-start | bytes 344072 | tf_op jit(solution)/shard_map/ppermute | solution.py:220
  35.3 1.4 %collective-permute-start.14 = (f32[32,1024]{1,0:T(8,128)S(1)}, f32[32,1024]{1,0:T(8,128)S(1)}, u32[]{:S(2)}, u32[]{:S(2)}) collective-permute-start(f32[32,1024]{1,0:T(8,128)S(1)} %get-tuple-element.69.refs_0_.refs_4_.refs_6_), channel_id=1, source_target_pairs={{0,1},{1,0},{2,3},{3,2},{4,5},{5,4},{6,7},{7,6},{8,9},{9,8},{10,11... | collective-permute-start | bytes 393224 | tf_op jit(solution)/shard_map/ppermute | solution.py:220
  35.4 1.5 %collective-permute-start.15 = (f32[32,1024]{1,0:T(8,128)S(1)}, f32[32,1024]{1,0:T(8,128)S(1)}, u32[]{:S(2)}, u32[]{:S(2)}) collective-permute-start(f32[32,1024]{1,0:T(8,128)S(1)} %get-tuple-element.70.refs_1_.refs_7_), channel_id=1, source_target_pairs={{0,1},{1,0},{2,3},{3,2},{4,5},{5,4},{6,7},{7,6},{8,9},{9,8},{10,11... | collective-permute-start | bytes 393224 | tf_op jit(solution)/shard_map/ppermute | solution.py:220
  37.7 11.7 %collective-permute-start.16 = (f32[32,1792]{1,0:T(8,128)S(1)}, f32[32,1792]{1,0:T(8,128)S(1)}, u32[]{:S(2)}, u32[]{:S(2)}) collective-permute-start(f32[32,1792]{1,0:T(8,128)S(1)} %get-tuple-element.72), channel_id=1, source_target_pairs={{0,4},{4,0},{8,12},{12,8},{16,20},{20,16},{24,28},{28,24},{1,5},{5... | collective-permute-start | bytes 688136 | tf_op jit(solution)/shard_map/ppermute | solution.py:220
  40.9 5.5 %collective-permute-start.18 = (f32[16,1792]{1,0:T(8,128)S(1)}, f32[16,1792]{1,0:T(8,128)S(1)}, u32[]{:S(2)}, u32[]{:S(2)}) collective-permute-start(f32[16,1792]{1,0:T(8,128)S(1)} %get-tuple-element.75), channel_id=1, source_target_pairs={{0,8},{4,12},{8,0},{12,4},{16,24},{20,28},{24,16},{28,20},{1,9},{5... | collective-permute-start | bytes 344072 | tf_op jit(solution)/shard_map/ppermute | solution.py:220
  42.7 8.6 %collective-permute-start.21 = (f32[8,1792]{1,0:T(8,128)S(1)}, f32[8,1792]{1,0:T(8,128)S(1)}, u32[]{:S(2)}, u32[]{:S(2)}) collective-permute-start(f32[8,1792]{1,0:T(8,128)S(1)} %get-tuple-element.83), channel_id=1, source_target_pairs={{0,16},{4,20},{8,24},{12,28},{16,0},{20,4},{24,8},{28,12},{1,17},{... | collective-permute-start | bytes 172040 | tf_op jit(solution)/shard_map/ppermute | solution.py:220
  45.3 10.5 %collective-permute-start.22 = (f32[8,1792]{1,0:T(8,128)S(1)}, f32[8,1792]{1,0:T(8,128)S(1)}, u32[]{:S(2)}, u32[]{:S(2)}) collective-permute-start(f32[8,1792]{1,0:T(8,128)S(1)} %get-tuple-element.84), channel_id=1, source_target_pairs={{0,16},{4,20},{8,24},{12,28},{16,0},{20,4},{24,8},{28,12},{1,17},{... | collective-permute-start | bytes 172040 | tf_op jit(solution)/shard_map/ppermute | solution.py:220
  46.4 9.4 %collective-permute-start.23 = (f32[8,1792]{1,0:T(8,128)S(1)}, f32[8,1792]{1,0:T(8,128)S(1)}, u32[]{:S(2)}, u32[]{:S(2)}) collective-permute-start(f32[8,1792]{1,0:T(8,128)S(1)} %get-tuple-element.85), channel_id=1, source_target_pairs={{0,16},{4,20},{8,24},{12,28},{16,0},{20,4},{24,8},{28,12},{1,17},{... | collective-permute-start | bytes 172040 | tf_op jit(solution)/shard_map/ppermute | solution.py:220
  49.4 8.2 %collective-permute-start.24 = (f32[8,1792]{1,0:T(8,128)S(1)}, f32[8,1792]{1,0:T(8,128)S(1)}, u32[]{:S(2)}, u32[]{:S(2)}) collective-permute-start(f32[8,1792]{1,0:T(8,128)S(1)} %get-tuple-element.86), channel_id=1, source_target_pairs={{0,16},{4,20},{8,24},{12,28},{16,0},{20,4},{24,8},{28,12},{1,17},{... | collective-permute-start | bytes 172040 | tf_op jit(solution)/shard_map/ppermute | solution.py:220
  49.6 8.1 %collective-permute-start.25 = (f32[8,1792]{1,0:T(8,128)S(1)}, f32[8,1792]{1,0:T(8,128)S(1)}, u32[]{:S(2)}, u32[]{:S(2)}) collective-permute-start(f32[8,1792]{1,0:T(8,128)S(1)} %get-tuple-element.87), channel_id=1, source_target_pairs={{0,8},{4,12},{8,0},{12,4},{16,24},{20,28},{24,16},{28,20},{1,9},{5... | collective-permute-start | bytes 172040 | tf_op jit(solution)/shard_map/ppermute | solution.py:220
  51.2 6.4 %collective-permute-start.26 = (f32[8,1792]{1,0:T(8,128)S(1)}, f32[8,1792]{1,0:T(8,128)S(1)}, u32[]{:S(2)}, u32[]{:S(2)}) collective-permute-start(f32[8,1792]{1,0:T(8,128)S(1)} %get-tuple-element.88), channel_id=1, source_target_pairs={{0,24},{4,28},{8,16},{12,20},{16,8},{20,12},{24,0},{28,4},{1,25},{... | collective-permute-start | bytes 172040 | tf_op jit(solution)/shard_map/ppermute | solution.py:220
